TPU v7x, 32 devices: a whole 2x2x4 slice. The times are simulated.
32 devices in a mesh: dp: 2 (over core), ret: 4 (over y, x), ctx: 4 (over z).
Axes of the slice: x: 2, y: 2, z: 4, core: 2. Of those that a mesh axis runs over, the one named last changes fastest.
Arguments:
- queries: bfloat16 [2, 2048, 4096], P('dp', 'ret', 'ctx'), may hold values from -6 to 6
- enc_states: bfloat16 [2, 8192, 896], P('dp', 'ret'), may hold values from -1600 to 1600
- w_key: bfloat16 [896, 4096], P(None, 'ctx'), may hold values from -0.1875 to 0.1875
- w_value: bfloat16 [896, 4096], P(None, 'ctx'), may hold values from -0.59765625 to 0.59765625
- shard_ids: int32 [2, 32, 2], P('dp', 'ret'), may hold values from 0 to 3, all different within a row; in each aligned block of 8 rows (0 to 7, 8 to 15, ..., all dimensions but the last counted through in order) at most 8 rows name the same one
- row_ids: int32 [2, 32, 2], P('dp', 'ret'), may hold values from 0 to 15
- grad_out: bfloat16 [2, 2048, 4096], P('dp', 'ret', 'ctx'), may hold values from -6 to 6
Outputs:
- attended: bfloat16 [2, 2048, 4096], P('dp', 'ret', 'ctx')
- grad_queries: bfloat16 [2, 2048, 4096], P('dp', 'ret', 'ctx')
- grad_w_key: float32 [896, 4096], P(('dp', 'ret'), 'ctx')
- grad_w_value: float32 [896, 4096], P(('dp', 'ret'), 'ctx')
Inputs may be any that keep to these rules, and one draw needn't show every extreme that they name: `shard_ids`: each block names 2 different shards; among the 8 blocks that one index of ret holds, no shard is named by more than 8 blocks, a bound that some block reaches.
All inputs are finite; a program needn't handle non-finite values.
Results may differ from a plain program's by a relative error of at most 0.019.
Values may be sent and summed in bfloat16 or wider, within the bound.
No kernel may reach another device: no remote copies, remote signals or barrier semaphores. Data moves between devices by JAX's collectives and lax.ppermute only.
A program may use at most 128 MiB of HBM per device.

v0:
```python
import math

import jax
import jax.numpy as jnp
from jax import lax
from jax.sharding import PartitionSpec as P

HEAD_DIM = 128
NEIGH_LEN = 128
NEIGHBOURS = 2


def normalize_rows(states):
    floats = states.astype(jnp.float32)
    mean_square = jnp.mean(floats * floats, axis=-1, keepdims=True)
    return (floats * lax.rsqrt(mean_square + 1e-06)).astype(jnp.bfloat16)


def contract_rows(lhs_rows, rhs_rows):
    return lax.dot_general(
        lhs_rows, rhs_rows, (((0,), (0,)), ((), ())), preferred_element_type=jnp.float32
    )


def attend(query_block, key_block, value_block, grad_block):
    score_scale = 1.0 / math.sqrt(HEAD_DIM)
    scores = (
        jnp.einsum("cthd,cjhd->chtj", query_block, key_block, preferred_element_type=jnp.float32)
        * score_scale
    )
    exponent = jnp.exp(scores)
    denominator = jnp.sum(exponent, axis=-1)
    numerator = jnp.einsum(
        "chtj,cjhd->cthd",
        exponent.astype(jnp.bfloat16),
        value_block,
        preferred_element_type=jnp.float32,
    )
    output = numerator / jnp.transpose(denominator, (0, 2, 1))[..., None]
    prob_grad = jnp.einsum(
        "cthd,cjhd->chtj", grad_block, value_block, preferred_element_type=jnp.float32
    )
    row_delta = jnp.transpose(jnp.sum(grad_block.astype(jnp.float32) * output, axis=-1), (0, 2, 1))
    probability = exponent / denominator[..., None]
    score_grad = (probability * (prob_grad - row_delta[..., None]) * score_scale).astype(
        jnp.bfloat16
    )
    grad_query = jnp.einsum(
        "chtj,cjhd->cthd", score_grad, key_block, preferred_element_type=jnp.float32
    ).astype(jnp.bfloat16)
    grad_key = jnp.einsum(
        "chtj,cthd->cjhd", score_grad, query_block, preferred_element_type=jnp.float32
    ).astype(jnp.bfloat16)
    grad_value = jnp.einsum(
        "chtj,cthd->cjhd",
        probability.astype(jnp.bfloat16),
        grad_block,
        preferred_element_type=jnp.float32,
    ).astype(jnp.bfloat16)
    return (output.astype(jnp.bfloat16), grad_query, grad_key, grad_value)


def local(queries, enc_states, w_key, w_value, shard_ids, row_ids, grad_out):
    n_ret = lax.axis_size("ret")
    me_index = lax.axis_index("ret")
    blocks = shard_ids.shape[1]
    request_count = blocks * NEIGHBOURS
    capacity = request_count * 2 // n_ret
    feat_width = queries.shape[2]
    head_count = feat_width // HEAD_DIM
    db_dev = enc_states.shape[1] // NEIGH_LEN
    enc_width = enc_states.shape[2]
    context_rows = NEIGHBOURS * NEIGH_LEN
    every_shard, every_row = (
        lax.all_gather(shard_ids, "ret", axis=1, tiled=True),
        lax.all_gather(row_ids, "ret", axis=1, tiled=True),
    )
    req_shard = every_shard.reshape(n_ret, request_count)
    req_row = every_row.reshape(n_ret, request_count)
    positions = jnp.arange(request_count, dtype=jnp.int32)
    earlier = positions[None, :] < positions[:, None]
    same_shard = req_shard[:, :, None] == req_shard[:, None, :]
    slot_rank = jnp.sum((same_shard & earlier[None]).astype(jnp.int32), axis=2)
    own_shard = shard_ids.reshape(request_count)
    own_same = own_shard[:, None] == own_shard[None, :]
    own_rank = jnp.sum((own_same & earlier).astype(jnp.int32), axis=1)
    own_slot = own_shard * capacity + own_rank
    slot_iota = jnp.arange(capacity, dtype=jnp.int32)
    select = (req_shard[:, None, :] == me_index) & (
        slot_rank[:, None, :] == slot_iota[None, :, None]
    )
    filled = jnp.any(select, axis=2).reshape(-1)
    row_for = jnp.sum(jnp.where(select, req_row[:, None, :], 0), axis=2).reshape(-1)
    normed = normalize_rows(enc_states[0])
    normed_rows = normed.reshape(db_dev, NEIGH_LEN, enc_width)
    query_blocks = queries[0].reshape(blocks, -1, head_count, HEAD_DIM)
    grad_blocks = grad_out[0].reshape(blocks, -1, head_count, HEAD_DIM)
    both_weights = jnp.concatenate([w_key, w_value], axis=1)
    projected = jnp.dot(normed, both_weights, preferred_element_type=jnp.float32).astype(
        jnp.bfloat16
    )
    kv_table = projected.reshape(db_dev, NEIGH_LEN, 2 * feat_width)
    picked = jnp.take(kv_table, row_for, axis=0)
    outgoing = jnp.where(filled[:, None, None], picked, jnp.zeros_like(picked))
    outgoing = outgoing.reshape(n_ret, capacity, NEIGH_LEN, 2 * feat_width)
    incoming = lax.all_to_all(outgoing, "ret", split_axis=0, concat_axis=0, tiled=True)
    own_rows = jnp.take(
        incoming.reshape(n_ret * capacity, NEIGH_LEN, 2 * feat_width), own_slot, axis=0
    )
    own_rows = own_rows.reshape(blocks, context_rows, 2, head_count, HEAD_DIM)
    attended, grad_query, grad_key, grad_value = attend(
        query_blocks, own_rows[:, :, 0], own_rows[:, :, 1], grad_blocks
    )
    returned_grads = jnp.concatenate(
        [
            grad_key.reshape(request_count, NEIGH_LEN, feat_width),
            grad_value.reshape(request_count, NEIGH_LEN, feat_width),
        ],
        axis=2,
    )
    grad_slots = jnp.zeros((n_ret * capacity, NEIGH_LEN, 2 * feat_width), jnp.bfloat16)
    grad_slots = grad_slots.at[own_slot].set(returned_grads)
    arrived = lax.all_to_all(
        grad_slots.reshape(n_ret, capacity, NEIGH_LEN, 2 * feat_width),
        "ret",
        split_axis=0,
        concat_axis=0,
        tiled=True,
    )
    state_rows = jnp.take(normed_rows, row_for, axis=0)
    partial_value = contract_rows(
        state_rows.reshape(-1, enc_width), arrived.reshape(-1, 2 * feat_width)
    )
    summed = lax.psum_scatter(
        partial_value.astype(jnp.bfloat16), ("dp", "ret"), scatter_dimension=0, tiled=True
    ).astype(jnp.float32)
    grad_w_key = summed[:, :feat_width]
    grad_w_value = summed[:, feat_width:]
    return (
        attended.reshape(1, -1, feat_width),
        grad_query.reshape(1, -1, feat_width),
        grad_w_key,
        grad_w_value,
    )


def solution(mesh):
    placed = (
        P("dp", "ret", "ctx"),
        P("dp", "ret", None),
        P(None, "ctx"),
        P(None, "ctx"),
        P("dp", "ret", None),
        P("dp", "ret", None),
        P("dp", "ret", "ctx"),
    )
    return jax.shard_map(
        local,
        mesh=mesh,
        in_specs=placed,
        out_specs=(
            P("dp", "ret", "ctx"),
            P("dp", "ret", "ctx"),
            P(("dp", "ret"), "ctx"),
            P(("dp", "ret"), "ctx"),
        ),
        check_vma=False,
    )
```

profile of v0, /device:TPU:0, one launch (start us, length us, event | category | flops | bytes accessed | tf_op | source)
XLA Modules:
  0.0 620.7 jit_solution(1953729308087946052)
XLA Ops:
  7.2 0.8 copy.50
  7.9 0.8 copy.51
  8.7 9.6 %all_gather.6 = s32[1,32,2]{2,0,1:T(1,128)S(1)} all-gather(s32[1,8,2]{2,0,1:T(1,128)S(1)} %copy.50), channel_id=1, replica_groups=mesh['dp'=2,'ret'=4,'ctx'=4] {'ret'}, dimensions={1}, use_global_device_ids=true | all-gather | bytes 320 | tf_op jit(solution)/shard_map/all_gather | solution.py:75
  18.3 0.5 broadcast.207
  18.8 0.7 reduce.7
  19.5 0.1 broadcast_in_dim_reshape.2
  19.6 0.2 convert_reduce_fusion
  19.8 8.1 %all_gather.7 = s32[1,32,2]{2,0,1:T(1,128)S(1)} all-gather(s32[1,8,2]{2,0,1:T(1,128)S(1)} %copy.51), channel_id=1, replica_groups=mesh['dp'=2,'ret'=4,'ctx'=4] {'ret'}, dimensions={1}, use_global_device_ids=true | all-gather | bytes 320 | tf_op jit(solution)/shard_map/all_gather | solution.py:76
  27.9 0.7 reduce.6
  28.6 0.1 broadcast_in_dim.70
  28.7 0.1 fusion.24
  28.9 0.2 select_reduce_fusion
  29.0 0.1 reshape.212
  29.1 2.8 fusion
  32.0 13.7 %convolution_convert_fusion = bf16[2048,2048]{1,0:T(8,128)(2,1)} fusion(bf16[896,1024]{1,0:T(8,128)(2,1)} %param.10, bf16[896,1024]{1,0:T(8,128)(2,1)} %param.9, bf16[1,2048,896]{2,1,0:T(8,128)(2,1)} %param.8, f32[2048]{0:T(1024)S(1)} %get-tuple-element.9), kind=kOutput, calls=%fused_computation.7 | convolution fusion | flops 7533232128 | bytes 15736832 | tf_op jit(solution)/shard_map/dot_general | solution.py:99
  45.7 10.5 %gather_fusion = bf16[32,128,2048]{2,1,0:T(8,128)(2,1)} fusion(bf16[16,128,2048]{2,1,0:T(8,128)(2,1)} %bitcast.113, s32[1024]{0:T(1024)S(1)} %pad_clamp_fusion.1), kind=kCustom, calls=%fused_computation | custom fusion | bytes 33554560 | tf_op jit(solution)/shard_map/jit(_take)/gather | solution.py:103
  56.2 14.2 %select_select_fusion = bf16[4,8,128,2048]{3,2,1,0:T(8,128)(2,1)} fusion(bf16[4,8,128,2048]{3,2,1,0:T(8,128)(2,1)} %bitcast.110, pred[4,8]{1,0:T(4,128)(4,1)S(1)} %compare_and_fusion.1, pred[4,8]{1,0:T(4,128)(4,1)S(1)} %fusion.24), kind=kLoop, calls=%fused_computation.4 | loop fusion | flops 16777216 | bytes 33554496 | tf_op jit(solution)/shard_map/jit(_where)/select_n | solution.py:104
  70.4 7.3 %all-to-all-start = ((bf16[4,8,128,2048]{3,2,1,0:T(8,128)(2,1)}), bf16[4,8,128,2048]{3,2,1,0:T(8,128)(2,1)}, u32[]{:S(2)}, u32[]{:S(2)}) async-start(bf16[4,8,128,2048]{3,2,1,0:T(8,128)(2,1)} %select_select_fusion), calls=%async_computation | async-start | bytes 33554432 | tf_op jit(solution)/shard_map/all_to_all | solution.py:106
  77.7 0.0 copy-done.4
  77.7 0.1 copy.48
  77.8 0.1 copy.52
  77.9 0.1 mul.53
  78.0 0.1 reshape.210
  78.1 0.2 convert_reduce_fusion.1
  78.3 0.1 reduce_sum.59
  78.3 0.1 copy.49
  78.4 0.0 copy-done.1
  78.4 0.3 copy.64
  78.7 0.0 copy-done.2
  78.7 0.3 copy.65
  79.0 0.0 copy-start.3
  79.0 0.1 broadcast_bitcast_fusion
  79.1 176.9 %all-to-all-done = bf16[4,8,128,2048]{3,2,1,0:T(8,128)(2,1)} async-done(((bf16[4,8,128,2048]{3,2,1,0:T(8,128)(2,1)}), bf16[4,8,128,2048]{3,2,1,0:T(8,128)(2,1)}, u32[]{:S(2)}, u32[]{:S(2)}) %all-to-all-start) | async-done | bytes 16777248 | tf_op jit(solution)/shard_map/all_to_all | solution.py:106
  256.0 10.5 %gather_fusion.1 = bf16[16,128,2048]{2,1,0:T(8,128)(2,1)} fusion(bf16[32,128,2048]{2,1,0:T(8,128)(2,1)} %bitcast.6, s32[1024]{0:T(1024)S(1)} %pad_clamp_fusion), kind=kCustom, calls=%fused_computation.1 | custom fusion | bytes 16777280 | tf_op jit(solution)/shard_map/jit(_take)/gather | solution.py:107
  266.5 9.8 %copy.63 = bf16[256,8,16,128]{3,2,1,0:T(8,128)(2,1)} copy(bf16[256,8,16,128]{3,1,2,0:T(8,128)(2,1)} %bitcast.111) | data formatting | bytes 16777216
  276.3 5.9 copy_select_fusion
  282.2 1.7 bitcast_reduce_fusion
  283.9 2.5 convert_bitcast_fusion
  286.4 2.3 multiply_reduce_fusion
  288.8 2.9 fusion.3
  291.7 4.8 copy.62
  296.5 7.3 %reshape.218 = bf16[16,128,1024]{2,1,0:T(8,128)(2,1)} reshape(bf16[8,256,8,128]{3,2,1,0:T(8,128)(2,1)} %copy.62) | data formatting | bytes 8388608 | tf_op jit(solution)/shard_map/reshape | solution.py:117
  303.8 1.3 convert_bitcast_fusion.1
  305.1 4.8 copy.60
  309.9 7.3 %reshape.217 = bf16[16,128,1024]{2,1,0:T(8,128)(2,1)} reshape(bf16[8,256,8,128]{3,2,1,0:T(8,128)(2,1)} %copy.60) | data formatting | bytes 8388608 | tf_op jit(solution)/shard_map/reshape | solution.py:116
  317.2 8.2 %pad_maximum_fusion = bf16[16,128,2048]{2,1,0:T(8,128)(2,1)} fusion(bf16[16,128,1024]{2,1,0:T(8,128)(2,1)} %reshape.218, bf16[16,128,1024]{2,1,0:T(8,128)(2,1)} %reshape.217), kind=kLoop, calls=%fused_computation.5 | loop fusion | flops 16777216 | bytes 16777216 | tf_op jit(solution)/shard_map/concatenate | solution.py:114
  325.3 6.0 broadcast.174
  331.3 21.4 %scatter_fusion = bf16[32,128,2048]{2,1,0:T(8,128)(2,1)} fusion(bf16[32,128,2048]{2,1,0:T(8,128)(2,1)} %broadcast.174, s32[16]{0:T(128)S(1)} %fusion.26, bf16[16,128,2048]{2,1,0:T(8,128)(2,1)} %pad_maximum_fusion), kind=kCustom, calls=%fused_computation.3 | custom fusion | bytes 25165888 | tf_op jit(solution)/shard_map/scatter | solution.py:122
  352.7 7.0 %all-to-all-start.1 = ((bf16[4,8,128,2048]{3,2,1,0:T(8,128)(2,1)}), bf16[4,8,128,2048]{3,2,1,0:T(8,128)(2,1)}, u32[]{:S(2)}, u32[]{:S(2)}) async-start(bf16[4,8,128,2048]{3,2,1,0:T(8,128)(2,1)} %bitcast.109), calls=%async_computation.1 | async-start | bytes 33554432 | tf_op jit(solution)/shard_map/all_to_all | solution.py:123
  359.6 0.0 reduce-scatter.2.cloned.1.call-start
  359.7 0.1 reshape.216
  359.8 4.5 multiply_convert_fusion
  364.3 6.4 %gather_fusion.2 = bf16[32,128,896]{2,1,0:T(8,128)(2,1)} fusion(bf16[16,128,896]{2,1,0:T(8,128)(2,1)} %multiply_convert_fusion, s32[1024]{0:T(1024)S(1)} %pad_clamp_fusion.1), kind=kCustom, calls=%fused_computation.2 | custom fusion | bytes 14680192 | tf_op jit(solution)/shard_map/jit(_take)/gather | solution.py:130
  370.7 6.9 %broadcast_select_fusion = bf16[32,128,896]{2,1,0:T(8,128)(2,1)} fusion(bf16[32,128,896]{2,1,0:T(8,128)(2,1)} %gather_fusion.2, pred[32]{0:T(512)(128)(4,1)S(1)} %compare_and_fusion), kind=kLoop, calls=%fused_computation.13 | loop fusion | flops 3670016 | bytes 14680096 | tf_op jit(solution)/shard_map/jit(_take)/select_n | solution.py:130
  377.5 163.8 %all-to-all-done.1 = bf16[4,8,128,2048]{3,2,1,0:T(8,128)(2,1)} async-done(((bf16[4,8,128,2048]{3,2,1,0:T(8,128)(2,1)}), bf16[4,8,128,2048]{3,2,1,0:T(8,128)(2,1)}, u32[]{:S(2)}, u32[]{:S(2)}) %all-to-all-start.1) | async-done | bytes 16777248 | tf_op jit(solution)/shard_map/all_to_all | solution.py:123
  541.3 21.3 %convolution_convert_fusion.1 = bf16[896,2048]{1,0:T(8,128)(2,1)} fusion(bf16[4096,896]{1,0:T(8,128)(2,1)} %bitcast.115, bf16[4096,2048]{1,0:T(8,128)(2,1)} %bitcast.23), kind=kOutput, calls=%fused_computation.34 | convolution fusion | flops 15034220544 | bytes 27787264 | tf_op jit(solution)/shard_map/dot_general | solution.py:20
  562.6 0.0 reduce-scatter.2.cloned.1.call-update
  562.7 1.9 copy.55
  564.6 1.3 reshape.214
  565.8 3.0 fusion.17
  568.9 0.7 copy.58
  569.6 1.3 reshape.215
  570.9 41.0 %reduce-scatter.2.cloned.1.call-done = bf16[112,2048]{1,0:T(8,128)(2,1)} async-done(((bf16[896,2048]{1,0:T(8,128)(2,1)}), bf16[112,2048]{1,0:T(8,128)(2,1)}) %reduce-scatter.2.cloned.1.call-update) | async-done | bytes 458768 | tf_op jit(solution)/shard_map/reduce_scatter | solution.py:134
  611.8 2.1 fusion.31
  (17 shorter events, 0.1 us)
Async XLA Ops:
  70.4 7.3 %copy-start.4 = (s32[1,8,2]{1,2,0:T(2,128)S(1)}, s32[1,8,2]{1,2,0:T(2,128)}, u32[]{:S(2)}) copy-start(s32[1,8,2]{1,2,0:T(2,128)} %param.11) | copy-start | bytes 196
  70.4 8.0 %copy-start.1 = (bf16[1,512,1024]{2,1,0:T(8,128)(2,1)S(1)}, bf16[1,512,1024]{2,1,0:T(8,128)(2,1)}, u32[]{:S(2)}) copy-start(bf16[1,512,1024]{2,1,0:T(8,128)(2,1)} %param.7) | copy-start | bytes 3145732
  70.4 8.3 %copy-start.2 = (bf16[1,512,1024]{2,1,0:T(8,128)(2,1)S(1)}, bf16[1,512,1024]{2,1,0:T(8,128)(2,1)}, u32[]{:S(2)}) copy-start(bf16[1,512,1024]{2,1,0:T(8,128)(2,1)} %param.13) | copy-start | bytes 3145732
  70.4 185.6 %all-to-all-start = ((bf16[4,8,128,2048]{3,2,1,0:T(8,128)(2,1)}), bf16[4,8,128,2048]{3,2,1,0:T(8,128)(2,1)}, u32[]{:S(2)}, u32[]{:S(2)}) async-start(bf16[4,8,128,2048]{3,2,1,0:T(8,128)(2,1)} %select_select_fusion), calls=%async_computation | async-start | bytes 33554432 | tf_op jit(solution)/shard_map/all_to_all | solution.py:106
  79.0 207.4 %copy-start.3 = (bf16[64,8,8,128]{3,2,1,0:T(8,128)(2,1)}, bf16[64,8,8,128]{3,2,1,0:T(8,128)(2,1)S(1)}, u32[]{:S(2)}) copy-start(bf16[64,8,8,128]{3,2,1,0:T(8,128)(2,1)S(1)} %copy.65) | copy-start | bytes 3145732
  282.2 6.5 %copy-start = (bf16[8,256,2,8,128]{4,1,3,0,2:T(8,128)(2,1)}, bf16[8,256,2,8,128]{4,1,3,0,2:T(8,128)(2,1)S(1)}, u32[]{:S(2)}) copy-start(bf16[8,256,2,8,128]{4,1,3,0,2:T(8,128)(2,1)S(1)} %copy_select_fusion) | copy-start | bytes 25165828
  352.7 188.7 %all-to-all-start.1 = ((bf16[4,8,128,2048]{3,2,1,0:T(8,128)(2,1)}), bf16[4,8,128,2048]{3,2,1,0:T(8,128)(2,1)}, u32[]{:S(2)}, u32[]{:S(2)}) async-start(bf16[4,8,128,2048]{3,2,1,0:T(8,128)(2,1)} %bitcast.109), calls=%async_computation.1 | async-start | bytes 33554432 | tf_op jit(solution)/shard_map/all_to_all | solution.py:123
  359.6 252.2 %reduce-scatter.2.cloned.1.call-start = ((), (), s32[]{:S(2)}) async-start(), calls=%async_computation.3 | async-start | bytes 4128768 | tf_op jit(solution)/shard_map/reduce_scatter | solution.py:134
Sparse Core Ops, SparseCore 0:
  562.8 49.0 reduce-scatter.1
where the time goes:
time: 622 us; the launch traced here: 621 us
  waiting for transfers between devices  382 us (61%)
  local copies, waits for them, and re-layouts  99.4 us (16%)
  matrix products  48.8 us (8%)
  other arithmetic  44.6 us (7%)
  blocking collectives  17.7 us (3%)
  starting transfers between devices  14.3 us (2%)
  between operations  14.3 us (2%)
    all_to_all x1, waiting for transfers between devices, local(): lax.all_to_all(outgoing, 'ret', split_axis=0, concat_axis=0, tiled=True)  177 us
    all_to_all x1, waiting for transfers between devices, local(): lax.all_to_all(grad_slots.reshape(n_ret, capacity, NEIGH_LEN, 2 * feat_wi...  164 us
    reduce_scatter x1, waiting for transfers between devices, local(): lax.psum_scatter(partial_value.astype(jnp.bfloat16), ('dp', 'ret'), scatt...  41 us
    scatter x1, local copies, waits for them, and re-layouts, local(): grad_slots = grad_slots.at[own_slot].set(returned_grads)  21.4 us
    dot_general x1, matrix products, contract_rows(): lax.dot_general(lhs_rows, rhs_rows, (((0,), (0,)), ((), ())), preferred_e...  21.3 us
    select_n x1, other arithmetic, local(): outgoing = jnp.where(filled[:, None, None], picked, jnp.zeros_like(picked))  14.2 us
    dot_general x1, matrix products, local(): jnp.dot(normed, both_weights, preferred_element_type=jnp.float32)  13.7 us
  transfers between devices with their start and end apart: 3, of which 3 were waited for; matrix products, arithmetic and copies ran while one was open for 4% of the time, Pallas kernels for 0%

commit v1 on v0

v1 whole, which is shorter than its diff:
```python
import functools
import math

import jax
import jax.numpy as jnp
from jax import lax
from jax.experimental import pallas as pl
from jax.experimental.pallas import tpu as pltpu
from jax.sharding import PartitionSpec as P

HEAD_DIM = 128
NEIGH_LEN = 128
NEIGHBOURS = 2
VMEM_BYTES = 56 * 1024 * 1024

F32 = jnp.float32
BF16 = jnp.bfloat16


def contract(lhs, rhs, dims):
    return lax.dot_general(lhs, rhs, (dims, ((), ())), preferred_element_type=F32)


def normalize_rows(states):
    floats = states.astype(F32)
    mean_square = jnp.mean(floats * floats, axis=-1, keepdims=True)
    return (floats * lax.rsqrt(mean_square + 1e-06)).astype(BF16)


def block_grads(context, wk_ref, wv_ref, q_ref, go_ref, out_ref, gq_ref, dk_ref, dv_ref):
    score_scale = 1.0 / math.sqrt(HEAD_DIM)
    keys = jnp.dot(context, wk_ref[...], preferred_element_type=F32).astype(BF16)
    values = jnp.dot(context, wv_ref[...], preferred_element_type=F32).astype(BF16)
    for head in range(q_ref.shape[1] // HEAD_DIM):
        cols = slice(head * HEAD_DIM, (head + 1) * HEAD_DIM)
        key, value, query, grad = keys[:, cols], values[:, cols], q_ref[:, cols], go_ref[:, cols]
        expo = jnp.exp(contract(query, key, ((1,), (1,))) * score_scale)
        inverse = 1.0 / jnp.sum(expo, axis=-1, keepdims=True)
        output = jnp.dot(expo.astype(BF16), value, preferred_element_type=F32) * inverse
        out_ref[:, cols] = output.astype(BF16)
        dprob = contract(grad, value, ((1,), (1,)))
        delta = jnp.sum(grad.astype(F32) * output, axis=-1, keepdims=True)
        probs = expo * inverse
        dscore = (probs * (dprob - delta) * score_scale).astype(BF16)
        gq_ref[:, cols] = jnp.dot(dscore, key, preferred_element_type=F32).astype(BF16)
        dk_ref[:, cols] = contract(dscore, query, ((0,), (0,))).astype(BF16)
        dv_ref[:, cols] = contract(probs.astype(BF16), grad, ((0,), (0,))).astype(BF16)


def attend_kernel(
    slot_ref, first_ref, second_ref, wk_ref, wv_ref, q_ref, go_ref,
    out_ref, gq_ref, dwk_ref, dwv_ref, acck, accv, dk_ref, dv_ref,
):
    step = pl.program_id(0)

    @pl.when(step == 0)
    def _():
        acck[...] = jnp.zeros_like(acck)
        accv[...] = jnp.zeros_like(accv)

    width = first_ref.shape[-1]
    context = jnp.concatenate([first_ref[...].reshape(-1, width), second_ref[...].reshape(-1, width)], axis=0)
    block_grads(context, wk_ref, wv_ref, q_ref, go_ref, out_ref, gq_ref, dk_ref, dv_ref)
    acck[...] += contract(context, dk_ref[...], ((0,), (0,)))
    accv[...] += contract(context, dv_ref[...], ((0,), (0,)))

    @pl.when(step == pl.num_programs(0) - 1)
    def _():
        dwk_ref[...] = acck[...].astype(dwk_ref.dtype)
        dwv_ref[...] = accv[...].astype(dwv_ref.dtype)


def attend(incoming, slots, wk, wv, queries, grad_out):
    count = slots.shape[0]
    tokens, feat = queries.shape[0] // count, queries.shape[1]
    enc = wk.shape[0]
    whole = lambda shape: pl.BlockSpec(shape, lambda b, s: (0, 0))
    row_spec = pl.BlockSpec((tokens, feat), lambda b, s: (b, 0))
    neigh = lambda n: pl.BlockSpec((1, NEIGH_LEN, enc), lambda b, s: (s[b, n], 0, 0))
    return pl.pallas_call(
        attend_kernel,
        grid_spec=pltpu.PrefetchScalarGridSpec(
            num_scalar_prefetch=1,
            grid=(count,),
            in_specs=[neigh(0), neigh(1), whole((enc, feat)), whole((enc, feat)), row_spec, row_spec],
            out_specs=[row_spec, row_spec, whole((enc, feat)), whole((enc, feat))],
            scratch_shapes=[
                pltpu.VMEM((enc, feat), F32),
                pltpu.VMEM((enc, feat), F32),
                pltpu.VMEM((NEIGHBOURS * NEIGH_LEN, feat), BF16),
                pltpu.VMEM((NEIGHBOURS * NEIGH_LEN, feat), BF16),
            ],
        ),
        out_shape=[
            jax.ShapeDtypeStruct(queries.shape, BF16),
            jax.ShapeDtypeStruct(queries.shape, BF16),
            jax.ShapeDtypeStruct((enc, feat), BF16),
            jax.ShapeDtypeStruct((enc, feat), BF16),
        ],
        compiler_params=pltpu.CompilerParams(vmem_limit_bytes=VMEM_BYTES),
        name="attend_blocks",
    )(slots, incoming, incoming, wk, wv, queries, grad_out)


def pick_kernel(id_ref, normed_ref, out_ref):
    me = lax.axis_index("ret")
    for dest in range(out_ref.shape[0]):
        def body(req, used, dest=dest):
            mine = id_ref[dest, req, 0] == me

            @pl.when(mine)
            def _():
                out_ref[dest, used] = normed_ref[id_ref[dest, req, 1]]

            return used + jnp.where(mine, 1, 0)

        lax.fori_loop(0, id_ref.shape[1], body, jnp.int32(0))


def pick(ids, normed, capacity):
    n_ret = ids.shape[0]
    return pl.pallas_call(
        pick_kernel,
        in_specs=[pl.BlockSpec(memory_space=pltpu.SMEM), pl.BlockSpec(memory_space=pltpu.VMEM)],
        out_specs=pl.BlockSpec(memory_space=pltpu.VMEM),
        out_shape=jax.ShapeDtypeStruct((n_ret, capacity) + normed.shape[1:], BF16),
        compiler_params=pltpu.CompilerParams(vmem_limit_bytes=VMEM_BYTES),
        name="pick_rows",
    )(ids, normed)


def own_slots(shards, capacity):
    flat = shards.reshape(-1)
    place = jnp.arange(flat.shape[0], dtype=jnp.int32)
    earlier = (flat[:, None] == flat[None, :]) & (place[None, :] < place[:, None])
    return (flat * capacity + jnp.sum(earlier.astype(jnp.int32), axis=1)).reshape(shards.shape)


def local(queries, enc_states, w_key, w_value, shard_ids, row_ids, grad_out):
    n_ret = lax.axis_size("ret")
    blocks = shard_ids.shape[1]
    capacity = min(blocks, 2 * blocks * NEIGHBOURS // n_ret)
    enc = enc_states.shape[2]
    feat = queries.shape[2]
    own = jnp.stack([shard_ids[0], row_ids[0]], axis=-1).reshape(-1, 2)
    ids = lax.all_gather(own, "ret")
    normed = normalize_rows(enc_states[0]).reshape(-1, NEIGH_LEN, enc)
    outgoing = pick(ids, normed, capacity)
    incoming = lax.all_to_all(outgoing, "ret", split_axis=0, concat_axis=0, tiled=True)
    slots = own_slots(shard_ids[0], capacity)
    attended, grad_queries, dwk, dwv = attend(
        incoming.reshape(-1, NEIGH_LEN, enc), slots, w_key, w_value, queries[0], grad_out[0]
    )
    both = jnp.concatenate([dwk, dwv], axis=1)
    summed = lax.psum_scatter(both, ("dp", "ret"), scatter_dimension=0, tiled=True).astype(F32)
    return attended[None], grad_queries[None], summed[:, :feat], summed[:, feat:]


def solution(mesh):
    placed = (
        P("dp", "ret", "ctx"),
        P("dp", "ret", None),
        P(None, "ctx"),
        P(None, "ctx"),
        P("dp", "ret", None),
        P("dp", "ret", None),
        P("dp", "ret", "ctx"),
    )
    return jax.shard_map(
        local,
        mesh=mesh,
        in_specs=placed,
        out_specs=(
            P("dp", "ret", "ctx"),
            P("dp", "ret", "ctx"),
            P(("dp", "ret"), "ctx"),
            P(("dp", "ret"), "ctx"),
        ),
        check_vma=False,
    )
```

time: 622 us -> 232 us (0.37)
  waiting for transfers between devices: 382 us -> 127 us
  local copies, waits for them, and re-layouts: 99.4 us -> 4.7 us
  Pallas kernels: 0 us -> 57.9 us
  matrix products: 48.8 us -> 0 us
  other arithmetic: 44.6 us -> 12.4 us
  starting transfers between devices: 14.3 us -> 5.62 us
  blocking collectives: 17.7 us -> 9.51 us
    all_to_all x1 -> x0, waiting for transfers between devices: 164 us -> none  [local(): lax.all_to_all(grad_slots.reshape(n_ret, capacity, NEIGH_LEN, 2 * feat_wi...]
    all_to_all x1, waiting for transfers between devices: 177 us -> 78.3 us  [local(): lax.all_to_all(outgoing, 'ret', split_axis=0, concat_axis=0, tiled=True)]
    pallas_call x0 -> x2, Pallas kernels: none -> 57.9 us  [the longest x1 51.6 us: attend(): pl.pallas_call(attend_kernel, grid_spec=pltpu.PrefetchScalarGridSpec(num_...]
    dot_general x8 -> x0, matrix products: 48.8 us -> none  [the longest x1 21.3 us: contract_rows(): lax.dot_general(lhs_rows, rhs_rows, (((0,), (0,)), ((), ())), preferred_e...]
    gather x3 -> x0, local copies, waits for them, and re-layouts: 27.4 us -> none  [the longest x1 10.5 us: local(): jnp.take(incoming.reshape(n_ret * capacity, NEIGH_LEN, 2 * feat_width), o...]
    select_n x5 -> x0, other arithmetic: 27 us -> none  [the longest x1 14.2 us: local(): outgoing = jnp.where(filled[:, None, None], picked, jnp.zeros_like(picked))]
    scatter x1 -> x0, local copies, waits for them, and re-layouts: 21.4 us -> none  [local(): grad_slots = grad_slots.at[own_slot].set(returned_grads)]
    reshape x7 -> x0, local copies, waits for them, and re-layouts: 17.4 us -> none  [the longest x1 7.32 us: local(): grad_value.reshape(request_count, NEIGH_LEN, feat_width)]
  transfers between devices with their start and end apart: 3 -> 2, of which waited for: 3 -> 2; matrix products, arithmetic and copies ran while one was open for 4% -> 0% of each run, Pallas kernels for 0% -> 0%
where the time goes in v1:
time: 232 us
  waiting for transfers between devices  127 us (55%)
  Pallas kernels  57.9 us (25%)
  between operations  14.1 us (6%)
  other arithmetic  12.4 us (5%)
  blocking collectives  9.51 us (4%)
  starting transfers between devices  5.62 us (2%)
  local copies, waits for them, and re-layouts  4.7 us (2%)
    all_to_all x1, waiting for transfers between devices, local(): lax.all_to_all(outgoing, 'ret', split_axis=0, concat_axis=0, tiled=True)  78.3 us
    pallas_call x1, Pallas kernels, attend(): pl.pallas_call(attend_kernel, grid_spec=pltpu.PrefetchScalarGridSpec(num_...  51.6 us
    reduce_scatter x1, waiting for transfers between devices, local(): lax.psum_scatter(both, ('dp', 'ret'), scatter_dimension=0, tiled=True)  49.1 us
    all_gather x1, blocking collectives, local(): ids = lax.all_gather(own, 'ret')  9.51 us
    pallas_call x1, Pallas kernels, pick(): pl.pallas_call(pick_kernel, in_specs=[pl.BlockSpec(memory_space=pltpu.SME...  6.26 us
    all_to_all x1, starting transfers between devices, local(): lax.all_to_all(outgoing, 'ret', split_axis=0, concat_axis=0, tiled=True)  5.58 us
  transfers between devices with their start and end apart: 2, of which 2 were waited for; matrix products, arithmetic and copies ran while one was open for 0% of the time, Pallas kernels for 0%

profile of v1, /device:TPU:0, one launch (start us, length us, event | category | flops | bytes accessed | tf_op | source)
XLA Modules:
  0.0 231.7 jit_solution(14136715289220111260)
XLA Ops:
  7.2 0.8 copy.28
  7.9 0.1 stack.7
  8.0 0.8 copy.31
  8.8 0.1 stack.8
  8.9 9.5 %all_gather.3 = s32[4,16,2]{1,2,0:T(2,128)S(1)} all-gather(s32[1,16,2]{1,2,0:T(2,128)S(1)} %pad_add_fusion), channel_id=1, replica_groups=mesh['dp'=2,'ret'=4,'ctx'=4] {'ret'}, dimensions={0}, use_global_device_ids=true | all-gather | bytes 640 | tf_op jit(solution)/shard_map/all_gather | solution.py:146
  18.4 2.8 %multiply_reduce_fusion = f32[2048]{0:T(1024)S(1)} fusion(bf16[1,2048,896]{2,1,0:T(8,128)(2,1)} %param.8), kind=kLoop, calls=%fused_computation.1 | loop fusion | flops 5502976 | bytes 3678208 | tf_op jit(solution)/shard_map/reduce_sum | solution.py:26
  21.2 0.7 copy.32.id_ref
  21.9 4.5 %multiply_convert_fusion.normed_ref = bf16[16,128,896]{2,1,0:T(8,128)(2,1)} fusion(f32[16,128]{1,0:T(8,128)S(1)} %rsqrt_bitcast_fusion, bf16[16,128,896]{2,1,0:T(8,128)(2,1)} %bitcast.11), kind=kLoop, calls=%fused_computation | loop fusion | flops 5505024 | bytes 7348224 | tf_op jit(solution)/shard_map/convert_element_type | solution.py:27
  26.4 6.3 %pick_rows.1 = bf16[4,8,128,896]{3,2,1,0:T(8,128)(2,1)} custom-call(s32[4,16,2]{2,1,0:T(8,128)} %copy.32.id_ref, bf16[16,128,896]{2,1,0:T(8,128)(2,1)} %multiply_convert_fusion.normed_ref), custom_call_target="tpu_custom_call" | custom-call | tf_op jit(solution)/shard_map/pick_rows/pallas_call | solution.py:122
  32.7 0.0 copy-start
  32.7 5.6 %all-to-all-start = ((bf16[4,8,128,896]{3,2,1,0:T(8,128)(2,1)}), bf16[4,8,128,896]{3,2,1,0:T(8,128)(2,1)}, u32[]{:S(2)}, u32[]{:S(2)}) async-start(bf16[4,8,128,896]{3,2,1,0:T(8,128)(2,1)} %pick_rows.1), calls=%async_computation | async-start | bytes 14680064 | tf_op jit(solution)/shard_map/all_to_all | solution.py:149
  38.3 0.0 reduce-scatter.2.cloned.1.call-start
  38.3 0.1 eq.15
  38.4 0.0 copy-done
  38.4 0.1 copy.29
  38.5 0.2 convert_reduce_fusion
  38.7 0.1 reduce_sum.21
  38.8 0.6 add.18.slot_ref
  39.4 78.3 %all-to-all-done = bf16[4,8,128,896]{3,2,1,0:T(8,128)(2,1)} async-done(((bf16[4,8,128,896]{3,2,1,0:T(8,128)(2,1)}), bf16[4,8,128,896]{3,2,1,0:T(8,128)(2,1)}, u32[]{:S(2)}, u32[]{:S(2)}) %all-to-all-start) | async-done | bytes 7340064 | tf_op jit(solution)/shard_map/all_to_all | solution.py:149
  117.7 51.6 %attend_blocks.1 = (bf16[512,1024]{1,0:T(8,128)(2,1)}, bf16[512,1024]{1,0:T(8,128)(2,1)}, bf16[896,1024]{1,0:T(8,128)(2,1)}, bf16[896,1024]{1,0:T(8,128)(2,1)}) custom-call(s32[8,2]{1,0:T(8,128)} %add.18.slot_ref, bf16[32,128,896]{2,1,0:T(8,128)(2,1)} %bitcast.3.first_ref.second_ref, bf16[32,128,896]{2,1,0:T(8,128)(2,1)} %bitcast.3.first_ref.second_ref, ...), custom_call_target="tpu_custom_call" | custom-call | tf_op jit(solution)/shard_map/attend_blocks/pallas_call | solution.py:80
  169.3 4.3 %pad_maximum_fusion = bf16[896,2048]{1,0:T(8,128)(2,1)} fusion(bf16[896,1024]{1,0:T(8,128)(2,1)} %get-tuple-element.11, bf16[896,1024]{1,0:T(8,128)(2,1)} %get-tuple-element.10), kind=kLoop, calls=%fused_computation.2 | loop fusion | flops 7340032 | bytes 7340032 | tf_op jit(solution)/shard_map/concatenate | solution.py:154
  173.6 0.0 reduce-scatter.2.cloned.1.call-update
  173.6 49.1 %reduce-scatter.2.cloned.1.call-done = bf16[112,2048]{1,0:T(8,128)(2,1)} async-done(((bf16[896,2048]{1,0:T(8,128)(2,1)}), bf16[112,2048]{1,0:T(8,128)(2,1)}) %reduce-scatter.2.cloned.1.call-update) | async-done | bytes 458768 | tf_op jit(solution)/shard_map/reduce_scatter | solution.py:155
  222.8 2.1 fusion.1
  (3 shorter events, 0.0 us)
Async XLA Ops:
  32.7 5.7 %copy-start = (s32[1,8,2]{1,2,0:T(2,128)S(1)}, s32[1,8,2]{1,2,0:T(2,128)}, u32[]{:S(2)}) copy-start(s32[1,8,2]{1,2,0:T(2,128)} %param.11) | copy-start | bytes 196
  32.7 85.0 %all-to-all-start = ((bf16[4,8,128,896]{3,2,1,0:T(8,128)(2,1)}), bf16[4,8,128,896]{3,2,1,0:T(8,128)(2,1)}, u32[]{:S(2)}, u32[]{:S(2)}) async-start(bf16[4,8,128,896]{3,2,1,0:T(8,128)(2,1)} %pick_rows.1), calls=%async_computation | async-start | bytes 14680064 | tf_op jit(solution)/shard_map/all_to_all | solution.py:149
  38.3 184.5 %reduce-scatter.2.cloned.1.call-start = ((), (), s32[]{:S(2)}) async-start(), calls=%async_computation.2 | async-start | bytes 4128768 | tf_op jit(solution)/shard_map/reduce_scatter | solution.py:155
Sparse Core Ops, SparseCore 0:
  173.7 48.9 reduce-scatter.1

commit v2 on v1

v2 whole, which is shorter than its diff:
```python
import functools
import math

import jax
import jax.numpy as jnp
from jax import lax
from jax.experimental import pallas as pl
from jax.experimental.pallas import tpu as pltpu
from jax.sharding import PartitionSpec as P

HEAD_DIM = 128
NEIGH_LEN = 128
NEIGHBOURS = 2
HALF = NEIGH_LEN // 2
MIB = 1024 * 1024
ATTEND_MIB = 32
CHUNKS = ((3, True), (3, True), (2, False))

F32 = jnp.float32
BF16 = jnp.bfloat16
ANY = pl.BlockSpec(memory_space=pl.ANY)
SMEM = pl.BlockSpec(memory_space=pltpu.SMEM)
VMEM = pl.BlockSpec(memory_space=pltpu.VMEM)
HBM = pl.BlockSpec(memory_space=pltpu.HBM)


def params(mib):
    return pltpu.CompilerParams(vmem_limit_bytes=mib * MIB)


def contract(lhs, rhs, dims):
    return lax.dot_general(lhs, rhs, (dims, ((), ())), preferred_element_type=F32)


def swap(array, axis, bit):
    size = lax.axis_size(axis)
    return lax.ppermute(array, axis, [(i, i ^ bit) for i in range(size)])


def normalize_kernel(states_ref, out_ref):
    floats = states_ref[...].astype(F32)
    mean_square = jnp.mean(floats * floats, axis=-1, keepdims=True)
    out_ref[...] = (floats * lax.rsqrt(mean_square + 1e-06)).astype(BF16)


def normalize_rows(states):
    rows, width = states.shape
    tile = 512
    spec = pl.BlockSpec((tile, width), lambda i: (i, 0))
    return pl.pallas_call(
        normalize_kernel,
        grid=(rows // tile,),
        in_specs=[spec],
        out_specs=spec,
        out_shape=jax.ShapeDtypeStruct(states.shape, BF16),
        compiler_params=params(12),
        name="normalize_rows",
    )(states)


def exchange_ids(own):
    n_ret = lax.axis_size("ret")
    if n_ret <= 4:
        return jnp.stack([own] + [swap(own, "ret", k) for k in range(1, n_ret)])
    every = lax.all_gather(own, "ret")
    order = jnp.arange(n_ret, dtype=jnp.int32) ^ lax.axis_index("ret")
    return jnp.take(every, order, axis=0)


def pick_kernel(spans, id_ref, normed_ref, *refs):
    n_ret = id_ref.shape[0]
    outs, counts, sems = refs[: len(spans) * n_ret], refs[-2], refs[-1]
    me = lax.axis_index("ret")
    part = lax.rem(lax.axis_index("ctx"), 2)

    def copy(chunk, k, row, slot):
        source = normed_ref.at[row, part] if spans[chunk][2] else normed_ref.at[row]
        return pltpu.make_async_copy(source, outs[chunk * n_ret + k].at[slot], sems.at[chunk, k, slot])

    for chunk, (start, count, _) in enumerate(spans):
        for k in range(n_ret):

            def send(i, used, k=k, chunk=chunk, start=start):
                request = (start * NEIGHBOURS + i) * 2
                mine = id_ref[k, request] == me

                @pl.when(mine)
                def _():
                    copy(chunk, k, id_ref[k, request + 1], used).start()

                return used + jnp.where(mine, 1, 0)

            counts[chunk, k] = lax.fori_loop(0, count * NEIGHBOURS, send, jnp.int32(0))
    for chunk in range(len(spans)):
        for k in range(n_ret):

            def wait(i, carry, k=k, chunk=chunk):
                copy(chunk, k, 0, i).wait()
                return carry

            lax.fori_loop(0, counts[chunk, k], wait, 0)


def pick(ids, normed, spans, capacity):
    n_ret, width = ids.shape[0], normed.shape[-1]
    slots = [capacity(count) for _, count, _ in spans]
    shapes = [(cap, HALF, width) if pair else (cap, 2, HALF, width) for (_, _, pair), cap in zip(spans, slots)]
    shapes = [jax.ShapeDtypeStruct(shape, BF16) for shape in shapes for _ in range(n_ret)]
    picked = pl.pallas_call(
        functools.partial(pick_kernel, spans),
        in_specs=[SMEM, ANY],
        out_specs=[VMEM] * len(shapes),
        out_shape=shapes,
        scratch_shapes=[
            pltpu.SMEM((len(spans), n_ret), jnp.int32),
            pltpu.SemaphoreType.DMA((len(spans), n_ret, max(slots))),
        ],
        compiler_params=params(16),
        name="pick_rows",
    )(ids, normed)
    return [picked[i : i + n_ret] for i in range(0, len(picked), n_ret)]


def unpack_kernel(start, count, id_ref, *refs):
    *incoming, out_ref, ranks, sems = refs
    me = lax.axis_index("ret")

    def copy(k, rank, i):
        return pltpu.make_async_copy(incoming[k].at[rank], out_ref.at[i], sems.at[i])

    for k in range(len(incoming)):
        ranks[k] = 0
    for i in range(count * NEIGHBOURS):
        source = id_ref[(start * NEIGHBOURS + i) * 2] ^ me
        rank = ranks[source]
        ranks[source] = rank + 1
        for k in range(len(incoming)):

            @pl.when(source == k)
            def _(k=k, rank=rank, i=i):
                copy(k, rank, i).start()

    for i in range(count * NEIGHBOURS):
        copy(0, 0, i).wait()


def unpack(own, incoming, start, count):
    return pl.pallas_call(
        functools.partial(unpack_kernel, start, count),
        in_specs=[SMEM] + [ANY] * len(incoming),
        out_specs=VMEM,
        out_shape=jax.ShapeDtypeStruct((count * NEIGHBOURS,) + incoming[0].shape[1:], BF16),
        scratch_shapes=[
            pltpu.SMEM((len(incoming),), jnp.int32),
            pltpu.SemaphoreType.DMA((count * NEIGHBOURS,)),
        ],
        compiler_params=params(8),
        name="unpack_rows",
    )(own, *incoming)


def block_grads(context, wk_ref, wv_ref, q_ref, go_ref, out_ref, gq_ref, dk_ref, dv_ref):
    scale = 1.0 / math.sqrt(HEAD_DIM)
    keys = jnp.dot(context, wk_ref[...], preferred_element_type=F32).astype(BF16)
    values = jnp.dot(context, wv_ref[...], preferred_element_type=F32).astype(BF16)
    tokens, heads = q_ref.shape[0], q_ref.shape[1] // HEAD_DIM
    zero = jnp.zeros((tokens, HEAD_DIM), BF16)
    cols = [slice(head * HEAD_DIM, (head + 1) * HEAD_DIM) for head in range(heads)]

    def reader(head):
        upper = jnp.concatenate([q_ref[:, cols[head]], zero], axis=1)
        lower = jnp.concatenate([zero, go_ref[:, cols[head]]], axis=1)
        return jnp.concatenate([upper, lower], axis=0)

    def both(head):
        return jnp.concatenate([keys[:, cols[head]], values[:, cols[head]]], axis=1)

    def finish(head, probs, dscore):
        mixed = jnp.dot(jnp.concatenate([probs, dscore], axis=0), both(head), preferred_element_type=F32)
        out_ref[:, cols[head]] = mixed[:tokens, HEAD_DIM:].astype(BF16)
        gq_ref[:, cols[head]] = mixed[tokens:, :HEAD_DIM].astype(BF16)
        grads = contract(jnp.concatenate([dscore, probs], axis=0), reader(head), ((0,), (0,))).astype(BF16)
        dk_ref[:, cols[head]] = grads[:, :HEAD_DIM]
        dv_ref[:, cols[head]] = grads[:, HEAD_DIM:]

    ahead, lag = 3, 2
    products, weights = {}, {}
    for head in range(-ahead, heads + lag):
        if 0 <= head + ahead < heads:
            products[head + ahead] = contract(reader(head + ahead), both(head + ahead), ((1,), (1,)))
        if 0 <= head < heads:
            product = products.pop(head)
            expo, dprob = jnp.exp(product[:tokens] * scale), product[tokens:]
            inverse = 1.0 / jnp.sum(expo, axis=-1, keepdims=True)
            delta = jnp.sum(expo * dprob, axis=-1, keepdims=True) * inverse
            probs = expo * inverse
            weights[head] = (probs.astype(BF16), (probs * (dprob - delta) * scale).astype(BF16))
        if 0 <= head - lag < heads:
            finish(head - lag, *weights.pop(head - lag))


def attend_kernel(first, last, slot_ref, one_ref, two_ref, wk_ref, wv_ref, q_ref, go_ref, *refs):
    refs = list(refs[0 if first else 2 :])
    acc_in = [] if first else [refs.pop(0), refs.pop(0)]
    out_ref, gq_ref, *grad_refs, acck, accv, dk_ref, dv_ref, sems = refs
    accs, grads = (acck, accv), (dk_ref, dv_ref)
    step, steps = pl.program_id(0), pl.num_programs(0)
    loads = [pltpu.make_async_copy(src, dst, sems.at[i]) for i, (src, dst) in enumerate(zip(acc_in, accs))]

    @pl.when(step == 0)
    def _():
        for load in loads:
            load.start()

    width = one_ref.shape[-1]
    context = jnp.concatenate([one_ref[...].reshape(-1, width), two_ref[...].reshape(-1, width)], axis=0)
    block_grads(context, wk_ref, wv_ref, q_ref, go_ref, out_ref, gq_ref, dk_ref, dv_ref)

    @pl.when(step == 0)
    def _():
        for load in loads:
            load.wait()
        if first:
            for acc, grad in zip(accs, grads):
                acc[...] = contract(context, grad[...], ((0,), (0,)))

    @pl.when((step > 0) | (not first))
    def _():
        for acc, grad in zip(accs, grads):
            acc[...] += contract(context, grad[...], ((0,), (0,)))

    @pl.when(step == steps - 1)
    def _():
        if last:
            half = grad_refs[0].shape[0]
            dp = lax.axis_index("dp")
            for i, side in enumerate((1 - dp, dp)):
                for acc, grad_ref in zip(accs, grad_refs[2 * i : 2 * i + 2]):
                    grad_ref[...] = acc[pl.ds(pl.multiple_of(side * half, half), half), :].astype(BF16)
        else:
            stores = [pltpu.make_async_copy(acc, dst, sems.at[i]) for i, (acc, dst) in enumerate(zip(accs, grad_refs))]
            for store in stores:
                store.start()
            for store in stores:
                store.wait()


def attend(rows, slots, wk, wv, queries, grad_out, start, count, carried, last):
    blocks = slots.shape[0] // (2 * NEIGHBOURS)
    tokens, feat = queries.shape[0] // blocks, queries.shape[1]
    enc = wk.shape[0]
    whole = lambda shape: pl.BlockSpec(shape, lambda b, s: (0, 0))
    row = pl.BlockSpec((tokens, feat), lambda b, s: (start + b, 0))
    if len(rows) == 2:
        neighs = [pl.BlockSpec((NEIGHBOURS, HALF, enc), lambda b, s: (b, 0, 0))] * 2
    else:
        rows = rows * 2
        neighs = [pl.BlockSpec((1, 2, HALF, enc), lambda b, s, n=n: (b * NEIGHBOURS + n, 0, 0, 0)) for n in range(NEIGHBOURS)]
    row_shape = jax.ShapeDtypeStruct(queries.shape, BF16)
    if last:
        grad_shapes = [jax.ShapeDtypeStruct((enc // 2, feat), BF16)] * 4
        grad_specs = [whole((enc // 2, feat))] * 4
    else:
        grad_shapes = [jax.ShapeDtypeStruct((enc, feat), F32)] * 2
        grad_specs = [HBM] * 2
    return pl.pallas_call(
        functools.partial(attend_kernel, not carried, last),
        grid_spec=pltpu.PrefetchScalarGridSpec(
            num_scalar_prefetch=1,
            grid=(count,),
            in_specs=neighs + [whole((enc, feat))] * 2 + [row] * 2 + [HBM] * len(carried),
            out_specs=[row, row] + grad_specs,
            scratch_shapes=[
                pltpu.VMEM((enc, feat), F32),
                pltpu.VMEM((enc, feat), F32),
                pltpu.VMEM((NEIGHBOURS * NEIGH_LEN, feat), BF16),
                pltpu.VMEM((NEIGHBOURS * NEIGH_LEN, feat), BF16),
                pltpu.SemaphoreType.DMA((2,)),
            ],
        ),
        out_shape=[row_shape, row_shape] + grad_shapes,
        input_output_aliases={7: 0, 8: 1} if carried else {},
        compiler_params=params(ATTEND_MIB),
        name="attend_blocks",
    )(slots, *rows, wk, wv, queries, grad_out, *carried)


def fold_kernel(dims, count, *refs):
    ret = lax.axis_index("ret")
    for i in range(count):
        held_ref, arrived_ref = refs[i], refs[count + i]
        if dims is None:
            refs[2 * count + i][...] = held_ref[0].astype(F32) + arrived_ref[0].astype(F32)
            continue
        bit, place = dims[i]
        mine = (ret >> bit) & 1
        stride = 1 << place
        for j in range(held_ref.shape[0] // 2):
            base = (j // stride) * 2 * stride + j % stride
            for k, side in enumerate((1 - mine, mine)):
                row = base + side * stride
                total = held_ref[row].astype(F32) + arrived_ref[row].astype(F32)
                refs[(2 + k) * count + i][j] = total.astype(BF16)


def fold(held, arrived, dims):
    count = len(held)
    parts, rows, feat = held[0].shape
    if dims is None:
        shapes = [jax.ShapeDtypeStruct((rows, feat), F32)] * count
    else:
        shapes = [jax.ShapeDtypeStruct((parts // 2, rows, feat), BF16)] * (2 * count)
    return pl.pallas_call(
        functools.partial(fold_kernel, dims, count),
        in_specs=[VMEM] * (2 * count),
        out_specs=[VMEM] * len(shapes),
        out_shape=shapes,
        compiler_params=params(16),
        name="fold_grads",
    )(*held, *arrived)


def reduce_scatter(send, held):
    n_ret = lax.axis_size("ret")
    bits = n_ret.bit_length() - 1
    arrived = [swap(grad, "dp", 1) for grad in send]
    split = lambda grad: grad.reshape(n_ret, -1, grad.shape[-1])
    held, arrived = [split(grad) for grad in held], [split(grad) for grad in arrived]
    left = [list(range(bits)) for _ in held]
    for step in range(bits):
        bit = [step, bits - 1 - step]
        dims = tuple((b, bits_left.index(b)) for b, bits_left in zip(bit, left))
        *send, held0, held1 = fold(held, arrived, dims)
        held = [held0, held1]
        for b, bits_left in zip(bit, left):
            bits_left.remove(b)
        arrived = [swap(grad, "ret", 1 << b) for grad, b in zip(send, bit)]
    return fold(held, arrived, None)


def spans_of(blocks):
    spans, start = [], 0
    for count, pair in CHUNKS:
        spans.append((start, count, pair))
        start += count
    return spans if start == blocks else [(0, blocks, False)]


def local(queries, enc_states, w_key, w_value, shard_ids, row_ids, grad_out):
    n_ret = lax.axis_size("ret")
    blocks = shard_ids.shape[1]
    bound = blocks * NEIGHBOURS * 2 // n_ret
    enc = enc_states.shape[2]

    def capacity(count):
        return min(count, bound)

    own = jnp.stack([shard_ids[0], row_ids[0]], axis=-1).reshape(-1)
    ids = exchange_ids(own)
    normed = normalize_rows(enc_states[0]).reshape(-1, 2, HALF, enc)
    spans = spans_of(blocks)
    outgoing = pick(ids, normed, spans[:1], capacity)
    if len(spans) > 1:
        outgoing = outgoing + pick(ids, normed, spans[1:], capacity)
    carried, arrivals = [], []
    for slots in outgoing:
        slots = list(slots)
        if arrivals:
            for k in range(1, n_ret):
                arrivals[-1][k], slots[k] = lax.optimization_barrier((arrivals[-1][k], slots[k]))
        arrivals.append(slots[:1] + [swap(slots[k], "ret", k) for k in range(1, n_ret)])
    for incoming, (start, count, pair) in zip(arrivals, spans):
        mine = unpack(own, incoming, start, count)
        rows = [mine, swap(mine, "ctx", 1)] if pair else [mine]
        last = start + count == blocks
        carried = attend(rows, own, w_key, w_value, queries[0], grad_out[0], start, count, carried, last)
    attended, grad_queries, *grads = carried
    grad_w_key, grad_w_value = reduce_scatter(grads[:2], grads[2:])
    return attended[None], grad_queries[None], grad_w_key, grad_w_value


def solution(mesh):
    placed = (
        P("dp", "ret", "ctx"),
        P("dp", "ret", None),
        P(None, "ctx"),
        P(None, "ctx"),
        P("dp", "ret", None),
        P("dp", "ret", None),
        P("dp", "ret", "ctx"),
    )
    return jax.shard_map(
        local,
        mesh=mesh,
        in_specs=placed,
        out_specs=(
            P("dp", "ret", "ctx"),
            P("dp", "ret", "ctx"),
            P(("dp", "ret"), "ctx"),
            P(("dp", "ret"), "ctx"),
        ),
        check_vma=False,
    )
```

time: 232 us -> 118 us (0.51)
  waiting for transfers between devices: 127 us -> 40 us
  starting transfers between devices: 5.62 us -> 24.8 us
  between operations: 14.1 us -> 0.81 us
  other arithmetic: 12.4 us -> 0.71 us
  blocking collectives: 9.51 us -> 0 us
  Pallas kernels: 57.9 us -> 49.2 us
  local copies, waits for them, and re-layouts: 4.7 us -> 2.33 us
    all_to_all x1 -> x0, waiting for transfers between devices: 78.3 us -> none  [local(): lax.all_to_all(outgoing, 'ret', split_axis=0, concat_axis=0, tiled=True)]
    reduce_scatter x1 -> x0, waiting for transfers between devices: 49.1 us -> none  [local(): lax.psum_scatter(both, ('dp', 'ret'), scatter_dimension=0, tiled=True)]
    ppermute x0 -> x20, waiting for transfers between devices: none -> 40 us  [swap(): return lax.ppermute(array, axis, [(i, i ^ bit) for i in range(size)])]
    ppermute x0 -> x20, starting transfers between devices: none -> 24.8 us  [swap(): return lax.ppermute(array, axis, [(i, i ^ bit) for i in range(size)])]
    all_gather x1 -> x0, blocking collectives: 9.51 us -> none  [local(): ids = lax.all_gather(own, 'ret')]
    pallas_call x2 -> x12, Pallas kernels: 57.9 us -> 49.2 us  [the longest x3 32.7 us: attend(): pl.pallas_call(functools.partial(attend_kernel, not carried, last), grid_...]
    all_to_all x1 -> x0, starting transfers between devices: 5.58 us -> none  [local(): lax.all_to_all(outgoing, 'ret', split_axis=0, concat_axis=0, tiled=True)]
    convert_element_type x1 -> x0, other arithmetic: 4.52 us -> none  [normalize_rows(): return (floats * lax.rsqrt(mean_square + 1e-06)).astype(BF16)]
  transfers between devices with their start and end apart: 2 -> 20, of which waited for: 2 -> 12; matrix products, arithmetic and copies ran while one was open for 0% -> 0% of each run, Pallas kernels for 0% -> 20%
where the time goes in v2:
time: 118 us
  Pallas kernels  49.2 us (42%)
  waiting for transfers between devices  40 us (34%)
  starting transfers between devices  24.8 us (21%)
  local copies, waits for them, and re-layouts  2.33 us (2%)
    ppermute x20, waiting for transfers between devices, swap(): return lax.ppermute(array, axis, [(i, i ^ bit) for i in range(size)])  40 us
    pallas_call x3, Pallas kernels, attend(): pl.pallas_call(functools.partial(attend_kernel, not carried, last), grid_...  32.7 us
    ppermute x20, starting transfers between devices, swap(): return lax.ppermute(array, axis, [(i, i ^ bit) for i in range(size)])  24.8 us
    pallas_call x2, Pallas kernels, pick(): pl.pallas_call(functools.partial(pick_kernel, spans), in_specs=[SMEM, ANY...  8.33 us
    pallas_call x3, Pallas kernels, unpack(): pl.pallas_call(functools.partial(unpack_kernel, start, count), in_specs=[...  5.32 us
  transfers between devices with their start and end apart: 20, of which 12 were waited for; matrix products, arithmetic and copies ran while one was open for 0% of the time, Pallas kernels for 20%

profile of v2, /device:TPU:0, one launch (start us, length us, event | category | flops | bytes accessed | tf_op | source)
XLA Modules:
  0.0 117.8 jit_solution(11689607884640741607)
XLA Ops:
  0.6 0.7 pad_add_fusion
  1.3 0.1 copy.17
  1.4 0.1 reshape.26.id_ref.slot_ref
  1.5 4.0 %collective-permute-start.2 = (s32[32]{0:T(128)S(1)}, s32[32]{0:T(128)S(1)}, u32[]{:S(2)}, u32[]{:S(2)}) collective-permute-start(s32[32]{0:T(128)S(1)} %reshape.26.id_ref.slot_ref), channel_id=1, source_target_pairs={{0,12},{4,8},{8,4},{12,0},{1,13},{5,9},{9,5},{13,1},{2,14},{6,10},... | collective-permute-start | bytes 392 | tf_op jit(solution)/shard_map/ppermute | solution.py:37
  5.5 0.5 collective-permute-start.1
  6.0 0.1 collective-permute-start
  6.1 0.1 stack_reshape.3
  6.2 0.0 copy-start.4
  6.2 2.0 %copy-done.4 = bf16[1,2048,896]{2,1,0:T(8,128)(2,1)S(1)} copy-done((bf16[1,2048,896]{2,1,0:T(8,128)(2,1)S(1)}, bf16[1,2048,896]{2,1,0:T(8,128)(2,1)}, u32[]{:S(2)}) %copy-start.4) | copy-done | bytes 3670040
  8.3 1.2 %normalize_rows.1 = bf16[2048,896]{1,0:T(8,128)(2,1)S(1)} custom-call(bf16[2048,896]{1,0:T(8,128)(2,1)S(1)} %bitcast.23), custom_call_target="tpu_custom_call" | custom-call | tf_op jit(solution)/shard_map/normalize_rows/pallas_call | solution.py:50
  9.5 0.0 collective-permute-done.2
  9.5 0.0 collective-permute-done.1
  9.5 0.0 collective-permute-done
  9.5 2.8 %pick_rows.3 = (bf16[3,64,896]{2,1,0:T(8,128)(2,1)S(1)}, bf16[3,64,896]{2,1,0:T(8,128)(2,1)S(1)}, bf16[3,64,896]{2,1,0:T(8,128)(2,1)S(1)}, bf16[3,64,896]{2,1,0:T(8,128)(2,1)S(1)}) custom-call(s32[4,32]{1,0:T(4,128)S(1)} %pad_add_fusion.1.id_ref, bf16[16,2,64,896]{3,2,1,0:T(8,128)(2,1)S(1)} %bitcast.15), custom_call_target="tpu_custom_call" | custom-call | tf_op jit(solution)/shard_map/pick_rows/pallas_call | solution.py:109
  12.4 1.0 collective-permute-start.3
  13.4 1.7 %collective-permute-start.6 = (bf16[3,64,896]{2,1,0:T(8,128)(2,1)S(1)}, bf16[3,64,896]{2,1,0:T(8,128)(2,1)S(1)}, u32[]{:S(2)}, u32[]{:S(2)}) collective-permute-start(bf16[3,64,896]{2,1,0:T(8,128)(2,1)S(1)} %get-tuple-element.58), channel_id=1, source_target_pairs={{0,8},{4,12},{8,0},{12,4},{1,9},{5,13},{9,1},{13,5},{2,10},{6,14},... | collective-permute-start | bytes 1032200 | tf_op jit(solution)/shard_map/ppermute | solution.py:37
  15.1 0.0 copy-start.1
  15.1 0.0 copy-start.2
  15.1 0.9 collective-permute-start.9
  16.0 5.5 %pick_rows.2 = (bf16[3,64,896]{2,1,0:T(8,128)(2,1)S(1)}, bf16[3,64,896]{2,1,0:T(8,128)(2,1)S(1)}, bf16[3,64,896]{2,1,0:T(8,128)(2,1)S(1)}, bf16[3,64,896]{2,1,0:...) custom-call(s32[4,32]{1,0:T(4,128)S(1)} %pad_add_fusion.1.id_ref, ...), custom_call_target="tpu_custom_call" | custom-call | tf_op jit(solution)/shard_map/pick_rows/pallas_call | solution.py:109
  21.5 1.9 %collective-permute-done.3.refs_1_ = bf16[3,64,896]{2,1,0:T(8,128)(2,1)S(1)} collective-permute-done((bf16[3,64,896]{2,1,0:T(8,128)(2,1)S(1)}, bf16[3,64,896]{2,1,0:T(8,128)(2,1)S(1)}, u32[]{:S(2)}, u32[]{:S(2)}) %collective-permute-start.3) | collective-permute-done | bytes 344096 | tf_op jit(solution)/shard_map/ppermute | solution.py:37
  23.4 0.9 collective-permute-start.4
  24.4 4.2 %collective-permute-done.6.refs_2_ = bf16[3,64,896]{2,1,0:T(8,128)(2,1)S(1)} collective-permute-done((bf16[3,64,896]{2,1,0:T(8,128)(2,1)S(1)}, bf16[3,64,896]{2,1,0:T(8,128)(2,1)S(1)}, u32[]{:S(2)}, u32[]{:S(2)}) %collective-permute-start.6) | collective-permute-done | bytes 344096 | tf_op jit(solution)/shard_map/ppermute | solution.py:37
  28.6 2.5 %collective-permute-start.7 = (bf16[3,64,896]{2,1,0:T(8,128)(2,1)S(1)}, bf16[3,64,896]{2,1,0:T(8,128)(2,1)S(1)}, u32[]{:S(2)}, u32[]{:S(2)}) collective-permute-start(bf16[3,64,896]{2,1,0:T(8,128)(2,1)S(1)} %get-tuple-element.60), channel_id=1, source_target_pairs={{0,8},{4,12},{8,0},{12,4},{1,9},{5,13},{9,1},{13,5},{2,10},{6,14},... | collective-permute-start | bytes 1032200 | tf_op jit(solution)/shard_map/ppermute | solution.py:37
  31.1 0.0 collective-permute-done.9.refs_3_
  31.1 1.6 %collective-permute-start.10 = (bf16[3,64,896]{2,1,0:T(8,128)(2,1)S(1)}, bf16[3,64,896]{2,1,0:T(8,128)(2,1)S(1)}, u32[]{:S(2)}, u32[]{:S(2)}) collective-permute-start(bf16[3,64,896]{2,1,0:T(8,128)(2,1)S(1)} %get-tuple-element.65), channel_id=1, source_target_pairs={{0,12},{4,8},{8,4},{12,0},{1,13},{5,9},{9,5},{13,1},{2,14},{6,10},... | collective-permute-start | bytes 1032200 | tf_op jit(solution)/shard_map/ppermute | solution.py:37
  32.7 1.6 %unpack_rows.5.one_ref = bf16[6,64,896]{2,1,0:T(8,128)(2,1)S(1)} custom-call(s32[32]{0:T(128)S(1)} %reshape.26.id_ref.slot_ref, bf16[3,64,896]{2,1,0:T(8,128)(2,1)S(1)} %get-tuple-element.72.refs_0_, bf16[3,64,896]{2,1,0:T(8,128)(2,1)S(1)} %collective-permute-done.3.refs_1_, bf16[3,64,896]{2,1,0:T(8,128)(2,1)S(1)} %collective-permute-done.6.refs_2_, ...), custom_call_target="tpu_custom_call" | custom-call | tf_op jit(solution)/shard_map/unpack_rows/pallas_call | solution.py:148
  34.3 1.6 %collective-permute-start.13 = (bf16[6,64,896]{2,1,0:T(8,128)(2,1)S(1)}, bf16[6,64,896]{2,1,0:T(8,128)(2,1)S(1)}, u32[]{:S(2)}, u32[]{:S(2)}) collective-permute-start(bf16[6,64,896]{2,1,0:T(8,128)(2,1)S(1)} %unpack_rows.5.one_ref), channel_id=1, source_target_pairs={{0,1},{1,0},{2,3},{3,2},{4,5},{5,4},{6,7},{7,6},{8,9},{9,8},{10,11... | collective-permute-start | bytes 2064392 | tf_op jit(solution)/shard_map/ppermute | solution.py:37
  36.0 2.3 %collective-permute-done.4.refs_1_ = bf16[3,64,896]{2,1,0:T(8,128)(2,1)S(1)} collective-permute-done((bf16[3,64,896]{2,1,0:T(8,128)(2,1)S(1)}, bf16[3,64,896]{2,1,0:T(8,128)(2,1)S(1)}, u32[]{:S(2)}, u32[]{:S(2)}) %collective-permute-start.4) | collective-permute-done | bytes 344096 | tf_op jit(solution)/shard_map/ppermute | solution.py:37
  38.2 5.9 %collective-permute-done.7.refs_2_ = bf16[3,64,896]{2,1,0:T(8,128)(2,1)S(1)} collective-permute-done((bf16[3,64,896]{2,1,0:T(8,128)(2,1)S(1)}, bf16[3,64,896]{2,1,0:T(8,128)(2,1)S(1)}, u32[]{:S(2)}, u32[]{:S(2)}) %collective-permute-start.7) | collective-permute-done | bytes 344096 | tf_op jit(solution)/shard_map/ppermute | solution.py:37
  44.1 0.0 collective-permute-done.10.refs_3_
  44.1 1.6 %unpack_rows.4.one_ref = bf16[6,64,896]{2,1,0:T(8,128)(2,1)S(1)} custom-call(s32[32]{0:T(128)S(1)} %reshape.26.id_ref.slot_ref, bf16[3,64,896]{2,1,0:T(8,128)(2,1)S(1)} %get-tuple-element.68.refs_0_, bf16[3,64,896]{2,1,0:T(8,128)(2,1)S(1)} %collective-permute-done.4.refs_1_, bf16[3,64,896]{2,1,0:T(8,128)(2,1)S(1)} %collective-permute-done.7.refs_2_, ...), custom_call_target="tpu_custom_call" | custom-call | tf_op jit(solution)/shard_map/unpack_rows/pallas_call | solution.py:148
  45.8 1.7 %collective-permute-start.12 = (bf16[6,64,896]{2,1,0:T(8,128)(2,1)S(1)}, bf16[6,64,896]{2,1,0:T(8,128)(2,1)S(1)}, u32[]{:S(2)}, u32[]{:S(2)}) collective-permute-start(bf16[6,64,896]{2,1,0:T(8,128)(2,1)S(1)} %unpack_rows.4.one_ref), channel_id=1, source_target_pairs={{0,1},{1,0},{2,3},{3,2},{4,5},{5,4},{6,7},{7,6},{8,9},{9,8},{10,11... | collective-permute-start | bytes 2064392 | tf_op jit(solution)/shard_map/ppermute | solution.py:37
  47.4 1.5 %collective-permute-start.11 = (bf16[2,2,64,896]{3,2,1,0:T(8,128)(2,1)S(1)}, bf16[2,2,64,896]{3,2,1,0:T(8,128)(2,1)S(1)}, u32[]{:S(2)}, u32[]{:S(2)}) collective-permute-start(bf16[2,2,64,896]{3,2,1,0:T(8,128)(2,1)S(1)} %get-tuple-element.67), channel_id=1, source_target_pairs={{0,12},{4,8},{8,4},{12,0},{1,13},{5,9},{9,5},{13,1},{2,14},{6,10},... | collective-permute-start | bytes 1376264 | tf_op jit(solution)/shard_map/ppermute | solution.py:37
  49.0 1.6 %collective-permute-start.8 = (bf16[2,2,64,896]{3,2,1,0:T(8,128)(2,1)S(1)}, bf16[2,2,64,896]{3,2,1,0:T(8,128)(2,1)S(1)}, u32[]{:S(2)}, u32[]{:S(2)}) collective-permute-start(bf16[2,2,64,896]{3,2,1,0:T(8,128)(2,1)S(1)} %get-tuple-element.62), channel_id=1, source_target_pairs={{0,8},{4,12},{8,0},{12,4},{1,9},{5,13},{9,1},{13,5},{2,10},{6,14},... | collective-permute-start | bytes 1376264 | tf_op jit(solution)/shard_map/ppermute | solution.py:37
  50.6 0.4 collective-permute-start.5
  50.9 0.0 collective-permute-done.13.two_ref
  50.9 0.0 copy-done
  50.9 0.0 copy-done.1
  50.9 0.0 copy-done.2
  50.9 0.0 copy-done.3
  51.0 11.7 %attend_blocks.3 = (bf16[512,1024]{1,0:T(8,128)(2,1)}, bf16[512,1024]{1,0:T(8,128)(2,1)}, f32[896,1024]{1,0:T(8,128)S(1)}, f32[896,1024]{1,0:T(8,128)S(1)}) custom-call(s32[32]{0:T(128)S(1)} %reshape.26.id_ref.slot_ref, bf16[6,64,896]{2,1,0:T(8,128)(2,1)S(1)} %unpack_rows.5.one_ref, bf16[6,64,896]{2,1,0:T(8,128)(2,1)S(1)} %collective-permute-done.13.two_ref, ...), custom_call_target="tpu_custom_call" | custom-call | tf_op jit(solution)/shard_map/attend_blocks/pallas_call | solution.py:266
  62.7 0.0 collective-permute-done.11.refs_3_
  62.7 5.7 %collective-permute-done.8.refs_2_ = bf16[2,2,64,896]{3,2,1,0:T(8,128)(2,1)S(1)} collective-permute-done((bf16[2,2,64,896]{3,2,1,0:T(8,128)(2,1)S(1)}, bf16[2,2,64,896]{3,2,1,0:T(8,128)(2,1)S(1)}, u32[]{:S(2)}, u32[]{:S(2)}) %collective-permute-start.8) | collective-permute-done | bytes 458784 | tf_op jit(solution)/shard_map/ppermute | solution.py:37
  68.4 0.2 collective-permute-done.5.refs_1_
  68.6 2.0 %unpack_rows.3.one_ref.two_ref = bf16[4,2,64,896]{3,2,1,0:T(8,128)(2,1)S(1)} custom-call(s32[32]{0:T(128)S(1)} %reshape.26.id_ref.slot_ref, bf16[2,2,64,896]{3,2,1,0:T(8,128)(2,1)S(1)} %get-tuple-element.52.refs_0_, bf16[2,2,64,896]{3,2,1,0:T(8,128)(2,1)S(1)} %collective-permute-done.5.refs_1_, bf16[2,2,64,896]{3,2,1,0:T(8,128)(2,1)S(1)} %collective-permute-done.8.refs_2_, ...), custom_call_target="tpu_custom_call" | custom-call | tf_op jit(solution)/shard_map/unpack_rows/pallas_call | solution.py:148
  70.6 0.0 collective-permute-done.12.two_ref
  70.6 12.2 %attend_blocks.4 = (bf16[512,1024]{1,0:T(8,128)(2,1)}, bf16[512,1024]{1,0:T(8,128)(2,1)}, f32[896,1024]{1,0:T(8,128)S(1)}, f32[896,1024]{1,0:T(8,128)S(1)}) custom-call(s32[32]{0:T(128)S(1)} %reshape.26.id_ref.slot_ref, bf16[6,64,896]{2,1,0:T(8,128)(2,1)S(1)} %unpack_rows.4.one_ref, ...), custom_call_target="tpu_custom_call", output_to_operand_aliasing={{0}: (7, {}), {1}: (8, {})} | custom-call | tf_op jit(solution)/shard_map/attend_blocks/pallas_call | solution.py:266
  82.9 8.8 %attend_blocks.5 = (bf16[512,1024]{1,0:T(8,128)(2,1)}, bf16[512,1024]{1,0:T(8,128)(2,1)}, bf16[448,1024]{1,0:T(8,128)(2,1)S(1)}, bf16[448,1024]{1,0:T(8,128)(2,1...) custom-call(s32[32]{0:T(128)S(1)} %reshape.26.id_ref.slot_ref, ...), custom_call_target="tpu_custom_call", output_to_operand_aliasing={{0}: (7, {}), {1}: (8, {})} | custom-call | tf_op jit(solution)/shard_map/attend_blocks/pallas_call | solution.py:266
  91.7 0.1 collective-permute-start.14
  91.8 0.5 collective-permute-start.15
  92.3 2.0 %collective-permute-done.14 = bf16[448,1024]{1,0:T(8,128)(2,1)S(1)} collective-permute-done((bf16[448,1024]{1,0:T(8,128)(2,1)S(1)}, bf16[448,1024]{1,0:T(8,128)(2,1)S(1)}, u32[]{:S(2)}, u32[]{:S(2)}) %collective-permute-start.14) | collective-permute-done | bytes 917536 | tf_op jit(solution)/shard_map/ppermute | solution.py:37
  94.2 1.3 %collective-permute-done.15 = bf16[448,1024]{1,0:T(8,128)(2,1)S(1)} collective-permute-done((bf16[448,1024]{1,0:T(8,128)(2,1)S(1)}, bf16[448,1024]{1,0:T(8,128)(2,1)S(1)}, u32[]{:S(2)}, u32[]{:S(2)}) %collective-permute-start.15) | collective-permute-done | bytes 917536 | tf_op jit(solution)/shard_map/ppermute | solution.py:37
  95.5 0.4 fold_grads.3
  96.0 1.4 %collective-permute-start.16 = (bf16[2,112,1024]{2,1,0:T(8,128)(2,1)S(1)}, bf16[2,112,1024]{2,1,0:T(8,128)(2,1)S(1)}, u32[]{:S(2)}, u32[]{:S(2)}) collective-permute-start(bf16[2,112,1024]{2,1,0:T(8,128)(2,1)S(1)} %get-tuple-element.92), channel_id=1, source_target_pairs={{0,4},{4,0},{8,12},{12,8},{1,5},{5,1},{9,13},{13,9},{2,6},{6,2},{1... | collective-permute-start | bytes 1376264 | tf_op jit(solution)/shard_map/ppermute | solution.py:37
  97.3 0.6 collective-permute-start.17
  97.9 10.6 %collective-permute-done.16.refs_2_ = bf16[2,112,1024]{2,1,0:T(8,128)(2,1)S(1)} collective-permute-done((bf16[2,112,1024]{2,1,0:T(8,128)(2,1)S(1)}, bf16[2,112,1024]{2,1,0:T(8,128)(2,1)S(1)}, u32[]{:S(2)}, u32[]{:S(2)}) %collective-permute-start.16) | collective-permute-done | bytes 458784 | tf_op jit(solution)/shard_map/ppermute | solution.py:37
  108.6 1.0 collective-permute-done.17.refs_3_
  109.6 0.2 fold_grads.4
  109.8 0.7 collective-permute-start.18
  110.5 1.5 %collective-permute-start.19 = (bf16[1,112,1024]{2,1,0:T(8,128)(2,1)S(1)}, bf16[1,112,1024]{2,1,0:T(8,128)(2,1)S(1)}, u32[]{:S(2)}, u32[]{:S(2)}) collective-permute-start(bf16[1,112,1024]{2,1,0:T(8,128)(2,1)S(1)} %get-tuple-element.97), channel_id=1, source_target_pairs={{0,4},{4,0},{8,12},{12,8},{1,5},{5,1},{9,13},{13,9},{2,6},{6,2},{1... | collective-permute-start | bytes 688136 | tf_op jit(solution)/shard_map/ppermute | solution.py:37
  112.0 4.4 %collective-permute-done.18.refs_2_ = bf16[1,112,1024]{2,1,0:T(8,128)(2,1)S(1)} collective-permute-done((bf16[1,112,1024]{2,1,0:T(8,128)(2,1)S(1)}, bf16[1,112,1024]{2,1,0:T(8,128)(2,1)S(1)}, u32[]{:S(2)}, u32[]{:S(2)}) %collective-permute-start.18) | collective-permute-done | bytes 229408 | tf_op jit(solution)/shard_map/ppermute | solution.py:37
  116.4 0.4 collective-permute-done.19.refs_3_
  116.8 1.0 fold_grads.5
  (3 shorter events, 0.0 us)
Async XLA Ops:
  1.5 8.0 %collective-permute-start.2 = (s32[32]{0:T(128)S(1)}, s32[32]{0:T(128)S(1)}, u32[]{:S(2)}, u32[]{:S(2)}) collective-permute-start(s32[32]{0:T(128)S(1)} %reshape.26.id_ref.slot_ref), channel_id=1, source_target_pairs={{0,12},{4,8},{8,4},{12,0},{1,13},{5,9},{9,5},{13,1},{2,14},{6,10},... | collective-permute-start | bytes 392 | tf_op jit(solution)/shard_map/ppermute | solution.py:37
  5.5 4.0 %collective-permute-start.1 = (s32[32]{0:T(128)S(1)}, s32[32]{0:T(128)S(1)}, u32[]{:S(2)}, u32[]{:S(2)}) collective-permute-start(s32[32]{0:T(128)S(1)} %reshape.26.id_ref.slot_ref), channel_id=1, source_target_pairs={{0,8},{4,12},{8,0},{12,4},{1,9},{5,13},{9,1},{13,5},{2,10},{6,14},... | collective-permute-start | bytes 392 | tf_op jit(solution)/shard_map/ppermute | solution.py:37
  6.0 3.5 %collective-permute-start = (s32[32]{0:T(128)S(1)}, s32[32]{0:T(128)S(1)}, u32[]{:S(2)}, u32[]{:S(2)}) collective-permute-start(s32[32]{0:T(128)S(1)} %reshape.26.id_ref.slot_ref), channel_id=1, source_target_pairs={{0,4},{4,0},{8,12},{12,8},{1,5},{5,1},{9,13},{13,9},{2,6},{6,2},{1... | collective-permute-start | bytes 392 | tf_op jit(solution)/shard_map/ppermute | solution.py:37
  6.2 2.0 %copy-start.4 = (bf16[1,2048,896]{2,1,0:T(8,128)(2,1)S(1)}, bf16[1,2048,896]{2,1,0:T(8,128)(2,1)}, u32[]{:S(2)}) copy-start(bf16[1,2048,896]{2,1,0:T(8,128)(2,1)} %param.8) | copy-start | bytes 11010052
  12.4 11.1 %collective-permute-start.3 = (bf16[3,64,896]{2,1,0:T(8,128)(2,1)S(1)}, bf16[3,64,896]{2,1,0:T(8,128)(2,1)S(1)}, u32[]{:S(2)}, u32[]{:S(2)}) collective-permute-start(bf16[3,64,896]{2,1,0:T(8,128)(2,1)S(1)} %get-tuple-element.53), channel_id=1, source_target_pairs={{0,4},{4,0},{8,12},{12,8},{1,5},{5,1},{9,13},{13,9},{2,6},{6,2},{1... | collective-permute-start | bytes 1032200 | tf_op jit(solution)/shard_map/ppermute | solution.py:37
  13.4 15.2 %collective-permute-start.6 = (bf16[3,64,896]{2,1,0:T(8,128)(2,1)S(1)}, bf16[3,64,896]{2,1,0:T(8,128)(2,1)S(1)}, u32[]{:S(2)}, u32[]{:S(2)}) collective-permute-start(bf16[3,64,896]{2,1,0:T(8,128)(2,1)S(1)} %get-tuple-element.58), channel_id=1, source_target_pairs={{0,8},{4,12},{8,0},{12,4},{1,9},{5,13},{9,1},{13,5},{2,10},{6,14},... | collective-permute-start | bytes 1032200 | tf_op jit(solution)/shard_map/ppermute | solution.py:37
  15.1 35.9 %copy-start = (bf16[896,1024]{1,0:T(8,128)(2,1)S(1)}, bf16[896,1024]{1,0:T(8,128)(2,1)}, u32[]{:S(2)}) copy-start(bf16[896,1024]{1,0:T(8,128)(2,1)} %wk_ref.5) | copy-start | bytes 5505028
  15.1 35.9 %copy-start.1 = (bf16[896,1024]{1,0:T(8,128)(2,1)S(1)}, bf16[896,1024]{1,0:T(8,128)(2,1)}, u32[]{:S(2)}) copy-start(bf16[896,1024]{1,0:T(8,128)(2,1)} %wv_ref.5) | copy-start | bytes 5505028
  15.1 35.9 %copy-start.2 = (bf16[1,512,1024]{2,1,0:T(8,128)(2,1)S(1)}, bf16[1,512,1024]{2,1,0:T(8,128)(2,1)}, u32[]{:S(2)}) copy-start(bf16[1,512,1024]{2,1,0:T(8,128)(2,1)} %param.7) | copy-start | bytes 3145732
  15.1 35.9 %copy-start.3 = (bf16[1,512,1024]{2,1,0:T(8,128)(2,1)S(1)}, bf16[1,512,1024]{2,1,0:T(8,128)(2,1)}, u32[]{:S(2)}) copy-start(bf16[1,512,1024]{2,1,0:T(8,128)(2,1)} %param.13) | copy-start | bytes 3145732
  15.1 16.1 %collective-permute-start.9 = (bf16[3,64,896]{2,1,0:T(8,128)(2,1)S(1)}, bf16[3,64,896]{2,1,0:T(8,128)(2,1)S(1)}, u32[]{:S(2)}, u32[]{:S(2)}) collective-permute-start(bf16[3,64,896]{2,1,0:T(8,128)(2,1)S(1)} %get-tuple-element.63), channel_id=1, source_target_pairs={{0,12},{4,8},{8,4},{12,0},{1,13},{5,9},{9,5},{13,1},{2,14},{6,10},... | collective-permute-start | bytes 1032200 | tf_op jit(solution)/shard_map/ppermute | solution.py:37
  23.4 14.8 %collective-permute-start.4 = (bf16[3,64,896]{2,1,0:T(8,128)(2,1)S(1)}, bf16[3,64,896]{2,1,0:T(8,128)(2,1)S(1)}, u32[]{:S(2)}, u32[]{:S(2)}) collective-permute-start(bf16[3,64,896]{2,1,0:T(8,128)(2,1)S(1)} %get-tuple-element.55), channel_id=1, source_target_pairs={{0,4},{4,0},{8,12},{12,8},{1,5},{5,1},{9,13},{13,9},{2,6},{6,2},{1... | collective-permute-start | bytes 1032200 | tf_op jit(solution)/shard_map/ppermute | solution.py:37
  28.6 15.5 %collective-permute-start.7 = (bf16[3,64,896]{2,1,0:T(8,128)(2,1)S(1)}, bf16[3,64,896]{2,1,0:T(8,128)(2,1)S(1)}, u32[]{:S(2)}, u32[]{:S(2)}) collective-permute-start(bf16[3,64,896]{2,1,0:T(8,128)(2,1)S(1)} %get-tuple-element.60), channel_id=1, source_target_pairs={{0,8},{4,12},{8,0},{12,4},{1,9},{5,13},{9,1},{13,5},{2,10},{6,14},... | collective-permute-start | bytes 1032200 | tf_op jit(solution)/shard_map/ppermute | solution.py:37
  31.1 13.0 %collective-permute-start.10 = (bf16[3,64,896]{2,1,0:T(8,128)(2,1)S(1)}, bf16[3,64,896]{2,1,0:T(8,128)(2,1)S(1)}, u32[]{:S(2)}, u32[]{:S(2)}) collective-permute-start(bf16[3,64,896]{2,1,0:T(8,128)(2,1)S(1)} %get-tuple-element.65), channel_id=1, source_target_pairs={{0,12},{4,8},{8,4},{12,0},{1,13},{5,9},{9,5},{13,1},{2,14},{6,10},... | collective-permute-start | bytes 1032200 | tf_op jit(solution)/shard_map/ppermute | solution.py:37
  34.3 16.6 %collective-permute-start.13 = (bf16[6,64,896]{2,1,0:T(8,128)(2,1)S(1)}, bf16[6,64,896]{2,1,0:T(8,128)(2,1)S(1)}, u32[]{:S(2)}, u32[]{:S(2)}) collective-permute-start(bf16[6,64,896]{2,1,0:T(8,128)(2,1)S(1)} %unpack_rows.5.one_ref), channel_id=1, source_target_pairs={{0,1},{1,0},{2,3},{3,2},{4,5},{5,4},{6,7},{7,6},{8,9},{9,8},{10,11... | collective-permute-start | bytes 2064392 | tf_op jit(solution)/shard_map/ppermute | solution.py:37
  45.8 24.9 %collective-permute-start.12 = (bf16[6,64,896]{2,1,0:T(8,128)(2,1)S(1)}, bf16[6,64,896]{2,1,0:T(8,128)(2,1)S(1)}, u32[]{:S(2)}, u32[]{:S(2)}) collective-permute-start(bf16[6,64,896]{2,1,0:T(8,128)(2,1)S(1)} %unpack_rows.4.one_ref), channel_id=1, source_target_pairs={{0,1},{1,0},{2,3},{3,2},{4,5},{5,4},{6,7},{7,6},{8,9},{9,8},{10,11... | collective-permute-start | bytes 2064392 | tf_op jit(solution)/shard_map/ppermute | solution.py:37
  47.4 15.2 %collective-permute-start.11 = (bf16[2,2,64,896]{3,2,1,0:T(8,128)(2,1)S(1)}, bf16[2,2,64,896]{3,2,1,0:T(8,128)(2,1)S(1)}, u32[]{:S(2)}, u32[]{:S(2)}) collective-permute-start(bf16[2,2,64,896]{3,2,1,0:T(8,128)(2,1)S(1)} %get-tuple-element.67), channel_id=1, source_target_pairs={{0,12},{4,8},{8,4},{12,0},{1,13},{5,9},{9,5},{13,1},{2,14},{6,10},... | collective-permute-start | bytes 1376264 | tf_op jit(solution)/shard_map/ppermute | solution.py:37
  49.0 19.5 %collective-permute-start.8 = (bf16[2,2,64,896]{3,2,1,0:T(8,128)(2,1)S(1)}, bf16[2,2,64,896]{3,2,1,0:T(8,128)(2,1)S(1)}, u32[]{:S(2)}, u32[]{:S(2)}) collective-permute-start(bf16[2,2,64,896]{3,2,1,0:T(8,128)(2,1)S(1)} %get-tuple-element.62), channel_id=1, source_target_pairs={{0,8},{4,12},{8,0},{12,4},{1,9},{5,13},{9,1},{13,5},{2,10},{6,14},... | collective-permute-start | bytes 1376264 | tf_op jit(solution)/shard_map/ppermute | solution.py:37
  50.6 18.0 %collective-permute-start.5 = (bf16[2,2,64,896]{3,2,1,0:T(8,128)(2,1)S(1)}, bf16[2,2,64,896]{3,2,1,0:T(8,128)(2,1)S(1)}, u32[]{:S(2)}, u32[]{:S(2)}) collective-permute-start(bf16[2,2,64,896]{3,2,1,0:T(8,128)(2,1)S(1)} %get-tuple-element.57), channel_id=1, source_target_pairs={{0,4},{4,0},{8,12},{12,8},{1,5},{5,1},{9,13},{13,9},{2,6},{6,2},{1... | collective-permute-start | bytes 1376264 | tf_op jit(solution)/shard_map/ppermute | solution.py:37
  91.7 2.5 %collective-permute-start.14 = (bf16[448,1024]{1,0:T(8,128)(2,1)S(1)}, bf16[448,1024]{1,0:T(8,128)(2,1)S(1)}, u32[]{:S(2)}, u32[]{:S(2)}) collective-permute-start(bf16[448,1024]{1,0:T(8,128)(2,1)S(1)} %get-tuple-element.88), channel_id=1, source_target_pairs={{0,16},{16,0},{1,17},{17,1},{2,18},{18,2},{3,19},{19,3},{4,20},{20... | collective-permute-start | bytes 2752520 | tf_op jit(solution)/shard_map/ppermute | solution.py:37
  91.8 3.8 %collective-permute-start.15 = (bf16[448,1024]{1,0:T(8,128)(2,1)S(1)}, bf16[448,1024]{1,0:T(8,128)(2,1)S(1)}, u32[]{:S(2)}, u32[]{:S(2)}) collective-permute-start(bf16[448,1024]{1,0:T(8,128)(2,1)S(1)} %get-tuple-element.89), channel_id=1, source_target_pairs={{0,16},{16,0},{1,17},{17,1},{2,18},{18,2},{3,19},{19,3},{4,20},{20... | collective-permute-start | bytes 2752520 | tf_op jit(solution)/shard_map/ppermute | solution.py:37
  96.0 12.6 %collective-permute-start.16 = (bf16[2,112,1024]{2,1,0:T(8,128)(2,1)S(1)}, bf16[2,112,1024]{2,1,0:T(8,128)(2,1)S(1)}, u32[]{:S(2)}, u32[]{:S(2)}) collective-permute-start(bf16[2,112,1024]{2,1,0:T(8,128)(2,1)S(1)} %get-tuple-element.92), channel_id=1, source_target_pairs={{0,4},{4,0},{8,12},{12,8},{1,5},{5,1},{9,13},{13,9},{2,6},{6,2},{1... | collective-permute-start | bytes 1376264 | tf_op jit(solution)/shard_map/ppermute | solution.py:37
  97.3 12.3 %collective-permute-start.17 = (bf16[2,112,1024]{2,1,0:T(8,128)(2,1)S(1)}, bf16[2,112,1024]{2,1,0:T(8,128)(2,1)S(1)}, u32[]{:S(2)}, u32[]{:S(2)}) collective-permute-start(bf16[2,112,1024]{2,1,0:T(8,128)(2,1)S(1)} %get-tuple-element.93), channel_id=1, source_target_pairs={{0,8},{4,12},{8,0},{12,4},{1,9},{5,13},{9,1},{13,5},{2,10},{6,14},... | collective-permute-start | bytes 1376264 | tf_op jit(solution)/shard_map/ppermute | solution.py:37
  109.8 6.6 %collective-permute-start.18 = (bf16[1,112,1024]{2,1,0:T(8,128)(2,1)S(1)}, bf16[1,112,1024]{2,1,0:T(8,128)(2,1)S(1)}, u32[]{:S(2)}, u32[]{:S(2)}) collective-permute-start(bf16[1,112,1024]{2,1,0:T(8,128)(2,1)S(1)} %get-tuple-element.96), channel_id=1, source_target_pairs={{0,8},{4,12},{8,0},{12,4},{1,9},{5,13},{9,1},{13,5},{2,10},{6,14},... | collective-permute-start | bytes 688136 | tf_op jit(solution)/shard_map/ppermute | solution.py:37
  110.5 6.3 %collective-permute-start.19 = (bf16[1,112,1024]{2,1,0:T(8,128)(2,1)S(1)}, bf16[1,112,1024]{2,1,0:T(8,128)(2,1)S(1)}, u32[]{:S(2)}, u32[]{:S(2)}) collective-permute-start(bf16[1,112,1024]{2,1,0:T(8,128)(2,1)S(1)} %get-tuple-element.97), channel_id=1, source_target_pairs={{0,4},{4,0},{8,12},{12,8},{1,5},{5,1},{9,13},{13,9},{2,6},{6,2},{1... | collective-permute-start | bytes 688136 | tf_op jit(solution)/shard_map/ppermute | solution.py:37

commit v3 on v2

--- a/solution.py
+++ b/solution.py
@@ -13,7 +13,9 @@
 NEIGHBOURS = 2
 HALF = NEIGH_LEN // 2
 MIB = 1024 * 1024
-ATTEND_MIB = 32
+ATTEND_MIB = 26
+WEIGH_MIB = 26
+PIECES = 2
 CHUNKS = ((3, True), (3, True), (2, False))
 
 F32 = jnp.float32
@@ -159,21 +161,19 @@
     )(own, *incoming)
 
 
-def block_grads(context, wk_ref, wv_ref, q_ref, go_ref, out_ref, gq_ref, dk_ref, dv_ref):
+def block_grads(keys, values, query, grad, out_ref, gq_ref, dk_ref, dv_ref):
     scale = 1.0 / math.sqrt(HEAD_DIM)
-    keys = jnp.dot(context, wk_ref[...], preferred_element_type=F32).astype(BF16)
-    values = jnp.dot(context, wv_ref[...], preferred_element_type=F32).astype(BF16)
-    tokens, heads = q_ref.shape[0], q_ref.shape[1] // HEAD_DIM
+    tokens, heads = out_ref.shape[0], out_ref.shape[1] // HEAD_DIM
     zero = jnp.zeros((tokens, HEAD_DIM), BF16)
     cols = [slice(head * HEAD_DIM, (head + 1) * HEAD_DIM) for head in range(heads)]
 
     def reader(head):
-        upper = jnp.concatenate([q_ref[:, cols[head]], zero], axis=1)
-        lower = jnp.concatenate([zero, go_ref[:, cols[head]]], axis=1)
+        upper = jnp.concatenate([query(cols[head]), zero], axis=1)
+        lower = jnp.concatenate([zero, grad(cols[head])], axis=1)
         return jnp.concatenate([upper, lower], axis=0)
 
     def both(head):
-        return jnp.concatenate([keys[:, cols[head]], values[:, cols[head]]], axis=1)
+        return jnp.concatenate([keys(cols[head]), values(cols[head])], axis=1)
 
     def finish(head, probs, dscore):
         mixed = jnp.dot(jnp.concatenate([probs, dscore], axis=0), both(head), preferred_element_type=F32)
@@ -199,99 +199,141 @@
             finish(head - lag, *weights.pop(head - lag))
 
 
-def attend_kernel(first, last, slot_ref, one_ref, two_ref, wk_ref, wv_ref, q_ref, go_ref, *refs):
-    refs = list(refs[0 if first else 2 :])
-    acc_in = [] if first else [refs.pop(0), refs.pop(0)]
-    out_ref, gq_ref, *grad_refs, acck, accv, dk_ref, dv_ref, sems = refs
-    accs, grads = (acck, accv), (dk_ref, dv_ref)
-    step, steps = pl.program_id(0), pl.num_programs(0)
-    loads = [pltpu.make_async_copy(src, dst, sems.at[i]) for i, (src, dst) in enumerate(zip(acc_in, accs))]
-
-    @pl.when(step == 0)
-    def _():
-        for load in loads:
-            load.start()
-
-    width = one_ref.shape[-1]
-    context = jnp.concatenate([one_ref[...].reshape(-1, width), two_ref[...].reshape(-1, width)], axis=0)
-    block_grads(context, wk_ref, wv_ref, q_ref, go_ref, out_ref, gq_ref, dk_ref, dv_ref)
-
-    @pl.when(step == 0)
-    def _():
-        for load in loads:
-            load.wait()
-        if first:
-            for acc, grad in zip(accs, grads):
-                acc[...] = contract(context, grad[...], ((0,), (0,)))
-
-    @pl.when((step > 0) | (not first))
-    def _():
-        for acc, grad in zip(accs, grads):
-            acc[...] += contract(context, grad[...], ((0,), (0,)))
-
-    @pl.when(step == steps - 1)
-    def _():
-        if last:
-            half = grad_refs[0].shape[0]
-            dp = lax.axis_index("dp")
-            for i, side in enumerate((1 - dp, dp)):
-                for acc, grad_ref in zip(accs, grad_refs[2 * i : 2 * i + 2]):
-                    grad_ref[...] = acc[pl.ds(pl.multiple_of(side * half, half), half), :].astype(BF16)
-        else:
-            stores = [pltpu.make_async_copy(acc, dst, sems.at[i]) for i, (acc, dst) in enumerate(zip(accs, grad_refs))]
-            for store in stores:
-                store.start()
-            for store in stores:
-                store.wait()
-
-
-def attend(rows, slots, wk, wv, queries, grad_out, start, count, carried, last):
-    blocks = slots.shape[0] // (2 * NEIGHBOURS)
-    tokens, feat = queries.shape[0] // blocks, queries.shape[1]
+def attend_kernel(start, count, direct, first, id_ref, *refs):
+    refs = list(refs)
+    take = lambda n: [refs.pop(0) for _ in range(n)]
+    row_refs = take(direct if direct else 2)
+    wk_ref, wv_ref, q_in, go_in = take(4)
+    take(0 if first else 2)
+    out_hbm, gq_hbm, turned = take(3)
+    grad_refs = take(2 * PIECES)
+    q_ref, go_ref, out_ref, gq_ref, keys, values, dk_ref, dv_ref, rows, sems, row_sems, ranks = take(12)
+    size, width = rows.shape[1:]
+    feat = keys.shape[2]
+    blocks = pl.ds(start, count)
+
+    ins = [pltpu.make_async_copy(src.at[blocks], dst, sems.at[i]) for i, (src, dst) in enumerate(((q_in, q_ref), (go_in, go_ref)))]
+    if direct:
+        me = lax.axis_index("ret")
+
+        def fetch(k, rank, i):
+            b, n = divmod(i, NEIGHBOURS)
+            return pltpu.make_async_copy(row_refs[k].at[rank], rows.at[b, pl.ds(n * NEIGH_LEN, NEIGH_LEN)], row_sems.at[i])
+
+        for k in range(direct):
+            ranks[k] = 0
+        for i in range(count * NEIGHBOURS):
+            source = id_ref[(start * NEIGHBOURS + i) * 2] ^ me
+            rank = ranks[source]
+            ranks[source] = rank + 1
+            for k in range(direct):
+
+                @pl.when(source == k)
+                def _(k=k, rank=rank, i=i):
+                    fetch(k, rank, i).start()
+
+        for copy in ins:
+            copy.start()
+        for i in range(count * NEIGHBOURS):
+            fetch(0, 0, i).wait()
+    else:
+        for copy in ins:
+            copy.start()
+        part = size // 2
+        for i, ref in enumerate(row_refs):
+            rows[:, i * part : (i + 1) * part] = ref[...].reshape(count, part, width)
+
+    every = rows[...].reshape(-1, width)
+    turned[...] = every.T
+    for w_ref, target in ((wk_ref, keys), (wv_ref, values)):
+        product = jnp.dot(every, w_ref[...], preferred_element_type=F32).astype(BF16)
+        target[...] = product.reshape(count, size, feat)
+    for copy in ins:
+        copy.wait()
+
+    def block(b, carry):
+        pick = lambda ref: lambda cols: ref[b, :, cols]
+        block_grads(pick(keys), pick(values), pick(q_ref), pick(go_ref), out_ref.at[b], gq_ref.at[b], dk_ref.at[b], dv_ref.at[b])
+        return carry
+
+    lax.fori_loop(0, count, block, 0)
+    outs = [pltpu.make_async_copy(src, dst.at[blocks], sems.at[i]) for i, (src, dst) in enumerate(((out_ref, out_hbm), (gq_ref, gq_hbm)))]
+    for copy in outs:
+        copy.start()
+    span = feat // PIECES
+    for piece in range(PIECES):
+        cols = slice(piece * span, (piece + 1) * span)
+        for i, grad in enumerate((dk_ref, dv_ref)):
+            grad_refs[2 * piece + i][...] = grad[:, :, cols].reshape(-1, span)
+    for copy in outs:
+        copy.wait()
+
+
+def attend(rows, own, wk, wv, queries, grad_out, start, count, carried):
+    _, tokens, feat = queries.shape
     enc = wk.shape[0]
-    whole = lambda shape: pl.BlockSpec(shape, lambda b, s: (0, 0))
-    row = pl.BlockSpec((tokens, feat), lambda b, s: (start + b, 0))
-    if len(rows) == 2:
-        neighs = [pl.BlockSpec((NEIGHBOURS, HALF, enc), lambda b, s: (b, 0, 0))] * 2
-    else:
-        rows = rows * 2
-        neighs = [pl.BlockSpec((1, 2, HALF, enc), lambda b, s, n=n: (b * NEIGHBOURS + n, 0, 0, 0)) for n in range(NEIGHBOURS)]
+    context = NEIGHBOURS * NEIGH_LEN
+    direct = 0 if len(rows) == 2 else len(rows)
     row_shape = jax.ShapeDtypeStruct(queries.shape, BF16)
-    if last:
-        grad_shapes = [jax.ShapeDtypeStruct((enc // 2, feat), BF16)] * 4
-        grad_specs = [whole((enc // 2, feat))] * 4
-    else:
-        grad_shapes = [jax.ShapeDtypeStruct((enc, feat), F32)] * 2
-        grad_specs = [HBM] * 2
-    return pl.pallas_call(
-        functools.partial(attend_kernel, not carried, last),
-        grid_spec=pltpu.PrefetchScalarGridSpec(
-            num_scalar_prefetch=1,
-            grid=(count,),
-            in_specs=neighs + [whole((enc, feat))] * 2 + [row] * 2 + [HBM] * len(carried),
-            out_specs=[row, row] + grad_specs,
-            scratch_shapes=[
-                pltpu.VMEM((enc, feat), F32),
-                pltpu.VMEM((enc, feat), F32),
-                pltpu.VMEM((NEIGHBOURS * NEIGH_LEN, feat), BF16),
-                pltpu.VMEM((NEIGHBOURS * NEIGH_LEN, feat), BF16),
-                pltpu.SemaphoreType.DMA((2,)),
-            ],
-        ),
-        out_shape=[row_shape, row_shape] + grad_shapes,
-        input_output_aliases={7: 0, 8: 1} if carried else {},
+    if direct:
+        rows = [part.reshape(part.shape[0], NEIGH_LEN, enc) for part in rows]
+    turned_shape = jax.ShapeDtypeStruct((enc, count * context), BF16)
+    grad_shapes = [jax.ShapeDtypeStruct((count * context, feat // PIECES), BF16)] * (2 * PIECES)
+    aliased = 1 + len(rows) + 4
+    return pl.pallas_call(
+        functools.partial(attend_kernel, start, count, direct, not carried),
+        in_specs=[SMEM] + [ANY if direct else VMEM] * len(rows) + [VMEM] * 2 + [HBM] * 2 + [HBM] * len(carried),
+        out_specs=[HBM] * 2 + [VMEM] * (1 + 2 * PIECES),
+        scratch_shapes=[
+            pltpu.VMEM((count, tokens, feat), BF16),
+            pltpu.VMEM((count, tokens, feat), BF16),
+            pltpu.VMEM((count, tokens, feat), BF16),
+            pltpu.VMEM((count, tokens, feat), BF16),
+            pltpu.VMEM((count, context, feat), BF16),
+            pltpu.VMEM((count, context, feat), BF16),
+            pltpu.VMEM((count, context, feat), BF16),
+            pltpu.VMEM((count, context, feat), BF16),
+            pltpu.VMEM((count, context, enc), BF16),
+            pltpu.SemaphoreType.DMA((2,)),
+            pltpu.SemaphoreType.DMA((count * NEIGHBOURS,)),
+            pltpu.SMEM((max(direct, 1),), jnp.int32),
+        ],
+        out_shape=[row_shape, row_shape, turned_shape] + grad_shapes,
+        input_output_aliases={aliased: 0, aliased + 1: 1} if carried else {},
         compiler_params=params(ATTEND_MIB),
         name="attend_blocks",
-    )(slots, *rows, wk, wv, queries, grad_out, *carried)
+    )(own, *rows, wk, wv, queries, grad_out, *carried)
+
+
+def weigh_kernel(chunks, *refs):
+    half = refs[0].shape[0] // 2
+    dp = lax.axis_index("dp")
+    for i in range(2):
+        total = 0.0
+        for c in range(chunks):
+            total += jnp.dot(refs[c][...], refs[(1 + i) * chunks + c][...], preferred_element_type=F32)
+        refs[-1][...] = total
+        for j, side in enumerate((1 - dp, dp)):
+            refs[3 * chunks + 2 * j + i][...] = refs[-1][pl.ds(pl.multiple_of(side * half, half), half), :].astype(BF16)
+
+
+def weigh(turned, dks, dvs):
+    enc, width = turned[0].shape[0], dks[0].shape[1]
+    return pl.pallas_call(
+        functools.partial(weigh_kernel, len(turned)),
+        in_specs=[VMEM] * (3 * len(turned)),
+        out_specs=[VMEM] * 4,
+        out_shape=[jax.ShapeDtypeStruct((enc // 2, width), BF16)] * 4,
+        scratch_shapes=[pltpu.VMEM((enc, width), F32)],
+        compiler_params=params(WEIGH_MIB),
+        name="weigh_grads",
+    )(*turned, *dks, *dvs)
 
 
 def fold_kernel(dims, count, *refs):
     ret = lax.axis_index("ret")
     for i in range(count):
         held_ref, arrived_ref = refs[i], refs[count + i]
-        if dims is None:
-            refs[2 * count + i][...] = held_ref[0].astype(F32) + arrived_ref[0].astype(F32)
-            continue
         bit, place = dims[i]
         mine = (ret >> bit) & 1
         stride = 1 << place
@@ -305,11 +347,8 @@
 
 def fold(held, arrived, dims):
     count = len(held)
-    parts, rows, feat = held[0].shape
-    if dims is None:
-        shapes = [jax.ShapeDtypeStruct((rows, feat), F32)] * count
-    else:
-        shapes = [jax.ShapeDtypeStruct((parts // 2, rows, feat), BF16)] * (2 * count)
+    parts, rows, width = held[0].shape
+    shapes = [jax.ShapeDtypeStruct((parts // 2, rows, width), BF16)] * (2 * count)
     return pl.pallas_call(
         functools.partial(fold_kernel, dims, count),
         in_specs=[VMEM] * (2 * count),
@@ -320,22 +359,44 @@
     )(*held, *arrived)
 
 
+def join_kernel(*refs):
+    count = (len(refs) - 2) // 2
+    for i in range(count):
+        total = refs[i][0].astype(F32) + refs[count + i][0].astype(F32)
+        width = total.shape[1]
+        refs[2 * count + i % 2][:, i // 2 * width : (i // 2 + 1) * width] = total
+
+
+def join(held, arrived):
+    _, rows, width = held[0].shape
+    return pl.pallas_call(
+        join_kernel,
+        in_specs=[VMEM] * (2 * len(held)),
+        out_specs=[VMEM] * 2,
+        out_shape=[jax.ShapeDtypeStruct((rows, len(held) // 2 * width), F32)] * 2,
+        compiler_params=params(16),
+        name="join_grads",
+    )(*held, *arrived)
+
+
 def reduce_scatter(send, held):
     n_ret = lax.axis_size("ret")
     bits = n_ret.bit_length() - 1
     arrived = [swap(grad, "dp", 1) for grad in send]
     split = lambda grad: grad.reshape(n_ret, -1, grad.shape[-1])
     held, arrived = [split(grad) for grad in held], [split(grad) for grad in arrived]
-    left = [list(range(bits)) for _ in held]
+    left = [list(range(bits)) for _ in range(2)]
     for step in range(bits):
         bit = [step, bits - 1 - step]
         dims = tuple((b, bits_left.index(b)) for b, bits_left in zip(bit, left))
-        *send, held0, held1 = fold(held, arrived, dims)
-        held = [held0, held1]
         for b, bits_left in zip(bit, left):
             bits_left.remove(b)
-        arrived = [swap(grad, "ret", 1 << b) for grad, b in zip(send, bit)]
-    return fold(held, arrived, None)
+        for piece in range(0, len(held), 2):
+            pair = slice(piece, piece + 2)
+            parts = fold(held[pair], arrived[pair], dims)
+            held[pair] = parts[2:]
+            arrived[pair] = [swap(grad, "ret", 1 << b) for grad, b in zip(parts[:2], bit)]
+    return join(held, arrived)
 
 
 def spans_of(blocks):
@@ -362,6 +423,7 @@
     outgoing = pick(ids, normed, spans[:1], capacity)
     if len(spans) > 1:
         outgoing = outgoing + pick(ids, normed, spans[1:], capacity)
+    query_blocks, grad_blocks = (array.reshape(blocks, -1, array.shape[2]) for array in (queries, grad_out))
     carried, arrivals = [], []
     for slots in outgoing:
         slots = list(slots)
@@ -369,14 +431,37 @@
             for k in range(1, n_ret):
                 arrivals[-1][k], slots[k] = lax.optimization_barrier((arrivals[-1][k], slots[k]))
         arrivals.append(slots[:1] + [swap(slots[k], "ret", k) for k in range(1, n_ret)])
-    for incoming, (start, count, pair) in zip(arrivals, spans):
-        mine = unpack(own, incoming, start, count)
-        rows = [mine, swap(mine, "ctx", 1)] if pair else [mine]
-        last = start + count == blocks
-        carried = attend(rows, own, w_key, w_value, queries[0], grad_out[0], start, count, carried, last)
-    attended, grad_queries, *grads = carried
-    grad_w_key, grad_w_value = reduce_scatter(grads[:2], grads[2:])
-    return attended[None], grad_queries[None], grad_w_key, grad_w_value
+    rows, turned, found = [None] * len(spans), [], []
+
+    def prepare(i):
+        start, count, pair = spans[i]
+        if pair:
+            mine = unpack(own, arrivals[i], start, count)
+            rows[i] = [mine, swap(mine, "ctx", 1)]
+        else:
+            rows[i] = arrivals[i]
+
+    prepare(0)
+    for i, (start, count, pair) in enumerate(spans):
+        last = i + 1 == len(spans)
+        if not last and spans[i + 1][2]:
+            prepare(i + 1)
+            rows[i][0], rows[i + 1][0] = lax.optimization_barrier((rows[i][0], rows[i + 1][0]))
+        attended, grad_queries, flipped, *grads = attend(rows[i], own, w_key, w_value, query_blocks, grad_blocks, start, count, carried)
+        carried = [attended, grad_queries]
+        turned.append(flipped)
+        found.append(grads)
+        if not last and rows[i + 1] is None:
+            carried[0], arrivals[i + 1] = lax.optimization_barrier((carried[0], arrivals[i + 1]))
+            prepare(i + 1)
+    send, held = [], []
+    for piece in range(PIECES):
+        parts = weigh(turned, *([grads[2 * piece + i] for grads in found] for i in range(2)))
+        send += parts[:2]
+        held += parts[2:]
+    attended, grad_queries = carried
+    grad_w_key, grad_w_value = reduce_scatter(send, held)
+    return attended.reshape(queries.shape), grad_queries.reshape(queries.shape), grad_w_key, grad_w_value
 
 
 def solution(mesh):

time: 118 us -> 110 us (0.932)
  waiting for transfers between devices: 40 us -> 33.5 us
  Pallas kernels: 49.2 us -> 43.8 us
  starting transfers between devices: 24.8 us -> 28.4 us
    ppermute x20 -> x26, waiting for transfers between devices: 40 us -> 33.5 us  [swap(): return lax.ppermute(array, axis, [(i, i ^ bit) for i in range(size)])]
    ppermute x20 -> x26, starting transfers between devices: 24.8 us -> 28.4 us  [swap(): return lax.ppermute(array, axis, [(i, i ^ bit) for i in range(size)])]
    pallas_call x2, Pallas kernels: 8.33 us -> 4.93 us  [pick(): pl.pallas_call(functools.partial(pick_kernel, spans), in_specs=[SMEM, ANY...]
    pallas_call x3 -> x2, Pallas kernels: 5.32 us -> 3.27 us  [unpack(): pl.pallas_call(functools.partial(unpack_kernel, start, count), in_specs=[...]
    pallas_call x3 -> x6, Pallas kernels: 32.7 us -> 33.7 us  [the longest x3 24.2 us: attend(): pl.pallas_call(functools.partial(attend_kernel, start, count, direct, not...]
  transfers between devices with their start and end apart: 20 -> 26, of which waited for: 12 -> 12; matrix products, arithmetic and copies ran while one was open for 0% -> 0% of each run, Pallas kernels for 20% -> 27%
where the time goes in v3:
time: 110 us
  Pallas kernels  43.8 us (40%)
  waiting for transfers between devices  33.5 us (30%)
  starting transfers between devices  28.4 us (26%)
  local copies, waits for them, and re-layouts  2.33 us (2%)
    ppermute x26, waiting for transfers between devices, swap(): return lax.ppermute(array, axis, [(i, i ^ bit) for i in range(size)])  33.5 us
    ppermute x26, starting transfers between devices, swap(): return lax.ppermute(array, axis, [(i, i ^ bit) for i in range(size)])  28.4 us
    pallas_call x3, Pallas kernels, attend(): pl.pallas_call(functools.partial(attend_kernel, start, count, direct, not...  24.2 us
    pallas_call x2, Pallas kernels, weigh(): pl.pallas_call(functools.partial(weigh_kernel, len(turned)), in_specs=[VM...  8.57 us
    pallas_call x2, Pallas kernels, pick(): pl.pallas_call(functools.partial(pick_kernel, spans), in_specs=[SMEM, ANY...  4.93 us
    pallas_call x2, Pallas kernels, unpack(): pl.pallas_call(functools.partial(unpack_kernel, start, count), in_specs=[...  3.27 us
  transfers between devices with their start and end apart: 26, of which 12 were waited for; matrix products, arithmetic and copies ran while one was open for 0% of the time, Pallas kernels for 27%

profile of v3, /device:TPU:0, one launch (start us, length us, event | category | flops | bytes accessed | tf_op | source)
XLA Modules:
  0.0 109.6 jit_solution(6844083446815671252)
XLA Ops:
  0.6 0.7 pad_add_fusion
  1.3 0.1 copy.17
  1.4 0.1 reshape.62.id_ref
  1.5 4.0 %collective-permute-start.2 = (s32[32]{0:T(128)S(1)}, s32[32]{0:T(128)S(1)}, u32[]{:S(2)}, u32[]{:S(2)}) collective-permute-start(s32[32]{0:T(128)S(1)} %reshape.62.id_ref), channel_id=1, source_target_pairs={{0,12},{4,8},{8,4},{12,0},{1,13},{5,9},{9,5},{13,1},{2,14},{6,10},... | collective-permute-start | bytes 392 | tf_op jit(solution)/shard_map/ppermute | solution.py:39
  5.5 0.5 collective-permute-start.1
  6.0 0.1 collective-permute-start
  6.1 0.1 stack_reshape.3
  6.2 0.0 copy-start.4
  6.2 2.0 %copy-done.4 = bf16[1,2048,896]{2,1,0:T(8,128)(2,1)S(1)} copy-done((bf16[1,2048,896]{2,1,0:T(8,128)(2,1)S(1)}, bf16[1,2048,896]{2,1,0:T(8,128)(2,1)}, u32[]{:S(2)}) %copy-start.4) | copy-done | bytes 3670040
  8.3 1.2 %normalize_rows.1 = bf16[2048,896]{1,0:T(8,128)(2,1)S(1)} custom-call(bf16[2048,896]{1,0:T(8,128)(2,1)S(1)} %bitcast.31), custom_call_target="tpu_custom_call" | custom-call | tf_op jit(solution)/shard_map/normalize_rows/pallas_call | solution.py:52
  9.5 0.0 collective-permute-done
  9.5 1.9 %pick_rows.2 = (bf16[3,64,896]{2,1,0:T(8,128)(2,1)S(1)}, bf16[3,64,896]{2,1,0:T(8,128)(2,1)S(1)}, bf16[3,64,896]{2,1,0:T(8,128)(2,1)S(1)}, bf16[3,64,896]{2,1,0:T(8,128)(2,1)S(1)}) custom-call(s32[4,32]{1,0:T(4,128)S(1)} %pad_add_fusion.1.id_ref, bf16[16,2,64,896]{3,2,1,0:T(8,128)(2,1)S(1)} %bitcast.23), custom_call_target="tpu_custom_call" | custom-call | tf_op jit(solution)/shard_map/pick_rows/pallas_call | solution.py:111
  11.4 2.9 %collective-permute-start.3 = (bf16[3,64,896]{2,1,0:T(8,128)(2,1)S(1)}, bf16[3,64,896]{2,1,0:T(8,128)(2,1)S(1)}, u32[]{:S(2)}, u32[]{:S(2)}) collective-permute-start(bf16[3,64,896]{2,1,0:T(8,128)(2,1)S(1)} %get-tuple-element.83), channel_id=1, source_target_pairs={{0,4},{4,0},{8,12},{12,8},{1,5},{5,1},{9,13},{13,9},{2,6},{6,2},{1... | collective-permute-start | bytes 1032200 | tf_op jit(solution)/shard_map/ppermute | solution.py:39
  14.3 0.1 collective-permute-start.4
  14.4 1.4 %collective-permute-start.5 = (bf16[3,64,896]{2,1,0:T(8,128)(2,1)S(1)}, bf16[3,64,896]{2,1,0:T(8,128)(2,1)S(1)}, u32[]{:S(2)}, u32[]{:S(2)}) collective-permute-start(bf16[3,64,896]{2,1,0:T(8,128)(2,1)S(1)} %get-tuple-element.89), channel_id=1, source_target_pairs={{0,12},{4,8},{8,4},{12,0},{1,13},{5,9},{9,5},{13,1},{2,14},{6,10},... | collective-permute-start | bytes 1032200 | tf_op jit(solution)/shard_map/ppermute | solution.py:39
  15.9 3.1 %pick_rows.3 = (bf16[3,64,896]{2,1,0:T(8,128)(2,1)S(1)}, bf16[3,64,896]{2,1,0:T(8,128)(2,1)S(1)}, bf16[3,64,896]{2,1,0:T(8,128)(2,1)S(1)}, bf16[3,64,896]{2,1,0:...) custom-call(s32[4,32]{1,0:T(4,128)S(1)} %pad_add_fusion.1.id_ref, ...), custom_call_target="tpu_custom_call" | custom-call | tf_op jit(solution)/shard_map/pick_rows/pallas_call | solution.py:111
  18.9 4.4 %collective-permute-done.3.refs_1_ = bf16[3,64,896]{2,1,0:T(8,128)(2,1)S(1)} collective-permute-done((bf16[3,64,896]{2,1,0:T(8,128)(2,1)S(1)}, bf16[3,64,896]{2,1,0:T(8,128)(2,1)S(1)}, u32[]{:S(2)}, u32[]{:S(2)}) %collective-permute-start.3) | collective-permute-done | bytes 344096 | tf_op jit(solution)/shard_map/ppermute | solution.py:39
  23.3 2.0 %collective-permute-start.6 = (bf16[3,64,896]{2,1,0:T(8,128)(2,1)S(1)}, bf16[3,64,896]{2,1,0:T(8,128)(2,1)S(1)}, u32[]{:S(2)}, u32[]{:S(2)}) collective-permute-start(bf16[3,64,896]{2,1,0:T(8,128)(2,1)S(1)} %get-tuple-element.93), channel_id=1, source_target_pairs={{0,4},{4,0},{8,12},{12,8},{1,5},{5,1},{9,13},{13,9},{2,6},{6,2},{1... | collective-permute-start | bytes 1032200 | tf_op jit(solution)/shard_map/ppermute | solution.py:39
  25.3 6.2 %collective-permute-done.4.refs_2_ = bf16[3,64,896]{2,1,0:T(8,128)(2,1)S(1)} collective-permute-done((bf16[3,64,896]{2,1,0:T(8,128)(2,1)S(1)}, bf16[3,64,896]{2,1,0:T(8,128)(2,1)S(1)}, u32[]{:S(2)}, u32[]{:S(2)}) %collective-permute-start.4) | collective-permute-done | bytes 344096 | tf_op jit(solution)/shard_map/ppermute | solution.py:39
  31.6 0.0 collective-permute-done.5.refs_3_
  31.6 2.1 %collective-permute-start.8 = (bf16[3,64,896]{2,1,0:T(8,128)(2,1)S(1)}, bf16[3,64,896]{2,1,0:T(8,128)(2,1)S(1)}, u32[]{:S(2)}, u32[]{:S(2)}) collective-permute-start(bf16[3,64,896]{2,1,0:T(8,128)(2,1)S(1)} %get-tuple-element.99), channel_id=1, source_target_pairs={{0,12},{4,8},{8,4},{12,0},{1,13},{5,9},{9,5},{13,1},{2,14},{6,10},... | collective-permute-start | bytes 1032200 | tf_op jit(solution)/shard_map/ppermute | solution.py:39
  33.6 1.6 %unpack_rows.2.refs_0_ = bf16[6,64,896]{2,1,0:T(8,128)(2,1)S(1)} custom-call(s32[32]{0:T(128)S(1)} %reshape.62.id_ref, bf16[3,64,896]{2,1,0:T(8,128)(2,1)S(1)} %get-tuple-element.82.refs_0_, bf16[3,64,896]{2,1,0:T(8,128)(2,1)S(1)} %collective-permute-done.3.refs_1_, bf16[3,64,896]{2,1,0:T(8,128)(2,1)S(1)} %collective-permute-done.4.refs_2_, ...), custom_call_target="tpu_custom_call" | custom-call | tf_op jit(solution)/shard_map/unpack_rows/pallas_call | solution.py:150
  35.3 1.6 %collective-permute-start.10 = (bf16[6,64,896]{2,1,0:T(8,128)(2,1)S(1)}, bf16[6,64,896]{2,1,0:T(8,128)(2,1)S(1)}, u32[]{:S(2)}, u32[]{:S(2)}) collective-permute-start(bf16[6,64,896]{2,1,0:T(8,128)(2,1)S(1)} %unpack_rows.2.refs_0_), channel_id=1, source_target_pairs={{0,1},{1,0},{2,3},{3,2},{4,5},{5,4},{6,7},{7,6},{8,9},{9,8},{10,11... | collective-permute-start | bytes 2064392 | tf_op jit(solution)/shard_map/ppermute | solution.py:39
  36.9 1.2 %collective-permute-done.6.refs_1_ = bf16[3,64,896]{2,1,0:T(8,128)(2,1)S(1)} collective-permute-done((bf16[3,64,896]{2,1,0:T(8,128)(2,1)S(1)}, bf16[3,64,896]{2,1,0:T(8,128)(2,1)S(1)}, u32[]{:S(2)}, u32[]{:S(2)}) %collective-permute-start.6) | collective-permute-done | bytes 344096 | tf_op jit(solution)/shard_map/ppermute | solution.py:39
  38.1 7.9 %collective-permute-done.7.refs_2_ = bf16[3,64,896]{2,1,0:T(8,128)(2,1)S(1)} collective-permute-done((bf16[3,64,896]{2,1,0:T(8,128)(2,1)S(1)}, bf16[3,64,896]{2,1,0:T(8,128)(2,1)S(1)}, u32[]{:S(2)}, u32[]{:S(2)}) %collective-permute-start.7) | collective-permute-done | bytes 344096 | tf_op jit(solution)/shard_map/ppermute | solution.py:39
  46.0 1.6 %unpack_rows.3.refs_0_ = bf16[6,64,896]{2,1,0:T(8,128)(2,1)S(1)} custom-call(s32[32]{0:T(128)S(1)} %reshape.62.id_ref, bf16[3,64,896]{2,1,0:T(8,128)(2,1)S(1)} %get-tuple-element.92.refs_0_, bf16[3,64,896]{2,1,0:T(8,128)(2,1)S(1)} %collective-permute-done.6.refs_1_, bf16[3,64,896]{2,1,0:T(8,128)(2,1)S(1)} %collective-permute-done.7.refs_2_, ...), custom_call_target="tpu_custom_call" | custom-call | tf_op jit(solution)/shard_map/unpack_rows/pallas_call | solution.py:150
  47.6 1.6 %collective-permute-start.9 = (bf16[6,64,896]{2,1,0:T(8,128)(2,1)S(1)}, bf16[6,64,896]{2,1,0:T(8,128)(2,1)S(1)}, u32[]{:S(2)}, u32[]{:S(2)}) collective-permute-start(bf16[6,64,896]{2,1,0:T(8,128)(2,1)S(1)} %unpack_rows.3.refs_0_), channel_id=1, source_target_pairs={{0,1},{1,0},{2,3},{3,2},{4,5},{5,4},{6,7},{7,6},{8,9},{9,8},{10,11... | collective-permute-start | bytes 2064392 | tf_op jit(solution)/shard_map/ppermute | solution.py:39
  49.3 0.5 collective-permute-start.13
  49.8 0.6 collective-permute-start.12
  50.4 2.4 %collective-permute-start.11 = (bf16[2,2,64,896]{3,2,1,0:T(8,128)(2,1)S(1)}, bf16[2,2,64,896]{3,2,1,0:T(8,128)(2,1)S(1)}, u32[]{:S(2)}, u32[]{:S(2)}) collective-permute-start(bf16[2,2,64,896]{3,2,1,0:T(8,128)(2,1)S(1)} %get-tuple-element.108), channel_id=1, source_target_pairs={{0,4},{4,0},{8,12},{12,8},{1,5},{5,1},{9,13},{13,9},{2,6},{6,2},{1... | collective-permute-start | bytes 1376264 | tf_op jit(solution)/shard_map/ppermute | solution.py:39
  52.8 0.0 collective-permute-done.10.refs_1_
  52.8 8.4 %attend_blocks.3 = (bf16[8,64,1024]{2,1,0:T(8,128)(2,1)}, bf16[8,64,1024]{2,1,0:T(8,128)(2,1)}, bf16[896,768]{1,0:T(8,128)(2,1)S(1)}, bf16[768,512]{1,0:T(8,128)...) custom-call(s32[32]{0:T(128)S(1)} %reshape.62.id_ref, ...), custom_call_target="tpu_custom_call" | custom-call | tf_op jit(solution)/shard_map/attend_blocks/pallas_call | solution.py:283
  61.2 2.3 %collective-permute-done.9.refs_1_ = bf16[6,64,896]{2,1,0:T(8,128)(2,1)S(1)} collective-permute-done((bf16[6,64,896]{2,1,0:T(8,128)(2,1)S(1)}, bf16[6,64,896]{2,1,0:T(8,128)(2,1)S(1)}, u32[]{:S(2)}, u32[]{:S(2)}) %collective-permute-start.9) | collective-permute-done | bytes 688160 | tf_op jit(solution)/shard_map/ppermute | solution.py:39
  63.5 8.4 %attend_blocks.4 = (bf16[8,64,1024]{2,1,0:T(8,128)(2,1)}, bf16[8,64,1024]{2,1,0:T(8,128)(2,1)}, bf16[896,768]{1,0:T(8,128)(2,1)S(1)}, bf16[768,512]{1,0:T(8,128)...) custom-call(s32[32]{0:T(128)S(1)} %reshape.62.id_ref, ...), custom_call_target="tpu_custom_call", output_to_operand_aliasing={{0}: (7, {}), {1}: (8, {})} | custom-call | tf_op jit(solution)/shard_map/attend_blocks/pallas_call | solution.py:283
  71.9 0.0 collective-permute-done.12
  72.0 0.0 collective-permute-done.11
  72.0 7.3 %attend_blocks.5 = (bf16[8,64,1024]{2,1,0:T(8,128)(2,1)}, bf16[8,64,1024]{2,1,0:T(8,128)(2,1)}, bf16[896,512]{1,0:T(8,128)(2,1)S(1)}, bf16[512,512]{1,0:T(8,128)...) custom-call(s32[32]{0:T(128)S(1)} %reshape.62.id_ref, ...), custom_call_target="tpu_custom_call", output_to_operand_aliasing={{0}: (9, {}), {1}: (10, {})} | custom-call | tf_op jit(solution)/shard_map/attend_blocks/pallas_call | solution.py:283
  79.3 4.3 %weigh_grads.2 = (bf16[448,512]{1,0:T(8,128)(2,1)S(1)}, bf16[448,512]{1,0:T(8,128)(2,1)S(1)}, bf16[448,512]{1,0:T(8,128)(2,1)S(1)}, bf16[448,512]{1,0:T(8,128)(2,1)S(1)}) custom-call(bf16[896,768]{1,0:T(8,128)(2,1)S(1)} %get-tuple-element.119.refs_0_, bf16[896,768]{1,0:T(8,128)(2,1)S(1)} %get-tuple-element.120.refs_1_, ...), custom_call_target="tpu_custom_call" | custom-call | tf_op jit(solution)/shard_map/weigh_grads/pallas_call | solution.py:322
  83.6 0.1 collective-permute-start.14
  83.6 0.5 collective-permute-start.15
  84.1 4.3 %weigh_grads.3 = (bf16[448,512]{1,0:T(8,128)(2,1)S(1)}, bf16[448,512]{1,0:T(8,128)(2,1)S(1)}, bf16[448,512]{1,0:T(8,128)(2,1)S(1)}, bf16[448,512]{1,0:T(8,128)(2,1)S(1)}) custom-call(bf16[896,768]{1,0:T(8,128)(2,1)S(1)} %get-tuple-element.119.refs_0_, bf16[896,768]{1,0:T(8,128)(2,1)S(1)} %get-tuple-element.120.refs_1_, ...), custom_call_target="tpu_custom_call" | custom-call | tf_op jit(solution)/shard_map/weigh_grads/pallas_call | solution.py:322
  88.4 0.1 collective-permute-start.18
  88.6 0.4 collective-permute-start.19
  89.0 0.2 fold_grads.4
  89.3 0.6 collective-permute-start.16
  89.9 0.4 collective-permute-start.17
  90.3 0.0 collective-permute-done.18
  90.3 0.7 collective-permute-done.19
  91.0 0.2 fold_grads.6
  91.2 0.9 collective-permute-start.20
  92.1 1.6 %collective-permute-start.21 = (bf16[2,112,512]{2,1,0:T(8,128)(2,1)S(1)}, bf16[2,112,512]{2,1,0:T(8,128)(2,1)S(1)}, u32[]{:S(2)}, u32[]{:S(2)}) collective-permute-start(bf16[2,112,512]{2,1,0:T(8,128)(2,1)S(1)} %get-tuple-element.151), channel_id=1, source_target_pairs={{0,8},{4,12},{8,0},{12,4},{1,9},{5,13},{9,1},{13,5},{2,10},{6,14},... | collective-permute-start | bytes 688136 | tf_op jit(solution)/shard_map/ppermute | solution.py:39
  93.7 4.1 %collective-permute-done.16.refs_2_ = bf16[2,112,512]{2,1,0:T(8,128)(2,1)S(1)} collective-permute-done((bf16[2,112,512]{2,1,0:T(8,128)(2,1)S(1)}, bf16[2,112,512]{2,1,0:T(8,128)(2,1)S(1)}, u32[]{:S(2)}, u32[]{:S(2)}) %collective-permute-start.16) | collective-permute-done | bytes 229408 | tf_op jit(solution)/shard_map/ppermute | solution.py:39
  97.8 0.6 collective-permute-done.17.refs_3_
  98.4 0.1 fold_grads.5
  98.5 0.5 collective-permute-start.22
  98.9 1.5 %collective-permute-start.23 = (bf16[1,112,512]{2,1,0:T(8,128)(2,1)S(1)}, bf16[1,112,512]{2,1,0:T(8,128)(2,1)S(1)}, u32[]{:S(2)}, u32[]{:S(2)}) collective-permute-start(bf16[1,112,512]{2,1,0:T(8,128)(2,1)S(1)} %get-tuple-element.155), channel_id=1, source_target_pairs={{0,4},{4,0},{8,12},{12,8},{1,5},{5,1},{9,13},{13,9},{2,6},{6,2},{1... | collective-permute-start | bytes 344072 | tf_op jit(solution)/shard_map/ppermute | solution.py:39
  100.4 2.2 %collective-permute-done.20.refs_2_ = bf16[2,112,512]{2,1,0:T(8,128)(2,1)S(1)} collective-permute-done((bf16[2,112,512]{2,1,0:T(8,128)(2,1)S(1)}, bf16[2,112,512]{2,1,0:T(8,128)(2,1)S(1)}, u32[]{:S(2)}, u32[]{:S(2)}) %collective-permute-start.20) | collective-permute-done | bytes 229408 | tf_op jit(solution)/shard_map/ppermute | solution.py:39
  102.7 0.6 collective-permute-done.21.refs_3_
  103.3 0.1 fold_grads.7
  103.4 0.5 collective-permute-start.24
  103.9 1.5 %collective-permute-start.25 = (bf16[1,112,512]{2,1,0:T(8,128)(2,1)S(1)}, bf16[1,112,512]{2,1,0:T(8,128)(2,1)S(1)}, u32[]{:S(2)}, u32[]{:S(2)}) collective-permute-start(bf16[1,112,512]{2,1,0:T(8,128)(2,1)S(1)} %get-tuple-element.157), channel_id=1, source_target_pairs={{0,4},{4,0},{8,12},{12,8},{1,5},{5,1},{9,13},{13,9},{2,6},{6,2},{1... | collective-permute-start | bytes 344072 | tf_op jit(solution)/shard_map/ppermute | solution.py:39
  105.4 2.9 %collective-permute-done.24.refs_6_ = bf16[1,112,512]{2,1,0:T(8,128)(2,1)S(1)} collective-permute-done((bf16[1,112,512]{2,1,0:T(8,128)(2,1)S(1)}, bf16[1,112,512]{2,1,0:T(8,128)(2,1)S(1)}, u32[]{:S(2)}, u32[]{:S(2)}) %collective-permute-start.24) | collective-permute-done | bytes 114720 | tf_op jit(solution)/shard_map/ppermute | solution.py:39
  108.3 0.4 collective-permute-done.25.refs_7_
  108.6 1.0 join_grads.1
  (18 shorter events, 0.0 us)
Async XLA Ops:
  1.5 8.0 %collective-permute-start.2 = (s32[32]{0:T(128)S(1)}, s32[32]{0:T(128)S(1)}, u32[]{:S(2)}, u32[]{:S(2)}) collective-permute-start(s32[32]{0:T(128)S(1)} %reshape.62.id_ref), channel_id=1, source_target_pairs={{0,12},{4,8},{8,4},{12,0},{1,13},{5,9},{9,5},{13,1},{2,14},{6,10},... | collective-permute-start | bytes 392 | tf_op jit(solution)/shard_map/ppermute | solution.py:39
  5.5 4.0 %collective-permute-start.1 = (s32[32]{0:T(128)S(1)}, s32[32]{0:T(128)S(1)}, u32[]{:S(2)}, u32[]{:S(2)}) collective-permute-start(s32[32]{0:T(128)S(1)} %reshape.62.id_ref), channel_id=1, source_target_pairs={{0,8},{4,12},{8,0},{12,4},{1,9},{5,13},{9,1},{13,5},{2,10},{6,14},... | collective-permute-start | bytes 392 | tf_op jit(solution)/shard_map/ppermute | solution.py:39
  6.0 3.5 %collective-permute-start = (s32[32]{0:T(128)S(1)}, s32[32]{0:T(128)S(1)}, u32[]{:S(2)}, u32[]{:S(2)}) collective-permute-start(s32[32]{0:T(128)S(1)} %reshape.62.id_ref), channel_id=1, source_target_pairs={{0,4},{4,0},{8,12},{12,8},{1,5},{5,1},{9,13},{13,9},{2,6},{6,2},{1... | collective-permute-start | bytes 392 | tf_op jit(solution)/shard_map/ppermute | solution.py:39
  6.2 2.0 %copy-start.4 = (bf16[1,2048,896]{2,1,0:T(8,128)(2,1)S(1)}, bf16[1,2048,896]{2,1,0:T(8,128)(2,1)}, u32[]{:S(2)}) copy-start(bf16[1,2048,896]{2,1,0:T(8,128)(2,1)} %param.8) | copy-start | bytes 11010052
  11.4 11.9 %collective-permute-start.3 = (bf16[3,64,896]{2,1,0:T(8,128)(2,1)S(1)}, bf16[3,64,896]{2,1,0:T(8,128)(2,1)S(1)}, u32[]{:S(2)}, u32[]{:S(2)}) collective-permute-start(bf16[3,64,896]{2,1,0:T(8,128)(2,1)S(1)} %get-tuple-element.83), channel_id=1, source_target_pairs={{0,4},{4,0},{8,12},{12,8},{1,5},{5,1},{9,13},{13,9},{2,6},{6,2},{1... | collective-permute-start | bytes 1032200 | tf_op jit(solution)/shard_map/ppermute | solution.py:39
  14.3 17.2 %collective-permute-start.4 = (bf16[3,64,896]{2,1,0:T(8,128)(2,1)S(1)}, bf16[3,64,896]{2,1,0:T(8,128)(2,1)S(1)}, u32[]{:S(2)}, u32[]{:S(2)}) collective-permute-start(bf16[3,64,896]{2,1,0:T(8,128)(2,1)S(1)} %get-tuple-element.86), channel_id=1, source_target_pairs={{0,8},{4,12},{8,0},{12,4},{1,9},{5,13},{9,1},{13,5},{2,10},{6,14},... | collective-permute-start | bytes 1032200 | tf_op jit(solution)/shard_map/ppermute | solution.py:39
  14.4 17.1 %collective-permute-start.5 = (bf16[3,64,896]{2,1,0:T(8,128)(2,1)S(1)}, bf16[3,64,896]{2,1,0:T(8,128)(2,1)S(1)}, u32[]{:S(2)}, u32[]{:S(2)}) collective-permute-start(bf16[3,64,896]{2,1,0:T(8,128)(2,1)S(1)} %get-tuple-element.89), channel_id=1, source_target_pairs={{0,12},{4,8},{8,4},{12,0},{1,13},{5,9},{9,5},{13,1},{2,14},{6,10},... | collective-permute-start | bytes 1032200 | tf_op jit(solution)/shard_map/ppermute | solution.py:39
  15.9 36.9 %copy-start.2 = (bf16[1,512,1024]{2,1,0:T(8,128)(2,1)S(1)}, bf16[1,512,1024]{2,1,0:T(8,128)(2,1)}, u32[]{:S(2)}) copy-start(bf16[1,512,1024]{2,1,0:T(8,128)(2,1)} %param.7) | copy-start | bytes 3145732
  15.9 36.9 %copy-start.3 = (bf16[1,512,1024]{2,1,0:T(8,128)(2,1)S(1)}, bf16[1,512,1024]{2,1,0:T(8,128)(2,1)}, u32[]{:S(2)}) copy-start(bf16[1,512,1024]{2,1,0:T(8,128)(2,1)} %param.13) | copy-start | bytes 3145732
  23.3 14.8 %collective-permute-start.6 = (bf16[3,64,896]{2,1,0:T(8,128)(2,1)S(1)}, bf16[3,64,896]{2,1,0:T(8,128)(2,1)S(1)}, u32[]{:S(2)}, u32[]{:S(2)}) collective-permute-start(bf16[3,64,896]{2,1,0:T(8,128)(2,1)S(1)} %get-tuple-element.93), channel_id=1, source_target_pairs={{0,4},{4,0},{8,12},{12,8},{1,5},{5,1},{9,13},{13,9},{2,6},{6,2},{1... | collective-permute-start | bytes 1032200 | tf_op jit(solution)/shard_map/ppermute | solution.py:39
  31.6 14.4 %collective-permute-start.7 = (bf16[3,64,896]{2,1,0:T(8,128)(2,1)S(1)}, bf16[3,64,896]{2,1,0:T(8,128)(2,1)S(1)}, u32[]{:S(2)}, u32[]{:S(2)}) collective-permute-start(bf16[3,64,896]{2,1,0:T(8,128)(2,1)S(1)} %get-tuple-element.96), channel_id=1, source_target_pairs={{0,8},{4,12},{8,0},{12,4},{1,9},{5,13},{9,1},{13,5},{2,10},{6,14},... | collective-permute-start | bytes 1032200 | tf_op jit(solution)/shard_map/ppermute | solution.py:39
  31.6 14.4 %collective-permute-start.8 = (bf16[3,64,896]{2,1,0:T(8,128)(2,1)S(1)}, bf16[3,64,896]{2,1,0:T(8,128)(2,1)S(1)}, u32[]{:S(2)}, u32[]{:S(2)}) collective-permute-start(bf16[3,64,896]{2,1,0:T(8,128)(2,1)S(1)} %get-tuple-element.99), channel_id=1, source_target_pairs={{0,12},{4,8},{8,4},{12,0},{1,13},{5,9},{9,5},{13,1},{2,14},{6,10},... | collective-permute-start | bytes 1032200 | tf_op jit(solution)/shard_map/ppermute | solution.py:39
  33.6 19.1 %copy-start = (bf16[896,1024]{1,0:T(8,128)(2,1)S(1)}, bf16[896,1024]{1,0:T(8,128)(2,1)}, u32[]{:S(2)}) copy-start(bf16[896,1024]{1,0:T(8,128)(2,1)} %refs_4_.1) | copy-start | bytes 5505028
  33.6 19.1 %copy-start.1 = (bf16[896,1024]{1,0:T(8,128)(2,1)S(1)}, bf16[896,1024]{1,0:T(8,128)(2,1)}, u32[]{:S(2)}) copy-start(bf16[896,1024]{1,0:T(8,128)(2,1)} %refs_5_.1) | copy-start | bytes 5505028
  35.3 17.5 %collective-permute-start.10 = (bf16[6,64,896]{2,1,0:T(8,128)(2,1)S(1)}, bf16[6,64,896]{2,1,0:T(8,128)(2,1)S(1)}, u32[]{:S(2)}, u32[]{:S(2)}) collective-permute-start(bf16[6,64,896]{2,1,0:T(8,128)(2,1)S(1)} %unpack_rows.2.refs_0_), channel_id=1, source_target_pairs={{0,1},{1,0},{2,3},{3,2},{4,5},{5,4},{6,7},{7,6},{8,9},{9,8},{10,11... | collective-permute-start | bytes 2064392 | tf_op jit(solution)/shard_map/ppermute | solution.py:39
  47.6 15.9 %collective-permute-start.9 = (bf16[6,64,896]{2,1,0:T(8,128)(2,1)S(1)}, bf16[6,64,896]{2,1,0:T(8,128)(2,1)S(1)}, u32[]{:S(2)}, u32[]{:S(2)}) collective-permute-start(bf16[6,64,896]{2,1,0:T(8,128)(2,1)S(1)} %unpack_rows.3.refs_0_), channel_id=1, source_target_pairs={{0,1},{1,0},{2,3},{3,2},{4,5},{5,4},{6,7},{7,6},{8,9},{9,8},{10,11... | collective-permute-start | bytes 2064392 | tf_op jit(solution)/shard_map/ppermute | solution.py:39
  49.3 22.7 %collective-permute-start.13 = (bf16[2,2,64,896]{3,2,1,0:T(8,128)(2,1)S(1)}, bf16[2,2,64,896]{3,2,1,0:T(8,128)(2,1)S(1)}, u32[]{:S(2)}, u32[]{:S(2)}) collective-permute-start(bf16[2,2,64,896]{3,2,1,0:T(8,128)(2,1)S(1)} %get-tuple-element.110), channel_id=1, source_target_pairs={{0,12},{4,8},{8,4},{12,0},{1,13},{5,9},{9,5},{13,1},{2,14},{6,10},... | collective-permute-start | bytes 1376264 | tf_op jit(solution)/shard_map/ppermute | solution.py:39
  49.8 22.2 %collective-permute-start.12 = (bf16[2,2,64,896]{3,2,1,0:T(8,128)(2,1)S(1)}, bf16[2,2,64,896]{3,2,1,0:T(8,128)(2,1)S(1)}, u32[]{:S(2)}, u32[]{:S(2)}) collective-permute-start(bf16[2,2,64,896]{3,2,1,0:T(8,128)(2,1)S(1)} %get-tuple-element.109), channel_id=1, source_target_pairs={{0,8},{4,12},{8,0},{12,4},{1,9},{5,13},{9,1},{13,5},{2,10},{6,14},... | collective-permute-start | bytes 1376264 | tf_op jit(solution)/shard_map/ppermute | solution.py:39
  50.4 21.6 %collective-permute-start.11 = (bf16[2,2,64,896]{3,2,1,0:T(8,128)(2,1)S(1)}, bf16[2,2,64,896]{3,2,1,0:T(8,128)(2,1)S(1)}, u32[]{:S(2)}, u32[]{:S(2)}) collective-permute-start(bf16[2,2,64,896]{3,2,1,0:T(8,128)(2,1)S(1)} %get-tuple-element.108), channel_id=1, source_target_pairs={{0,4},{4,0},{8,12},{12,8},{1,5},{5,1},{9,13},{13,9},{2,6},{6,2},{1... | collective-permute-start | bytes 1376264 | tf_op jit(solution)/shard_map/ppermute | solution.py:39
  83.6 5.4 %collective-permute-start.14 = (bf16[448,512]{1,0:T(8,128)(2,1)S(1)}, bf16[448,512]{1,0:T(8,128)(2,1)S(1)}, u32[]{:S(2)}, u32[]{:S(2)}) collective-permute-start(bf16[448,512]{1,0:T(8,128)(2,1)S(1)} %get-tuple-element.130), channel_id=1, source_target_pairs={{0,16},{16,0},{1,17},{17,1},{2,18},{18,2},{3,19},{19,3},{4,20},{20... | collective-permute-start | bytes 1376264 | tf_op jit(solution)/shard_map/ppermute | solution.py:39
  83.6 5.4 %collective-permute-start.15 = (bf16[448,512]{1,0:T(8,128)(2,1)S(1)}, bf16[448,512]{1,0:T(8,128)(2,1)S(1)}, u32[]{:S(2)}, u32[]{:S(2)}) collective-permute-start(bf16[448,512]{1,0:T(8,128)(2,1)S(1)} %get-tuple-element.131), channel_id=1, source_target_pairs={{0,16},{16,0},{1,17},{17,1},{2,18},{18,2},{3,19},{19,3},{4,20},{20... | collective-permute-start | bytes 1376264 | tf_op jit(solution)/shard_map/ppermute | solution.py:39
  88.4 1.9 %collective-permute-start.18 = (bf16[448,512]{1,0:T(8,128)(2,1)S(1)}, bf16[448,512]{1,0:T(8,128)(2,1)S(1)}, u32[]{:S(2)}, u32[]{:S(2)}) collective-permute-start(bf16[448,512]{1,0:T(8,128)(2,1)S(1)} %get-tuple-element.146), channel_id=1, source_target_pairs={{0,16},{16,0},{1,17},{17,1},{2,18},{18,2},{3,19},{19,3},{4,20},{20... | collective-permute-start | bytes 1376264 | tf_op jit(solution)/shard_map/ppermute | solution.py:39
  88.6 2.4 %collective-permute-start.19 = (bf16[448,512]{1,0:T(8,128)(2,1)S(1)}, bf16[448,512]{1,0:T(8,128)(2,1)S(1)}, u32[]{:S(2)}, u32[]{:S(2)}) collective-permute-start(bf16[448,512]{1,0:T(8,128)(2,1)S(1)} %get-tuple-element.147), channel_id=1, source_target_pairs={{0,16},{16,0},{1,17},{17,1},{2,18},{18,2},{3,19},{19,3},{4,20},{20... | collective-permute-start | bytes 1376264 | tf_op jit(solution)/shard_map/ppermute | solution.py:39
  89.3 8.5 %collective-permute-start.16 = (bf16[2,112,512]{2,1,0:T(8,128)(2,1)S(1)}, bf16[2,112,512]{2,1,0:T(8,128)(2,1)S(1)}, u32[]{:S(2)}, u32[]{:S(2)}) collective-permute-start(bf16[2,112,512]{2,1,0:T(8,128)(2,1)S(1)} %get-tuple-element.134), channel_id=1, source_target_pairs={{0,4},{4,0},{8,12},{12,8},{1,5},{5,1},{9,13},{13,9},{2,6},{6,2},{1... | collective-permute-start | bytes 688136 | tf_op jit(solution)/shard_map/ppermute | solution.py:39
  89.9 8.5 %collective-permute-start.17 = (bf16[2,112,512]{2,1,0:T(8,128)(2,1)S(1)}, bf16[2,112,512]{2,1,0:T(8,128)(2,1)S(1)}, u32[]{:S(2)}, u32[]{:S(2)}) collective-permute-start(bf16[2,112,512]{2,1,0:T(8,128)(2,1)S(1)} %get-tuple-element.135), channel_id=1, source_target_pairs={{0,8},{4,12},{8,0},{12,4},{1,9},{5,13},{9,1},{13,5},{2,10},{6,14},... | collective-permute-start | bytes 688136 | tf_op jit(solution)/shard_map/ppermute | solution.py:39
  91.2 11.5 %collective-permute-start.20 = (bf16[2,112,512]{2,1,0:T(8,128)(2,1)S(1)}, bf16[2,112,512]{2,1,0:T(8,128)(2,1)S(1)}, u32[]{:S(2)}, u32[]{:S(2)}) collective-permute-start(bf16[2,112,512]{2,1,0:T(8,128)(2,1)S(1)} %get-tuple-element.150), channel_id=1, source_target_pairs={{0,4},{4,0},{8,12},{12,8},{1,5},{5,1},{9,13},{13,9},{2,6},{6,2},{1... | collective-permute-start | bytes 688136 | tf_op jit(solution)/shard_map/ppermute | solution.py:39
  92.1 11.2 %collective-permute-start.21 = (bf16[2,112,512]{2,1,0:T(8,128)(2,1)S(1)}, bf16[2,112,512]{2,1,0:T(8,128)(2,1)S(1)}, u32[]{:S(2)}, u32[]{:S(2)}) collective-permute-start(bf16[2,112,512]{2,1,0:T(8,128)(2,1)S(1)} %get-tuple-element.151), channel_id=1, source_target_pairs={{0,8},{4,12},{8,0},{12,4},{1,9},{5,13},{9,1},{13,5},{2,10},{6,14},... | collective-permute-start | bytes 688136 | tf_op jit(solution)/shard_map/ppermute | solution.py:39
  98.5 6.9 %collective-permute-start.22 = (bf16[1,112,512]{2,1,0:T(8,128)(2,1)S(1)}, bf16[1,112,512]{2,1,0:T(8,128)(2,1)S(1)}, u32[]{:S(2)}, u32[]{:S(2)}) collective-permute-start(bf16[1,112,512]{2,1,0:T(8,128)(2,1)S(1)} %get-tuple-element.154), channel_id=1, source_target_pairs={{0,8},{4,12},{8,0},{12,4},{1,9},{5,13},{9,1},{13,5},{2,10},{6,14},... | collective-permute-start | bytes 344072 | tf_op jit(solution)/shard_map/ppermute | solution.py:39
  98.9 6.4 %collective-permute-start.23 = (bf16[1,112,512]{2,1,0:T(8,128)(2,1)S(1)}, bf16[1,112,512]{2,1,0:T(8,128)(2,1)S(1)}, u32[]{:S(2)}, u32[]{:S(2)}) collective-permute-start(bf16[1,112,512]{2,1,0:T(8,128)(2,1)S(1)} %get-tuple-element.155), channel_id=1, source_target_pairs={{0,4},{4,0},{8,12},{12,8},{1,5},{5,1},{9,13},{13,9},{2,6},{6,2},{1... | collective-permute-start | bytes 344072 | tf_op jit(solution)/shard_map/ppermute | solution.py:39
  103.4 4.9 %collective-permute-start.24 = (bf16[1,112,512]{2,1,0:T(8,128)(2,1)S(1)}, bf16[1,112,512]{2,1,0:T(8,128)(2,1)S(1)}, u32[]{:S(2)}, u32[]{:S(2)}) collective-permute-start(bf16[1,112,512]{2,1,0:T(8,128)(2,1)S(1)} %get-tuple-element.156), channel_id=1, source_target_pairs={{0,8},{4,12},{8,0},{12,4},{1,9},{5,13},{9,1},{13,5},{2,10},{6,14},... | collective-permute-start | bytes 344072 | tf_op jit(solution)/shard_map/ppermute | solution.py:39
  103.9 4.8 %collective-permute-start.25 = (bf16[1,112,512]{2,1,0:T(8,128)(2,1)S(1)}, bf16[1,112,512]{2,1,0:T(8,128)(2,1)S(1)}, u32[]{:S(2)}, u32[]{:S(2)}) collective-permute-start(bf16[1,112,512]{2,1,0:T(8,128)(2,1)S(1)} %get-tuple-element.157), channel_id=1, source_target_pairs={{0,4},{4,0},{8,12},{12,8},{1,5},{5,1},{9,13},{13,9},{2,6},{6,2},{1... | collective-permute-start | bytes 344072 | tf_op jit(solution)/shard_map/ppermute | solution.py:39

commit v4 on v3

v4 whole, which is shorter than its diff:
```python
import functools
import math

import jax
import jax.numpy as jnp
from jax import lax
from jax.experimental import pallas as pl
from jax.experimental.pallas import tpu as pltpu
from jax.sharding import PartitionSpec as P

HEAD_DIM = 128
NEIGH_LEN = 128
NEIGHBOURS = 2
HALF = NEIGH_LEN // 2
MIB = 1024 * 1024
ATTEND_MIB = 26
WEIGH_MIB = 26
PIECES = 2
FIRST_PIECE = 6 / 8
CHUNKS = ((3, True), (3, True), (2, False))

F32 = jnp.float32
BF16 = jnp.bfloat16
ANY = pl.BlockSpec(memory_space=pl.ANY)
SMEM = pl.BlockSpec(memory_space=pltpu.SMEM)
VMEM = pl.BlockSpec(memory_space=pltpu.VMEM)
HBM = pl.BlockSpec(memory_space=pltpu.HBM)


def params(mib):
    return pltpu.CompilerParams(vmem_limit_bytes=mib * MIB)


def piece_heads(heads):
    return [0, int(heads * FIRST_PIECE), heads]


def contract(lhs, rhs, dims):
    return lax.dot_general(lhs, rhs, (dims, ((), ())), preferred_element_type=F32)


def swap(array, axis, bit):
    size = lax.axis_size(axis)
    return lax.ppermute(array, axis, [(i, i ^ bit) for i in range(size)])


def normalize_kernel(states_ref, out_ref):
    floats = states_ref[...].astype(F32)
    mean_square = jnp.mean(floats * floats, axis=-1, keepdims=True)
    out_ref[...] = (floats * lax.rsqrt(mean_square + 1e-06)).astype(BF16)


def normalize_rows(states):
    rows, width = states.shape
    tile = 512
    spec = pl.BlockSpec((tile, width), lambda i: (i, 0))
    return pl.pallas_call(
        normalize_kernel,
        grid=(rows // tile,),
        in_specs=[spec],
        out_specs=spec,
        out_shape=jax.ShapeDtypeStruct(states.shape, BF16),
        compiler_params=params(12),
        name="normalize_rows",
    )(states)


def exchange_ids(own):
    n_ret = lax.axis_size("ret")
    if n_ret <= 4:
        return jnp.stack([own] + [swap(own, "ret", k) for k in range(1, n_ret)])
    every = lax.all_gather(own, "ret")
    order = jnp.arange(n_ret, dtype=jnp.int32) ^ lax.axis_index("ret")
    return jnp.take(every, order, axis=0)


def pick_kernel(spans, id_ref, normed_ref, *outs):
    n_ret = id_ref.shape[0]
    me = lax.axis_index("ret")
    part = lax.rem(lax.axis_index("ctx"), 2)
    for chunk, (start, count, pair) in enumerate(spans):
        for k in range(n_ret):
            out_ref = outs[chunk * n_ret + k]

            def send(i, used, k=k, start=start, pair=pair, out_ref=out_ref):
                request = (start * NEIGHBOURS + i) * 2
                mine = id_ref[k, request] == me

                @pl.when(mine)
                def _():
                    row = id_ref[k, request + 1]
                    out_ref[used] = normed_ref[row, part] if pair else normed_ref[row]

                return used + jnp.where(mine, 1, 0)

            lax.fori_loop(0, count * NEIGHBOURS, send, jnp.int32(0))


def pick(ids, normed, spans, capacity):
    n_ret, width = ids.shape[0], normed.shape[-1]
    slots = [capacity(count) for _, count, _ in spans]
    shapes = [(cap, HALF, width) if pair else (cap, 2, HALF, width) for (_, _, pair), cap in zip(spans, slots)]
    shapes = [jax.ShapeDtypeStruct(shape, BF16) for shape in shapes for _ in range(n_ret)]
    picked = pl.pallas_call(
        functools.partial(pick_kernel, spans),
        in_specs=[SMEM, VMEM],
        out_specs=[VMEM] * len(shapes),
        out_shape=shapes,
        compiler_params=params(16),
        name="pick_rows",
    )(ids, normed)
    return [picked[i : i + n_ret] for i in range(0, len(picked), n_ret)]


def unpack_kernel(start, count, id_ref, *refs):
    *incoming, out_ref, ranks = refs
    place_rows(start, count, id_ref, incoming, ranks, lambda i: out_ref.at[i])


def place_rows(start, count, id_ref, incoming, ranks, target):
    me = lax.axis_index("ret")
    for k in range(len(incoming)):
        ranks[k] = 0
    for i in range(count * NEIGHBOURS):
        source = id_ref[(start * NEIGHBOURS + i) * 2] ^ me
        rank = ranks[source]
        ranks[source] = rank + 1
        for k in range(len(incoming)):

            @pl.when(source == k)
            def _(k=k, rank=rank, i=i):
                target(i)[...] = incoming[k][rank]


def unpack(own, incoming, start, count):
    return pl.pallas_call(
        functools.partial(unpack_kernel, start, count),
        in_specs=[SMEM] + [VMEM] * len(incoming),
        out_specs=VMEM,
        out_shape=jax.ShapeDtypeStruct((count * NEIGHBOURS,) + incoming[0].shape[1:], BF16),
        scratch_shapes=[pltpu.SMEM((len(incoming),), jnp.int32)],
        compiler_params=params(8),
        name="unpack_rows",
    )(own, *incoming)


def block_grads(keys, values, query, grad, out_ref, gq_ref, grad_refs):
    scale = 1.0 / math.sqrt(HEAD_DIM)
    tokens, heads = out_ref.shape[0], out_ref.shape[1] // HEAD_DIM
    zero = jnp.zeros((tokens, HEAD_DIM), BF16)
    bounds = piece_heads(heads)
    cols = [slice(head * HEAD_DIM, (head + 1) * HEAD_DIM) for head in range(heads)]

    def reader(head):
        upper = jnp.concatenate([query(cols[head]), zero], axis=1)
        lower = jnp.concatenate([zero, grad(cols[head])], axis=1)
        return jnp.concatenate([upper, lower], axis=0)

    def both(head):
        return jnp.concatenate([keys(cols[head]), values(cols[head])], axis=1)

    def finish(head, probs, dscore):
        mixed = jnp.dot(jnp.concatenate([probs, dscore], axis=0), both(head), preferred_element_type=F32)
        out_ref[:, cols[head]] = mixed[:tokens, HEAD_DIM:].astype(BF16)
        gq_ref[:, cols[head]] = mixed[tokens:, :HEAD_DIM].astype(BF16)
        grads = contract(jnp.concatenate([dscore, probs], axis=0), reader(head), ((0,), (0,))).astype(BF16)
        piece = int(head >= bounds[1])
        place = cols[head - bounds[piece]]
        grad_refs[2 * piece][:, place] = grads[:, :HEAD_DIM]
        grad_refs[2 * piece + 1][:, place] = grads[:, HEAD_DIM:]

    ahead, lag = 3, 2
    products, weights = {}, {}
    for head in range(-ahead, heads + lag):
        if 0 <= head + ahead < heads:
            products[head + ahead] = contract(reader(head + ahead), both(head + ahead), ((1,), (1,)))
        if 0 <= head < heads:
            product = products.pop(head)
            expo, dprob = jnp.exp(product[:tokens] * scale), product[tokens:]
            inverse = 1.0 / jnp.sum(expo, axis=-1, keepdims=True)
            delta = jnp.sum(expo * dprob, axis=-1, keepdims=True) * inverse
            probs = expo * inverse
            weights[head] = (probs.astype(BF16), (probs * (dprob - delta) * scale).astype(BF16))
        if 0 <= head - lag < heads:
            finish(head - lag, *weights.pop(head - lag))


def attend_kernel(start, count, direct, first, id_ref, *refs):
    refs = list(refs)
    take = lambda n: [refs.pop(0) for _ in range(n)]
    row_refs = take(direct if direct else 2)
    wk_ref, wv_ref, q_ref, go_ref = take(4)
    take(0 if first else 2)
    out_hbm, gq_hbm, turned = take(3)
    grad_refs = take(2 * PIECES)
    out_ref, gq_ref, keys, values, rows, sems, ranks = take(7)
    size, width = rows.shape[1:]
    feat = keys.shape[2]
    if direct:
        place_rows(start, count, id_ref, row_refs, ranks, lambda i: rows.at[i // NEIGHBOURS, pl.ds(i % NEIGHBOURS * NEIGH_LEN, NEIGH_LEN)])
    else:
        part = size // 2
        for i, ref in enumerate(row_refs):
            rows[:, i * part : (i + 1) * part] = ref[...].reshape(count, part, width)

    every = rows[...].reshape(-1, width)
    turned[...] = every.T
    for w_ref, target in ((wk_ref, keys), (wv_ref, values)):
        product = jnp.dot(every, w_ref[...], preferred_element_type=F32).astype(BF16)
        target[...] = product.reshape(count, size, feat)

    def stores(b):
        pairs = ((out_ref, out_hbm), (gq_ref, gq_hbm))
        return [pltpu.make_async_copy(src.at[b], dst.at[start + b], sems.at[b, i]) for i, (src, dst) in enumerate(pairs)]

    def block(b, carry):
        pick = lambda ref, at: lambda cols: ref[at, :, cols]
        inputs = pick(keys, b), pick(values, b), pick(q_ref, start + b), pick(go_ref, start + b)
        block_grads(*inputs, out_ref.at[b], gq_ref.at[b], [ref.at[b] for ref in grad_refs])
        for store in stores(b):
            store.start()
        return carry

    lax.fori_loop(0, count, block, 0)
    for b in range(count):
        for store in stores(b):
            store.wait()


def attend(rows, own, wk, wv, queries, grad_out, start, count, carried):
    _, tokens, feat = queries.shape
    enc = wk.shape[0]
    context = NEIGHBOURS * NEIGH_LEN
    direct = 0 if len(rows) == 2 else len(rows)
    row_shape = jax.ShapeDtypeStruct(queries.shape, BF16)
    if direct:
        rows = [part.reshape(part.shape[0], NEIGH_LEN, enc) for part in rows]
    turned_shape = jax.ShapeDtypeStruct((enc, count * context), BF16)
    bounds = piece_heads(feat // HEAD_DIM)
    widths = [(bounds[piece + 1] - bounds[piece]) * HEAD_DIM for piece in range(PIECES) for _ in range(2)]
    grad_shapes = [jax.ShapeDtypeStruct((count, context, width), BF16) for width in widths]
    aliased = 1 + len(rows) + 4
    return pl.pallas_call(
        functools.partial(attend_kernel, start, count, direct, not carried),
        in_specs=[SMEM] + [VMEM] * len(rows) + [VMEM] * 4 + [HBM] * len(carried),
        out_specs=[HBM] * 2 + [VMEM] * (1 + 2 * PIECES),
        scratch_shapes=[
            pltpu.VMEM((count, tokens, feat), BF16),
            pltpu.VMEM((count, tokens, feat), BF16),
            pltpu.VMEM((count, context, feat), BF16),
            pltpu.VMEM((count, context, feat), BF16),
            pltpu.VMEM((count, context, enc), BF16),
            pltpu.SemaphoreType.DMA((count, 2)),
            pltpu.SMEM((max(direct, 1),), jnp.int32),
        ],
        out_shape=[row_shape, row_shape, turned_shape] + grad_shapes,
        input_output_aliases={aliased: 0, aliased + 1: 1} if carried else {},
        compiler_params=params(ATTEND_MIB),
        name="attend_blocks",
    )(own, *rows, wk, wv, queries, grad_out, *carried)


def weigh_kernel(chunks, carried, last, *refs):
    refs = list(refs)
    take = lambda n: [refs.pop(0) for _ in range(n)]
    turned, grads = take(chunks), [take(chunks) for _ in range(2)]
    before = take(2) if carried else []
    half = turned[0].shape[0] // 2
    dp = lax.axis_index("dp")
    for i in range(2):
        total = before[i][...] if carried else 0.0
        for c in range(chunks):
            grad = grads[i][c][...]
            total += jnp.dot(turned[c][...], grad.reshape(-1, grad.shape[-1]), preferred_element_type=F32)
        if not last:
            refs[i][...] = total
            continue
        refs[-1][...] = total
        for j, side in enumerate((1 - dp, dp)):
            refs[2 * j + i][...] = refs[-1][pl.ds(pl.multiple_of(side * half, half), half), :].astype(BF16)


def weigh(turned, dks, dvs, before, last):
    enc, width = turned[0].shape[0], dks[0].shape[-1]
    shapes = [jax.ShapeDtypeStruct((enc // 2, width), BF16)] * 4 if last else [jax.ShapeDtypeStruct((enc, width), F32)] * 2
    return pl.pallas_call(
        functools.partial(weigh_kernel, len(turned), bool(before), last),
        in_specs=[VMEM] * (3 * len(turned) + len(before)),
        out_specs=[VMEM] * len(shapes),
        out_shape=shapes,
        scratch_shapes=[pltpu.VMEM((enc, width), F32)] if last else [],
        compiler_params=params(WEIGH_MIB),
        name="weigh_grads",
    )(*turned, *dks, *dvs, *before)


def fold_kernel(dims, count, *refs):
    ret = lax.axis_index("ret")
    for i in range(count):
        held_ref, arrived_ref = refs[i], refs[count + i]
        bit, place = dims[i]
        mine = (ret >> bit) & 1
        stride = 1 << place
        for j in range(held_ref.shape[0] // 2):
            base = (j // stride) * 2 * stride + j % stride
            for k, side in enumerate((1 - mine, mine)):
                row = base + side * stride
                total = held_ref[row].astype(F32) + arrived_ref[row].astype(F32)
                refs[(2 + k) * count + i][j] = total.astype(BF16)


def fold(held, arrived, dims):
    count = len(held)
    parts, rows, width = held[0].shape
    shapes = [jax.ShapeDtypeStruct((parts // 2, rows, width), BF16)] * (2 * count)
    return pl.pallas_call(
        functools.partial(fold_kernel, dims, count),
        in_specs=[VMEM] * (2 * count),
        out_specs=[VMEM] * len(shapes),
        out_shape=shapes,
        compiler_params=params(16),
        name="fold_grads",
    )(*held, *arrived)


def join_kernel(*refs):
    count = (len(refs) - 2) // 2
    place = [0, 0]
    for i in range(count):
        total = refs[i][0].astype(F32) + refs[count + i][0].astype(F32)
        width = total.shape[1]
        refs[2 * count + i % 2][:, place[i % 2] : place[i % 2] + width] = total
        place[i % 2] += width


def join(held, arrived):
    rows, feat = held[0].shape[1], sum(part.shape[2] for part in held) // 2
    return pl.pallas_call(
        join_kernel,
        in_specs=[VMEM] * (2 * len(held)),
        out_specs=[VMEM] * 2,
        out_shape=[jax.ShapeDtypeStruct((rows, feat), F32)] * 2,
        compiler_params=params(16),
        name="join_grads",
    )(*held, *arrived)


class Sums:
    def __init__(self, send, held):
        self.bits = lax.axis_size("ret").bit_length() - 1
        self.left = [list(range(self.bits)) for _ in held]
        self.held = self.split(held)
        self.arrived = self.split([swap(grad, "dp", 1) for grad in send])
        self.steps = 0

    def split(self, grads):
        return [grad.reshape(1 << self.bits, -1, grad.shape[-1]) for grad in grads]

    def fold(self):
        self.bit = [self.steps, self.bits - 1 - self.steps]
        dims = tuple((bit, left.index(bit)) for bit, left in zip(self.bit, self.left))
        for bit, left in zip(self.bit, self.left):
            left.remove(bit)
        parts = fold(self.held, self.arrived, dims)
        self.send, self.held = list(parts[:2]), list(parts[2:])
        self.steps += 1

    def exchange(self):
        self.arrived = [swap(grad, "ret", 1 << bit) for grad, bit in zip(self.send, self.bit)]


def spans_of(blocks):
    spans, start = [], 0
    for count, pair in CHUNKS:
        spans.append((start, count, pair))
        start += count
    return spans if start == blocks else [(0, blocks, False)]


def local(queries, enc_states, w_key, w_value, shard_ids, row_ids, grad_out):
    n_ret = lax.axis_size("ret")
    blocks = shard_ids.shape[1]
    bound = blocks * NEIGHBOURS * 2 // n_ret
    enc = enc_states.shape[2]

    def capacity(count):
        return min(count, bound)

    own = jnp.stack([shard_ids[0], row_ids[0]], axis=-1).reshape(-1)
    ids = exchange_ids(own)
    normed = normalize_rows(enc_states[0]).reshape(-1, 2, HALF, enc)
    spans = spans_of(blocks)
    outgoing = pick(ids, normed, spans[:1], capacity)
    if len(spans) > 1:
        outgoing = outgoing + pick(ids, normed, spans[1:], capacity)
    query_blocks, grad_blocks = (array.reshape(blocks, -1, array.shape[2]) for array in (queries, grad_out))
    carried, arrivals = [], []
    for slots in outgoing:
        slots = list(slots)
        if arrivals:
            for k in range(1, n_ret):
                arrivals[-1][k], slots[k] = lax.optimization_barrier((arrivals[-1][k], slots[k]))
        arrivals.append(slots[:1] + [swap(slots[k], "ret", k) for k in range(1, n_ret)])
    rows, turned, found, sums, early = [None] * len(spans), [], [], [[]] * PIECES, None

    def weigh_piece(turned, found, piece, before, last):
        return list(weigh(turned, *([grads[2 * piece + i] for grads in found] for i in range(2)), before, last))


    def prepare(i):
        start, count, pair = spans[i]
        if pair:
            mine = unpack(own, arrivals[i], start, count)
            rows[i] = [mine, swap(mine, "ctx", 1)]
        else:
            rows[i] = arrivals[i]

    prepare(0)
    for i, (start, count, pair) in enumerate(spans):
        last = i + 1 == len(spans)
        if not last and spans[i + 1][2]:
            prepare(i + 1)
            rows[i][0], rows[i + 1][0] = lax.optimization_barrier((rows[i][0], rows[i + 1][0]))
        attended, grad_queries, flipped, *grads = attend(rows[i], own, w_key, w_value, query_blocks, grad_blocks, start, count, carried)
        carried = [attended, grad_queries]
        turned.append(flipped)
        found.append(grads)
        if i == 0 and not last:
            early = turned, found
            turned, found = [], []
            sums[0] = weigh_piece(*early, 0, [], False)
            sums[0][0], rows[1][0] = lax.optimization_barrier((sums[0][0], rows[1][0]))
        if not last and rows[i + 1] is None:
            carried[0], arrivals[i + 1] = lax.optimization_barrier((carried[0], arrivals[i + 1]))
            prepare(i + 1)
    states, parts = [], None
    for piece in range(PIECES):
        if parts:
            if early:
                parts[0], early[0][0] = lax.optimization_barrier((parts[0], early[0][0]))
                sums[piece] = weigh_piece(*early, piece, [], False)
            states.append(Sums(parts[:2], parts[2:]))
            states[-1].fold()
            states[-1].send, turned[0] = lax.optimization_barrier((states[-1].send, turned[0]))
        parts = weigh_piece(turned, found, piece, sums[piece], True)
    states.append(Sums(parts[:2], parts[2:]))
    states[-1].fold()
    for step in range(states[0].bits):
        for state in states:
            if step:
                state.fold()
            state.exchange()
    attended, grad_queries = carried
    grad_w_key, grad_w_value = join(sum([state.held for state in states], []), sum([state.arrived for state in states], []))
    return attended.reshape(queries.shape), grad_queries.reshape(queries.shape), grad_w_key, grad_w_value


def solution(mesh):
    placed = (
        P("dp", "ret", "ctx"),
        P("dp", "ret", None),
        P(None, "ctx"),
        P(None, "ctx"),
        P("dp", "ret", None),
        P("dp", "ret", None),
        P("dp", "ret", "ctx"),
    )
    return jax.shard_map(
        local,
        mesh=mesh,
        in_specs=placed,
        out_specs=(
            P("dp", "ret", "ctx"),
            P("dp", "ret", "ctx"),
            P(("dp", "ret"), "ctx"),
            P(("dp", "ret"), "ctx"),
        ),
        check_vma=False,
    )
```

time: 110 us -> 103 us (0.936)
  Pallas kernels: 43.8 us -> 38.2 us
  waiting for transfers between devices: 33.5 us -> 30.3 us
  starting transfers between devices: 28.4 us -> 30.9 us
    ppermute x26, waiting for transfers between devices: 33.5 us -> 30.3 us  [swap(): return lax.ppermute(array, axis, [(i, i ^ bit) for i in range(size)])]
    ppermute x26, starting transfers between devices: 28.4 us -> 30.9 us  [swap(): return lax.ppermute(array, axis, [(i, i ^ bit) for i in range(size)])]
    pallas_call x3, Pallas kernels: 24.2 us -> 21.9 us  [attend(): pl.pallas_call(functools.partial(attend_kernel, start, count, direct, not...]
    pallas_call x2, Pallas kernels: 3.27 us -> 1.47 us  [unpack(): pl.pallas_call(functools.partial(unpack_kernel, start, count), in_specs=[...]
    pallas_call x4 -> x6, Pallas kernels: 13.5 us -> 11.9 us  [the longest x4 9.53 us: weigh(): pl.pallas_call(functools.partial(weigh_kernel, len(turned), bool(before),...]
  transfers between devices with their start and end apart: 26 -> 26, of which waited for: 12 -> 12; matrix products, arithmetic and copies ran while one was open for 0% -> 0% of each run, Pallas kernels for 27% -> 24%
where the time goes in v4:
time: 103 us
  Pallas kernels  38.2 us (37%)
  starting transfers between devices  30.9 us (30%)
  waiting for transfers between devices  30.3 us (29%)
  local copies, waits for them, and re-layouts  2.33 us (2%)
    ppermute x26, starting transfers between devices, swap(): return lax.ppermute(array, axis, [(i, i ^ bit) for i in range(size)])  30.9 us
    ppermute x26, waiting for transfers between devices, swap(): return lax.ppermute(array, axis, [(i, i ^ bit) for i in range(size)])  30.3 us
    pallas_call x3, Pallas kernels, attend(): pl.pallas_call(functools.partial(attend_kernel, start, count, direct, not...  21.9 us
    pallas_call x4, Pallas kernels, weigh(): pl.pallas_call(functools.partial(weigh_kernel, len(turned), bool(before),...  9.53 us
    pallas_call x2, Pallas kernels, pick(): pl.pallas_call(functools.partial(pick_kernel, spans), in_specs=[SMEM, VME...  2.38 us
  transfers between devices with their start and end apart: 26, of which 12 were waited for; matrix products, arithmetic and copies ran while one was open for 0% of the time, Pallas kernels for 24%

profile of v4, /device:TPU:0, one launch (start us, length us, event | category | flops | bytes accessed | tf_op | source)
XLA Modules:
  0.0 103.2 jit_solution(18314178597112534798)
XLA Ops:
  0.6 0.7 pad_add_fusion
  1.3 0.1 copy.17
  1.4 0.1 reshape.62.id_ref
  1.5 4.0 %collective-permute-start.2 = (s32[32]{0:T(128)S(1)}, s32[32]{0:T(128)S(1)}, u32[]{:S(2)}, u32[]{:S(2)}) collective-permute-start(s32[32]{0:T(128)S(1)} %reshape.62.id_ref), channel_id=1, source_target_pairs={{0,12},{4,8},{8,4},{12,0},{1,13},{5,9},{9,5},{13,1},{2,14},{6,10},... | collective-permute-start | bytes 392 | tf_op jit(solution)/shard_map/ppermute | solution.py:44
  5.5 0.5 collective-permute-start.1
  6.0 0.1 collective-permute-start
  6.1 0.1 stack_reshape.3
  6.2 0.0 copy-start.4
  6.2 2.0 %copy-done.4 = bf16[1,2048,896]{2,1,0:T(8,128)(2,1)S(1)} copy-done((bf16[1,2048,896]{2,1,0:T(8,128)(2,1)S(1)}, bf16[1,2048,896]{2,1,0:T(8,128)(2,1)}, u32[]{:S(2)}) %copy-start.4) | copy-done | bytes 3670040
  8.3 1.2 %normalize_rows.1 = bf16[2048,896]{1,0:T(8,128)(2,1)S(1)} custom-call(bf16[2048,896]{1,0:T(8,128)(2,1)S(1)} %bitcast.31), custom_call_target="tpu_custom_call" | custom-call | tf_op jit(solution)/shard_map/normalize_rows/pallas_call | solution.py:57
  9.5 0.0 collective-permute-done.2
  9.5 0.0 collective-permute-done
  9.5 1.0 pick_rows.2
  10.6 2.0 %collective-permute-start.3 = (bf16[3,64,896]{2,1,0:T(8,128)(2,1)S(1)}, bf16[3,64,896]{2,1,0:T(8,128)(2,1)S(1)}, u32[]{:S(2)}, u32[]{:S(2)}) collective-permute-start(bf16[3,64,896]{2,1,0:T(8,128)(2,1)S(1)} %get-tuple-element.94), channel_id=1, source_target_pairs={{0,4},{4,0},{8,12},{12,8},{1,5},{5,1},{9,13},{13,9},{2,6},{6,2},{1... | collective-permute-start | bytes 1032200 | tf_op jit(solution)/shard_map/ppermute | solution.py:44
  12.6 1.4 %collective-permute-start.4 = (bf16[3,64,896]{2,1,0:T(8,128)(2,1)S(1)}, bf16[3,64,896]{2,1,0:T(8,128)(2,1)S(1)}, u32[]{:S(2)}, u32[]{:S(2)}) collective-permute-start(bf16[3,64,896]{2,1,0:T(8,128)(2,1)S(1)} %get-tuple-element.97), channel_id=1, source_target_pairs={{0,8},{4,12},{8,0},{12,4},{1,9},{5,13},{9,1},{13,5},{2,10},{6,14},... | collective-permute-start | bytes 1032200 | tf_op jit(solution)/shard_map/ppermute | solution.py:44
  14.0 0.2 collective-permute-start.5
  14.2 1.4 %pick_rows.3 = (bf16[3,64,896]{2,1,0:T(8,128)(2,1)S(1)}, bf16[3,64,896]{2,1,0:T(8,128)(2,1)S(1)}, bf16[3,64,896]{2,1,0:T(8,128)(2,1)S(1)}, bf16[3,64,896]{2,1,0:...) custom-call(s32[4,32]{1,0:T(4,128)S(1)} %pad_add_fusion.1.id_ref, ...), custom_call_target="tpu_custom_call" | custom-call | tf_op jit(solution)/shard_map/pick_rows/pallas_call | solution.py:104
  15.5 6.1 %collective-permute-done.3.refs_1_ = bf16[3,64,896]{2,1,0:T(8,128)(2,1)S(1)} collective-permute-done((bf16[3,64,896]{2,1,0:T(8,128)(2,1)S(1)}, bf16[3,64,896]{2,1,0:T(8,128)(2,1)S(1)}, u32[]{:S(2)}, u32[]{:S(2)}) %collective-permute-start.3) | collective-permute-done | bytes 344096 | tf_op jit(solution)/shard_map/ppermute | solution.py:44
  21.6 2.0 %collective-permute-start.6 = (bf16[3,64,896]{2,1,0:T(8,128)(2,1)S(1)}, bf16[3,64,896]{2,1,0:T(8,128)(2,1)S(1)}, u32[]{:S(2)}, u32[]{:S(2)}) collective-permute-start(bf16[3,64,896]{2,1,0:T(8,128)(2,1)S(1)} %get-tuple-element.104), channel_id=1, source_target_pairs={{0,4},{4,0},{8,12},{12,8},{1,5},{5,1},{9,13},{13,9},{2,6},{6,2},{1... | collective-permute-start | bytes 1032200 | tf_op jit(solution)/shard_map/ppermute | solution.py:44
  23.6 5.0 %collective-permute-done.4.refs_2_ = bf16[3,64,896]{2,1,0:T(8,128)(2,1)S(1)} collective-permute-done((bf16[3,64,896]{2,1,0:T(8,128)(2,1)S(1)}, bf16[3,64,896]{2,1,0:T(8,128)(2,1)S(1)}, u32[]{:S(2)}, u32[]{:S(2)}) %collective-permute-start.4) | collective-permute-done | bytes 344096 | tf_op jit(solution)/shard_map/ppermute | solution.py:44
  28.7 2.6 %collective-permute-start.7 = (bf16[3,64,896]{2,1,0:T(8,128)(2,1)S(1)}, bf16[3,64,896]{2,1,0:T(8,128)(2,1)S(1)}, u32[]{:S(2)}, u32[]{:S(2)}) collective-permute-start(bf16[3,64,896]{2,1,0:T(8,128)(2,1)S(1)} %get-tuple-element.107), channel_id=1, source_target_pairs={{0,8},{4,12},{8,0},{12,4},{1,9},{5,13},{9,1},{13,5},{2,10},{6,14},... | collective-permute-start | bytes 1032200 | tf_op jit(solution)/shard_map/ppermute | solution.py:44
  31.3 0.0 collective-permute-done.5.refs_3_
  31.3 0.6 collective-permute-start.8
  31.9 0.7 unpack_rows.2.refs_0_
  32.7 1.6 %collective-permute-start.9 = (bf16[6,64,896]{2,1,0:T(8,128)(2,1)S(1)}, bf16[6,64,896]{2,1,0:T(8,128)(2,1)S(1)}, u32[]{:S(2)}, u32[]{:S(2)}) collective-permute-start(bf16[6,64,896]{2,1,0:T(8,128)(2,1)S(1)} %unpack_rows.2.refs_0_), channel_id=1, source_target_pairs={{0,1},{1,0},{2,3},{3,2},{4,5},{5,4},{6,7},{7,6},{8,9},{9,8},{10,11... | collective-permute-start | bytes 2064392 | tf_op jit(solution)/shard_map/ppermute | solution.py:44
  34.3 2.1 %collective-permute-done.6.refs_1_ = bf16[3,64,896]{2,1,0:T(8,128)(2,1)S(1)} collective-permute-done((bf16[3,64,896]{2,1,0:T(8,128)(2,1)S(1)}, bf16[3,64,896]{2,1,0:T(8,128)(2,1)S(1)}, u32[]{:S(2)}, u32[]{:S(2)}) %collective-permute-start.6) | collective-permute-done | bytes 344096 | tf_op jit(solution)/shard_map/ppermute | solution.py:44
  36.4 7.5 %collective-permute-done.7.refs_2_ = bf16[3,64,896]{2,1,0:T(8,128)(2,1)S(1)} collective-permute-done((bf16[3,64,896]{2,1,0:T(8,128)(2,1)S(1)}, bf16[3,64,896]{2,1,0:T(8,128)(2,1)S(1)}, u32[]{:S(2)}, u32[]{:S(2)}) %collective-permute-start.7) | collective-permute-done | bytes 344096 | tf_op jit(solution)/shard_map/ppermute | solution.py:44
  43.9 0.7 unpack_rows.3.refs_0_
  44.6 1.5 %collective-permute-start.10 = (bf16[6,64,896]{2,1,0:T(8,128)(2,1)S(1)}, bf16[6,64,896]{2,1,0:T(8,128)(2,1)S(1)}, u32[]{:S(2)}, u32[]{:S(2)}) collective-permute-start(bf16[6,64,896]{2,1,0:T(8,128)(2,1)S(1)} %unpack_rows.3.refs_0_), channel_id=1, source_target_pairs={{0,1},{1,0},{2,3},{3,2},{4,5},{5,4},{6,7},{7,6},{8,9},{9,8},{10,11... | collective-permute-start | bytes 2064392 | tf_op jit(solution)/shard_map/ppermute | solution.py:44
  46.2 1.1 %collective-permute-start.13 = (bf16[2,2,64,896]{3,2,1,0:T(8,128)(2,1)S(1)}, bf16[2,2,64,896]{3,2,1,0:T(8,128)(2,1)S(1)}, u32[]{:S(2)}, u32[]{:S(2)}) collective-permute-start(bf16[2,2,64,896]{3,2,1,0:T(8,128)(2,1)S(1)} %get-tuple-element.126), channel_id=1, source_target_pairs={{0,12},{4,8},{8,4},{12,0},{1,13},{5,9},{9,5},{13,1},{2,14},{6,10},... | collective-permute-start | bytes 1376264 | tf_op jit(solution)/shard_map/ppermute | solution.py:44
  47.2 1.2 %collective-permute-start.12 = (bf16[2,2,64,896]{3,2,1,0:T(8,128)(2,1)S(1)}, bf16[2,2,64,896]{3,2,1,0:T(8,128)(2,1)S(1)}, u32[]{:S(2)}, u32[]{:S(2)}) collective-permute-start(bf16[2,2,64,896]{3,2,1,0:T(8,128)(2,1)S(1)} %get-tuple-element.125), channel_id=1, source_target_pairs={{0,8},{4,12},{8,0},{12,4},{1,9},{5,13},{9,1},{13,5},{2,10},{6,14},... | collective-permute-start | bytes 1376264 | tf_op jit(solution)/shard_map/ppermute | solution.py:44
  48.4 1.2 %collective-permute-start.11 = (bf16[2,2,64,896]{3,2,1,0:T(8,128)(2,1)S(1)}, bf16[2,2,64,896]{3,2,1,0:T(8,128)(2,1)S(1)}, u32[]{:S(2)}, u32[]{:S(2)}) collective-permute-start(bf16[2,2,64,896]{3,2,1,0:T(8,128)(2,1)S(1)} %get-tuple-element.124), channel_id=1, source_target_pairs={{0,4},{4,0},{8,12},{12,8},{1,5},{5,1},{9,13},{13,9},{2,6},{6,2},{1... | collective-permute-start | bytes 1376264 | tf_op jit(solution)/shard_map/ppermute | solution.py:44
  49.7 7.9 %attend_blocks.3 = (bf16[8,64,1024]{2,1,0:T(8,128)(2,1)}, bf16[8,64,1024]{2,1,0:T(8,128)(2,1)}, bf16[896,768]{1,0:T(8,128)(2,1)S(1)}, bf16[3,256,768]{2,1,0:T(8,...) custom-call(s32[32]{0:T(128)S(1)} %reshape.62.id_ref, ...), custom_call_target="tpu_custom_call" | custom-call | tf_op jit(solution)/shard_map/attend_blocks/pallas_call | solution.py:243
  57.6 2.3 %weigh_grads.4 = (f32[896,768]{1,0:T(8,128)S(1)}, f32[896,768]{1,0:T(8,128)S(1)}) custom-call(bf16[896,768]{1,0:T(8,128)(2,1)S(1)} %get-tuple-element.161.refs_0_, bf16[3,256,768]{2,1,0:T(8,128)(2,1)S(1)} %get-tuple-element.115.refs_1_, bf16[3,256,768]{2,1,0:T(8,128)(2,1)S(1)} %get-tuple-element.116.refs_2_), custom_call_target="tpu_custom_call" | custom-call | tf_op jit(solution)/shard_map/weigh_grads/pallas_call | solution.py:286
  59.9 0.6 collective-permute-done.10.refs_1_
  60.6 7.9 %attend_blocks.4 = (bf16[8,64,1024]{2,1,0:T(8,128)(2,1)}, bf16[8,64,1024]{2,1,0:T(8,128)(2,1)}, bf16[896,768]{1,0:T(8,128)(2,1)S(1)}, bf16[3,256,768]{2,1,0:T(8,...) custom-call(s32[32]{0:T(128)S(1)} %reshape.62.id_ref, ...), custom_call_target="tpu_custom_call", output_to_operand_aliasing={{0}: (7, {}), {1}: (8, {})} | custom-call | tf_op jit(solution)/shard_map/attend_blocks/pallas_call | solution.py:243
  68.5 6.1 %attend_blocks.5 = (bf16[8,64,1024]{2,1,0:T(8,128)(2,1)}, bf16[8,64,1024]{2,1,0:T(8,128)(2,1)}, bf16[896,512]{1,0:T(8,128)(2,1)S(1)}, bf16[2,256,768]{2,1,0:T(8,...) custom-call(s32[32]{0:T(128)S(1)} %reshape.62.id_ref, ...), custom_call_target="tpu_custom_call", output_to_operand_aliasing={{0}: (9, {}), {1}: (10, {})} | custom-call | tf_op jit(solution)/shard_map/attend_blocks/pallas_call | solution.py:243
  74.6 4.7 %weigh_grads.5 = (bf16[448,768]{1,0:T(8,128)(2,1)S(1)}, bf16[448,768]{1,0:T(8,128)(2,1)S(1)}, bf16[448,768]{1,0:T(8,128)(2,1)S(1)}, bf16[448,768]{1,0:T(8,128)(2,1)S(1)}) custom-call(bf16[896,768]{1,0:T(8,128)(2,1)S(1)} %get-tuple-element.156.refs_0_, bf16[896,512]{1,0:T(8,128)(2,1)S(1)} %get-tuple-element.136.refs_1_, ...), custom_call_target="tpu_custom_call" | custom-call | tf_op jit(solution)/shard_map/weigh_grads/pallas_call | solution.py:286
  79.3 0.1 collective-permute-start.14
  79.4 0.5 collective-permute-start.15
  79.9 1.6 %collective-permute-done.14 = bf16[448,768]{1,0:T(8,128)(2,1)S(1)} collective-permute-done((bf16[448,768]{1,0:T(8,128)(2,1)S(1)}, bf16[448,768]{1,0:T(8,128)(2,1)S(1)}, u32[]{:S(2)}, u32[]{:S(2)}) %collective-permute-start.14) | collective-permute-done | bytes 688160 | tf_op jit(solution)/shard_map/ppermute | solution.py:44
  81.6 1.0 collective-permute-done.15
  82.5 0.3 fold_grads.4
  82.9 0.7 collective-permute-start.16
  83.5 1.4 %collective-permute-start.17 = (bf16[2,112,768]{2,1,0:T(8,128)(2,1)S(1)}, bf16[2,112,768]{2,1,0:T(8,128)(2,1)S(1)}, u32[]{:S(2)}, u32[]{:S(2)}) collective-permute-start(bf16[2,112,768]{2,1,0:T(8,128)(2,1)S(1)} %get-tuple-element.153), channel_id=1, source_target_pairs={{0,8},{4,12},{8,0},{12,4},{1,9},{5,13},{9,1},{13,5},{2,10},{6,14},... | collective-permute-start | bytes 1032200 | tf_op jit(solution)/shard_map/ppermute | solution.py:44
  84.9 0.9 weigh_grads.6
  85.8 1.6 %weigh_grads.7 = (bf16[448,256]{1,0:T(8,128)(2,1)S(1)}, bf16[448,256]{1,0:T(8,128)(2,1)S(1)}, bf16[448,256]{1,0:T(8,128)(2,1)S(1)}, bf16[448,256]{1,0:T(8,128)(2,1)S(1)}) custom-call(bf16[896,768]{1,0:T(8,128)(2,1)S(1)} %get-tuple-element.156.refs_0_, bf16[896,512]{1,0:T(8,128)(2,1)S(1)} %get-tuple-element.136.refs_1_, ...), custom_call_target="tpu_custom_call" | custom-call | tf_op jit(solution)/shard_map/weigh_grads/pallas_call | solution.py:286
  87.4 0.1 collective-permute-start.18
  87.5 0.5 collective-permute-start.19
  88.0 1.0 collective-permute-done.18
  89.0 0.3 collective-permute-done.19
  89.3 0.1 fold_grads.6
  89.4 1.6 %collective-permute-start.20 = (bf16[2,112,256]{2,1,0:T(8,128)(2,1)S(1)}, bf16[2,112,256]{2,1,0:T(8,128)(2,1)S(1)}, u32[]{:S(2)}, u32[]{:S(2)}) collective-permute-start(bf16[2,112,256]{2,1,0:T(8,128)(2,1)S(1)} %get-tuple-element.172), channel_id=1, source_target_pairs={{0,4},{4,0},{8,12},{12,8},{1,5},{5,1},{9,13},{13,9},{2,6},{6,2},{1... | collective-permute-start | bytes 344072 | tf_op jit(solution)/shard_map/ppermute | solution.py:44
  91.0 0.6 collective-permute-start.21
  91.6 2.1 %collective-permute-done.16.refs_2_ = bf16[2,112,768]{2,1,0:T(8,128)(2,1)S(1)} collective-permute-done((bf16[2,112,768]{2,1,0:T(8,128)(2,1)S(1)}, bf16[2,112,768]{2,1,0:T(8,128)(2,1)S(1)}, u32[]{:S(2)}, u32[]{:S(2)}) %collective-permute-start.16) | collective-permute-done | bytes 344096 | tf_op jit(solution)/shard_map/ppermute | solution.py:44
  93.7 0.2 fold_grads.5
  93.9 1.7 %collective-permute-start.22 = (bf16[1,112,768]{2,1,0:T(8,128)(2,1)S(1)}, bf16[1,112,768]{2,1,0:T(8,128)(2,1)S(1)}, u32[]{:S(2)}, u32[]{:S(2)}) collective-permute-start(bf16[1,112,768]{2,1,0:T(8,128)(2,1)S(1)} %get-tuple-element.176), channel_id=1, source_target_pairs={{0,8},{4,12},{8,0},{12,4},{1,9},{5,13},{9,1},{13,5},{2,10},{6,14},... | collective-permute-start | bytes 516104 | tf_op jit(solution)/shard_map/ppermute | solution.py:44
  95.6 2.0 %collective-permute-start.23 = (bf16[1,112,768]{2,1,0:T(8,128)(2,1)S(1)}, bf16[1,112,768]{2,1,0:T(8,128)(2,1)S(1)}, u32[]{:S(2)}, u32[]{:S(2)}) collective-permute-start(bf16[1,112,768]{2,1,0:T(8,128)(2,1)S(1)} %get-tuple-element.177), channel_id=1, source_target_pairs={{0,4},{4,0},{8,12},{12,8},{1,5},{5,1},{9,13},{13,9},{2,6},{6,2},{1... | collective-permute-start | bytes 516104 | tf_op jit(solution)/shard_map/ppermute | solution.py:44
  97.6 0.1 fold_grads.7
  97.7 0.2 collective-permute-start.24
  97.8 1.6 %collective-permute-start.25 = (bf16[1,112,256]{2,1,0:T(8,128)(2,1)S(1)}, bf16[1,112,256]{2,1,0:T(8,128)(2,1)S(1)}, u32[]{:S(2)}, u32[]{:S(2)}) collective-permute-start(bf16[1,112,256]{2,1,0:T(8,128)(2,1)S(1)} %get-tuple-element.179), channel_id=1, source_target_pairs={{0,4},{4,0},{8,12},{12,8},{1,5},{5,1},{9,13},{13,9},{2,6},{6,2},{1... | collective-permute-start | bytes 172040 | tf_op jit(solution)/shard_map/ppermute | solution.py:44
  99.4 2.5 %collective-permute-done.24.refs_6_ = bf16[1,112,256]{2,1,0:T(8,128)(2,1)S(1)} collective-permute-done((bf16[1,112,256]{2,1,0:T(8,128)(2,1)S(1)}, bf16[1,112,256]{2,1,0:T(8,128)(2,1)S(1)}, u32[]{:S(2)}, u32[]{:S(2)}) %collective-permute-start.24) | collective-permute-done | bytes 57376 | tf_op jit(solution)/shard_map/ppermute | solution.py:44
  101.9 0.3 collective-permute-done.25.refs_7_
  102.2 1.0 join_grads.1
  (20 shorter events, 0.1 us)
Async XLA Ops:
  1.5 8.0 %collective-permute-start.2 = (s32[32]{0:T(128)S(1)}, s32[32]{0:T(128)S(1)}, u32[]{:S(2)}, u32[]{:S(2)}) collective-permute-start(s32[32]{0:T(128)S(1)} %reshape.62.id_ref), channel_id=1, source_target_pairs={{0,12},{4,8},{8,4},{12,0},{1,13},{5,9},{9,5},{13,1},{2,14},{6,10},... | collective-permute-start | bytes 392 | tf_op jit(solution)/shard_map/ppermute | solution.py:44
  5.5 4.0 %collective-permute-start.1 = (s32[32]{0:T(128)S(1)}, s32[32]{0:T(128)S(1)}, u32[]{:S(2)}, u32[]{:S(2)}) collective-permute-start(s32[32]{0:T(128)S(1)} %reshape.62.id_ref), channel_id=1, source_target_pairs={{0,8},{4,12},{8,0},{12,4},{1,9},{5,13},{9,1},{13,5},{2,10},{6,14},... | collective-permute-start | bytes 392 | tf_op jit(solution)/shard_map/ppermute | solution.py:44
  6.0 3.5 %collective-permute-start = (s32[32]{0:T(128)S(1)}, s32[32]{0:T(128)S(1)}, u32[]{:S(2)}, u32[]{:S(2)}) collective-permute-start(s32[32]{0:T(128)S(1)} %reshape.62.id_ref), channel_id=1, source_target_pairs={{0,4},{4,0},{8,12},{12,8},{1,5},{5,1},{9,13},{13,9},{2,6},{6,2},{1... | collective-permute-start | bytes 392 | tf_op jit(solution)/shard_map/ppermute | solution.py:44
  6.2 2.0 %copy-start.4 = (bf16[1,2048,896]{2,1,0:T(8,128)(2,1)S(1)}, bf16[1,2048,896]{2,1,0:T(8,128)(2,1)}, u32[]{:S(2)}) copy-start(bf16[1,2048,896]{2,1,0:T(8,128)(2,1)} %param.8) | copy-start | bytes 11010052
  10.6 11.1 %collective-permute-start.3 = (bf16[3,64,896]{2,1,0:T(8,128)(2,1)S(1)}, bf16[3,64,896]{2,1,0:T(8,128)(2,1)S(1)}, u32[]{:S(2)}, u32[]{:S(2)}) collective-permute-start(bf16[3,64,896]{2,1,0:T(8,128)(2,1)S(1)} %get-tuple-element.94), channel_id=1, source_target_pairs={{0,4},{4,0},{8,12},{12,8},{1,5},{5,1},{9,13},{13,9},{2,6},{6,2},{1... | collective-permute-start | bytes 1032200 | tf_op jit(solution)/shard_map/ppermute | solution.py:44
  12.6 16.0 %collective-permute-start.4 = (bf16[3,64,896]{2,1,0:T(8,128)(2,1)S(1)}, bf16[3,64,896]{2,1,0:T(8,128)(2,1)S(1)}, u32[]{:S(2)}, u32[]{:S(2)}) collective-permute-start(bf16[3,64,896]{2,1,0:T(8,128)(2,1)S(1)} %get-tuple-element.97), channel_id=1, source_target_pairs={{0,8},{4,12},{8,0},{12,4},{1,9},{5,13},{9,1},{13,5},{2,10},{6,14},... | collective-permute-start | bytes 1032200 | tf_op jit(solution)/shard_map/ppermute | solution.py:44
  14.0 17.3 %collective-permute-start.5 = (bf16[3,64,896]{2,1,0:T(8,128)(2,1)S(1)}, bf16[3,64,896]{2,1,0:T(8,128)(2,1)S(1)}, u32[]{:S(2)}, u32[]{:S(2)}) collective-permute-start(bf16[3,64,896]{2,1,0:T(8,128)(2,1)S(1)} %get-tuple-element.100), channel_id=1, source_target_pairs={{0,12},{4,8},{8,4},{12,0},{1,13},{5,9},{9,5},{13,1},{2,14},{6,10},... | collective-permute-start | bytes 1032200 | tf_op jit(solution)/shard_map/ppermute | solution.py:44
  14.2 35.5 %copy-start.2 = (bf16[1,512,1024]{2,1,0:T(8,128)(2,1)S(1)}, bf16[1,512,1024]{2,1,0:T(8,128)(2,1)}, u32[]{:S(2)}) copy-start(bf16[1,512,1024]{2,1,0:T(8,128)(2,1)} %param.7) | copy-start | bytes 3145732
  14.2 35.5 %copy-start.3 = (bf16[1,512,1024]{2,1,0:T(8,128)(2,1)S(1)}, bf16[1,512,1024]{2,1,0:T(8,128)(2,1)}, u32[]{:S(2)}) copy-start(bf16[1,512,1024]{2,1,0:T(8,128)(2,1)} %param.13) | copy-start | bytes 3145732
  21.6 14.8 %collective-permute-start.6 = (bf16[3,64,896]{2,1,0:T(8,128)(2,1)S(1)}, bf16[3,64,896]{2,1,0:T(8,128)(2,1)S(1)}, u32[]{:S(2)}, u32[]{:S(2)}) collective-permute-start(bf16[3,64,896]{2,1,0:T(8,128)(2,1)S(1)} %get-tuple-element.104), channel_id=1, source_target_pairs={{0,4},{4,0},{8,12},{12,8},{1,5},{5,1},{9,13},{13,9},{2,6},{6,2},{1... | collective-permute-start | bytes 1032200 | tf_op jit(solution)/shard_map/ppermute | solution.py:44
  28.7 15.2 %collective-permute-start.7 = (bf16[3,64,896]{2,1,0:T(8,128)(2,1)S(1)}, bf16[3,64,896]{2,1,0:T(8,128)(2,1)S(1)}, u32[]{:S(2)}, u32[]{:S(2)}) collective-permute-start(bf16[3,64,896]{2,1,0:T(8,128)(2,1)S(1)} %get-tuple-element.107), channel_id=1, source_target_pairs={{0,8},{4,12},{8,0},{12,4},{1,9},{5,13},{9,1},{13,5},{2,10},{6,14},... | collective-permute-start | bytes 1032200 | tf_op jit(solution)/shard_map/ppermute | solution.py:44
  31.3 12.6 %collective-permute-start.8 = (bf16[3,64,896]{2,1,0:T(8,128)(2,1)S(1)}, bf16[3,64,896]{2,1,0:T(8,128)(2,1)S(1)}, u32[]{:S(2)}, u32[]{:S(2)}) collective-permute-start(bf16[3,64,896]{2,1,0:T(8,128)(2,1)S(1)} %get-tuple-element.110), channel_id=1, source_target_pairs={{0,12},{4,8},{8,4},{12,0},{1,13},{5,9},{9,5},{13,1},{2,14},{6,10},... | collective-permute-start | bytes 1032200 | tf_op jit(solution)/shard_map/ppermute | solution.py:44
  31.9 17.7 %copy-start = (bf16[896,1024]{1,0:T(8,128)(2,1)S(1)}, bf16[896,1024]{1,0:T(8,128)(2,1)}, u32[]{:S(2)}) copy-start(bf16[896,1024]{1,0:T(8,128)(2,1)} %refs_4_.1) | copy-start | bytes 5505028
  31.9 17.7 %copy-start.1 = (bf16[896,1024]{1,0:T(8,128)(2,1)S(1)}, bf16[896,1024]{1,0:T(8,128)(2,1)}, u32[]{:S(2)}) copy-start(bf16[896,1024]{1,0:T(8,128)(2,1)} %refs_5_.1) | copy-start | bytes 5505028
  32.7 17.0 %collective-permute-start.9 = (bf16[6,64,896]{2,1,0:T(8,128)(2,1)S(1)}, bf16[6,64,896]{2,1,0:T(8,128)(2,1)S(1)}, u32[]{:S(2)}, u32[]{:S(2)}) collective-permute-start(bf16[6,64,896]{2,1,0:T(8,128)(2,1)S(1)} %unpack_rows.2.refs_0_), channel_id=1, source_target_pairs={{0,1},{1,0},{2,3},{3,2},{4,5},{5,4},{6,7},{7,6},{8,9},{9,8},{10,11... | collective-permute-start | bytes 2064392 | tf_op jit(solution)/shard_map/ppermute | solution.py:44
  44.6 15.9 %collective-permute-start.10 = (bf16[6,64,896]{2,1,0:T(8,128)(2,1)S(1)}, bf16[6,64,896]{2,1,0:T(8,128)(2,1)S(1)}, u32[]{:S(2)}, u32[]{:S(2)}) collective-permute-start(bf16[6,64,896]{2,1,0:T(8,128)(2,1)S(1)} %unpack_rows.3.refs_0_), channel_id=1, source_target_pairs={{0,1},{1,0},{2,3},{3,2},{4,5},{5,4},{6,7},{7,6},{8,9},{9,8},{10,11... | collective-permute-start | bytes 2064392 | tf_op jit(solution)/shard_map/ppermute | solution.py:44
  46.2 22.3 %collective-permute-start.13 = (bf16[2,2,64,896]{3,2,1,0:T(8,128)(2,1)S(1)}, bf16[2,2,64,896]{3,2,1,0:T(8,128)(2,1)S(1)}, u32[]{:S(2)}, u32[]{:S(2)}) collective-permute-start(bf16[2,2,64,896]{3,2,1,0:T(8,128)(2,1)S(1)} %get-tuple-element.126), channel_id=1, source_target_pairs={{0,12},{4,8},{8,4},{12,0},{1,13},{5,9},{9,5},{13,1},{2,14},{6,10},... | collective-permute-start | bytes 1376264 | tf_op jit(solution)/shard_map/ppermute | solution.py:44
  47.2 21.3 %collective-permute-start.12 = (bf16[2,2,64,896]{3,2,1,0:T(8,128)(2,1)S(1)}, bf16[2,2,64,896]{3,2,1,0:T(8,128)(2,1)S(1)}, u32[]{:S(2)}, u32[]{:S(2)}) collective-permute-start(bf16[2,2,64,896]{3,2,1,0:T(8,128)(2,1)S(1)} %get-tuple-element.125), channel_id=1, source_target_pairs={{0,8},{4,12},{8,0},{12,4},{1,9},{5,13},{9,1},{13,5},{2,10},{6,14},... | collective-permute-start | bytes 1376264 | tf_op jit(solution)/shard_map/ppermute | solution.py:44
  48.4 20.1 %collective-permute-start.11 = (bf16[2,2,64,896]{3,2,1,0:T(8,128)(2,1)S(1)}, bf16[2,2,64,896]{3,2,1,0:T(8,128)(2,1)S(1)}, u32[]{:S(2)}, u32[]{:S(2)}) collective-permute-start(bf16[2,2,64,896]{3,2,1,0:T(8,128)(2,1)S(1)} %get-tuple-element.124), channel_id=1, source_target_pairs={{0,4},{4,0},{8,12},{12,8},{1,5},{5,1},{9,13},{13,9},{2,6},{6,2},{1... | collective-permute-start | bytes 1376264 | tf_op jit(solution)/shard_map/ppermute | solution.py:44
  79.3 2.2 %collective-permute-start.14 = (bf16[448,768]{1,0:T(8,128)(2,1)S(1)}, bf16[448,768]{1,0:T(8,128)(2,1)S(1)}, u32[]{:S(2)}, u32[]{:S(2)}) collective-permute-start(bf16[448,768]{1,0:T(8,128)(2,1)S(1)} %get-tuple-element.146), channel_id=1, source_target_pairs={{0,16},{16,0},{1,17},{17,1},{2,18},{18,2},{3,19},{19,3},{4,20},{20... | collective-permute-start | bytes 2064392 | tf_op jit(solution)/shard_map/ppermute | solution.py:44
  79.4 3.1 %collective-permute-start.15 = (bf16[448,768]{1,0:T(8,128)(2,1)S(1)}, bf16[448,768]{1,0:T(8,128)(2,1)S(1)}, u32[]{:S(2)}, u32[]{:S(2)}) collective-permute-start(bf16[448,768]{1,0:T(8,128)(2,1)S(1)} %get-tuple-element.147), channel_id=1, source_target_pairs={{0,16},{16,0},{1,17},{17,1},{2,18},{18,2},{3,19},{19,3},{4,20},{20... | collective-permute-start | bytes 2064392 | tf_op jit(solution)/shard_map/ppermute | solution.py:44
  82.9 10.8 %collective-permute-start.16 = (bf16[2,112,768]{2,1,0:T(8,128)(2,1)S(1)}, bf16[2,112,768]{2,1,0:T(8,128)(2,1)S(1)}, u32[]{:S(2)}, u32[]{:S(2)}) collective-permute-start(bf16[2,112,768]{2,1,0:T(8,128)(2,1)S(1)} %get-tuple-element.152), channel_id=1, source_target_pairs={{0,4},{4,0},{8,12},{12,8},{1,5},{5,1},{9,13},{13,9},{2,6},{6,2},{1... | collective-permute-start | bytes 1032200 | tf_op jit(solution)/shard_map/ppermute | solution.py:44
  83.5 10.2 %collective-permute-start.17 = (bf16[2,112,768]{2,1,0:T(8,128)(2,1)S(1)}, bf16[2,112,768]{2,1,0:T(8,128)(2,1)S(1)}, u32[]{:S(2)}, u32[]{:S(2)}) collective-permute-start(bf16[2,112,768]{2,1,0:T(8,128)(2,1)S(1)} %get-tuple-element.153), channel_id=1, source_target_pairs={{0,8},{4,12},{8,0},{12,4},{1,9},{5,13},{9,1},{13,5},{2,10},{6,14},... | collective-permute-start | bytes 1032200 | tf_op jit(solution)/shard_map/ppermute | solution.py:44
  87.4 1.6 %collective-permute-start.18 = (bf16[448,256]{1,0:T(8,128)(2,1)S(1)}, bf16[448,256]{1,0:T(8,128)(2,1)S(1)}, u32[]{:S(2)}, u32[]{:S(2)}) collective-permute-start(bf16[448,256]{1,0:T(8,128)(2,1)S(1)} %get-tuple-element.168), channel_id=1, source_target_pairs={{0,16},{16,0},{1,17},{17,1},{2,18},{18,2},{3,19},{19,3},{4,20},{20... | collective-permute-start | bytes 688136 | tf_op jit(solution)/shard_map/ppermute | solution.py:44
  87.5 1.8 %collective-permute-start.19 = (bf16[448,256]{1,0:T(8,128)(2,1)S(1)}, bf16[448,256]{1,0:T(8,128)(2,1)S(1)}, u32[]{:S(2)}, u32[]{:S(2)}) collective-permute-start(bf16[448,256]{1,0:T(8,128)(2,1)S(1)} %get-tuple-element.169), channel_id=1, source_target_pairs={{0,16},{16,0},{1,17},{17,1},{2,18},{18,2},{3,19},{19,3},{4,20},{20... | collective-permute-start | bytes 688136 | tf_op jit(solution)/shard_map/ppermute | solution.py:44
  89.4 8.2 %collective-permute-start.20 = (bf16[2,112,256]{2,1,0:T(8,128)(2,1)S(1)}, bf16[2,112,256]{2,1,0:T(8,128)(2,1)S(1)}, u32[]{:S(2)}, u32[]{:S(2)}) collective-permute-start(bf16[2,112,256]{2,1,0:T(8,128)(2,1)S(1)} %get-tuple-element.172), channel_id=1, source_target_pairs={{0,4},{4,0},{8,12},{12,8},{1,5},{5,1},{9,13},{13,9},{2,6},{6,2},{1... | collective-permute-start | bytes 344072 | tf_op jit(solution)/shard_map/ppermute | solution.py:44
  91.0 6.6 %collective-permute-start.21 = (bf16[2,112,256]{2,1,0:T(8,128)(2,1)S(1)}, bf16[2,112,256]{2,1,0:T(8,128)(2,1)S(1)}, u32[]{:S(2)}, u32[]{:S(2)}) collective-permute-start(bf16[2,112,256]{2,1,0:T(8,128)(2,1)S(1)} %get-tuple-element.173), channel_id=1, source_target_pairs={{0,8},{4,12},{8,0},{12,4},{1,9},{5,13},{9,1},{13,5},{2,10},{6,14},... | collective-permute-start | bytes 344072 | tf_op jit(solution)/shard_map/ppermute | solution.py:44
  93.9 8.3 %collective-permute-start.22 = (bf16[1,112,768]{2,1,0:T(8,128)(2,1)S(1)}, bf16[1,112,768]{2,1,0:T(8,128)(2,1)S(1)}, u32[]{:S(2)}, u32[]{:S(2)}) collective-permute-start(bf16[1,112,768]{2,1,0:T(8,128)(2,1)S(1)} %get-tuple-element.176), channel_id=1, source_target_pairs={{0,8},{4,12},{8,0},{12,4},{1,9},{5,13},{9,1},{13,5},{2,10},{6,14},... | collective-permute-start | bytes 516104 | tf_op jit(solution)/shard_map/ppermute | solution.py:44
  95.6 6.6 %collective-permute-start.23 = (bf16[1,112,768]{2,1,0:T(8,128)(2,1)S(1)}, bf16[1,112,768]{2,1,0:T(8,128)(2,1)S(1)}, u32[]{:S(2)}, u32[]{:S(2)}) collective-permute-start(bf16[1,112,768]{2,1,0:T(8,128)(2,1)S(1)} %get-tuple-element.177), channel_id=1, source_target_pairs={{0,4},{4,0},{8,12},{12,8},{1,5},{5,1},{9,13},{13,9},{2,6},{6,2},{1... | collective-permute-start | bytes 516104 | tf_op jit(solution)/shard_map/ppermute | solution.py:44
  97.7 4.2 %collective-permute-start.24 = (bf16[1,112,256]{2,1,0:T(8,128)(2,1)S(1)}, bf16[1,112,256]{2,1,0:T(8,128)(2,1)S(1)}, u32[]{:S(2)}, u32[]{:S(2)}) collective-permute-start(bf16[1,112,256]{2,1,0:T(8,128)(2,1)S(1)} %get-tuple-element.178), channel_id=1, source_target_pairs={{0,8},{4,12},{8,0},{12,4},{1,9},{5,13},{9,1},{13,5},{2,10},{6,14},... | collective-permute-start | bytes 172040 | tf_op jit(solution)/shard_map/ppermute | solution.py:44
  97.8 4.4 %collective-permute-start.25 = (bf16[1,112,256]{2,1,0:T(8,128)(2,1)S(1)}, bf16[1,112,256]{2,1,0:T(8,128)(2,1)S(1)}, u32[]{:S(2)}, u32[]{:S(2)}) collective-permute-start(bf16[1,112,256]{2,1,0:T(8,128)(2,1)S(1)} %get-tuple-element.179), channel_id=1, source_target_pairs={{0,4},{4,0},{8,12},{12,8},{1,5},{5,1},{9,13},{13,9},{2,6},{6,2},{1... | collective-permute-start | bytes 172040 | tf_op jit(solution)/shard_map/ppermute | solution.py:44

commit v5 on v4

--- a/solution.py
+++ b/solution.py
@@ -16,6 +16,8 @@
 ATTEND_MIB = 26
 WEIGH_MIB = 26
 PIECES = 2
+PROJECT_FIRST = True
+MERGE = False
 FIRST_PIECE = 6 / 8
 CHUNKS = ((3, True), (3, True), (2, False))
 
@@ -185,99 +187,138 @@
             finish(head - lag, *weights.pop(head - lag))
 
 
-def attend_kernel(start, count, direct, first, id_ref, *refs):
+def project_kernel(rows_ref, wk_ref, wv_ref, k_ref, v_ref):
+    rows = rows_ref[...].reshape(-1, rows_ref.shape[-1])
+    for w_ref, target in ((wk_ref, k_ref), (wv_ref, v_ref)):
+        target[...] = jnp.dot(rows, w_ref[...], preferred_element_type=F32).astype(BF16).reshape(target.shape)
+
+
+def project(rows, wk, wv):
+    count, feat = rows.shape[0] // NEIGHBOURS, wk.shape[1]
+    shape = jax.ShapeDtypeStruct((count, NEIGHBOURS * rows.shape[1], feat), BF16)
+    return pl.pallas_call(
+        project_kernel,
+        in_specs=[VMEM] * 3,
+        out_specs=[VMEM] * 2,
+        out_shape=[shape] * 2,
+        compiler_params=params(16),
+        name="project_rows",
+    )(rows, wk, wv)
+
+
+def weigh_sum(turned, grads, before):
+    total = 0.0 if before is None else before[...]
+    for turn, grad in zip(turned, grads):
+        values = grad[...]
+        total += jnp.dot(turn[...], values.reshape(-1, values.shape[-1]), preferred_element_type=F32)
+    return total
+
+
+def weigh_halves(total, scratch, targets):
+    half = scratch.shape[0] // 2
+    dp = lax.axis_index("dp")
+    scratch[...] = total
+    for target, side in zip(targets, (1 - dp, dp)):
+        target[...] = scratch[pl.ds(pl.multiple_of(side * half, half), half), :].astype(BF16)
+
+
+def attend_kernel(start, count, sources, pair, done, first, tail, id_ref, *refs):
     refs = list(refs)
     take = lambda n: [refs.pop(0) for _ in range(n)]
-    row_refs = take(direct if direct else 2)
+    row_refs = take(sources)
+    ready = take(2 if done else 0)
     wk_ref, wv_ref, q_ref, go_ref = take(4)
+    tail_refs = take(3 * tail + 2 if tail else 0)
     take(0 if first else 2)
     out_hbm, gq_hbm, turned = take(3)
     grad_refs = take(2 * PIECES)
+    tail_outs = take(4 if tail else 0)
     out_ref, gq_ref, keys, values, rows, sems, ranks = take(7)
     size, width = rows.shape[1:]
-    feat = keys.shape[2]
-    if direct:
+    part, feat = keys.shape[1:]
+    if pair:
+        for i, ref in enumerate(row_refs):
+            rows[:, i * (size // 2) : (i + 1) * (size // 2)] = ref[...].reshape(count, size // 2, width)
+    else:
         place_rows(start, count, id_ref, row_refs, ranks, lambda i: rows.at[i // NEIGHBOURS, pl.ds(i % NEIGHBOURS * NEIGH_LEN, NEIGH_LEN)])
-    else:
-        part = size // 2
-        for i, ref in enumerate(row_refs):
-            rows[:, i * part : (i + 1) * part] = ref[...].reshape(count, part, width)
-
-    every = rows[...].reshape(-1, width)
-    turned[...] = every.T
+
+    rest = (row_refs[1] if done else rows)[...].reshape(-1, width)
     for w_ref, target in ((wk_ref, keys), (wv_ref, values)):
-        product = jnp.dot(every, w_ref[...], preferred_element_type=F32).astype(BF16)
-        target[...] = product.reshape(count, size, feat)
+        product = jnp.dot(rest, w_ref[...], preferred_element_type=F32).astype(BF16)
+        target[...] = product.reshape(count, part, feat)
 
     def stores(b):
         pairs = ((out_ref, out_hbm), (gq_ref, gq_hbm))
         return [pltpu.make_async_copy(src.at[b], dst.at[start + b], sems.at[b, i]) for i, (src, dst) in enumerate(pairs)]
 
     def block(b, carry):
-        pick = lambda ref, at: lambda cols: ref[at, :, cols]
-        inputs = pick(keys, b), pick(values, b), pick(q_ref, start + b), pick(go_ref, start + b)
-        block_grads(*inputs, out_ref.at[b], gq_ref.at[b], [ref.at[b] for ref in grad_refs])
+        def pick(at, *parts):
+            return lambda cols: jnp.concatenate([ref[at, :, cols] for ref in parts], axis=0)
+
+        context = pick(b, *ready[:1], keys), pick(b, *ready[1:], values)
+        block_grads(*context, pick(start + b, q_ref), pick(start + b, go_ref), out_ref.at[b], gq_ref.at[b], [ref.at[b] for ref in grad_refs])
         for store in stores(b):
             store.start()
         return carry
 
     lax.fori_loop(0, count, block, 0)
+    turned[...] = rows[...].reshape(-1, width).T
+    if tail:
+        for i in range(2):
+            total = weigh_sum(tail_refs[:tail] + [turned], tail_refs[(1 + i) * tail : (2 + i) * tail] + [grad_refs[i]], tail_refs[3 * tail + i])
+            weigh_halves(total, refs[0], tail_outs[i::2])
     for b in range(count):
         for store in stores(b):
             store.wait()
 
 
-def attend(rows, own, wk, wv, queries, grad_out, start, count, carried):
+def attend(rows, ready, own, wk, wv, queries, grad_out, start, count, pair, carried, tail):
     _, tokens, feat = queries.shape
     enc = wk.shape[0]
     context = NEIGHBOURS * NEIGH_LEN
-    direct = 0 if len(rows) == 2 else len(rows)
     row_shape = jax.ShapeDtypeStruct(queries.shape, BF16)
-    if direct:
+    if not pair:
         rows = [part.reshape(part.shape[0], NEIGH_LEN, enc) for part in rows]
     turned_shape = jax.ShapeDtypeStruct((enc, count * context), BF16)
     bounds = piece_heads(feat // HEAD_DIM)
     widths = [(bounds[piece + 1] - bounds[piece]) * HEAD_DIM for piece in range(PIECES) for _ in range(2)]
     grad_shapes = [jax.ShapeDtypeStruct((count, context, width), BF16) for width in widths]
-    aliased = 1 + len(rows) + 4
-    return pl.pallas_call(
-        functools.partial(attend_kernel, start, count, direct, not carried),
-        in_specs=[SMEM] + [VMEM] * len(rows) + [VMEM] * 4 + [HBM] * len(carried),
-        out_specs=[HBM] * 2 + [VMEM] * (1 + 2 * PIECES),
+    fresh = context // 2 if ready else context
+    weighed = [jax.ShapeDtypeStruct((enc // 2, widths[0]), BF16)] * (4 if tail else 0)
+    aliased = 1 + len(rows) + len(ready) + 4 + len(tail)
+    settings = start, count, len(rows), pair, bool(ready), not carried, len(tail) // 3
+    return pl.pallas_call(
+        functools.partial(attend_kernel, *settings),
+        in_specs=[SMEM] + [VMEM] * (len(rows) + len(ready) + 4 + len(tail)) + [HBM] * len(carried),
+        out_specs=[HBM] * 2 + [VMEM] * (1 + 2 * PIECES + len(weighed)),
         scratch_shapes=[
             pltpu.VMEM((count, tokens, feat), BF16),
             pltpu.VMEM((count, tokens, feat), BF16),
-            pltpu.VMEM((count, context, feat), BF16),
-            pltpu.VMEM((count, context, feat), BF16),
+            pltpu.VMEM((count, fresh, feat), BF16),
+            pltpu.VMEM((count, fresh, feat), BF16),
             pltpu.VMEM((count, context, enc), BF16),
             pltpu.SemaphoreType.DMA((count, 2)),
-            pltpu.SMEM((max(direct, 1),), jnp.int32),
-        ],
-        out_shape=[row_shape, row_shape, turned_shape] + grad_shapes,
+            pltpu.SMEM((len(rows),), jnp.int32),
+        ]
+        + [pltpu.VMEM((enc, widths[0]), F32)] * bool(tail),
+        out_shape=[row_shape, row_shape, turned_shape] + grad_shapes + weighed,
         input_output_aliases={aliased: 0, aliased + 1: 1} if carried else {},
         compiler_params=params(ATTEND_MIB),
         name="attend_blocks",
-    )(own, *rows, wk, wv, queries, grad_out, *carried)
+    )(own, *rows, *ready, wk, wv, queries, grad_out, *tail, *carried)
 
 
 def weigh_kernel(chunks, carried, last, *refs):
     refs = list(refs)
     take = lambda n: [refs.pop(0) for _ in range(n)]
     turned, grads = take(chunks), [take(chunks) for _ in range(2)]
-    before = take(2) if carried else []
-    half = turned[0].shape[0] // 2
-    dp = lax.axis_index("dp")
+    before = take(2) if carried else [None] * 2
     for i in range(2):
-        total = before[i][...] if carried else 0.0
-        for c in range(chunks):
-            grad = grads[i][c][...]
-            total += jnp.dot(turned[c][...], grad.reshape(-1, grad.shape[-1]), preferred_element_type=F32)
-        if not last:
+        total = weigh_sum(turned, grads[i], before[i])
+        if last:
+            weigh_halves(total, refs[-1], refs[i:4:2])
+        else:
             refs[i][...] = total
-            continue
-        refs[-1][...] = total
-        for j, side in enumerate((1 - dp, dp)):
-            refs[2 * j + i][...] = refs[-1][pl.ds(pl.multiple_of(side * half, half), half), :].astype(BF16)
 
 
 def weigh(turned, dks, dvs, before, last):
@@ -402,6 +443,7 @@
                 arrivals[-1][k], slots[k] = lax.optimization_barrier((arrivals[-1][k], slots[k]))
         arrivals.append(slots[:1] + [swap(slots[k], "ret", k) for k in range(1, n_ret)])
     rows, turned, found, sums, early = [None] * len(spans), [], [], [[]] * PIECES, None
+    ready = [[] for _ in spans]
 
     def weigh_piece(turned, found, piece, before, last):
         return list(weigh(turned, *([grads[2 * piece + i] for grads in found] for i in range(2)), before, last))
@@ -412,6 +454,8 @@
         if pair:
             mine = unpack(own, arrivals[i], start, count)
             rows[i] = [mine, swap(mine, "ctx", 1)]
+            if PROJECT_FIRST:
+                ready[i] = list(project(mine, w_key, w_value))
         else:
             rows[i] = arrivals[i]
 
@@ -419,9 +463,16 @@
     for i, (start, count, pair) in enumerate(spans):
         last = i + 1 == len(spans)
         if not last and spans[i + 1][2]:
+            if ready[i]:
+                ready[i][0], arrivals[i + 1] = lax.optimization_barrier((ready[i][0], arrivals[i + 1]))
             prepare(i + 1)
             rows[i][0], rows[i + 1][0] = lax.optimization_barrier((rows[i][0], rows[i + 1][0]))
-        attended, grad_queries, flipped, *grads = attend(rows[i], own, w_key, w_value, query_blocks, grad_blocks, start, count, carried)
+        tail = []
+        if MERGE and last and early and found:
+            tail = turned + [grads[n] for n in range(2) for grads in found] + sums[0]
+        results = attend(rows[i], ready[i], own, w_key, w_value, query_blocks, grad_blocks, start, count, pair, carried, tail)
+        attended, grad_queries, flipped = results[:3]
+        grads, parts = results[3 : 3 + 2 * PIECES], list(results[3 + 2 * PIECES :])
         carried = [attended, grad_queries]
         turned.append(flipped)
         found.append(grads)
@@ -433,16 +484,17 @@
         if not last and rows[i + 1] is None:
             carried[0], arrivals[i + 1] = lax.optimization_barrier((carried[0], arrivals[i + 1]))
             prepare(i + 1)
-    states, parts = [], None
+    states = []
     for piece in range(PIECES):
-        if parts:
+        if piece:
             if early:
                 parts[0], early[0][0] = lax.optimization_barrier((parts[0], early[0][0]))
                 sums[piece] = weigh_piece(*early, piece, [], False)
             states.append(Sums(parts[:2], parts[2:]))
             states[-1].fold()
             states[-1].send, turned[0] = lax.optimization_barrier((states[-1].send, turned[0]))
-        parts = weigh_piece(turned, found, piece, sums[piece], True)
+        if piece or not parts:
+            parts = weigh_piece(turned, found, piece, sums[piece], True)
     states.append(Sums(parts[:2], parts[2:]))
     states[-1].fold()
     for step in range(states[0].bits):

time: 103 us -> 102 us (level)
  waiting for transfers between devices: 30.3 us -> 28 us
    ppermute x26, waiting for transfers between devices: 30.3 us -> 28 us  [swap(): return lax.ppermute(array, axis, [(i, i ^ bit) for i in range(size)])]
    pallas_call x3 -> x5, Pallas kernels: 21.9 us -> 22.4 us  [the longest x3 18.8 us: attend(): pl.pallas_call(functools.partial(attend_kernel, *settings), in_specs=[SME...]
  transfers between devices with their start and end apart: 26 -> 26, of which waited for: 12 -> 12; matrix products, arithmetic and copies ran while one was open for 0% -> 0% of each run, Pallas kernels for 24% -> 25%
where the time goes in v5:
time: 102 us
  Pallas kernels  38.9 us (38%)
  starting transfers between devices  30.7 us (30%)
  waiting for transfers between devices  28 us (27%)
  local copies, waits for them, and re-layouts  2.33 us (2%)
    ppermute x26, starting transfers between devices, swap(): return lax.ppermute(array, axis, [(i, i ^ bit) for i in range(size)])  30.7 us
    ppermute x26, waiting for transfers between devices, swap(): return lax.ppermute(array, axis, [(i, i ^ bit) for i in range(size)])  28 us
    pallas_call x3, Pallas kernels, attend(): pl.pallas_call(functools.partial(attend_kernel, *settings), in_specs=[SME...  18.8 us
    pallas_call x4, Pallas kernels, weigh(): pl.pallas_call(functools.partial(weigh_kernel, len(turned), bool(before),...  9.53 us
    pallas_call x2, Pallas kernels, project(): pl.pallas_call(project_kernel, in_specs=[VMEM] * 3, out_specs=[VMEM] * 2,...  3.57 us
    pallas_call x2, Pallas kernels, pick(): pl.pallas_call(functools.partial(pick_kernel, spans), in_specs=[SMEM, VME...  2.65 us
    unnamed x10, local copies, waits for them, and re-layouts  2.06 us
  transfers between devices with their start and end apart: 26, of which 12 were waited for; matrix products, arithmetic and copies ran while one was open for 0% of the time, Pallas kernels for 25%

profile of v5, /device:TPU:0, one launch (start us, length us, event | category | flops | bytes accessed | tf_op | source)
XLA Modules:
  0.0 101.6 jit_solution(1477087746945743757)
XLA Ops:
  0.6 0.7 pad_add_fusion
  1.3 0.1 copy.17
  1.4 0.1 reshape.62.id_ref
  1.5 4.0 %collective-permute-start.2 = (s32[32]{0:T(128)S(1)}, s32[32]{0:T(128)S(1)}, u32[]{:S(2)}, u32[]{:S(2)}) collective-permute-start(s32[32]{0:T(128)S(1)} %reshape.62.id_ref), channel_id=1, source_target_pairs={{0,12},{4,8},{8,4},{12,0},{1,13},{5,9},{9,5},{13,1},{2,14},{6,10},... | collective-permute-start | bytes 392 | tf_op jit(solution)/shard_map/ppermute | solution.py:46
  5.5 0.5 collective-permute-start.1
  6.0 0.1 collective-permute-start
  6.1 0.1 stack_reshape.3
  6.2 0.0 copy-start.4
  6.2 2.0 %copy-done.4 = bf16[1,2048,896]{2,1,0:T(8,128)(2,1)S(1)} copy-done((bf16[1,2048,896]{2,1,0:T(8,128)(2,1)S(1)}, bf16[1,2048,896]{2,1,0:T(8,128)(2,1)}, u32[]{:S(2)}) %copy-start.4) | copy-done | bytes 3670040
  8.3 1.2 %normalize_rows.1 = bf16[2048,896]{1,0:T(8,128)(2,1)S(1)} custom-call(bf16[2048,896]{1,0:T(8,128)(2,1)S(1)} %bitcast.31), custom_call_target="tpu_custom_call" | custom-call | tf_op jit(solution)/shard_map/normalize_rows/pallas_call | solution.py:59
  9.5 0.0 collective-permute-done
  9.5 1.1 %pick_rows.2 = (bf16[3,64,896]{2,1,0:T(8,128)(2,1)S(1)}, bf16[3,64,896]{2,1,0:T(8,128)(2,1)S(1)}, bf16[3,64,896]{2,1,0:T(8,128)(2,1)S(1)}, bf16[3,64,896]{2,1,0:T(8,128)(2,1)S(1)}) custom-call(s32[4,32]{1,0:T(4,128)S(1)} %pad_add_fusion.1.id_ref, bf16[16,2,64,896]{3,2,1,0:T(8,128)(2,1)S(1)} %bitcast.23), custom_call_target="tpu_custom_call" | custom-call | tf_op jit(solution)/shard_map/pick_rows/pallas_call | solution.py:106
  10.7 1.8 %collective-permute-start.3 = (bf16[3,64,896]{2,1,0:T(8,128)(2,1)S(1)}, bf16[3,64,896]{2,1,0:T(8,128)(2,1)S(1)}, u32[]{:S(2)}, u32[]{:S(2)}) collective-permute-start(bf16[3,64,896]{2,1,0:T(8,128)(2,1)S(1)} %get-tuple-element.103), channel_id=1, source_target_pairs={{0,4},{4,0},{8,12},{12,8},{1,5},{5,1},{9,13},{13,9},{2,6},{6,2},{1... | collective-permute-start | bytes 1032200 | tf_op jit(solution)/shard_map/ppermute | solution.py:46
  12.5 1.5 %collective-permute-start.4 = (bf16[3,64,896]{2,1,0:T(8,128)(2,1)S(1)}, bf16[3,64,896]{2,1,0:T(8,128)(2,1)S(1)}, u32[]{:S(2)}, u32[]{:S(2)}) collective-permute-start(bf16[3,64,896]{2,1,0:T(8,128)(2,1)S(1)} %get-tuple-element.106), channel_id=1, source_target_pairs={{0,8},{4,12},{8,0},{12,4},{1,9},{5,13},{9,1},{13,5},{2,10},{6,14},... | collective-permute-start | bytes 1032200 | tf_op jit(solution)/shard_map/ppermute | solution.py:46
  14.1 0.2 collective-permute-start.5
  14.2 1.5 %pick_rows.3 = (bf16[3,64,896]{2,1,0:T(8,128)(2,1)S(1)}, bf16[3,64,896]{2,1,0:T(8,128)(2,1)S(1)}, bf16[3,64,896]{2,1,0:T(8,128)(2,1)S(1)}, bf16[3,64,896]{2,1,0:...) custom-call(s32[4,32]{1,0:T(4,128)S(1)} %pad_add_fusion.1.id_ref, ...), custom_call_target="tpu_custom_call" | custom-call | tf_op jit(solution)/shard_map/pick_rows/pallas_call | solution.py:106
  15.8 6.0 %collective-permute-done.3.refs_1_ = bf16[3,64,896]{2,1,0:T(8,128)(2,1)S(1)} collective-permute-done((bf16[3,64,896]{2,1,0:T(8,128)(2,1)S(1)}, bf16[3,64,896]{2,1,0:T(8,128)(2,1)S(1)}, u32[]{:S(2)}, u32[]{:S(2)}) %collective-permute-start.3) | collective-permute-done | bytes 344096 | tf_op jit(solution)/shard_map/ppermute | solution.py:46
  21.7 1.8 %collective-permute-start.6 = (bf16[3,64,896]{2,1,0:T(8,128)(2,1)S(1)}, bf16[3,64,896]{2,1,0:T(8,128)(2,1)S(1)}, u32[]{:S(2)}, u32[]{:S(2)}) collective-permute-start(bf16[3,64,896]{2,1,0:T(8,128)(2,1)S(1)} %get-tuple-element.114), channel_id=1, source_target_pairs={{0,4},{4,0},{8,12},{12,8},{1,5},{5,1},{9,13},{13,9},{2,6},{6,2},{1... | collective-permute-start | bytes 1032200 | tf_op jit(solution)/shard_map/ppermute | solution.py:46
  23.5 5.2 %collective-permute-done.4.refs_2_ = bf16[3,64,896]{2,1,0:T(8,128)(2,1)S(1)} collective-permute-done((bf16[3,64,896]{2,1,0:T(8,128)(2,1)S(1)}, bf16[3,64,896]{2,1,0:T(8,128)(2,1)S(1)}, u32[]{:S(2)}, u32[]{:S(2)}) %collective-permute-start.4) | collective-permute-done | bytes 344096 | tf_op jit(solution)/shard_map/ppermute | solution.py:46
  28.7 2.6 %collective-permute-start.7 = (bf16[3,64,896]{2,1,0:T(8,128)(2,1)S(1)}, bf16[3,64,896]{2,1,0:T(8,128)(2,1)S(1)}, u32[]{:S(2)}, u32[]{:S(2)}) collective-permute-start(bf16[3,64,896]{2,1,0:T(8,128)(2,1)S(1)} %get-tuple-element.117), channel_id=1, source_target_pairs={{0,8},{4,12},{8,0},{12,4},{1,9},{5,13},{9,1},{13,5},{2,10},{6,14},... | collective-permute-start | bytes 1032200 | tf_op jit(solution)/shard_map/ppermute | solution.py:46
  31.3 0.5 collective-permute-start.8
  31.8 0.7 unpack_rows.2.rows_ref.refs_0_
  32.6 1.6 %collective-permute-start.9 = (bf16[6,64,896]{2,1,0:T(8,128)(2,1)S(1)}, bf16[6,64,896]{2,1,0:T(8,128)(2,1)S(1)}, u32[]{:S(2)}, u32[]{:S(2)}) collective-permute-start(bf16[6,64,896]{2,1,0:T(8,128)(2,1)S(1)} %unpack_rows.2.rows_ref.refs_0_), channel_id=1, source_target_pairs={{0,1},{1,0},{2,3},{3,2},{4,5},{5,4},{6,7},{7,6},{8,9},{9,8},{10,11... | collective-permute-start | bytes 2064392 | tf_op jit(solution)/shard_map/ppermute | solution.py:46
  34.2 1.8 %project_rows.2 = (bf16[3,128,1024]{2,1,0:T(8,128)(2,1)S(1)}, bf16[3,128,1024]{2,1,0:T(8,128)(2,1)S(1)}) custom-call(bf16[6,64,896]{2,1,0:T(8,128)(2,1)S(1)} %unpack_rows.2.rows_ref.refs_0_, bf16[896,1024]{1,0:T(8,128)(2,1)S(1)} %copy-done, bf16[896,1024]{1,0:T(8,128)(2,1)S(1)} %copy-done.1), custom_call_target="tpu_custom_call" | custom-call | tf_op jit(solution)/shard_map/project_rows/pallas_call | solution.py:199
  36.0 0.5 collective-permute-done.6.refs_1_
  36.5 7.4 %collective-permute-done.7.refs_2_ = bf16[3,64,896]{2,1,0:T(8,128)(2,1)S(1)} collective-permute-done((bf16[3,64,896]{2,1,0:T(8,128)(2,1)S(1)}, bf16[3,64,896]{2,1,0:T(8,128)(2,1)S(1)}, u32[]{:S(2)}, u32[]{:S(2)}) %collective-permute-start.7) | collective-permute-done | bytes 344096 | tf_op jit(solution)/shard_map/ppermute | solution.py:46
  43.9 0.7 unpack_rows.3.rows_ref.refs_0_
  44.7 1.5 %collective-permute-start.10 = (bf16[6,64,896]{2,1,0:T(8,128)(2,1)S(1)}, bf16[6,64,896]{2,1,0:T(8,128)(2,1)S(1)}, u32[]{:S(2)}, u32[]{:S(2)}) collective-permute-start(bf16[6,64,896]{2,1,0:T(8,128)(2,1)S(1)} %unpack_rows.3.rows_ref.refs_0_), channel_id=1, source_target_pairs={{0,1},{1,0},{2,3},{3,2},{4,5},{5,4},{6,7},{7,6},{8,9},{9,8},{10,11... | collective-permute-start | bytes 2064392 | tf_op jit(solution)/shard_map/ppermute | solution.py:46
  46.2 1.0 collective-permute-start.13
  47.2 1.3 %collective-permute-start.12 = (bf16[2,2,64,896]{3,2,1,0:T(8,128)(2,1)S(1)}, bf16[2,2,64,896]{3,2,1,0:T(8,128)(2,1)S(1)}, u32[]{:S(2)}, u32[]{:S(2)}) collective-permute-start(bf16[2,2,64,896]{3,2,1,0:T(8,128)(2,1)S(1)} %get-tuple-element.143), channel_id=1, source_target_pairs={{0,8},{4,12},{8,0},{12,4},{1,9},{5,13},{9,1},{13,5},{2,10},{6,14},... | collective-permute-start | bytes 1376264 | tf_op jit(solution)/shard_map/ppermute | solution.py:46
  48.5 1.2 %collective-permute-start.11 = (bf16[2,2,64,896]{3,2,1,0:T(8,128)(2,1)S(1)}, bf16[2,2,64,896]{3,2,1,0:T(8,128)(2,1)S(1)}, u32[]{:S(2)}, u32[]{:S(2)}) collective-permute-start(bf16[2,2,64,896]{3,2,1,0:T(8,128)(2,1)S(1)} %get-tuple-element.142), channel_id=1, source_target_pairs={{0,4},{4,0},{8,12},{12,8},{1,5},{5,1},{9,13},{13,9},{2,6},{6,2},{1... | collective-permute-start | bytes 1376264 | tf_op jit(solution)/shard_map/ppermute | solution.py:46
  49.7 1.8 %project_rows.3 = (bf16[3,128,1024]{2,1,0:T(8,128)(2,1)S(1)}, bf16[3,128,1024]{2,1,0:T(8,128)(2,1)S(1)}) custom-call(bf16[6,64,896]{2,1,0:T(8,128)(2,1)S(1)} %unpack_rows.3.rows_ref.refs_0_, bf16[896,1024]{1,0:T(8,128)(2,1)S(1)} %copy-done, bf16[896,1024]{1,0:T(8,128)(2,1)S(1)} %copy-done.1), custom_call_target="tpu_custom_call" | custom-call | tf_op jit(solution)/shard_map/project_rows/pallas_call | solution.py:199
  51.5 6.4 %attend_blocks.3 = (bf16[8,64,1024]{2,1,0:T(8,128)(2,1)}, bf16[8,64,1024]{2,1,0:T(8,128)(2,1)}, bf16[896,768]{1,0:T(8,128)(2,1)S(1)}, bf16[3,256,768]{2,1,0:T(8,...) custom-call(s32[32]{0:T(128)S(1)} %reshape.62.id_ref, ...), custom_call_target="tpu_custom_call" | custom-call | tf_op jit(solution)/shard_map/attend_blocks/pallas_call | solution.py:290
  57.9 2.3 %weigh_grads.4 = (f32[896,768]{1,0:T(8,128)S(1)}, f32[896,768]{1,0:T(8,128)S(1)}) custom-call(bf16[896,768]{1,0:T(8,128)(2,1)S(1)} %get-tuple-element.179.refs_0_, bf16[3,256,768]{2,1,0:T(8,128)(2,1)S(1)} %get-tuple-element.131.refs_1_, bf16[3,256,768]{2,1,0:T(8,128)(2,1)S(1)} %get-tuple-element.132.refs_2_), custom_call_target="tpu_custom_call" | custom-call | tf_op jit(solution)/shard_map/weigh_grads/pallas_call | solution.py:327
  60.2 0.3 collective-permute-done.10.refs_1_
  60.5 6.4 %attend_blocks.4 = (bf16[8,64,1024]{2,1,0:T(8,128)(2,1)}, bf16[8,64,1024]{2,1,0:T(8,128)(2,1)}, bf16[896,768]{1,0:T(8,128)(2,1)S(1)}, bf16[3,256,768]{2,1,0:T(8,...) custom-call(s32[32]{0:T(128)S(1)} %reshape.62.id_ref, ...), custom_call_target="tpu_custom_call", output_to_operand_aliasing={{0}: (9, {}), {1}: (10, {})} | custom-call | tf_op jit(solution)/shard_map/attend_blocks/pallas_call | solution.py:290
  66.9 6.1 %attend_blocks.5 = (bf16[8,64,1024]{2,1,0:T(8,128)(2,1)}, bf16[8,64,1024]{2,1,0:T(8,128)(2,1)}, bf16[896,512]{1,0:T(8,128)(2,1)S(1)}, bf16[2,256,768]{2,1,0:T(8,...) custom-call(s32[32]{0:T(128)S(1)} %reshape.62.id_ref, ...), custom_call_target="tpu_custom_call", output_to_operand_aliasing={{0}: (9, {}), {1}: (10, {})} | custom-call | tf_op jit(solution)/shard_map/attend_blocks/pallas_call | solution.py:290
  73.0 4.7 %weigh_grads.5 = (bf16[448,768]{1,0:T(8,128)(2,1)S(1)}, bf16[448,768]{1,0:T(8,128)(2,1)S(1)}, bf16[448,768]{1,0:T(8,128)(2,1)S(1)}, bf16[448,768]{1,0:T(8,128)(2,1)S(1)}) custom-call(bf16[896,768]{1,0:T(8,128)(2,1)S(1)} %get-tuple-element.174.refs_0_, bf16[896,512]{1,0:T(8,128)(2,1)S(1)} %get-tuple-element.154.refs_1_, ...), custom_call_target="tpu_custom_call" | custom-call | tf_op jit(solution)/shard_map/weigh_grads/pallas_call | solution.py:327
  77.7 0.1 collective-permute-start.14
  77.8 0.5 collective-permute-start.15
  78.3 1.6 %collective-permute-done.14 = bf16[448,768]{1,0:T(8,128)(2,1)S(1)} collective-permute-done((bf16[448,768]{1,0:T(8,128)(2,1)S(1)}, bf16[448,768]{1,0:T(8,128)(2,1)S(1)}, u32[]{:S(2)}, u32[]{:S(2)}) %collective-permute-start.14) | collective-permute-done | bytes 688160 | tf_op jit(solution)/shard_map/ppermute | solution.py:46
  79.9 1.0 collective-permute-done.15
  80.9 0.3 fold_grads.4
  81.2 0.8 collective-permute-start.16
  82.1 1.3 %collective-permute-start.17 = (bf16[2,112,768]{2,1,0:T(8,128)(2,1)S(1)}, bf16[2,112,768]{2,1,0:T(8,128)(2,1)S(1)}, u32[]{:S(2)}, u32[]{:S(2)}) collective-permute-start(bf16[2,112,768]{2,1,0:T(8,128)(2,1)S(1)} %get-tuple-element.171), channel_id=1, source_target_pairs={{0,8},{4,12},{8,0},{12,4},{1,9},{5,13},{9,1},{13,5},{2,10},{6,14},... | collective-permute-start | bytes 1032200 | tf_op jit(solution)/shard_map/ppermute | solution.py:46
  83.4 0.9 weigh_grads.6
  84.2 1.6 %weigh_grads.7 = (bf16[448,256]{1,0:T(8,128)(2,1)S(1)}, bf16[448,256]{1,0:T(8,128)(2,1)S(1)}, bf16[448,256]{1,0:T(8,128)(2,1)S(1)}, bf16[448,256]{1,0:T(8,128)(2,1)S(1)}) custom-call(bf16[896,768]{1,0:T(8,128)(2,1)S(1)} %get-tuple-element.174.refs_0_, bf16[896,512]{1,0:T(8,128)(2,1)S(1)} %get-tuple-element.154.refs_1_, ...), custom_call_target="tpu_custom_call" | custom-call | tf_op jit(solution)/shard_map/weigh_grads/pallas_call | solution.py:327
  85.9 0.1 collective-permute-start.18
  86.0 0.5 collective-permute-start.19
  86.4 1.0 collective-permute-done.18
  87.4 0.3 collective-permute-done.19
  87.8 0.1 fold_grads.6
  87.9 1.6 %collective-permute-start.20 = (bf16[2,112,256]{2,1,0:T(8,128)(2,1)S(1)}, bf16[2,112,256]{2,1,0:T(8,128)(2,1)S(1)}, u32[]{:S(2)}, u32[]{:S(2)}) collective-permute-start(bf16[2,112,256]{2,1,0:T(8,128)(2,1)S(1)} %get-tuple-element.190), channel_id=1, source_target_pairs={{0,4},{4,0},{8,12},{12,8},{1,5},{5,1},{9,13},{13,9},{2,6},{6,2},{1... | collective-permute-start | bytes 344072 | tf_op jit(solution)/shard_map/ppermute | solution.py:46
  89.5 0.4 collective-permute-start.21
  89.9 2.1 %collective-permute-done.16.refs_2_ = bf16[2,112,768]{2,1,0:T(8,128)(2,1)S(1)} collective-permute-done((bf16[2,112,768]{2,1,0:T(8,128)(2,1)S(1)}, bf16[2,112,768]{2,1,0:T(8,128)(2,1)S(1)}, u32[]{:S(2)}, u32[]{:S(2)}) %collective-permute-start.16) | collective-permute-done | bytes 344096 | tf_op jit(solution)/shard_map/ppermute | solution.py:46
  92.0 0.2 fold_grads.5
  92.2 1.9 %collective-permute-start.22 = (bf16[1,112,768]{2,1,0:T(8,128)(2,1)S(1)}, bf16[1,112,768]{2,1,0:T(8,128)(2,1)S(1)}, u32[]{:S(2)}, u32[]{:S(2)}) collective-permute-start(bf16[1,112,768]{2,1,0:T(8,128)(2,1)S(1)} %get-tuple-element.194), channel_id=1, source_target_pairs={{0,8},{4,12},{8,0},{12,4},{1,9},{5,13},{9,1},{13,5},{2,10},{6,14},... | collective-permute-start | bytes 516104 | tf_op jit(solution)/shard_map/ppermute | solution.py:46
  94.1 2.0 %collective-permute-start.23 = (bf16[1,112,768]{2,1,0:T(8,128)(2,1)S(1)}, bf16[1,112,768]{2,1,0:T(8,128)(2,1)S(1)}, u32[]{:S(2)}, u32[]{:S(2)}) collective-permute-start(bf16[1,112,768]{2,1,0:T(8,128)(2,1)S(1)} %get-tuple-element.195), channel_id=1, source_target_pairs={{0,4},{4,0},{8,12},{12,8},{1,5},{5,1},{9,13},{13,9},{2,6},{6,2},{1... | collective-permute-start | bytes 516104 | tf_op jit(solution)/shard_map/ppermute | solution.py:46
  96.1 0.1 fold_grads.7
  96.1 0.1 collective-permute-start.24
  96.3 1.6 %collective-permute-start.25 = (bf16[1,112,256]{2,1,0:T(8,128)(2,1)S(1)}, bf16[1,112,256]{2,1,0:T(8,128)(2,1)S(1)}, u32[]{:S(2)}, u32[]{:S(2)}) collective-permute-start(bf16[1,112,256]{2,1,0:T(8,128)(2,1)S(1)} %get-tuple-element.197), channel_id=1, source_target_pairs={{0,4},{4,0},{8,12},{12,8},{1,5},{5,1},{9,13},{13,9},{2,6},{6,2},{1... | collective-permute-start | bytes 172040 | tf_op jit(solution)/shard_map/ppermute | solution.py:46
  97.9 2.5 %collective-permute-done.24.refs_6_ = bf16[1,112,256]{2,1,0:T(8,128)(2,1)S(1)} collective-permute-done((bf16[1,112,256]{2,1,0:T(8,128)(2,1)S(1)}, bf16[1,112,256]{2,1,0:T(8,128)(2,1)S(1)}, u32[]{:S(2)}, u32[]{:S(2)}) %collective-permute-start.24) | collective-permute-done | bytes 57376 | tf_op jit(solution)/shard_map/ppermute | solution.py:46
  100.4 0.2 collective-permute-done.25.refs_7_
  100.6 1.0 join_grads.1
  (22 shorter events, 0.1 us)
Async XLA Ops:
  1.5 8.0 %collective-permute-start.2 = (s32[32]{0:T(128)S(1)}, s32[32]{0:T(128)S(1)}, u32[]{:S(2)}, u32[]{:S(2)}) collective-permute-start(s32[32]{0:T(128)S(1)} %reshape.62.id_ref), channel_id=1, source_target_pairs={{0,12},{4,8},{8,4},{12,0},{1,13},{5,9},{9,5},{13,1},{2,14},{6,10},... | collective-permute-start | bytes 392 | tf_op jit(solution)/shard_map/ppermute | solution.py:46
  5.5 4.0 %collective-permute-start.1 = (s32[32]{0:T(128)S(1)}, s32[32]{0:T(128)S(1)}, u32[]{:S(2)}, u32[]{:S(2)}) collective-permute-start(s32[32]{0:T(128)S(1)} %reshape.62.id_ref), channel_id=1, source_target_pairs={{0,8},{4,12},{8,0},{12,4},{1,9},{5,13},{9,1},{13,5},{2,10},{6,14},... | collective-permute-start | bytes 392 | tf_op jit(solution)/shard_map/ppermute | solution.py:46
  6.0 3.5 %collective-permute-start = (s32[32]{0:T(128)S(1)}, s32[32]{0:T(128)S(1)}, u32[]{:S(2)}, u32[]{:S(2)}) collective-permute-start(s32[32]{0:T(128)S(1)} %reshape.62.id_ref), channel_id=1, source_target_pairs={{0,4},{4,0},{8,12},{12,8},{1,5},{5,1},{9,13},{13,9},{2,6},{6,2},{1... | collective-permute-start | bytes 392 | tf_op jit(solution)/shard_map/ppermute | solution.py:46
  6.2 2.0 %copy-start.4 = (bf16[1,2048,896]{2,1,0:T(8,128)(2,1)S(1)}, bf16[1,2048,896]{2,1,0:T(8,128)(2,1)}, u32[]{:S(2)}) copy-start(bf16[1,2048,896]{2,1,0:T(8,128)(2,1)} %param.8) | copy-start | bytes 11010052
  10.7 11.1 %collective-permute-start.3 = (bf16[3,64,896]{2,1,0:T(8,128)(2,1)S(1)}, bf16[3,64,896]{2,1,0:T(8,128)(2,1)S(1)}, u32[]{:S(2)}, u32[]{:S(2)}) collective-permute-start(bf16[3,64,896]{2,1,0:T(8,128)(2,1)S(1)} %get-tuple-element.103), channel_id=1, source_target_pairs={{0,4},{4,0},{8,12},{12,8},{1,5},{5,1},{9,13},{13,9},{2,6},{6,2},{1... | collective-permute-start | bytes 1032200 | tf_op jit(solution)/shard_map/ppermute | solution.py:46
  12.5 16.2 %collective-permute-start.4 = (bf16[3,64,896]{2,1,0:T(8,128)(2,1)S(1)}, bf16[3,64,896]{2,1,0:T(8,128)(2,1)S(1)}, u32[]{:S(2)}, u32[]{:S(2)}) collective-permute-start(bf16[3,64,896]{2,1,0:T(8,128)(2,1)S(1)} %get-tuple-element.106), channel_id=1, source_target_pairs={{0,8},{4,12},{8,0},{12,4},{1,9},{5,13},{9,1},{13,5},{2,10},{6,14},... | collective-permute-start | bytes 1032200 | tf_op jit(solution)/shard_map/ppermute | solution.py:46
  14.1 17.2 %collective-permute-start.5 = (bf16[3,64,896]{2,1,0:T(8,128)(2,1)S(1)}, bf16[3,64,896]{2,1,0:T(8,128)(2,1)S(1)}, u32[]{:S(2)}, u32[]{:S(2)}) collective-permute-start(bf16[3,64,896]{2,1,0:T(8,128)(2,1)S(1)} %get-tuple-element.109), channel_id=1, source_target_pairs={{0,12},{4,8},{8,4},{12,0},{1,13},{5,9},{9,5},{13,1},{2,14},{6,10},... | collective-permute-start | bytes 1032200 | tf_op jit(solution)/shard_map/ppermute | solution.py:46
  14.2 20.0 %copy-start.1 = (bf16[896,1024]{1,0:T(8,128)(2,1)S(1)}, bf16[896,1024]{1,0:T(8,128)(2,1)}, u32[]{:S(2)}) copy-start(bf16[896,1024]{1,0:T(8,128)(2,1)} %refs_5_.5) | copy-start | bytes 5505028
  15.8 18.5 %copy-start = (bf16[896,1024]{1,0:T(8,128)(2,1)S(1)}, bf16[896,1024]{1,0:T(8,128)(2,1)}, u32[]{:S(2)}) copy-start(bf16[896,1024]{1,0:T(8,128)(2,1)} %refs_4_.5) | copy-start | bytes 5505028
  21.7 14.8 %collective-permute-start.6 = (bf16[3,64,896]{2,1,0:T(8,128)(2,1)S(1)}, bf16[3,64,896]{2,1,0:T(8,128)(2,1)S(1)}, u32[]{:S(2)}, u32[]{:S(2)}) collective-permute-start(bf16[3,64,896]{2,1,0:T(8,128)(2,1)S(1)} %get-tuple-element.114), channel_id=1, source_target_pairs={{0,4},{4,0},{8,12},{12,8},{1,5},{5,1},{9,13},{13,9},{2,6},{6,2},{1... | collective-permute-start | bytes 1032200 | tf_op jit(solution)/shard_map/ppermute | solution.py:46
  28.7 15.2 %collective-permute-start.7 = (bf16[3,64,896]{2,1,0:T(8,128)(2,1)S(1)}, bf16[3,64,896]{2,1,0:T(8,128)(2,1)S(1)}, u32[]{:S(2)}, u32[]{:S(2)}) collective-permute-start(bf16[3,64,896]{2,1,0:T(8,128)(2,1)S(1)} %get-tuple-element.117), channel_id=1, source_target_pairs={{0,8},{4,12},{8,0},{12,4},{1,9},{5,13},{9,1},{13,5},{2,10},{6,14},... | collective-permute-start | bytes 1032200 | tf_op jit(solution)/shard_map/ppermute | solution.py:46
  31.3 12.6 %collective-permute-start.8 = (bf16[3,64,896]{2,1,0:T(8,128)(2,1)S(1)}, bf16[3,64,896]{2,1,0:T(8,128)(2,1)S(1)}, u32[]{:S(2)}, u32[]{:S(2)}) collective-permute-start(bf16[3,64,896]{2,1,0:T(8,128)(2,1)S(1)} %get-tuple-element.120), channel_id=1, source_target_pairs={{0,12},{4,8},{8,4},{12,0},{1,13},{5,9},{9,5},{13,1},{2,14},{6,10},... | collective-permute-start | bytes 1032200 | tf_op jit(solution)/shard_map/ppermute | solution.py:46
  32.6 18.9 %collective-permute-start.9 = (bf16[6,64,896]{2,1,0:T(8,128)(2,1)S(1)}, bf16[6,64,896]{2,1,0:T(8,128)(2,1)S(1)}, u32[]{:S(2)}, u32[]{:S(2)}) collective-permute-start(bf16[6,64,896]{2,1,0:T(8,128)(2,1)S(1)} %unpack_rows.2.rows_ref.refs_0_), channel_id=1, source_target_pairs={{0,1},{1,0},{2,3},{3,2},{4,5},{5,4},{6,7},{7,6},{8,9},{9,8},{10,11... | collective-permute-start | bytes 2064392 | tf_op jit(solution)/shard_map/ppermute | solution.py:46
  44.7 6.8 %copy-start.2 = (bf16[1,512,1024]{2,1,0:T(8,128)(2,1)S(1)}, bf16[1,512,1024]{2,1,0:T(8,128)(2,1)}, u32[]{:S(2)}) copy-start(bf16[1,512,1024]{2,1,0:T(8,128)(2,1)} %param.7) | copy-start | bytes 3145732
  44.7 6.8 %copy-start.3 = (bf16[1,512,1024]{2,1,0:T(8,128)(2,1)S(1)}, bf16[1,512,1024]{2,1,0:T(8,128)(2,1)}, u32[]{:S(2)}) copy-start(bf16[1,512,1024]{2,1,0:T(8,128)(2,1)} %param.13) | copy-start | bytes 3145732
  44.7 15.8 %collective-permute-start.10 = (bf16[6,64,896]{2,1,0:T(8,128)(2,1)S(1)}, bf16[6,64,896]{2,1,0:T(8,128)(2,1)S(1)}, u32[]{:S(2)}, u32[]{:S(2)}) collective-permute-start(bf16[6,64,896]{2,1,0:T(8,128)(2,1)S(1)} %unpack_rows.3.rows_ref.refs_0_), channel_id=1, source_target_pairs={{0,1},{1,0},{2,3},{3,2},{4,5},{5,4},{6,7},{7,6},{8,9},{9,8},{10,11... | collective-permute-start | bytes 2064392 | tf_op jit(solution)/shard_map/ppermute | solution.py:46
  46.2 20.6 %collective-permute-start.13 = (bf16[2,2,64,896]{3,2,1,0:T(8,128)(2,1)S(1)}, bf16[2,2,64,896]{3,2,1,0:T(8,128)(2,1)S(1)}, u32[]{:S(2)}, u32[]{:S(2)}) collective-permute-start(bf16[2,2,64,896]{3,2,1,0:T(8,128)(2,1)S(1)} %get-tuple-element.144), channel_id=1, source_target_pairs={{0,12},{4,8},{8,4},{12,0},{1,13},{5,9},{9,5},{13,1},{2,14},{6,10},... | collective-permute-start | bytes 1376264 | tf_op jit(solution)/shard_map/ppermute | solution.py:46
  47.2 19.6 %collective-permute-start.12 = (bf16[2,2,64,896]{3,2,1,0:T(8,128)(2,1)S(1)}, bf16[2,2,64,896]{3,2,1,0:T(8,128)(2,1)S(1)}, u32[]{:S(2)}, u32[]{:S(2)}) collective-permute-start(bf16[2,2,64,896]{3,2,1,0:T(8,128)(2,1)S(1)} %get-tuple-element.143), channel_id=1, source_target_pairs={{0,8},{4,12},{8,0},{12,4},{1,9},{5,13},{9,1},{13,5},{2,10},{6,14},... | collective-permute-start | bytes 1376264 | tf_op jit(solution)/shard_map/ppermute | solution.py:46
  48.5 18.4 %collective-permute-start.11 = (bf16[2,2,64,896]{3,2,1,0:T(8,128)(2,1)S(1)}, bf16[2,2,64,896]{3,2,1,0:T(8,128)(2,1)S(1)}, u32[]{:S(2)}, u32[]{:S(2)}) collective-permute-start(bf16[2,2,64,896]{3,2,1,0:T(8,128)(2,1)S(1)} %get-tuple-element.142), channel_id=1, source_target_pairs={{0,4},{4,0},{8,12},{12,8},{1,5},{5,1},{9,13},{13,9},{2,6},{6,2},{1... | collective-permute-start | bytes 1376264 | tf_op jit(solution)/shard_map/ppermute | solution.py:46
  77.7 2.2 %collective-permute-start.14 = (bf16[448,768]{1,0:T(8,128)(2,1)S(1)}, bf16[448,768]{1,0:T(8,128)(2,1)S(1)}, u32[]{:S(2)}, u32[]{:S(2)}) collective-permute-start(bf16[448,768]{1,0:T(8,128)(2,1)S(1)} %get-tuple-element.164), channel_id=1, source_target_pairs={{0,16},{16,0},{1,17},{17,1},{2,18},{18,2},{3,19},{19,3},{4,20},{20... | collective-permute-start | bytes 2064392 | tf_op jit(solution)/shard_map/ppermute | solution.py:46
  77.8 3.1 %collective-permute-start.15 = (bf16[448,768]{1,0:T(8,128)(2,1)S(1)}, bf16[448,768]{1,0:T(8,128)(2,1)S(1)}, u32[]{:S(2)}, u32[]{:S(2)}) collective-permute-start(bf16[448,768]{1,0:T(8,128)(2,1)S(1)} %get-tuple-element.165), channel_id=1, source_target_pairs={{0,16},{16,0},{1,17},{17,1},{2,18},{18,2},{3,19},{19,3},{4,20},{20... | collective-permute-start | bytes 2064392 | tf_op jit(solution)/shard_map/ppermute | solution.py:46
  81.2 10.8 %collective-permute-start.16 = (bf16[2,112,768]{2,1,0:T(8,128)(2,1)S(1)}, bf16[2,112,768]{2,1,0:T(8,128)(2,1)S(1)}, u32[]{:S(2)}, u32[]{:S(2)}) collective-permute-start(bf16[2,112,768]{2,1,0:T(8,128)(2,1)S(1)} %get-tuple-element.170), channel_id=1, source_target_pairs={{0,4},{4,0},{8,12},{12,8},{1,5},{5,1},{9,13},{13,9},{2,6},{6,2},{1... | collective-permute-start | bytes 1032200 | tf_op jit(solution)/shard_map/ppermute | solution.py:46
  82.1 9.9 %collective-permute-start.17 = (bf16[2,112,768]{2,1,0:T(8,128)(2,1)S(1)}, bf16[2,112,768]{2,1,0:T(8,128)(2,1)S(1)}, u32[]{:S(2)}, u32[]{:S(2)}) collective-permute-start(bf16[2,112,768]{2,1,0:T(8,128)(2,1)S(1)} %get-tuple-element.171), channel_id=1, source_target_pairs={{0,8},{4,12},{8,0},{12,4},{1,9},{5,13},{9,1},{13,5},{2,10},{6,14},... | collective-permute-start | bytes 1032200 | tf_op jit(solution)/shard_map/ppermute | solution.py:46
  85.9 1.6 %collective-permute-start.18 = (bf16[448,256]{1,0:T(8,128)(2,1)S(1)}, bf16[448,256]{1,0:T(8,128)(2,1)S(1)}, u32[]{:S(2)}, u32[]{:S(2)}) collective-permute-start(bf16[448,256]{1,0:T(8,128)(2,1)S(1)} %get-tuple-element.186), channel_id=1, source_target_pairs={{0,16},{16,0},{1,17},{17,1},{2,18},{18,2},{3,19},{19,3},{4,20},{20... | collective-permute-start | bytes 688136 | tf_op jit(solution)/shard_map/ppermute | solution.py:46
  86.0 1.8 %collective-permute-start.19 = (bf16[448,256]{1,0:T(8,128)(2,1)S(1)}, bf16[448,256]{1,0:T(8,128)(2,1)S(1)}, u32[]{:S(2)}, u32[]{:S(2)}) collective-permute-start(bf16[448,256]{1,0:T(8,128)(2,1)S(1)} %get-tuple-element.187), channel_id=1, source_target_pairs={{0,16},{16,0},{1,17},{17,1},{2,18},{18,2},{3,19},{19,3},{4,20},{20... | collective-permute-start | bytes 688136 | tf_op jit(solution)/shard_map/ppermute | solution.py:46
  87.9 8.2 %collective-permute-start.20 = (bf16[2,112,256]{2,1,0:T(8,128)(2,1)S(1)}, bf16[2,112,256]{2,1,0:T(8,128)(2,1)S(1)}, u32[]{:S(2)}, u32[]{:S(2)}) collective-permute-start(bf16[2,112,256]{2,1,0:T(8,128)(2,1)S(1)} %get-tuple-element.190), channel_id=1, source_target_pairs={{0,4},{4,0},{8,12},{12,8},{1,5},{5,1},{9,13},{13,9},{2,6},{6,2},{1... | collective-permute-start | bytes 344072 | tf_op jit(solution)/shard_map/ppermute | solution.py:46
  89.5 6.6 %collective-permute-start.21 = (bf16[2,112,256]{2,1,0:T(8,128)(2,1)S(1)}, bf16[2,112,256]{2,1,0:T(8,128)(2,1)S(1)}, u32[]{:S(2)}, u32[]{:S(2)}) collective-permute-start(bf16[2,112,256]{2,1,0:T(8,128)(2,1)S(1)} %get-tuple-element.191), channel_id=1, source_target_pairs={{0,8},{4,12},{8,0},{12,4},{1,9},{5,13},{9,1},{13,5},{2,10},{6,14},... | collective-permute-start | bytes 344072 | tf_op jit(solution)/shard_map/ppermute | solution.py:46
  92.2 8.4 %collective-permute-start.22 = (bf16[1,112,768]{2,1,0:T(8,128)(2,1)S(1)}, bf16[1,112,768]{2,1,0:T(8,128)(2,1)S(1)}, u32[]{:S(2)}, u32[]{:S(2)}) collective-permute-start(bf16[1,112,768]{2,1,0:T(8,128)(2,1)S(1)} %get-tuple-element.194), channel_id=1, source_target_pairs={{0,8},{4,12},{8,0},{12,4},{1,9},{5,13},{9,1},{13,5},{2,10},{6,14},... | collective-permute-start | bytes 516104 | tf_op jit(solution)/shard_map/ppermute | solution.py:46
  94.1 6.5 %collective-permute-start.23 = (bf16[1,112,768]{2,1,0:T(8,128)(2,1)S(1)}, bf16[1,112,768]{2,1,0:T(8,128)(2,1)S(1)}, u32[]{:S(2)}, u32[]{:S(2)}) collective-permute-start(bf16[1,112,768]{2,1,0:T(8,128)(2,1)S(1)} %get-tuple-element.195), channel_id=1, source_target_pairs={{0,4},{4,0},{8,12},{12,8},{1,5},{5,1},{9,13},{13,9},{2,6},{6,2},{1... | collective-permute-start | bytes 516104 | tf_op jit(solution)/shard_map/ppermute | solution.py:46
  96.1 4.2 %collective-permute-start.24 = (bf16[1,112,256]{2,1,0:T(8,128)(2,1)S(1)}, bf16[1,112,256]{2,1,0:T(8,128)(2,1)S(1)}, u32[]{:S(2)}, u32[]{:S(2)}) collective-permute-start(bf16[1,112,256]{2,1,0:T(8,128)(2,1)S(1)} %get-tuple-element.196), channel_id=1, source_target_pairs={{0,8},{4,12},{8,0},{12,4},{1,9},{5,13},{9,1},{13,5},{2,10},{6,14},... | collective-permute-start | bytes 172040 | tf_op jit(solution)/shard_map/ppermute | solution.py:46
  96.3 4.3 %collective-permute-start.25 = (bf16[1,112,256]{2,1,0:T(8,128)(2,1)S(1)}, bf16[1,112,256]{2,1,0:T(8,128)(2,1)S(1)}, u32[]{:S(2)}, u32[]{:S(2)}) collective-permute-start(bf16[1,112,256]{2,1,0:T(8,128)(2,1)S(1)} %get-tuple-element.197), channel_id=1, source_target_pairs={{0,4},{4,0},{8,12},{12,8},{1,5},{5,1},{9,13},{13,9},{2,6},{6,2},{1... | collective-permute-start | bytes 172040 | tf_op jit(solution)/shard_map/ppermute | solution.py:46

commit v6 on v5

--- a/solution.py
+++ b/solution.py
@@ -16,8 +16,8 @@
 ATTEND_MIB = 26
 WEIGH_MIB = 26
 PIECES = 2
+SIDES = (((False,), (True,)), ((False, True),))
 PROJECT_FIRST = True
-MERGE = False
 FIRST_PIECE = 6 / 8
 CHUNKS = ((3, True), (3, True), (2, False))
 
@@ -206,33 +206,15 @@
     )(rows, wk, wv)
 
 
-def weigh_sum(turned, grads, before):
-    total = 0.0 if before is None else before[...]
-    for turn, grad in zip(turned, grads):
-        values = grad[...]
-        total += jnp.dot(turn[...], values.reshape(-1, values.shape[-1]), preferred_element_type=F32)
-    return total
-
-
-def weigh_halves(total, scratch, targets):
-    half = scratch.shape[0] // 2
-    dp = lax.axis_index("dp")
-    scratch[...] = total
-    for target, side in zip(targets, (1 - dp, dp)):
-        target[...] = scratch[pl.ds(pl.multiple_of(side * half, half), half), :].astype(BF16)
-
-
-def attend_kernel(start, count, sources, pair, done, first, tail, id_ref, *refs):
+def attend_kernel(start, count, sources, pair, done, first, id_ref, *refs):
     refs = list(refs)
     take = lambda n: [refs.pop(0) for _ in range(n)]
     row_refs = take(sources)
     ready = take(2 if done else 0)
     wk_ref, wv_ref, q_ref, go_ref = take(4)
-    tail_refs = take(3 * tail + 2 if tail else 0)
     take(0 if first else 2)
     out_hbm, gq_hbm, turned = take(3)
     grad_refs = take(2 * PIECES)
-    tail_outs = take(4 if tail else 0)
     out_ref, gq_ref, keys, values, rows, sems, ranks = take(7)
     size, width = rows.shape[1:]
     part, feat = keys.shape[1:]
@@ -263,16 +245,12 @@
 
     lax.fori_loop(0, count, block, 0)
     turned[...] = rows[...].reshape(-1, width).T
-    if tail:
-        for i in range(2):
-            total = weigh_sum(tail_refs[:tail] + [turned], tail_refs[(1 + i) * tail : (2 + i) * tail] + [grad_refs[i]], tail_refs[3 * tail + i])
-            weigh_halves(total, refs[0], tail_outs[i::2])
     for b in range(count):
         for store in stores(b):
             store.wait()
 
 
-def attend(rows, ready, own, wk, wv, queries, grad_out, start, count, pair, carried, tail):
+def attend(rows, ready, own, wk, wv, queries, grad_out, start, count, pair, carried):
     _, tokens, feat = queries.shape
     enc = wk.shape[0]
     context = NEIGHBOURS * NEIGH_LEN
@@ -284,13 +262,12 @@
     widths = [(bounds[piece + 1] - bounds[piece]) * HEAD_DIM for piece in range(PIECES) for _ in range(2)]
     grad_shapes = [jax.ShapeDtypeStruct((count, context, width), BF16) for width in widths]
     fresh = context // 2 if ready else context
-    weighed = [jax.ShapeDtypeStruct((enc // 2, widths[0]), BF16)] * (4 if tail else 0)
-    aliased = 1 + len(rows) + len(ready) + 4 + len(tail)
-    settings = start, count, len(rows), pair, bool(ready), not carried, len(tail) // 3
+    aliased = 1 + len(rows) + len(ready) + 4
+    settings = start, count, len(rows), pair, bool(ready), not carried
     return pl.pallas_call(
         functools.partial(attend_kernel, *settings),
-        in_specs=[SMEM] + [VMEM] * (len(rows) + len(ready) + 4 + len(tail)) + [HBM] * len(carried),
-        out_specs=[HBM] * 2 + [VMEM] * (1 + 2 * PIECES + len(weighed)),
+        in_specs=[SMEM] + [VMEM] * (len(rows) + len(ready) + 4) + [HBM] * len(carried),
+        out_specs=[HBM] * 2 + [VMEM] * (1 + 2 * PIECES),
         scratch_shapes=[
             pltpu.VMEM((count, tokens, feat), BF16),
             pltpu.VMEM((count, tokens, feat), BF16),
@@ -299,37 +276,46 @@
             pltpu.VMEM((count, context, enc), BF16),
             pltpu.SemaphoreType.DMA((count, 2)),
             pltpu.SMEM((len(rows),), jnp.int32),
-        ]
-        + [pltpu.VMEM((enc, widths[0]), F32)] * bool(tail),
-        out_shape=[row_shape, row_shape, turned_shape] + grad_shapes + weighed,
+        ],
+        out_shape=[row_shape, row_shape, turned_shape] + grad_shapes,
         input_output_aliases={aliased: 0, aliased + 1: 1} if carried else {},
         compiler_params=params(ATTEND_MIB),
         name="attend_blocks",
-    )(own, *rows, *ready, wk, wv, queries, grad_out, *tail, *carried)
-
-
-def weigh_kernel(chunks, carried, last, *refs):
+    )(own, *rows, *ready, wk, wv, queries, grad_out, *carried)
+
+
+def weigh_kernel(chunks, carried, sides, *refs):
     refs = list(refs)
     take = lambda n: [refs.pop(0) for _ in range(n)]
     turned, grads = take(chunks), [take(chunks) for _ in range(2)]
-    before = take(2) if carried else [None] * 2
-    for i in range(2):
-        total = weigh_sum(turned, grads[i], before[i])
-        if last:
-            weigh_halves(total, refs[-1], refs[i:4:2])
-        else:
-            refs[i][...] = total
-
-
-def weigh(turned, dks, dvs, before, last):
+    before = take(2) if carried else []
+    enc = turned[0].shape[0]
+    for side in sides:
+        rows = slice(0, enc)
+        if side is not None:
+            half = lax.axis_index("dp") if side else 1 - lax.axis_index("dp")
+            rows = pl.ds(pl.multiple_of(half * (enc // 2), enc // 2), enc // 2)
+        for i in range(2):
+            total = before[i][rows, :] if carried else 0.0
+            for turn, ref in zip(turned, grads[i]):
+                grad = ref[...]
+                total += jnp.dot(turn[rows, :], grad.reshape(-1, grad.shape[-1]), preferred_element_type=F32)
+            target = refs.pop(0)
+            target[...] = total.astype(target.dtype)
+
+
+def weigh(turned, dks, dvs, before, sides):
     enc, width = turned[0].shape[0], dks[0].shape[-1]
-    shapes = [jax.ShapeDtypeStruct((enc // 2, width), BF16)] * 4 if last else [jax.ShapeDtypeStruct((enc, width), F32)] * 2
-    return pl.pallas_call(
-        functools.partial(weigh_kernel, len(turned), bool(before), last),
+    shapes = [
+        jax.ShapeDtypeStruct((enc, width), F32) if side is None else jax.ShapeDtypeStruct((enc // 2, width), BF16)
+        for side in sides
+        for _ in range(2)
+    ]
+    return pl.pallas_call(
+        functools.partial(weigh_kernel, len(turned), bool(before), sides),
         in_specs=[VMEM] * (3 * len(turned) + len(before)),
         out_specs=[VMEM] * len(shapes),
         out_shape=shapes,
-        scratch_shapes=[pltpu.VMEM((enc, width), F32)] if last else [],
         compiler_params=params(WEIGH_MIB),
         name="weigh_grads",
     )(*turned, *dks, *dvs, *before)
@@ -445,8 +431,8 @@
     rows, turned, found, sums, early = [None] * len(spans), [], [], [[]] * PIECES, None
     ready = [[] for _ in spans]
 
-    def weigh_piece(turned, found, piece, before, last):
-        return list(weigh(turned, *([grads[2 * piece + i] for grads in found] for i in range(2)), before, last))
+    def weigh_piece(turned, found, piece, before, sides):
+        return list(weigh(turned, *([grads[2 * piece + i] for grads in found] for i in range(2)), before, sides))
 
 
     def prepare(i):
@@ -467,19 +453,15 @@
                 ready[i][0], arrivals[i + 1] = lax.optimization_barrier((ready[i][0], arrivals[i + 1]))
             prepare(i + 1)
             rows[i][0], rows[i + 1][0] = lax.optimization_barrier((rows[i][0], rows[i + 1][0]))
-        tail = []
-        if MERGE and last and early and found:
-            tail = turned + [grads[n] for n in range(2) for grads in found] + sums[0]
-        results = attend(rows[i], ready[i], own, w_key, w_value, query_blocks, grad_blocks, start, count, pair, carried, tail)
-        attended, grad_queries, flipped = results[:3]
-        grads, parts = results[3 : 3 + 2 * PIECES], list(results[3 + 2 * PIECES :])
+        results = attend(rows[i], ready[i], own, w_key, w_value, query_blocks, grad_blocks, start, count, pair, carried)
+        attended, grad_queries, flipped, *grads = results
         carried = [attended, grad_queries]
         turned.append(flipped)
         found.append(grads)
         if i == 0 and not last:
             early = turned, found
             turned, found = [], []
-            sums[0] = weigh_piece(*early, 0, [], False)
+            sums[0] = weigh_piece(*early, 0, [], (None,))
             sums[0][0], rows[1][0] = lax.optimization_barrier((sums[0][0], rows[1][0]))
         if not last and rows[i + 1] is None:
             carried[0], arrivals[i + 1] = lax.optimization_barrier((carried[0], arrivals[i + 1]))
@@ -489,12 +471,13 @@
         if piece:
             if early:
                 parts[0], early[0][0] = lax.optimization_barrier((parts[0], early[0][0]))
-                sums[piece] = weigh_piece(*early, piece, [], False)
+                sums[piece] = weigh_piece(*early, piece, [], (None,))
             states.append(Sums(parts[:2], parts[2:]))
             states[-1].fold()
             states[-1].send, turned[0] = lax.optimization_barrier((states[-1].send, turned[0]))
-        if piece or not parts:
-            parts = weigh_piece(turned, found, piece, sums[piece], True)
+        parts = []
+        for sides in SIDES[piece]:
+            parts += weigh_piece(turned, found, piece, sums[piece], sides)
     states.append(Sums(parts[:2], parts[2:]))
     states[-1].fold()
     for step in range(states[0].bits):

time: 102 us -> 99.1 us (0.972)
  Pallas kernels: 38.9 us -> 37.5 us
  waiting for transfers between devices: 28 us -> 26.8 us
    ppermute x26, waiting for transfers between devices: 28 us -> 26.8 us  [swap(): return lax.ppermute(array, axis, [(i, i ^ bit) for i in range(size)])]
    pallas_call x4 -> x5, Pallas kernels: 9.53 us -> 8.44 us  [weigh(): pl.pallas_call(functools.partial(weigh_kernel, len(turned), bool(before),...]
  transfers between devices with their start and end apart: 26 -> 26, of which waited for: 12 -> 11; matrix products, arithmetic and copies ran while one was open for 0% -> 0% of each run, Pallas kernels for 25% -> 27%
where the time goes in v6:
time: 99.1 us; the launch traced here: 99 us
  Pallas kernels  37.5 us (38%)
  starting transfers between devices  30.7 us (31%)
  waiting for transfers between devices  26.8 us (27%)
  local copies, waits for them, and re-layouts  2.33 us (2%)
    ppermute x26, starting transfers between devices, swap(): return lax.ppermute(array, axis, [(i, i ^ bit) for i in range(size)])  30.7 us
    ppermute x26, waiting for transfers between devices, swap(): return lax.ppermute(array, axis, [(i, i ^ bit) for i in range(size)])  26.8 us
    pallas_call x3, Pallas kernels, attend(): pl.pallas_call(functools.partial(attend_kernel, *settings), in_specs=[SME...  18.8 us
    pallas_call x5, Pallas kernels, weigh(): pl.pallas_call(functools.partial(weigh_kernel, len(turned), bool(before),...  8.44 us
    pallas_call x2, Pallas kernels, project(): pl.pallas_call(project_kernel, in_specs=[VMEM] * 3, out_specs=[VMEM] * 2,...  3.57 us
    pallas_call x2, Pallas kernels, pick(): pl.pallas_call(functools.partial(pick_kernel, spans), in_specs=[SMEM, VME...  2.34 us
    unnamed x10, local copies, waits for them, and re-layouts  2.06 us
  transfers between devices with their start and end apart: 26, of which 11 were waited for; matrix products, arithmetic and copies ran while one was open for 0% of the time, Pallas kernels for 27%

profile of v6, /device:TPU:0, one launch (start us, length us, event | category | flops | bytes accessed | tf_op | source)
XLA Modules:
  0.0 99.0 jit_solution(1750952946572584069)
XLA Ops:
  0.6 0.7 pad_add_fusion
  1.3 0.1 copy.17
  1.4 0.1 reshape.62.id_ref
  1.5 4.0 %collective-permute-start.2 = (s32[32]{0:T(128)S(1)}, s32[32]{0:T(128)S(1)}, u32[]{:S(2)}, u32[]{:S(2)}) collective-permute-start(s32[32]{0:T(128)S(1)} %reshape.62.id_ref), channel_id=1, source_target_pairs={{0,12},{4,8},{8,4},{12,0},{1,13},{5,9},{9,5},{13,1},{2,14},{6,10},... | collective-permute-start | bytes 392 | tf_op jit(solution)/shard_map/ppermute | solution.py:46
  5.5 0.5 collective-permute-start.1
  6.0 0.1 collective-permute-start
  6.1 0.1 stack_reshape.3
  6.2 2.0 %copy-done.4 = bf16[1,2048,896]{2,1,0:T(8,128)(2,1)S(1)} copy-done((bf16[1,2048,896]{2,1,0:T(8,128)(2,1)S(1)}, bf16[1,2048,896]{2,1,0:T(8,128)(2,1)}, u32[]{:S(2)}) %copy-start.4) | copy-done | bytes 3670040
  8.3 1.2 %normalize_rows.1 = bf16[2048,896]{1,0:T(8,128)(2,1)S(1)} custom-call(bf16[2048,896]{1,0:T(8,128)(2,1)S(1)} %bitcast.31), custom_call_target="tpu_custom_call" | custom-call | tf_op jit(solution)/shard_map/normalize_rows/pallas_call | solution.py:59
  9.5 0.0 collective-permute-done
  9.5 1.0 %pick_rows.2 = (bf16[3,64,896]{2,1,0:T(8,128)(2,1)S(1)}, bf16[3,64,896]{2,1,0:T(8,128)(2,1)S(1)}, bf16[3,64,896]{2,1,0:T(8,128)(2,1)S(1)}, bf16[3,64,896]{2,1,0:T(8,128)(2,1)S(1)}) custom-call(s32[4,32]{1,0:T(4,128)S(1)} %pad_add_fusion.1.id_ref, bf16[16,2,64,896]{3,2,1,0:T(8,128)(2,1)S(1)} %bitcast.23), custom_call_target="tpu_custom_call" | custom-call | tf_op jit(solution)/shard_map/pick_rows/pallas_call | solution.py:106
  10.5 2.1 %collective-permute-start.3 = (bf16[3,64,896]{2,1,0:T(8,128)(2,1)S(1)}, bf16[3,64,896]{2,1,0:T(8,128)(2,1)S(1)}, u32[]{:S(2)}, u32[]{:S(2)}) collective-permute-start(bf16[3,64,896]{2,1,0:T(8,128)(2,1)S(1)} %get-tuple-element.103), channel_id=1, source_target_pairs={{0,4},{4,0},{8,12},{12,8},{1,5},{5,1},{9,13},{13,9},{2,6},{6,2},{1... | collective-permute-start | bytes 1032200 | tf_op jit(solution)/shard_map/ppermute | solution.py:46
  12.6 1.4 %collective-permute-start.4 = (bf16[3,64,896]{2,1,0:T(8,128)(2,1)S(1)}, bf16[3,64,896]{2,1,0:T(8,128)(2,1)S(1)}, u32[]{:S(2)}, u32[]{:S(2)}) collective-permute-start(bf16[3,64,896]{2,1,0:T(8,128)(2,1)S(1)} %get-tuple-element.106), channel_id=1, source_target_pairs={{0,8},{4,12},{8,0},{12,4},{1,9},{5,13},{9,1},{13,5},{2,10},{6,14},... | collective-permute-start | bytes 1032200 | tf_op jit(solution)/shard_map/ppermute | solution.py:46
  14.0 0.1 collective-permute-start.5
  14.1 1.3 %pick_rows.3 = (bf16[3,64,896]{2,1,0:T(8,128)(2,1)S(1)}, bf16[3,64,896]{2,1,0:T(8,128)(2,1)S(1)}, bf16[3,64,896]{2,1,0:T(8,128)(2,1)S(1)}, bf16[3,64,896]{2,1,0:...) custom-call(s32[4,32]{1,0:T(4,128)S(1)} %pad_add_fusion.1.id_ref, ...), custom_call_target="tpu_custom_call" | custom-call | tf_op jit(solution)/shard_map/pick_rows/pallas_call | solution.py:106
  15.5 6.1 %collective-permute-done.3.refs_1_ = bf16[3,64,896]{2,1,0:T(8,128)(2,1)S(1)} collective-permute-done((bf16[3,64,896]{2,1,0:T(8,128)(2,1)S(1)}, bf16[3,64,896]{2,1,0:T(8,128)(2,1)S(1)}, u32[]{:S(2)}, u32[]{:S(2)}) %collective-permute-start.3) | collective-permute-done | bytes 344096 | tf_op jit(solution)/shard_map/ppermute | solution.py:46
  21.6 2.0 %collective-permute-start.6 = (bf16[3,64,896]{2,1,0:T(8,128)(2,1)S(1)}, bf16[3,64,896]{2,1,0:T(8,128)(2,1)S(1)}, u32[]{:S(2)}, u32[]{:S(2)}) collective-permute-start(bf16[3,64,896]{2,1,0:T(8,128)(2,1)S(1)} %get-tuple-element.114), channel_id=1, source_target_pairs={{0,4},{4,0},{8,12},{12,8},{1,5},{5,1},{9,13},{13,9},{2,6},{6,2},{1... | collective-permute-start | bytes 1032200 | tf_op jit(solution)/shard_map/ppermute | solution.py:46
  23.6 5.1 %collective-permute-done.4.refs_2_ = bf16[3,64,896]{2,1,0:T(8,128)(2,1)S(1)} collective-permute-done((bf16[3,64,896]{2,1,0:T(8,128)(2,1)S(1)}, bf16[3,64,896]{2,1,0:T(8,128)(2,1)S(1)}, u32[]{:S(2)}, u32[]{:S(2)}) %collective-permute-start.4) | collective-permute-done | bytes 344096 | tf_op jit(solution)/shard_map/ppermute | solution.py:46
  28.7 2.6 %collective-permute-start.7 = (bf16[3,64,896]{2,1,0:T(8,128)(2,1)S(1)}, bf16[3,64,896]{2,1,0:T(8,128)(2,1)S(1)}, u32[]{:S(2)}, u32[]{:S(2)}) collective-permute-start(bf16[3,64,896]{2,1,0:T(8,128)(2,1)S(1)} %get-tuple-element.117), channel_id=1, source_target_pairs={{0,8},{4,12},{8,0},{12,4},{1,9},{5,13},{9,1},{13,5},{2,10},{6,14},... | collective-permute-start | bytes 1032200 | tf_op jit(solution)/shard_map/ppermute | solution.py:46
  31.3 0.6 collective-permute-start.8
  31.9 0.7 unpack_rows.2.rows_ref.refs_0_
  32.7 1.6 %collective-permute-start.9 = (bf16[6,64,896]{2,1,0:T(8,128)(2,1)S(1)}, bf16[6,64,896]{2,1,0:T(8,128)(2,1)S(1)}, u32[]{:S(2)}, u32[]{:S(2)}) collective-permute-start(bf16[6,64,896]{2,1,0:T(8,128)(2,1)S(1)} %unpack_rows.2.rows_ref.refs_0_), channel_id=1, source_target_pairs={{0,1},{1,0},{2,3},{3,2},{4,5},{5,4},{6,7},{7,6},{8,9},{9,8},{10,11... | collective-permute-start | bytes 2064392 | tf_op jit(solution)/shard_map/ppermute | solution.py:46
  34.3 1.8 %project_rows.2 = (bf16[3,128,1024]{2,1,0:T(8,128)(2,1)S(1)}, bf16[3,128,1024]{2,1,0:T(8,128)(2,1)S(1)}) custom-call(bf16[6,64,896]{2,1,0:T(8,128)(2,1)S(1)} %unpack_rows.2.rows_ref.refs_0_, bf16[896,1024]{1,0:T(8,128)(2,1)S(1)} %copy-done, bf16[896,1024]{1,0:T(8,128)(2,1)S(1)} %copy-done.1), custom_call_target="tpu_custom_call" | custom-call | tf_op jit(solution)/shard_map/project_rows/pallas_call | solution.py:199
  36.1 0.3 collective-permute-done.6.refs_1_
  36.4 7.5 %collective-permute-done.7.refs_2_ = bf16[3,64,896]{2,1,0:T(8,128)(2,1)S(1)} collective-permute-done((bf16[3,64,896]{2,1,0:T(8,128)(2,1)S(1)}, bf16[3,64,896]{2,1,0:T(8,128)(2,1)S(1)}, u32[]{:S(2)}, u32[]{:S(2)}) %collective-permute-start.7) | collective-permute-done | bytes 344096 | tf_op jit(solution)/shard_map/ppermute | solution.py:46
  43.9 0.7 unpack_rows.3.rows_ref.refs_0_
  44.6 0.0 copy-start.3
  44.7 1.5 %collective-permute-start.10 = (bf16[6,64,896]{2,1,0:T(8,128)(2,1)S(1)}, bf16[6,64,896]{2,1,0:T(8,128)(2,1)S(1)}, u32[]{:S(2)}, u32[]{:S(2)}) collective-permute-start(bf16[6,64,896]{2,1,0:T(8,128)(2,1)S(1)} %unpack_rows.3.rows_ref.refs_0_), channel_id=1, source_target_pairs={{0,1},{1,0},{2,3},{3,2},{4,5},{5,4},{6,7},{7,6},{8,9},{9,8},{10,11... | collective-permute-start | bytes 2064392 | tf_op jit(solution)/shard_map/ppermute | solution.py:46
  46.2 1.1 %collective-permute-start.13 = (bf16[2,2,64,896]{3,2,1,0:T(8,128)(2,1)S(1)}, bf16[2,2,64,896]{3,2,1,0:T(8,128)(2,1)S(1)}, u32[]{:S(2)}, u32[]{:S(2)}) collective-permute-start(bf16[2,2,64,896]{3,2,1,0:T(8,128)(2,1)S(1)} %get-tuple-element.144), channel_id=1, source_target_pairs={{0,12},{4,8},{8,4},{12,0},{1,13},{5,9},{9,5},{13,1},{2,14},{6,10},... | collective-permute-start | bytes 1376264 | tf_op jit(solution)/shard_map/ppermute | solution.py:46
  47.3 1.2 %collective-permute-start.12 = (bf16[2,2,64,896]{3,2,1,0:T(8,128)(2,1)S(1)}, bf16[2,2,64,896]{3,2,1,0:T(8,128)(2,1)S(1)}, u32[]{:S(2)}, u32[]{:S(2)}) collective-permute-start(bf16[2,2,64,896]{3,2,1,0:T(8,128)(2,1)S(1)} %get-tuple-element.143), channel_id=1, source_target_pairs={{0,8},{4,12},{8,0},{12,4},{1,9},{5,13},{9,1},{13,5},{2,10},{6,14},... | collective-permute-start | bytes 1376264 | tf_op jit(solution)/shard_map/ppermute | solution.py:46
  48.5 1.2 %collective-permute-start.11 = (bf16[2,2,64,896]{3,2,1,0:T(8,128)(2,1)S(1)}, bf16[2,2,64,896]{3,2,1,0:T(8,128)(2,1)S(1)}, u32[]{:S(2)}, u32[]{:S(2)}) collective-permute-start(bf16[2,2,64,896]{3,2,1,0:T(8,128)(2,1)S(1)} %get-tuple-element.142), channel_id=1, source_target_pairs={{0,4},{4,0},{8,12},{12,8},{1,5},{5,1},{9,13},{13,9},{2,6},{6,2},{1... | collective-permute-start | bytes 1376264 | tf_op jit(solution)/shard_map/ppermute | solution.py:46
  49.7 1.8 %project_rows.3 = (bf16[3,128,1024]{2,1,0:T(8,128)(2,1)S(1)}, bf16[3,128,1024]{2,1,0:T(8,128)(2,1)S(1)}) custom-call(bf16[6,64,896]{2,1,0:T(8,128)(2,1)S(1)} %unpack_rows.3.rows_ref.refs_0_, bf16[896,1024]{1,0:T(8,128)(2,1)S(1)} %copy-done, bf16[896,1024]{1,0:T(8,128)(2,1)S(1)} %copy-done.1), custom_call_target="tpu_custom_call" | custom-call | tf_op jit(solution)/shard_map/project_rows/pallas_call | solution.py:199
  51.5 6.4 %attend_blocks.3 = (bf16[8,64,1024]{2,1,0:T(8,128)(2,1)}, bf16[8,64,1024]{2,1,0:T(8,128)(2,1)}, bf16[896,768]{1,0:T(8,128)(2,1)S(1)}, bf16[3,256,768]{2,1,0:T(8,...) custom-call(s32[32]{0:T(128)S(1)} %reshape.62.id_ref, ...), custom_call_target="tpu_custom_call" | custom-call | tf_op jit(solution)/shard_map/attend_blocks/pallas_call | solution.py:267
  57.9 2.3 %weigh_grads.5 = (f32[896,768]{1,0:T(8,128)S(1)}, f32[896,768]{1,0:T(8,128)S(1)}) custom-call(bf16[896,768]{1,0:T(8,128)(2,1)S(1)} %get-tuple-element.179.refs_0_, bf16[3,256,768]{2,1,0:T(8,128)(2,1)S(1)} %get-tuple-element.131.refs_1_, bf16[3,256,768]{2,1,0:T(8,128)(2,1)S(1)} %get-tuple-element.132.refs_2_), custom_call_target="tpu_custom_call" | custom-call | tf_op jit(solution)/shard_map/weigh_grads/pallas_call | solution.py:314
  60.2 0.4 collective-permute-done.10.refs_1_
  60.6 6.4 %attend_blocks.4 = (bf16[8,64,1024]{2,1,0:T(8,128)(2,1)}, bf16[8,64,1024]{2,1,0:T(8,128)(2,1)}, bf16[896,768]{1,0:T(8,128)(2,1)S(1)}, bf16[3,256,768]{2,1,0:T(8,...) custom-call(s32[32]{0:T(128)S(1)} %reshape.62.id_ref, ...), custom_call_target="tpu_custom_call", output_to_operand_aliasing={{0}: (9, {}), {1}: (10, {})} | custom-call | tf_op jit(solution)/shard_map/attend_blocks/pallas_call | solution.py:267
  67.0 6.1 %attend_blocks.5 = (bf16[8,64,1024]{2,1,0:T(8,128)(2,1)}, bf16[8,64,1024]{2,1,0:T(8,128)(2,1)}, bf16[896,512]{1,0:T(8,128)(2,1)S(1)}, bf16[2,256,768]{2,1,0:T(8,...) custom-call(s32[32]{0:T(128)S(1)} %reshape.62.id_ref, ...), custom_call_target="tpu_custom_call", output_to_operand_aliasing={{0}: (9, {}), {1}: (10, {})} | custom-call | tf_op jit(solution)/shard_map/attend_blocks/pallas_call | solution.py:267
  73.1 2.0 %weigh_grads.7 = (bf16[448,768]{1,0:T(8,128)(2,1)S(1)}, bf16[448,768]{1,0:T(8,128)(2,1)S(1)}) custom-call(bf16[896,768]{1,0:T(8,128)(2,1)S(1)} %get-tuple-element.174.refs_0_, bf16[896,512]{1,0:T(8,128)(2,1)S(1)} %get-tuple-element.154.refs_1_, bf16[3,256,768]{2,1,0:T(8,128)(2,1)S(1)} %get-tuple-element.155.refs_2_, ...), custom_call_target="tpu_custom_call" | custom-call | tf_op jit(solution)/shard_map/weigh_grads/pallas_call | solution.py:314
  75.0 0.1 collective-permute-start.14
  75.1 0.5 collective-permute-start.15
  75.6 1.9 %weigh_grads.6 = (bf16[448,768]{1,0:T(8,128)(2,1)S(1)}, bf16[448,768]{1,0:T(8,128)(2,1)S(1)}) custom-call(bf16[896,768]{1,0:T(8,128)(2,1)S(1)} %get-tuple-element.174.refs_0_, bf16[896,512]{1,0:T(8,128)(2,1)S(1)} %get-tuple-element.154.refs_1_, bf16[3,256,768]{2,1,0:T(8,128)(2,1)S(1)} %get-tuple-element.155.refs_2_, ...), custom_call_target="tpu_custom_call" | custom-call | tf_op jit(solution)/shard_map/weigh_grads/pallas_call | solution.py:314
  77.6 0.7 collective-permute-done.15
  78.2 0.3 fold_grads.4
  78.5 0.7 collective-permute-start.16
  79.2 1.4 %collective-permute-start.17 = (bf16[2,112,768]{2,1,0:T(8,128)(2,1)S(1)}, bf16[2,112,768]{2,1,0:T(8,128)(2,1)S(1)}, u32[]{:S(2)}, u32[]{:S(2)}) collective-permute-start(bf16[2,112,768]{2,1,0:T(8,128)(2,1)S(1)} %get-tuple-element.171), channel_id=1, source_target_pairs={{0,8},{4,12},{8,0},{12,4},{1,9},{5,13},{9,1},{13,5},{2,10},{6,14},... | collective-permute-start | bytes 1032200 | tf_op jit(solution)/shard_map/ppermute | solution.py:46
  80.6 0.9 weigh_grads.8
  81.5 1.4 %weigh_grads.9 = (bf16[448,256]{1,0:T(8,128)(2,1)S(1)}, bf16[448,256]{1,0:T(8,128)(2,1)S(1)}, bf16[448,256]{1,0:T(8,128)(2,1)S(1)}, bf16[448,256]{1,0:T(8,128)(2,1)S(1)}) custom-call(bf16[896,768]{1,0:T(8,128)(2,1)S(1)} %get-tuple-element.174.refs_0_, bf16[896,512]{1,0:T(8,128)(2,1)S(1)} %get-tuple-element.154.refs_1_, ...), custom_call_target="tpu_custom_call" | custom-call | tf_op jit(solution)/shard_map/weigh_grads/pallas_call | solution.py:314
  82.9 0.1 collective-permute-start.18
  82.9 0.5 collective-permute-start.19
  83.4 1.0 collective-permute-done.18
  84.4 0.3 collective-permute-done.19
  84.7 0.1 fold_grads.6
  84.9 1.5 %collective-permute-start.20 = (bf16[2,112,256]{2,1,0:T(8,128)(2,1)S(1)}, bf16[2,112,256]{2,1,0:T(8,128)(2,1)S(1)}, u32[]{:S(2)}, u32[]{:S(2)}) collective-permute-start(bf16[2,112,256]{2,1,0:T(8,128)(2,1)S(1)} %get-tuple-element.190), channel_id=1, source_target_pairs={{0,4},{4,0},{8,12},{12,8},{1,5},{5,1},{9,13},{13,9},{2,6},{6,2},{1... | collective-permute-start | bytes 344072 | tf_op jit(solution)/shard_map/ppermute | solution.py:46
  86.4 0.6 collective-permute-start.21
  87.0 2.5 %collective-permute-done.16.refs_2_ = bf16[2,112,768]{2,1,0:T(8,128)(2,1)S(1)} collective-permute-done((bf16[2,112,768]{2,1,0:T(8,128)(2,1)S(1)}, bf16[2,112,768]{2,1,0:T(8,128)(2,1)S(1)}, u32[]{:S(2)}, u32[]{:S(2)}) %collective-permute-start.16) | collective-permute-done | bytes 344096 | tf_op jit(solution)/shard_map/ppermute | solution.py:46
  89.5 0.2 fold_grads.5
  89.7 1.9 %collective-permute-start.22 = (bf16[1,112,768]{2,1,0:T(8,128)(2,1)S(1)}, bf16[1,112,768]{2,1,0:T(8,128)(2,1)S(1)}, u32[]{:S(2)}, u32[]{:S(2)}) collective-permute-start(bf16[1,112,768]{2,1,0:T(8,128)(2,1)S(1)} %get-tuple-element.194), channel_id=1, source_target_pairs={{0,8},{4,12},{8,0},{12,4},{1,9},{5,13},{9,1},{13,5},{2,10},{6,14},... | collective-permute-start | bytes 516104 | tf_op jit(solution)/shard_map/ppermute | solution.py:46
  91.6 1.7 %collective-permute-start.23 = (bf16[1,112,768]{2,1,0:T(8,128)(2,1)S(1)}, bf16[1,112,768]{2,1,0:T(8,128)(2,1)S(1)}, u32[]{:S(2)}, u32[]{:S(2)}) collective-permute-start(bf16[1,112,768]{2,1,0:T(8,128)(2,1)S(1)} %get-tuple-element.195), channel_id=1, source_target_pairs={{0,4},{4,0},{8,12},{12,8},{1,5},{5,1},{9,13},{13,9},{2,6},{6,2},{1... | collective-permute-start | bytes 516104 | tf_op jit(solution)/shard_map/ppermute | solution.py:46
  93.2 0.1 fold_grads.7
  93.3 0.5 collective-permute-start.24
  93.8 1.2 %collective-permute-start.25 = (bf16[1,112,256]{2,1,0:T(8,128)(2,1)S(1)}, bf16[1,112,256]{2,1,0:T(8,128)(2,1)S(1)}, u32[]{:S(2)}, u32[]{:S(2)}) collective-permute-start(bf16[1,112,256]{2,1,0:T(8,128)(2,1)S(1)} %get-tuple-element.197), channel_id=1, source_target_pairs={{0,4},{4,0},{8,12},{12,8},{1,5},{5,1},{9,13},{13,9},{2,6},{6,2},{1... | collective-permute-start | bytes 172040 | tf_op jit(solution)/shard_map/ppermute | solution.py:46
  95.0 2.5 %collective-permute-done.24.refs_6_ = bf16[1,112,256]{2,1,0:T(8,128)(2,1)S(1)} collective-permute-done((bf16[1,112,256]{2,1,0:T(8,128)(2,1)S(1)}, bf16[1,112,256]{2,1,0:T(8,128)(2,1)S(1)}, u32[]{:S(2)}, u32[]{:S(2)}) %collective-permute-start.24) | collective-permute-done | bytes 57376 | tf_op jit(solution)/shard_map/ppermute | solution.py:46
  97.5 0.4 collective-permute-done.25.refs_7_
  98.0 1.0 %join_grads.1 = (f32[112,1024]{1,0:T(8,128)}, f32[112,1024]{1,0:T(8,128)}) custom-call(bf16[1,112,768]{2,1,0:T(8,128)(2,1)S(1)} %get-tuple-element.172.refs_0_, bf16[1,112,768]{2,1,0:T(8,128)(2,1)S(1)} %get-tuple-element.173.refs_1_, bf16[1,112,256]{2,1,0:T(8,128)(2,1)S(1)} %get-tuple-element.192.refs_2_, ...), custom_call_target="tpu_custom_call" | custom-call | tf_op jit(solution)/shard_map/join_grads/pallas_call | solution.py:365
  (23 shorter events, 0.1 us)
Async XLA Ops:
  1.5 8.0 %collective-permute-start.2 = (s32[32]{0:T(128)S(1)}, s32[32]{0:T(128)S(1)}, u32[]{:S(2)}, u32[]{:S(2)}) collective-permute-start(s32[32]{0:T(128)S(1)} %reshape.62.id_ref), channel_id=1, source_target_pairs={{0,12},{4,8},{8,4},{12,0},{1,13},{5,9},{9,5},{13,1},{2,14},{6,10},... | collective-permute-start | bytes 392 | tf_op jit(solution)/shard_map/ppermute | solution.py:46
  5.5 4.0 %collective-permute-start.1 = (s32[32]{0:T(128)S(1)}, s32[32]{0:T(128)S(1)}, u32[]{:S(2)}, u32[]{:S(2)}) collective-permute-start(s32[32]{0:T(128)S(1)} %reshape.62.id_ref), channel_id=1, source_target_pairs={{0,8},{4,12},{8,0},{12,4},{1,9},{5,13},{9,1},{13,5},{2,10},{6,14},... | collective-permute-start | bytes 392 | tf_op jit(solution)/shard_map/ppermute | solution.py:46
  6.0 3.5 %collective-permute-start = (s32[32]{0:T(128)S(1)}, s32[32]{0:T(128)S(1)}, u32[]{:S(2)}, u32[]{:S(2)}) collective-permute-start(s32[32]{0:T(128)S(1)} %reshape.62.id_ref), channel_id=1, source_target_pairs={{0,4},{4,0},{8,12},{12,8},{1,5},{5,1},{9,13},{13,9},{2,6},{6,2},{1... | collective-permute-start | bytes 392 | tf_op jit(solution)/shard_map/ppermute | solution.py:46
  6.2 2.0 %copy-start.4 = (bf16[1,2048,896]{2,1,0:T(8,128)(2,1)S(1)}, bf16[1,2048,896]{2,1,0:T(8,128)(2,1)}, u32[]{:S(2)}) copy-start(bf16[1,2048,896]{2,1,0:T(8,128)(2,1)} %param.8) | copy-start | bytes 11010052
  10.5 11.1 %collective-permute-start.3 = (bf16[3,64,896]{2,1,0:T(8,128)(2,1)S(1)}, bf16[3,64,896]{2,1,0:T(8,128)(2,1)S(1)}, u32[]{:S(2)}, u32[]{:S(2)}) collective-permute-start(bf16[3,64,896]{2,1,0:T(8,128)(2,1)S(1)} %get-tuple-element.103), channel_id=1, source_target_pairs={{0,4},{4,0},{8,12},{12,8},{1,5},{5,1},{9,13},{13,9},{2,6},{6,2},{1... | collective-permute-start | bytes 1032200 | tf_op jit(solution)/shard_map/ppermute | solution.py:46
  12.6 16.1 %collective-permute-start.4 = (bf16[3,64,896]{2,1,0:T(8,128)(2,1)S(1)}, bf16[3,64,896]{2,1,0:T(8,128)(2,1)S(1)}, u32[]{:S(2)}, u32[]{:S(2)}) collective-permute-start(bf16[3,64,896]{2,1,0:T(8,128)(2,1)S(1)} %get-tuple-element.106), channel_id=1, source_target_pairs={{0,8},{4,12},{8,0},{12,4},{1,9},{5,13},{9,1},{13,5},{2,10},{6,14},... | collective-permute-start | bytes 1032200 | tf_op jit(solution)/shard_map/ppermute | solution.py:46
  14.0 17.2 %collective-permute-start.5 = (bf16[3,64,896]{2,1,0:T(8,128)(2,1)S(1)}, bf16[3,64,896]{2,1,0:T(8,128)(2,1)S(1)}, u32[]{:S(2)}, u32[]{:S(2)}) collective-permute-start(bf16[3,64,896]{2,1,0:T(8,128)(2,1)S(1)} %get-tuple-element.109), channel_id=1, source_target_pairs={{0,12},{4,8},{8,4},{12,0},{1,13},{5,9},{9,5},{13,1},{2,14},{6,10},... | collective-permute-start | bytes 1032200 | tf_op jit(solution)/shard_map/ppermute | solution.py:46
  14.1 20.2 %copy-start.1 = (bf16[896,1024]{1,0:T(8,128)(2,1)S(1)}, bf16[896,1024]{1,0:T(8,128)(2,1)}, u32[]{:S(2)}) copy-start(bf16[896,1024]{1,0:T(8,128)(2,1)} %refs_5_.5) | copy-start | bytes 5505028
  15.5 18.8 %copy-start = (bf16[896,1024]{1,0:T(8,128)(2,1)S(1)}, bf16[896,1024]{1,0:T(8,128)(2,1)}, u32[]{:S(2)}) copy-start(bf16[896,1024]{1,0:T(8,128)(2,1)} %refs_4_.5) | copy-start | bytes 5505028
  21.6 14.8 %collective-permute-start.6 = (bf16[3,64,896]{2,1,0:T(8,128)(2,1)S(1)}, bf16[3,64,896]{2,1,0:T(8,128)(2,1)S(1)}, u32[]{:S(2)}, u32[]{:S(2)}) collective-permute-start(bf16[3,64,896]{2,1,0:T(8,128)(2,1)S(1)} %get-tuple-element.114), channel_id=1, source_target_pairs={{0,4},{4,0},{8,12},{12,8},{1,5},{5,1},{9,13},{13,9},{2,6},{6,2},{1... | collective-permute-start | bytes 1032200 | tf_op jit(solution)/shard_map/ppermute | solution.py:46
  28.7 15.2 %collective-permute-start.7 = (bf16[3,64,896]{2,1,0:T(8,128)(2,1)S(1)}, bf16[3,64,896]{2,1,0:T(8,128)(2,1)S(1)}, u32[]{:S(2)}, u32[]{:S(2)}) collective-permute-start(bf16[3,64,896]{2,1,0:T(8,128)(2,1)S(1)} %get-tuple-element.117), channel_id=1, source_target_pairs={{0,8},{4,12},{8,0},{12,4},{1,9},{5,13},{9,1},{13,5},{2,10},{6,14},... | collective-permute-start | bytes 1032200 | tf_op jit(solution)/shard_map/ppermute | solution.py:46
  31.3 12.6 %collective-permute-start.8 = (bf16[3,64,896]{2,1,0:T(8,128)(2,1)S(1)}, bf16[3,64,896]{2,1,0:T(8,128)(2,1)S(1)}, u32[]{:S(2)}, u32[]{:S(2)}) collective-permute-start(bf16[3,64,896]{2,1,0:T(8,128)(2,1)S(1)} %get-tuple-element.120), channel_id=1, source_target_pairs={{0,12},{4,8},{8,4},{12,0},{1,13},{5,9},{9,5},{13,1},{2,14},{6,10},... | collective-permute-start | bytes 1032200 | tf_op jit(solution)/shard_map/ppermute | solution.py:46
  32.7 18.8 %collective-permute-start.9 = (bf16[6,64,896]{2,1,0:T(8,128)(2,1)S(1)}, bf16[6,64,896]{2,1,0:T(8,128)(2,1)S(1)}, u32[]{:S(2)}, u32[]{:S(2)}) collective-permute-start(bf16[6,64,896]{2,1,0:T(8,128)(2,1)S(1)} %unpack_rows.2.rows_ref.refs_0_), channel_id=1, source_target_pairs={{0,1},{1,0},{2,3},{3,2},{4,5},{5,4},{6,7},{7,6},{8,9},{9,8},{10,11... | collective-permute-start | bytes 2064392 | tf_op jit(solution)/shard_map/ppermute | solution.py:46
  44.6 6.8 %copy-start.2 = (bf16[1,512,1024]{2,1,0:T(8,128)(2,1)S(1)}, bf16[1,512,1024]{2,1,0:T(8,128)(2,1)}, u32[]{:S(2)}) copy-start(bf16[1,512,1024]{2,1,0:T(8,128)(2,1)} %param.7) | copy-start | bytes 3145732
  44.6 6.8 %copy-start.3 = (bf16[1,512,1024]{2,1,0:T(8,128)(2,1)S(1)}, bf16[1,512,1024]{2,1,0:T(8,128)(2,1)}, u32[]{:S(2)}) copy-start(bf16[1,512,1024]{2,1,0:T(8,128)(2,1)} %param.13) | copy-start | bytes 3145732
  44.7 15.9 %collective-permute-start.10 = (bf16[6,64,896]{2,1,0:T(8,128)(2,1)S(1)}, bf16[6,64,896]{2,1,0:T(8,128)(2,1)S(1)}, u32[]{:S(2)}, u32[]{:S(2)}) collective-permute-start(bf16[6,64,896]{2,1,0:T(8,128)(2,1)S(1)} %unpack_rows.3.rows_ref.refs_0_), channel_id=1, source_target_pairs={{0,1},{1,0},{2,3},{3,2},{4,5},{5,4},{6,7},{7,6},{8,9},{9,8},{10,11... | collective-permute-start | bytes 2064392 | tf_op jit(solution)/shard_map/ppermute | solution.py:46
  46.2 20.8 %collective-permute-start.13 = (bf16[2,2,64,896]{3,2,1,0:T(8,128)(2,1)S(1)}, bf16[2,2,64,896]{3,2,1,0:T(8,128)(2,1)S(1)}, u32[]{:S(2)}, u32[]{:S(2)}) collective-permute-start(bf16[2,2,64,896]{3,2,1,0:T(8,128)(2,1)S(1)} %get-tuple-element.144), channel_id=1, source_target_pairs={{0,12},{4,8},{8,4},{12,0},{1,13},{5,9},{9,5},{13,1},{2,14},{6,10},... | collective-permute-start | bytes 1376264 | tf_op jit(solution)/shard_map/ppermute | solution.py:46
  47.3 19.7 %collective-permute-start.12 = (bf16[2,2,64,896]{3,2,1,0:T(8,128)(2,1)S(1)}, bf16[2,2,64,896]{3,2,1,0:T(8,128)(2,1)S(1)}, u32[]{:S(2)}, u32[]{:S(2)}) collective-permute-start(bf16[2,2,64,896]{3,2,1,0:T(8,128)(2,1)S(1)} %get-tuple-element.143), channel_id=1, source_target_pairs={{0,8},{4,12},{8,0},{12,4},{1,9},{5,13},{9,1},{13,5},{2,10},{6,14},... | collective-permute-start | bytes 1376264 | tf_op jit(solution)/shard_map/ppermute | solution.py:46
  48.5 18.5 %collective-permute-start.11 = (bf16[2,2,64,896]{3,2,1,0:T(8,128)(2,1)S(1)}, bf16[2,2,64,896]{3,2,1,0:T(8,128)(2,1)S(1)}, u32[]{:S(2)}, u32[]{:S(2)}) collective-permute-start(bf16[2,2,64,896]{3,2,1,0:T(8,128)(2,1)S(1)} %get-tuple-element.142), channel_id=1, source_target_pairs={{0,4},{4,0},{8,12},{12,8},{1,5},{5,1},{9,13},{13,9},{2,6},{6,2},{1... | collective-permute-start | bytes 1376264 | tf_op jit(solution)/shard_map/ppermute | solution.py:46
  75.0 2.5 %collective-permute-start.14 = (bf16[448,768]{1,0:T(8,128)(2,1)S(1)}, bf16[448,768]{1,0:T(8,128)(2,1)S(1)}, u32[]{:S(2)}, u32[]{:S(2)}) collective-permute-start(bf16[448,768]{1,0:T(8,128)(2,1)S(1)} %get-tuple-element.164), channel_id=1, source_target_pairs={{0,16},{16,0},{1,17},{17,1},{2,18},{18,2},{3,19},{19,3},{4,20},{20... | collective-permute-start | bytes 2064392 | tf_op jit(solution)/shard_map/ppermute | solution.py:46
  75.1 3.1 %collective-permute-start.15 = (bf16[448,768]{1,0:T(8,128)(2,1)S(1)}, bf16[448,768]{1,0:T(8,128)(2,1)S(1)}, u32[]{:S(2)}, u32[]{:S(2)}) collective-permute-start(bf16[448,768]{1,0:T(8,128)(2,1)S(1)} %get-tuple-element.165), channel_id=1, source_target_pairs={{0,16},{16,0},{1,17},{17,1},{2,18},{18,2},{3,19},{19,3},{4,20},{20... | collective-permute-start | bytes 2064392 | tf_op jit(solution)/shard_map/ppermute | solution.py:46
  78.5 11.0 %collective-permute-start.16 = (bf16[2,112,768]{2,1,0:T(8,128)(2,1)S(1)}, bf16[2,112,768]{2,1,0:T(8,128)(2,1)S(1)}, u32[]{:S(2)}, u32[]{:S(2)}) collective-permute-start(bf16[2,112,768]{2,1,0:T(8,128)(2,1)S(1)} %get-tuple-element.170), channel_id=1, source_target_pairs={{0,4},{4,0},{8,12},{12,8},{1,5},{5,1},{9,13},{13,9},{2,6},{6,2},{1... | collective-permute-start | bytes 1032200 | tf_op jit(solution)/shard_map/ppermute | solution.py:46
  79.2 10.3 %collective-permute-start.17 = (bf16[2,112,768]{2,1,0:T(8,128)(2,1)S(1)}, bf16[2,112,768]{2,1,0:T(8,128)(2,1)S(1)}, u32[]{:S(2)}, u32[]{:S(2)}) collective-permute-start(bf16[2,112,768]{2,1,0:T(8,128)(2,1)S(1)} %get-tuple-element.171), channel_id=1, source_target_pairs={{0,8},{4,12},{8,0},{12,4},{1,9},{5,13},{9,1},{13,5},{2,10},{6,14},... | collective-permute-start | bytes 1032200 | tf_op jit(solution)/shard_map/ppermute | solution.py:46
  82.9 1.6 %collective-permute-start.18 = (bf16[448,256]{1,0:T(8,128)(2,1)S(1)}, bf16[448,256]{1,0:T(8,128)(2,1)S(1)}, u32[]{:S(2)}, u32[]{:S(2)}) collective-permute-start(bf16[448,256]{1,0:T(8,128)(2,1)S(1)} %get-tuple-element.186), channel_id=1, source_target_pairs={{0,16},{16,0},{1,17},{17,1},{2,18},{18,2},{3,19},{19,3},{4,20},{20... | collective-permute-start | bytes 688136 | tf_op jit(solution)/shard_map/ppermute | solution.py:46
  82.9 1.8 %collective-permute-start.19 = (bf16[448,256]{1,0:T(8,128)(2,1)S(1)}, bf16[448,256]{1,0:T(8,128)(2,1)S(1)}, u32[]{:S(2)}, u32[]{:S(2)}) collective-permute-start(bf16[448,256]{1,0:T(8,128)(2,1)S(1)} %get-tuple-element.187), channel_id=1, source_target_pairs={{0,16},{16,0},{1,17},{17,1},{2,18},{18,2},{3,19},{19,3},{4,20},{20... | collective-permute-start | bytes 688136 | tf_op jit(solution)/shard_map/ppermute | solution.py:46
  84.9 8.4 %collective-permute-start.20 = (bf16[2,112,256]{2,1,0:T(8,128)(2,1)S(1)}, bf16[2,112,256]{2,1,0:T(8,128)(2,1)S(1)}, u32[]{:S(2)}, u32[]{:S(2)}) collective-permute-start(bf16[2,112,256]{2,1,0:T(8,128)(2,1)S(1)} %get-tuple-element.190), channel_id=1, source_target_pairs={{0,4},{4,0},{8,12},{12,8},{1,5},{5,1},{9,13},{13,9},{2,6},{6,2},{1... | collective-permute-start | bytes 344072 | tf_op jit(solution)/shard_map/ppermute | solution.py:46
  86.4 6.9 %collective-permute-start.21 = (bf16[2,112,256]{2,1,0:T(8,128)(2,1)S(1)}, bf16[2,112,256]{2,1,0:T(8,128)(2,1)S(1)}, u32[]{:S(2)}, u32[]{:S(2)}) collective-permute-start(bf16[2,112,256]{2,1,0:T(8,128)(2,1)S(1)} %get-tuple-element.191), channel_id=1, source_target_pairs={{0,8},{4,12},{8,0},{12,4},{1,9},{5,13},{9,1},{13,5},{2,10},{6,14},... | collective-permute-start | bytes 344072 | tf_op jit(solution)/shard_map/ppermute | solution.py:46
  89.7 8.3 %collective-permute-start.22 = (bf16[1,112,768]{2,1,0:T(8,128)(2,1)S(1)}, bf16[1,112,768]{2,1,0:T(8,128)(2,1)S(1)}, u32[]{:S(2)}, u32[]{:S(2)}) collective-permute-start(bf16[1,112,768]{2,1,0:T(8,128)(2,1)S(1)} %get-tuple-element.194), channel_id=1, source_target_pairs={{0,8},{4,12},{8,0},{12,4},{1,9},{5,13},{9,1},{13,5},{2,10},{6,14},... | collective-permute-start | bytes 516104 | tf_op jit(solution)/shard_map/ppermute | solution.py:46
  91.6 6.4 %collective-permute-start.23 = (bf16[1,112,768]{2,1,0:T(8,128)(2,1)S(1)}, bf16[1,112,768]{2,1,0:T(8,128)(2,1)S(1)}, u32[]{:S(2)}, u32[]{:S(2)}) collective-permute-start(bf16[1,112,768]{2,1,0:T(8,128)(2,1)S(1)} %get-tuple-element.195), channel_id=1, source_target_pairs={{0,4},{4,0},{8,12},{12,8},{1,5},{5,1},{9,13},{13,9},{2,6},{6,2},{1... | collective-permute-start | bytes 516104 | tf_op jit(solution)/shard_map/ppermute | solution.py:46
  93.3 4.2 %collective-permute-start.24 = (bf16[1,112,256]{2,1,0:T(8,128)(2,1)S(1)}, bf16[1,112,256]{2,1,0:T(8,128)(2,1)S(1)}, u32[]{:S(2)}, u32[]{:S(2)}) collective-permute-start(bf16[1,112,256]{2,1,0:T(8,128)(2,1)S(1)} %get-tuple-element.196), channel_id=1, source_target_pairs={{0,8},{4,12},{8,0},{12,4},{1,9},{5,13},{9,1},{13,5},{2,10},{6,14},... | collective-permute-start | bytes 172040 | tf_op jit(solution)/shard_map/ppermute | solution.py:46
  93.8 4.2 %collective-permute-start.25 = (bf16[1,112,256]{2,1,0:T(8,128)(2,1)S(1)}, bf16[1,112,256]{2,1,0:T(8,128)(2,1)S(1)}, u32[]{:S(2)}, u32[]{:S(2)}) collective-permute-start(bf16[1,112,256]{2,1,0:T(8,128)(2,1)S(1)} %get-tuple-element.197), channel_id=1, source_target_pairs={{0,4},{4,0},{8,12},{12,8},{1,5},{5,1},{9,13},{13,9},{2,6},{6,2},{1... | collective-permute-start | bytes 172040 | tf_op jit(solution)/shard_map/ppermute | solution.py:46

commit v7 on v6

--- a/solution.py
+++ b/solution.py
@@ -171,7 +171,7 @@
         grad_refs[2 * piece][:, place] = grads[:, :HEAD_DIM]
         grad_refs[2 * piece + 1][:, place] = grads[:, HEAD_DIM:]
 
-    ahead, lag = 3, 2
+    ahead, lag = 4, 3
     products, weights = {}, {}
     for head in range(-ahead, heads + lag):
         if 0 <= head + ahead < heads:
@@ -206,16 +206,15 @@
     )(rows, wk, wv)
 
 
-def attend_kernel(start, count, sources, pair, done, first, id_ref, *refs):
+def attend_kernel(start, count, sources, pair, done, id_ref, *refs):
     refs = list(refs)
     take = lambda n: [refs.pop(0) for _ in range(n)]
     row_refs = take(sources)
     ready = take(2 if done else 0)
     wk_ref, wv_ref, q_ref, go_ref = take(4)
-    take(0 if first else 2)
-    out_hbm, gq_hbm, turned = take(3)
+    out_ref, gq_ref, turned = take(3)
     grad_refs = take(2 * PIECES)
-    out_ref, gq_ref, keys, values, rows, sems, ranks = take(7)
+    keys, values, rows, ranks = take(4)
     size, width = rows.shape[1:]
     part, feat = keys.shape[1:]
     if pair:
@@ -229,32 +228,23 @@
         product = jnp.dot(rest, w_ref[...], preferred_element_type=F32).astype(BF16)
         target[...] = product.reshape(count, part, feat)
 
-    def stores(b):
-        pairs = ((out_ref, out_hbm), (gq_ref, gq_hbm))
-        return [pltpu.make_async_copy(src.at[b], dst.at[start + b], sems.at[b, i]) for i, (src, dst) in enumerate(pairs)]
-
     def block(b, carry):
         def pick(at, *parts):
             return lambda cols: jnp.concatenate([ref[at, :, cols] for ref in parts], axis=0)
 
         context = pick(b, *ready[:1], keys), pick(b, *ready[1:], values)
         block_grads(*context, pick(start + b, q_ref), pick(start + b, go_ref), out_ref.at[b], gq_ref.at[b], [ref.at[b] for ref in grad_refs])
-        for store in stores(b):
-            store.start()
         return carry
 
     lax.fori_loop(0, count, block, 0)
     turned[...] = rows[...].reshape(-1, width).T
-    for b in range(count):
-        for store in stores(b):
-            store.wait()
-
-
-def attend(rows, ready, own, wk, wv, queries, grad_out, start, count, pair, carried):
+
+
+def attend(rows, ready, own, wk, wv, queries, grad_out, start, count, pair):
     _, tokens, feat = queries.shape
     enc = wk.shape[0]
     context = NEIGHBOURS * NEIGH_LEN
-    row_shape = jax.ShapeDtypeStruct(queries.shape, BF16)
+    row_shape = jax.ShapeDtypeStruct((count, tokens, feat), BF16)
     if not pair:
         rows = [part.reshape(part.shape[0], NEIGH_LEN, enc) for part in rows]
     turned_shape = jax.ShapeDtypeStruct((enc, count * context), BF16)
@@ -262,26 +252,21 @@
     widths = [(bounds[piece + 1] - bounds[piece]) * HEAD_DIM for piece in range(PIECES) for _ in range(2)]
     grad_shapes = [jax.ShapeDtypeStruct((count, context, width), BF16) for width in widths]
     fresh = context // 2 if ready else context
-    aliased = 1 + len(rows) + len(ready) + 4
-    settings = start, count, len(rows), pair, bool(ready), not carried
+    settings = start, count, len(rows), pair, bool(ready)
     return pl.pallas_call(
         functools.partial(attend_kernel, *settings),
-        in_specs=[SMEM] + [VMEM] * (len(rows) + len(ready) + 4) + [HBM] * len(carried),
-        out_specs=[HBM] * 2 + [VMEM] * (1 + 2 * PIECES),
+        in_specs=[SMEM] + [VMEM] * (len(rows) + len(ready) + 4),
+        out_specs=[VMEM] * (3 + 2 * PIECES),
         scratch_shapes=[
-            pltpu.VMEM((count, tokens, feat), BF16),
-            pltpu.VMEM((count, tokens, feat), BF16),
             pltpu.VMEM((count, fresh, feat), BF16),
             pltpu.VMEM((count, fresh, feat), BF16),
             pltpu.VMEM((count, context, enc), BF16),
-            pltpu.SemaphoreType.DMA((count, 2)),
             pltpu.SMEM((len(rows),), jnp.int32),
         ],
         out_shape=[row_shape, row_shape, turned_shape] + grad_shapes,
-        input_output_aliases={aliased: 0, aliased + 1: 1} if carried else {},
         compiler_params=params(ATTEND_MIB),
         name="attend_blocks",
-    )(own, *rows, *ready, wk, wv, queries, grad_out, *carried)
+    )(own, *rows, *ready, wk, wv, queries, grad_out)
 
 
 def weigh_kernel(chunks, carried, sides, *refs):
@@ -421,7 +406,7 @@
     if len(spans) > 1:
         outgoing = outgoing + pick(ids, normed, spans[1:], capacity)
     query_blocks, grad_blocks = (array.reshape(blocks, -1, array.shape[2]) for array in (queries, grad_out))
-    carried, arrivals = [], []
+    attended, grad_queries, arrivals = [], [], []
     for slots in outgoing:
         slots = list(slots)
         if arrivals:
@@ -453,9 +438,10 @@
                 ready[i][0], arrivals[i + 1] = lax.optimization_barrier((ready[i][0], arrivals[i + 1]))
             prepare(i + 1)
             rows[i][0], rows[i + 1][0] = lax.optimization_barrier((rows[i][0], rows[i + 1][0]))
-        results = attend(rows[i], ready[i], own, w_key, w_value, query_blocks, grad_blocks, start, count, pair, carried)
-        attended, grad_queries, flipped, *grads = results
-        carried = [attended, grad_queries]
+        results = attend(rows[i], ready[i], own, w_key, w_value, query_blocks, grad_blocks, start, count, pair)
+        out, gq, flipped, *grads = results
+        attended.append(out)
+        grad_queries.append(gq)
         turned.append(flipped)
         found.append(grads)
         if i == 0 and not last:
@@ -464,7 +450,7 @@
             sums[0] = weigh_piece(*early, 0, [], (None,))
             sums[0][0], rows[1][0] = lax.optimization_barrier((sums[0][0], rows[1][0]))
         if not last and rows[i + 1] is None:
-            carried[0], arrivals[i + 1] = lax.optimization_barrier((carried[0], arrivals[i + 1]))
+            attended[-1], arrivals[i + 1] = lax.optimization_barrier((attended[-1], arrivals[i + 1]))
             prepare(i + 1)
     states = []
     for piece in range(PIECES):
@@ -485,9 +471,9 @@
             if step:
                 state.fold()
             state.exchange()
-    attended, grad_queries = carried
     grad_w_key, grad_w_value = join(sum([state.held for state in states], []), sum([state.arrived for state in states], []))
-    return attended.reshape(queries.shape), grad_queries.reshape(queries.shape), grad_w_key, grad_w_value
+    attended, grad_queries = (jnp.concatenate(blocks).reshape(queries.shape) for blocks in (attended, grad_queries))
+    return attended, grad_queries, grad_w_key, grad_w_value
 
 
 def solution(mesh):

time: 99.1 us -> 98.4 us (level)
  other arithmetic: 0.71 us -> 2.26 us
  waiting for transfers between devices: 26.8 us -> 25.6 us
  Pallas kernels: 37.5 us -> 36.5 us
    concatenate x0 -> x1, other arithmetic: none -> 1.55 us  [local(): jnp.concatenate(blocks).reshape(queries.shape)]
    ppermute x26, waiting for transfers between devices: 26.8 us -> 25.6 us  [swap(): return lax.ppermute(array, axis, [(i, i ^ bit) for i in range(size)])]
    pallas_call x3, Pallas kernels: 18.8 us -> 17.7 us  [attend(): pl.pallas_call(functools.partial(attend_kernel, *settings), in_specs=[SME...]
  transfers between devices with their start and end apart: 26 -> 26, of which waited for: 11 -> 11; matrix products, arithmetic and copies ran while one was open for 0% -> 2% of each run, Pallas kernels for 27% -> 27%
where the time goes in v7:
time: 98.4 us; the launch traced here: 98.2 us
  Pallas kernels  36.5 us (37%)
  starting transfers between devices  30.7 us (31%)
  waiting for transfers between devices  25.6 us (26%)
  local copies, waits for them, and re-layouts  2.33 us (2%)
  other arithmetic  2.26 us (2%)
    ppermute x26, starting transfers between devices, swap(): return lax.ppermute(array, axis, [(i, i ^ bit) for i in range(size)])  30.7 us
    ppermute x26, waiting for transfers between devices, swap(): return lax.ppermute(array, axis, [(i, i ^ bit) for i in range(size)])  25.6 us
    pallas_call x3, Pallas kernels, attend(): pl.pallas_call(functools.partial(attend_kernel, *settings), in_specs=[SME...  17.7 us
    pallas_call x5, Pallas kernels, weigh(): pl.pallas_call(functools.partial(weigh_kernel, len(turned), bool(before),...  8.45 us
    pallas_call x2, Pallas kernels, project(): pl.pallas_call(project_kernel, in_specs=[VMEM] * 3, out_specs=[VMEM] * 2,...  3.59 us
    pallas_call x2, Pallas kernels, pick(): pl.pallas_call(functools.partial(pick_kernel, spans), in_specs=[SMEM, VME...  2.34 us
    unnamed x10, local copies, waits for them, and re-layouts  2.06 us
  transfers between devices with their start and end apart: 26, of which 11 were waited for; matrix products, arithmetic and copies ran while one was open for 2% of the time, Pallas kernels for 27%

profile of v7, /device:TPU:0, one launch (start us, length us, event | category | flops | bytes accessed | tf_op | source)
XLA Modules:
  0.0 98.2 jit_solution(6312024419772948372)
XLA Ops:
  0.6 0.7 pad_add_fusion
  1.3 0.1 copy.13
  1.4 0.1 reshape.62.id_ref
  1.5 4.0 %collective-permute-start.2 = (s32[32]{0:T(128)S(1)}, s32[32]{0:T(128)S(1)}, u32[]{:S(2)}, u32[]{:S(2)}) collective-permute-start(s32[32]{0:T(128)S(1)} %reshape.62.id_ref), channel_id=1, source_target_pairs={{0,12},{4,8},{8,4},{12,0},{1,13},{5,9},{9,5},{13,1},{2,14},{6,10},... | collective-permute-start | bytes 392 | tf_op jit(solution)/shard_map/ppermute | solution.py:46
  5.5 0.5 collective-permute-start.1
  6.0 0.1 collective-permute-start
  6.1 0.1 stack_reshape.3
  6.2 2.0 %copy-done.4 = bf16[1,2048,896]{2,1,0:T(8,128)(2,1)S(1)} copy-done((bf16[1,2048,896]{2,1,0:T(8,128)(2,1)S(1)}, bf16[1,2048,896]{2,1,0:T(8,128)(2,1)}, u32[]{:S(2)}) %copy-start.4) | copy-done | bytes 3670040
  8.3 1.2 %normalize_rows.1 = bf16[2048,896]{1,0:T(8,128)(2,1)S(1)} custom-call(bf16[2048,896]{1,0:T(8,128)(2,1)S(1)} %bitcast.31), custom_call_target="tpu_custom_call" | custom-call | tf_op jit(solution)/shard_map/normalize_rows/pallas_call | solution.py:59
  9.5 0.0 collective-permute-done
  9.5 1.0 %pick_rows.2 = (bf16[3,64,896]{2,1,0:T(8,128)(2,1)S(1)}, bf16[3,64,896]{2,1,0:T(8,128)(2,1)S(1)}, bf16[3,64,896]{2,1,0:T(8,128)(2,1)S(1)}, bf16[3,64,896]{2,1,0:T(8,128)(2,1)S(1)}) custom-call(s32[4,32]{1,0:T(4,128)S(1)} %pad_add_fusion.1.id_ref, bf16[16,2,64,896]{3,2,1,0:T(8,128)(2,1)S(1)} %bitcast.23), custom_call_target="tpu_custom_call" | custom-call | tf_op jit(solution)/shard_map/pick_rows/pallas_call | solution.py:106
  10.6 2.0 %collective-permute-start.3 = (bf16[3,64,896]{2,1,0:T(8,128)(2,1)S(1)}, bf16[3,64,896]{2,1,0:T(8,128)(2,1)S(1)}, u32[]{:S(2)}, u32[]{:S(2)}) collective-permute-start(bf16[3,64,896]{2,1,0:T(8,128)(2,1)S(1)} %get-tuple-element.103), channel_id=1, source_target_pairs={{0,4},{4,0},{8,12},{12,8},{1,5},{5,1},{9,13},{13,9},{2,6},{6,2},{1... | collective-permute-start | bytes 1032200 | tf_op jit(solution)/shard_map/ppermute | solution.py:46
  12.6 1.4 %collective-permute-start.4 = (bf16[3,64,896]{2,1,0:T(8,128)(2,1)S(1)}, bf16[3,64,896]{2,1,0:T(8,128)(2,1)S(1)}, u32[]{:S(2)}, u32[]{:S(2)}) collective-permute-start(bf16[3,64,896]{2,1,0:T(8,128)(2,1)S(1)} %get-tuple-element.106), channel_id=1, source_target_pairs={{0,8},{4,12},{8,0},{12,4},{1,9},{5,13},{9,1},{13,5},{2,10},{6,14},... | collective-permute-start | bytes 1032200 | tf_op jit(solution)/shard_map/ppermute | solution.py:46
  14.0 0.1 collective-permute-start.5
  14.1 1.3 %pick_rows.3 = (bf16[3,64,896]{2,1,0:T(8,128)(2,1)S(1)}, bf16[3,64,896]{2,1,0:T(8,128)(2,1)S(1)}, bf16[3,64,896]{2,1,0:T(8,128)(2,1)S(1)}, bf16[3,64,896]{2,1,0:...) custom-call(s32[4,32]{1,0:T(4,128)S(1)} %pad_add_fusion.1.id_ref, ...), custom_call_target="tpu_custom_call" | custom-call | tf_op jit(solution)/shard_map/pick_rows/pallas_call | solution.py:106
  15.5 6.2 %collective-permute-done.3.refs_1_ = bf16[3,64,896]{2,1,0:T(8,128)(2,1)S(1)} collective-permute-done((bf16[3,64,896]{2,1,0:T(8,128)(2,1)S(1)}, bf16[3,64,896]{2,1,0:T(8,128)(2,1)S(1)}, u32[]{:S(2)}, u32[]{:S(2)}) %collective-permute-start.3) | collective-permute-done | bytes 344096 | tf_op jit(solution)/shard_map/ppermute | solution.py:46
  21.6 2.0 %collective-permute-start.6 = (bf16[3,64,896]{2,1,0:T(8,128)(2,1)S(1)}, bf16[3,64,896]{2,1,0:T(8,128)(2,1)S(1)}, u32[]{:S(2)}, u32[]{:S(2)}) collective-permute-start(bf16[3,64,896]{2,1,0:T(8,128)(2,1)S(1)} %get-tuple-element.114), channel_id=1, source_target_pairs={{0,4},{4,0},{8,12},{12,8},{1,5},{5,1},{9,13},{13,9},{2,6},{6,2},{1... | collective-permute-start | bytes 1032200 | tf_op jit(solution)/shard_map/ppermute | solution.py:46
  23.6 5.1 %collective-permute-done.4.refs_2_ = bf16[3,64,896]{2,1,0:T(8,128)(2,1)S(1)} collective-permute-done((bf16[3,64,896]{2,1,0:T(8,128)(2,1)S(1)}, bf16[3,64,896]{2,1,0:T(8,128)(2,1)S(1)}, u32[]{:S(2)}, u32[]{:S(2)}) %collective-permute-start.4) | collective-permute-done | bytes 344096 | tf_op jit(solution)/shard_map/ppermute | solution.py:46
  28.7 2.6 %collective-permute-start.7 = (bf16[3,64,896]{2,1,0:T(8,128)(2,1)S(1)}, bf16[3,64,896]{2,1,0:T(8,128)(2,1)S(1)}, u32[]{:S(2)}, u32[]{:S(2)}) collective-permute-start(bf16[3,64,896]{2,1,0:T(8,128)(2,1)S(1)} %get-tuple-element.117), channel_id=1, source_target_pairs={{0,8},{4,12},{8,0},{12,4},{1,9},{5,13},{9,1},{13,5},{2,10},{6,14},... | collective-permute-start | bytes 1032200 | tf_op jit(solution)/shard_map/ppermute | solution.py:46
  31.3 0.6 collective-permute-start.8
  31.9 0.7 unpack_rows.2.rows_ref.refs_0_
  32.7 1.6 %collective-permute-start.9 = (bf16[6,64,896]{2,1,0:T(8,128)(2,1)S(1)}, bf16[6,64,896]{2,1,0:T(8,128)(2,1)S(1)}, u32[]{:S(2)}, u32[]{:S(2)}) collective-permute-start(bf16[6,64,896]{2,1,0:T(8,128)(2,1)S(1)} %unpack_rows.2.rows_ref.refs_0_), channel_id=1, source_target_pairs={{0,1},{1,0},{2,3},{3,2},{4,5},{5,4},{6,7},{7,6},{8,9},{9,8},{10,11... | collective-permute-start | bytes 2064392 | tf_op jit(solution)/shard_map/ppermute | solution.py:46
  34.3 1.8 %project_rows.2 = (bf16[3,128,1024]{2,1,0:T(8,128)(2,1)S(1)}, bf16[3,128,1024]{2,1,0:T(8,128)(2,1)S(1)}) custom-call(bf16[6,64,896]{2,1,0:T(8,128)(2,1)S(1)} %unpack_rows.2.rows_ref.refs_0_, bf16[896,1024]{1,0:T(8,128)(2,1)S(1)} %copy-done, bf16[896,1024]{1,0:T(8,128)(2,1)S(1)} %copy-done.1), custom_call_target="tpu_custom_call" | custom-call | tf_op jit(solution)/shard_map/project_rows/pallas_call | solution.py:199
  36.1 0.3 collective-permute-done.6.refs_1_
  36.4 7.5 %collective-permute-done.7.refs_2_ = bf16[3,64,896]{2,1,0:T(8,128)(2,1)S(1)} collective-permute-done((bf16[3,64,896]{2,1,0:T(8,128)(2,1)S(1)}, bf16[3,64,896]{2,1,0:T(8,128)(2,1)S(1)}, u32[]{:S(2)}, u32[]{:S(2)}) %collective-permute-start.7) | collective-permute-done | bytes 344096 | tf_op jit(solution)/shard_map/ppermute | solution.py:46
  43.9 0.7 unpack_rows.3.rows_ref.refs_0_
  44.7 1.5 %collective-permute-start.10 = (bf16[6,64,896]{2,1,0:T(8,128)(2,1)S(1)}, bf16[6,64,896]{2,1,0:T(8,128)(2,1)S(1)}, u32[]{:S(2)}, u32[]{:S(2)}) collective-permute-start(bf16[6,64,896]{2,1,0:T(8,128)(2,1)S(1)} %unpack_rows.3.rows_ref.refs_0_), channel_id=1, source_target_pairs={{0,1},{1,0},{2,3},{3,2},{4,5},{5,4},{6,7},{7,6},{8,9},{9,8},{10,11... | collective-permute-start | bytes 2064392 | tf_op jit(solution)/shard_map/ppermute | solution.py:46
  46.2 1.0 %collective-permute-start.13 = (bf16[2,2,64,896]{3,2,1,0:T(8,128)(2,1)S(1)}, bf16[2,2,64,896]{3,2,1,0:T(8,128)(2,1)S(1)}, u32[]{:S(2)}, u32[]{:S(2)}) collective-permute-start(bf16[2,2,64,896]{3,2,1,0:T(8,128)(2,1)S(1)} %get-tuple-element.143), channel_id=1, source_target_pairs={{0,12},{4,8},{8,4},{12,0},{1,13},{5,9},{9,5},{13,1},{2,14},{6,10},... | collective-permute-start | bytes 1376264 | tf_op jit(solution)/shard_map/ppermute | solution.py:46
  47.2 1.2 %collective-permute-start.12 = (bf16[2,2,64,896]{3,2,1,0:T(8,128)(2,1)S(1)}, bf16[2,2,64,896]{3,2,1,0:T(8,128)(2,1)S(1)}, u32[]{:S(2)}, u32[]{:S(2)}) collective-permute-start(bf16[2,2,64,896]{3,2,1,0:T(8,128)(2,1)S(1)} %get-tuple-element.142), channel_id=1, source_target_pairs={{0,8},{4,12},{8,0},{12,4},{1,9},{5,13},{9,1},{13,5},{2,10},{6,14},... | collective-permute-start | bytes 1376264 | tf_op jit(solution)/shard_map/ppermute | solution.py:46
  48.5 1.2 %collective-permute-start.11 = (bf16[2,2,64,896]{3,2,1,0:T(8,128)(2,1)S(1)}, bf16[2,2,64,896]{3,2,1,0:T(8,128)(2,1)S(1)}, u32[]{:S(2)}, u32[]{:S(2)}) collective-permute-start(bf16[2,2,64,896]{3,2,1,0:T(8,128)(2,1)S(1)} %get-tuple-element.141), channel_id=1, source_target_pairs={{0,4},{4,0},{8,12},{12,8},{1,5},{5,1},{9,13},{13,9},{2,6},{6,2},{1... | collective-permute-start | bytes 1376264 | tf_op jit(solution)/shard_map/ppermute | solution.py:46
  49.7 1.8 %project_rows.3 = (bf16[3,128,1024]{2,1,0:T(8,128)(2,1)S(1)}, bf16[3,128,1024]{2,1,0:T(8,128)(2,1)S(1)}) custom-call(bf16[6,64,896]{2,1,0:T(8,128)(2,1)S(1)} %unpack_rows.3.rows_ref.refs_0_, bf16[896,1024]{1,0:T(8,128)(2,1)S(1)} %copy-done, bf16[896,1024]{1,0:T(8,128)(2,1)S(1)} %copy-done.1), custom_call_target="tpu_custom_call" | custom-call | tf_op jit(solution)/shard_map/project_rows/pallas_call | solution.py:199
  51.5 6.1 %attend_blocks.3 = (bf16[3,64,1024]{2,1,0:T(8,128)(2,1)S(1)}, bf16[3,64,1024]{2,1,0:T(8,128)(2,1)S(1)}, bf16[896,768]{1,0:T(8,128)(2,1)S(1)}, bf16[3,256,768]{2,...) custom-call(s32[32]{0:T(128)S(1)} %reshape.62.id_ref, ...), custom_call_target="tpu_custom_call" | custom-call | tf_op jit(solution)/shard_map/attend_blocks/pallas_call | solution.py:256
  57.6 2.3 %weigh_grads.5 = (f32[896,768]{1,0:T(8,128)S(1)}, f32[896,768]{1,0:T(8,128)S(1)}) custom-call(bf16[896,768]{1,0:T(8,128)(2,1)S(1)} %get-tuple-element.179.refs_0_, bf16[3,256,768]{2,1,0:T(8,128)(2,1)S(1)} %get-tuple-element.132.refs_1_, bf16[3,256,768]{2,1,0:T(8,128)(2,1)S(1)} %get-tuple-element.133.refs_2_), custom_call_target="tpu_custom_call" | custom-call | tf_op jit(solution)/shard_map/weigh_grads/pallas_call | solution.py:299
  59.9 0.6 collective-permute-done.10.refs_1_
  60.5 6.0 %attend_blocks.4 = (bf16[3,64,1024]{2,1,0:T(8,128)(2,1)S(1)}, bf16[3,64,1024]{2,1,0:T(8,128)(2,1)S(1)}, bf16[896,768]{1,0:T(8,128)(2,1)S(1)}, bf16[3,256,768]{2,...) custom-call(s32[32]{0:T(128)S(1)} %reshape.62.id_ref, ...), custom_call_target="tpu_custom_call" | custom-call | tf_op jit(solution)/shard_map/attend_blocks/pallas_call | solution.py:256
  66.6 5.7 %attend_blocks.5 = (bf16[2,64,1024]{2,1,0:T(8,128)(2,1)S(1)}, bf16[2,64,1024]{2,1,0:T(8,128)(2,1)S(1)}, bf16[896,512]{1,0:T(8,128)(2,1)S(1)}, bf16[2,256,768]{2,...) custom-call(s32[32]{0:T(128)S(1)} %reshape.62.id_ref, ...), custom_call_target="tpu_custom_call" | custom-call | tf_op jit(solution)/shard_map/attend_blocks/pallas_call | solution.py:256
  72.3 2.0 %weigh_grads.7 = (bf16[448,768]{1,0:T(8,128)(2,1)S(1)}, bf16[448,768]{1,0:T(8,128)(2,1)S(1)}) custom-call(bf16[896,768]{1,0:T(8,128)(2,1)S(1)} %get-tuple-element.174.refs_0_, bf16[896,512]{1,0:T(8,128)(2,1)S(1)} %get-tuple-element.154.refs_1_, bf16[3,256,768]{2,1,0:T(8,128)(2,1)S(1)} %get-tuple-element.155.refs_2_, ...), custom_call_target="tpu_custom_call" | custom-call | tf_op jit(solution)/shard_map/weigh_grads/pallas_call | solution.py:299
  74.2 0.1 collective-permute-start.14
  74.3 0.5 collective-permute-start.15
  74.8 2.0 %weigh_grads.6 = (bf16[448,768]{1,0:T(8,128)(2,1)S(1)}, bf16[448,768]{1,0:T(8,128)(2,1)S(1)}) custom-call(bf16[896,768]{1,0:T(8,128)(2,1)S(1)} %get-tuple-element.174.refs_0_, bf16[896,512]{1,0:T(8,128)(2,1)S(1)} %get-tuple-element.154.refs_1_, bf16[3,256,768]{2,1,0:T(8,128)(2,1)S(1)} %get-tuple-element.155.refs_2_, ...), custom_call_target="tpu_custom_call" | custom-call | tf_op jit(solution)/shard_map/weigh_grads/pallas_call | solution.py:299
  76.8 0.6 collective-permute-done.15
  77.4 0.3 fold_grads.4
  77.8 0.8 collective-permute-start.16
  78.5 1.3 %collective-permute-start.17 = (bf16[2,112,768]{2,1,0:T(8,128)(2,1)S(1)}, bf16[2,112,768]{2,1,0:T(8,128)(2,1)S(1)}, u32[]{:S(2)}, u32[]{:S(2)}) collective-permute-start(bf16[2,112,768]{2,1,0:T(8,128)(2,1)S(1)} %get-tuple-element.171), channel_id=1, source_target_pairs={{0,8},{4,12},{8,0},{12,4},{1,9},{5,13},{9,1},{13,5},{2,10},{6,14},... | collective-permute-start | bytes 1032200 | tf_op jit(solution)/shard_map/ppermute | solution.py:46
  79.8 0.9 weigh_grads.8
  80.7 1.4 %weigh_grads.9 = (bf16[448,256]{1,0:T(8,128)(2,1)S(1)}, bf16[448,256]{1,0:T(8,128)(2,1)S(1)}, bf16[448,256]{1,0:T(8,128)(2,1)S(1)}, bf16[448,256]{1,0:T(8,128)(2,1)S(1)}) custom-call(bf16[896,768]{1,0:T(8,128)(2,1)S(1)} %get-tuple-element.174.refs_0_, bf16[896,512]{1,0:T(8,128)(2,1)S(1)} %get-tuple-element.154.refs_1_, ...), custom_call_target="tpu_custom_call" | custom-call | tf_op jit(solution)/shard_map/weigh_grads/pallas_call | solution.py:299
  82.1 0.1 collective-permute-start.18
  82.2 0.5 collective-permute-start.19
  82.7 1.0 collective-permute-done.18
  83.6 0.3 collective-permute-done.19
  84.0 0.1 fold_grads.6
  84.1 1.5 %collective-permute-start.20 = (bf16[2,112,256]{2,1,0:T(8,128)(2,1)S(1)}, bf16[2,112,256]{2,1,0:T(8,128)(2,1)S(1)}, u32[]{:S(2)}, u32[]{:S(2)}) collective-permute-start(bf16[2,112,256]{2,1,0:T(8,128)(2,1)S(1)} %get-tuple-element.190), channel_id=1, source_target_pairs={{0,4},{4,0},{8,12},{12,8},{1,5},{5,1},{9,13},{13,9},{2,6},{6,2},{1... | collective-permute-start | bytes 344072 | tf_op jit(solution)/shard_map/ppermute | solution.py:46
  85.6 0.6 collective-permute-start.21
  86.2 2.5 %collective-permute-done.16.refs_2_ = bf16[2,112,768]{2,1,0:T(8,128)(2,1)S(1)} collective-permute-done((bf16[2,112,768]{2,1,0:T(8,128)(2,1)S(1)}, bf16[2,112,768]{2,1,0:T(8,128)(2,1)S(1)}, u32[]{:S(2)}, u32[]{:S(2)}) %collective-permute-start.16) | collective-permute-done | bytes 344096 | tf_op jit(solution)/shard_map/ppermute | solution.py:46
  88.7 0.2 fold_grads.5
  88.9 1.9 %collective-permute-start.22 = (bf16[1,112,768]{2,1,0:T(8,128)(2,1)S(1)}, bf16[1,112,768]{2,1,0:T(8,128)(2,1)S(1)}, u32[]{:S(2)}, u32[]{:S(2)}) collective-permute-start(bf16[1,112,768]{2,1,0:T(8,128)(2,1)S(1)} %get-tuple-element.194), channel_id=1, source_target_pairs={{0,8},{4,12},{8,0},{12,4},{1,9},{5,13},{9,1},{13,5},{2,10},{6,14},... | collective-permute-start | bytes 516104 | tf_op jit(solution)/shard_map/ppermute | solution.py:46
  90.8 1.7 %collective-permute-start.23 = (bf16[1,112,768]{2,1,0:T(8,128)(2,1)S(1)}, bf16[1,112,768]{2,1,0:T(8,128)(2,1)S(1)}, u32[]{:S(2)}, u32[]{:S(2)}) collective-permute-start(bf16[1,112,768]{2,1,0:T(8,128)(2,1)S(1)} %get-tuple-element.195), channel_id=1, source_target_pairs={{0,4},{4,0},{8,12},{12,8},{1,5},{5,1},{9,13},{13,9},{2,6},{6,2},{1... | collective-permute-start | bytes 516104 | tf_op jit(solution)/shard_map/ppermute | solution.py:46
  92.5 0.1 fold_grads.7
  92.5 0.5 collective-permute-start.24
  93.0 1.3 %collective-permute-start.25 = (bf16[1,112,256]{2,1,0:T(8,128)(2,1)S(1)}, bf16[1,112,256]{2,1,0:T(8,128)(2,1)S(1)}, u32[]{:S(2)}, u32[]{:S(2)}) collective-permute-start(bf16[1,112,256]{2,1,0:T(8,128)(2,1)S(1)} %get-tuple-element.197), channel_id=1, source_target_pairs={{0,4},{4,0},{8,12},{12,8},{1,5},{5,1},{9,13},{13,9},{2,6},{6,2},{1... | collective-permute-start | bytes 172040 | tf_op jit(solution)/shard_map/ppermute | solution.py:46
  94.3 1.6 %pad_maximum_fusion = (bf16[8,64,1024]{2,1,0:T(8,128)(2,1)}, bf16[8,64,1024]{2,1,0:T(8,128)(2,1)}) fusion(bf16[2,64,1024]{2,1,0:T(8,128)(2,1)S(1)} %get-tuple-element.149, bf16[3,64,1024]{2,1,0:T(8,128)(2,1)S(1)} %get-tuple-element.144, bf16[3,64,1024]{2,1,0:T(8,128)(2,1)S(1)} %get-tuple-element.130, bf16[2,64,1024]{2,1,0:T(8,128)(2,1)S(1)} %get-tuple-element.152, ...), kind=kLoop, calls=%fused_computation | loop fusion | flops 2097152 | bytes 4194304 | tf_op jit(solution)/shard_map/concatenate | solution.py:475
  95.8 0.9 collective-permute-done.24.refs_6_
  96.8 0.4 collective-permute-done.25.refs_7_
  97.2 1.0 %join_grads.1 = (f32[112,1024]{1,0:T(8,128)}, f32[112,1024]{1,0:T(8,128)}) custom-call(bf16[1,112,768]{2,1,0:T(8,128)(2,1)S(1)} %get-tuple-element.172.refs_0_, bf16[1,112,768]{2,1,0:T(8,128)(2,1)S(1)} %get-tuple-element.173.refs_1_, bf16[1,112,256]{2,1,0:T(8,128)(2,1)S(1)} %get-tuple-element.192.refs_2_, ...), custom_call_target="tpu_custom_call" | custom-call | tf_op jit(solution)/shard_map/join_grads/pallas_call | solution.py:350
  (24 shorter events, 0.1 us)
Async XLA Ops:
  1.5 8.0 %collective-permute-start.2 = (s32[32]{0:T(128)S(1)}, s32[32]{0:T(128)S(1)}, u32[]{:S(2)}, u32[]{:S(2)}) collective-permute-start(s32[32]{0:T(128)S(1)} %reshape.62.id_ref), channel_id=1, source_target_pairs={{0,12},{4,8},{8,4},{12,0},{1,13},{5,9},{9,5},{13,1},{2,14},{6,10},... | collective-permute-start | bytes 392 | tf_op jit(solution)/shard_map/ppermute | solution.py:46
  5.5 4.0 %collective-permute-start.1 = (s32[32]{0:T(128)S(1)}, s32[32]{0:T(128)S(1)}, u32[]{:S(2)}, u32[]{:S(2)}) collective-permute-start(s32[32]{0:T(128)S(1)} %reshape.62.id_ref), channel_id=1, source_target_pairs={{0,8},{4,12},{8,0},{12,4},{1,9},{5,13},{9,1},{13,5},{2,10},{6,14},... | collective-permute-start | bytes 392 | tf_op jit(solution)/shard_map/ppermute | solution.py:46
  6.0 3.5 %collective-permute-start = (s32[32]{0:T(128)S(1)}, s32[32]{0:T(128)S(1)}, u32[]{:S(2)}, u32[]{:S(2)}) collective-permute-start(s32[32]{0:T(128)S(1)} %reshape.62.id_ref), channel_id=1, source_target_pairs={{0,4},{4,0},{8,12},{12,8},{1,5},{5,1},{9,13},{13,9},{2,6},{6,2},{1... | collective-permute-start | bytes 392 | tf_op jit(solution)/shard_map/ppermute | solution.py:46
  6.2 2.0 %copy-start.4 = (bf16[1,2048,896]{2,1,0:T(8,128)(2,1)S(1)}, bf16[1,2048,896]{2,1,0:T(8,128)(2,1)}, u32[]{:S(2)}) copy-start(bf16[1,2048,896]{2,1,0:T(8,128)(2,1)} %param.8) | copy-start | bytes 11010052
  10.6 11.1 %collective-permute-start.3 = (bf16[3,64,896]{2,1,0:T(8,128)(2,1)S(1)}, bf16[3,64,896]{2,1,0:T(8,128)(2,1)S(1)}, u32[]{:S(2)}, u32[]{:S(2)}) collective-permute-start(bf16[3,64,896]{2,1,0:T(8,128)(2,1)S(1)} %get-tuple-element.103), channel_id=1, source_target_pairs={{0,4},{4,0},{8,12},{12,8},{1,5},{5,1},{9,13},{13,9},{2,6},{6,2},{1... | collective-permute-start | bytes 1032200 | tf_op jit(solution)/shard_map/ppermute | solution.py:46
  12.6 16.1 %collective-permute-start.4 = (bf16[3,64,896]{2,1,0:T(8,128)(2,1)S(1)}, bf16[3,64,896]{2,1,0:T(8,128)(2,1)S(1)}, u32[]{:S(2)}, u32[]{:S(2)}) collective-permute-start(bf16[3,64,896]{2,1,0:T(8,128)(2,1)S(1)} %get-tuple-element.106), channel_id=1, source_target_pairs={{0,8},{4,12},{8,0},{12,4},{1,9},{5,13},{9,1},{13,5},{2,10},{6,14},... | collective-permute-start | bytes 1032200 | tf_op jit(solution)/shard_map/ppermute | solution.py:46
  14.0 17.3 %collective-permute-start.5 = (bf16[3,64,896]{2,1,0:T(8,128)(2,1)S(1)}, bf16[3,64,896]{2,1,0:T(8,128)(2,1)S(1)}, u32[]{:S(2)}, u32[]{:S(2)}) collective-permute-start(bf16[3,64,896]{2,1,0:T(8,128)(2,1)S(1)} %get-tuple-element.109), channel_id=1, source_target_pairs={{0,12},{4,8},{8,4},{12,0},{1,13},{5,9},{9,5},{13,1},{2,14},{6,10},... | collective-permute-start | bytes 1032200 | tf_op jit(solution)/shard_map/ppermute | solution.py:46
  14.1 20.2 %copy-start.1 = (bf16[896,1024]{1,0:T(8,128)(2,1)S(1)}, bf16[896,1024]{1,0:T(8,128)(2,1)}, u32[]{:S(2)}) copy-start(bf16[896,1024]{1,0:T(8,128)(2,1)} %refs_5_.5) | copy-start | bytes 5505028
  15.5 18.8 %copy-start = (bf16[896,1024]{1,0:T(8,128)(2,1)S(1)}, bf16[896,1024]{1,0:T(8,128)(2,1)}, u32[]{:S(2)}) copy-start(bf16[896,1024]{1,0:T(8,128)(2,1)} %refs_4_.5) | copy-start | bytes 5505028
  21.6 14.8 %collective-permute-start.6 = (bf16[3,64,896]{2,1,0:T(8,128)(2,1)S(1)}, bf16[3,64,896]{2,1,0:T(8,128)(2,1)S(1)}, u32[]{:S(2)}, u32[]{:S(2)}) collective-permute-start(bf16[3,64,896]{2,1,0:T(8,128)(2,1)S(1)} %get-tuple-element.114), channel_id=1, source_target_pairs={{0,4},{4,0},{8,12},{12,8},{1,5},{5,1},{9,13},{13,9},{2,6},{6,2},{1... | collective-permute-start | bytes 1032200 | tf_op jit(solution)/shard_map/ppermute | solution.py:46
  28.7 15.2 %collective-permute-start.7 = (bf16[3,64,896]{2,1,0:T(8,128)(2,1)S(1)}, bf16[3,64,896]{2,1,0:T(8,128)(2,1)S(1)}, u32[]{:S(2)}, u32[]{:S(2)}) collective-permute-start(bf16[3,64,896]{2,1,0:T(8,128)(2,1)S(1)} %get-tuple-element.117), channel_id=1, source_target_pairs={{0,8},{4,12},{8,0},{12,4},{1,9},{5,13},{9,1},{13,5},{2,10},{6,14},... | collective-permute-start | bytes 1032200 | tf_op jit(solution)/shard_map/ppermute | solution.py:46
  31.3 12.6 %collective-permute-start.8 = (bf16[3,64,896]{2,1,0:T(8,128)(2,1)S(1)}, bf16[3,64,896]{2,1,0:T(8,128)(2,1)S(1)}, u32[]{:S(2)}, u32[]{:S(2)}) collective-permute-start(bf16[3,64,896]{2,1,0:T(8,128)(2,1)S(1)} %get-tuple-element.120), channel_id=1, source_target_pairs={{0,12},{4,8},{8,4},{12,0},{1,13},{5,9},{9,5},{13,1},{2,14},{6,10},... | collective-permute-start | bytes 1032200 | tf_op jit(solution)/shard_map/ppermute | solution.py:46
  32.7 18.8 %collective-permute-start.9 = (bf16[6,64,896]{2,1,0:T(8,128)(2,1)S(1)}, bf16[6,64,896]{2,1,0:T(8,128)(2,1)S(1)}, u32[]{:S(2)}, u32[]{:S(2)}) collective-permute-start(bf16[6,64,896]{2,1,0:T(8,128)(2,1)S(1)} %unpack_rows.2.rows_ref.refs_0_), channel_id=1, source_target_pairs={{0,1},{1,0},{2,3},{3,2},{4,5},{5,4},{6,7},{7,6},{8,9},{9,8},{10,11... | collective-permute-start | bytes 2064392 | tf_op jit(solution)/shard_map/ppermute | solution.py:46
  44.6 6.9 %copy-start.2 = (bf16[1,512,1024]{2,1,0:T(8,128)(2,1)S(1)}, bf16[1,512,1024]{2,1,0:T(8,128)(2,1)}, u32[]{:S(2)}) copy-start(bf16[1,512,1024]{2,1,0:T(8,128)(2,1)} %param.7) | copy-start | bytes 3145732
  44.7 6.9 %copy-start.3 = (bf16[1,512,1024]{2,1,0:T(8,128)(2,1)S(1)}, bf16[1,512,1024]{2,1,0:T(8,128)(2,1)}, u32[]{:S(2)}) copy-start(bf16[1,512,1024]{2,1,0:T(8,128)(2,1)} %param.13) | copy-start | bytes 3145732
  44.7 15.9 %collective-permute-start.10 = (bf16[6,64,896]{2,1,0:T(8,128)(2,1)S(1)}, bf16[6,64,896]{2,1,0:T(8,128)(2,1)S(1)}, u32[]{:S(2)}, u32[]{:S(2)}) collective-permute-start(bf16[6,64,896]{2,1,0:T(8,128)(2,1)S(1)} %unpack_rows.3.rows_ref.refs_0_), channel_id=1, source_target_pairs={{0,1},{1,0},{2,3},{3,2},{4,5},{5,4},{6,7},{7,6},{8,9},{9,8},{10,11... | collective-permute-start | bytes 2064392 | tf_op jit(solution)/shard_map/ppermute | solution.py:46
  46.2 20.4 %collective-permute-start.13 = (bf16[2,2,64,896]{3,2,1,0:T(8,128)(2,1)S(1)}, bf16[2,2,64,896]{3,2,1,0:T(8,128)(2,1)S(1)}, u32[]{:S(2)}, u32[]{:S(2)}) collective-permute-start(bf16[2,2,64,896]{3,2,1,0:T(8,128)(2,1)S(1)} %get-tuple-element.143), channel_id=1, source_target_pairs={{0,12},{4,8},{8,4},{12,0},{1,13},{5,9},{9,5},{13,1},{2,14},{6,10},... | collective-permute-start | bytes 1376264 | tf_op jit(solution)/shard_map/ppermute | solution.py:46
  47.2 19.4 %collective-permute-start.12 = (bf16[2,2,64,896]{3,2,1,0:T(8,128)(2,1)S(1)}, bf16[2,2,64,896]{3,2,1,0:T(8,128)(2,1)S(1)}, u32[]{:S(2)}, u32[]{:S(2)}) collective-permute-start(bf16[2,2,64,896]{3,2,1,0:T(8,128)(2,1)S(1)} %get-tuple-element.142), channel_id=1, source_target_pairs={{0,8},{4,12},{8,0},{12,4},{1,9},{5,13},{9,1},{13,5},{2,10},{6,14},... | collective-permute-start | bytes 1376264 | tf_op jit(solution)/shard_map/ppermute | solution.py:46
  48.5 18.1 %collective-permute-start.11 = (bf16[2,2,64,896]{3,2,1,0:T(8,128)(2,1)S(1)}, bf16[2,2,64,896]{3,2,1,0:T(8,128)(2,1)S(1)}, u32[]{:S(2)}, u32[]{:S(2)}) collective-permute-start(bf16[2,2,64,896]{3,2,1,0:T(8,128)(2,1)S(1)} %get-tuple-element.141), channel_id=1, source_target_pairs={{0,4},{4,0},{8,12},{12,8},{1,5},{5,1},{9,13},{13,9},{2,6},{6,2},{1... | collective-permute-start | bytes 1376264 | tf_op jit(solution)/shard_map/ppermute | solution.py:46
  74.2 2.5 %collective-permute-start.14 = (bf16[448,768]{1,0:T(8,128)(2,1)S(1)}, bf16[448,768]{1,0:T(8,128)(2,1)S(1)}, u32[]{:S(2)}, u32[]{:S(2)}) collective-permute-start(bf16[448,768]{1,0:T(8,128)(2,1)S(1)} %get-tuple-element.164), channel_id=1, source_target_pairs={{0,16},{16,0},{1,17},{17,1},{2,18},{18,2},{3,19},{19,3},{4,20},{20... | collective-permute-start | bytes 2064392 | tf_op jit(solution)/shard_map/ppermute | solution.py:46
  74.3 3.1 %collective-permute-start.15 = (bf16[448,768]{1,0:T(8,128)(2,1)S(1)}, bf16[448,768]{1,0:T(8,128)(2,1)S(1)}, u32[]{:S(2)}, u32[]{:S(2)}) collective-permute-start(bf16[448,768]{1,0:T(8,128)(2,1)S(1)} %get-tuple-element.165), channel_id=1, source_target_pairs={{0,16},{16,0},{1,17},{17,1},{2,18},{18,2},{3,19},{19,3},{4,20},{20... | collective-permute-start | bytes 2064392 | tf_op jit(solution)/shard_map/ppermute | solution.py:46
  77.8 11.0 %collective-permute-start.16 = (bf16[2,112,768]{2,1,0:T(8,128)(2,1)S(1)}, bf16[2,112,768]{2,1,0:T(8,128)(2,1)S(1)}, u32[]{:S(2)}, u32[]{:S(2)}) collective-permute-start(bf16[2,112,768]{2,1,0:T(8,128)(2,1)S(1)} %get-tuple-element.170), channel_id=1, source_target_pairs={{0,4},{4,0},{8,12},{12,8},{1,5},{5,1},{9,13},{13,9},{2,6},{6,2},{1... | collective-permute-start | bytes 1032200 | tf_op jit(solution)/shard_map/ppermute | solution.py:46
  78.5 10.2 %collective-permute-start.17 = (bf16[2,112,768]{2,1,0:T(8,128)(2,1)S(1)}, bf16[2,112,768]{2,1,0:T(8,128)(2,1)S(1)}, u32[]{:S(2)}, u32[]{:S(2)}) collective-permute-start(bf16[2,112,768]{2,1,0:T(8,128)(2,1)S(1)} %get-tuple-element.171), channel_id=1, source_target_pairs={{0,8},{4,12},{8,0},{12,4},{1,9},{5,13},{9,1},{13,5},{2,10},{6,14},... | collective-permute-start | bytes 1032200 | tf_op jit(solution)/shard_map/ppermute | solution.py:46
  82.1 1.6 %collective-permute-start.18 = (bf16[448,256]{1,0:T(8,128)(2,1)S(1)}, bf16[448,256]{1,0:T(8,128)(2,1)S(1)}, u32[]{:S(2)}, u32[]{:S(2)}) collective-permute-start(bf16[448,256]{1,0:T(8,128)(2,1)S(1)} %get-tuple-element.186), channel_id=1, source_target_pairs={{0,16},{16,0},{1,17},{17,1},{2,18},{18,2},{3,19},{19,3},{4,20},{20... | collective-permute-start | bytes 688136 | tf_op jit(solution)/shard_map/ppermute | solution.py:46
  82.2 1.8 %collective-permute-start.19 = (bf16[448,256]{1,0:T(8,128)(2,1)S(1)}, bf16[448,256]{1,0:T(8,128)(2,1)S(1)}, u32[]{:S(2)}, u32[]{:S(2)}) collective-permute-start(bf16[448,256]{1,0:T(8,128)(2,1)S(1)} %get-tuple-element.187), channel_id=1, source_target_pairs={{0,16},{16,0},{1,17},{17,1},{2,18},{18,2},{3,19},{19,3},{4,20},{20... | collective-permute-start | bytes 688136 | tf_op jit(solution)/shard_map/ppermute | solution.py:46
  84.1 8.4 %collective-permute-start.20 = (bf16[2,112,256]{2,1,0:T(8,128)(2,1)S(1)}, bf16[2,112,256]{2,1,0:T(8,128)(2,1)S(1)}, u32[]{:S(2)}, u32[]{:S(2)}) collective-permute-start(bf16[2,112,256]{2,1,0:T(8,128)(2,1)S(1)} %get-tuple-element.190), channel_id=1, source_target_pairs={{0,4},{4,0},{8,12},{12,8},{1,5},{5,1},{9,13},{13,9},{2,6},{6,2},{1... | collective-permute-start | bytes 344072 | tf_op jit(solution)/shard_map/ppermute | solution.py:46
  85.6 6.9 %collective-permute-start.21 = (bf16[2,112,256]{2,1,0:T(8,128)(2,1)S(1)}, bf16[2,112,256]{2,1,0:T(8,128)(2,1)S(1)}, u32[]{:S(2)}, u32[]{:S(2)}) collective-permute-start(bf16[2,112,256]{2,1,0:T(8,128)(2,1)S(1)} %get-tuple-element.191), channel_id=1, source_target_pairs={{0,8},{4,12},{8,0},{12,4},{1,9},{5,13},{9,1},{13,5},{2,10},{6,14},... | collective-permute-start | bytes 344072 | tf_op jit(solution)/shard_map/ppermute | solution.py:46
  88.9 8.3 %collective-permute-start.22 = (bf16[1,112,768]{2,1,0:T(8,128)(2,1)S(1)}, bf16[1,112,768]{2,1,0:T(8,128)(2,1)S(1)}, u32[]{:S(2)}, u32[]{:S(2)}) collective-permute-start(bf16[1,112,768]{2,1,0:T(8,128)(2,1)S(1)} %get-tuple-element.194), channel_id=1, source_target_pairs={{0,8},{4,12},{8,0},{12,4},{1,9},{5,13},{9,1},{13,5},{2,10},{6,14},... | collective-permute-start | bytes 516104 | tf_op jit(solution)/shard_map/ppermute | solution.py:46
  90.8 6.4 %collective-permute-start.23 = (bf16[1,112,768]{2,1,0:T(8,128)(2,1)S(1)}, bf16[1,112,768]{2,1,0:T(8,128)(2,1)S(1)}, u32[]{:S(2)}, u32[]{:S(2)}) collective-permute-start(bf16[1,112,768]{2,1,0:T(8,128)(2,1)S(1)} %get-tuple-element.195), channel_id=1, source_target_pairs={{0,4},{4,0},{8,12},{12,8},{1,5},{5,1},{9,13},{13,9},{2,6},{6,2},{1... | collective-permute-start | bytes 516104 | tf_op jit(solution)/shard_map/ppermute | solution.py:46
  92.5 4.2 %collective-permute-start.24 = (bf16[1,112,256]{2,1,0:T(8,128)(2,1)S(1)}, bf16[1,112,256]{2,1,0:T(8,128)(2,1)S(1)}, u32[]{:S(2)}, u32[]{:S(2)}) collective-permute-start(bf16[1,112,256]{2,1,0:T(8,128)(2,1)S(1)} %get-tuple-element.196), channel_id=1, source_target_pairs={{0,8},{4,12},{8,0},{12,4},{1,9},{5,13},{9,1},{13,5},{2,10},{6,14},... | collective-permute-start | bytes 172040 | tf_op jit(solution)/shard_map/ppermute | solution.py:46
  93.0 4.2 %collective-permute-start.25 = (bf16[1,112,256]{2,1,0:T(8,128)(2,1)S(1)}, bf16[1,112,256]{2,1,0:T(8,128)(2,1)S(1)}, u32[]{:S(2)}, u32[]{:S(2)}) collective-permute-start(bf16[1,112,256]{2,1,0:T(8,128)(2,1)S(1)} %get-tuple-element.197), channel_id=1, source_target_pairs={{0,4},{4,0},{8,12},{12,8},{1,5},{5,1},{9,13},{13,9},{2,6},{6,2},{1... | collective-permute-start | bytes 172040 | tf_op jit(solution)/shard_map/ppermute | solution.py:46

commit v8 on v7

--- a/solution.py
+++ b/solution.py
@@ -16,7 +16,7 @@
 ATTEND_MIB = 26
 WEIGH_MIB = 26
 PIECES = 2
-SIDES = (((False,), (True,)), ((False, True),))
+SIDES = ((((False,), (0,)), ((False,), (1,)), ((True,), (0, 1))), (((False, True), (0, 1)),))
 PROJECT_FIRST = True
 FIRST_PIECE = 6 / 8
 CHUNKS = ((3, True), (3, True), (2, False))
@@ -269,18 +269,18 @@
     )(own, *rows, *ready, wk, wv, queries, grad_out)
 
 
-def weigh_kernel(chunks, carried, sides, *refs):
+def weigh_kernel(chunks, streams, carried, sides, *refs):
     refs = list(refs)
     take = lambda n: [refs.pop(0) for _ in range(n)]
-    turned, grads = take(chunks), [take(chunks) for _ in range(2)]
-    before = take(2) if carried else []
+    turned, grads = take(chunks), [take(chunks) for _ in range(streams)]
+    before = take(streams) if carried else []
     enc = turned[0].shape[0]
     for side in sides:
         rows = slice(0, enc)
         if side is not None:
             half = lax.axis_index("dp") if side else 1 - lax.axis_index("dp")
             rows = pl.ds(pl.multiple_of(half * (enc // 2), enc // 2), enc // 2)
-        for i in range(2):
+        for i in range(streams):
             total = before[i][rows, :] if carried else 0.0
             for turn, ref in zip(turned, grads[i]):
                 grad = ref[...]
@@ -289,21 +289,21 @@
             target[...] = total.astype(target.dtype)
 
 
-def weigh(turned, dks, dvs, before, sides):
-    enc, width = turned[0].shape[0], dks[0].shape[-1]
+def weigh(turned, grads, before, sides):
+    enc, width = turned[0].shape[0], grads[0][0].shape[-1]
     shapes = [
         jax.ShapeDtypeStruct((enc, width), F32) if side is None else jax.ShapeDtypeStruct((enc // 2, width), BF16)
         for side in sides
-        for _ in range(2)
+        for _ in grads
     ]
     return pl.pallas_call(
-        functools.partial(weigh_kernel, len(turned), bool(before), sides),
-        in_specs=[VMEM] * (3 * len(turned) + len(before)),
+        functools.partial(weigh_kernel, len(turned), len(grads), bool(before), sides),
+        in_specs=[VMEM] * ((1 + len(grads)) * len(turned) + len(before)),
         out_specs=[VMEM] * len(shapes),
         out_shape=shapes,
         compiler_params=params(WEIGH_MIB),
         name="weigh_grads",
-    )(*turned, *dks, *dvs, *before)
+    )(*turned, *sum(grads, []), *before)
 
 
 def fold_kernel(dims, count, *refs):
@@ -416,8 +416,9 @@
     rows, turned, found, sums, early = [None] * len(spans), [], [], [[]] * PIECES, None
     ready = [[] for _ in spans]
 
-    def weigh_piece(turned, found, piece, before, sides):
-        return list(weigh(turned, *([grads[2 * piece + i] for grads in found] for i in range(2)), before, sides))
+    def weigh_piece(turned, found, piece, before, sides, streams=(0, 1)):
+        before = [before[i] for i in streams] if before else []
+        return list(weigh(turned, [[grads[2 * piece + i] for grads in found] for i in streams], before, sides))
 
 
     def prepare(i):
@@ -462,8 +463,8 @@
             states[-1].fold()
             states[-1].send, turned[0] = lax.optimization_barrier((states[-1].send, turned[0]))
         parts = []
-        for sides in SIDES[piece]:
-            parts += weigh_piece(turned, found, piece, sums[piece], sides)
+        for sides, streams in SIDES[piece]:
+            parts += weigh_piece(turned, found, piece, sums[piece], sides, streams)
     states.append(Sums(parts[:2], parts[2:]))
     states[-1].fold()
     for step in range(states[0].bits):

time: 98.4 us -> 98 us (level)
    pallas_call x5 -> x6, Pallas kernels: 8.45 us -> 8.66 us  [weigh(): pl.pallas_call(functools.partial(weigh_kernel, len(turned), len(grads), b...]
  transfers between devices with their start and end apart: 26 -> 26, of which waited for: 11 -> 10; matrix products, arithmetic and copies ran while one was open for 2% -> 2% of each run, Pallas kernels for 27% -> 28%
where the time goes in v8:
time: 98 us; the launch traced here: 97.9 us
  Pallas kernels  36.8 us (38%)
  starting transfers between devices  30.2 us (31%)
  waiting for transfers between devices  25.3 us (26%)
  local copies, waits for them, and re-layouts  2.33 us (2%)
  other arithmetic  2.26 us (2%)
    ppermute x26, starting transfers between devices, swap(): return lax.ppermute(array, axis, [(i, i ^ bit) for i in range(size)])  30.2 us
    ppermute x26, waiting for transfers between devices, swap(): return lax.ppermute(array, axis, [(i, i ^ bit) for i in range(size)])  25.3 us
    pallas_call x3, Pallas kernels, attend(): pl.pallas_call(functools.partial(attend_kernel, *settings), in_specs=[SME...  17.7 us
    pallas_call x6, Pallas kernels, weigh(): pl.pallas_call(functools.partial(weigh_kernel, len(turned), len(grads), b...  8.66 us
    pallas_call x2, Pallas kernels, project(): pl.pallas_call(project_kernel, in_specs=[VMEM] * 3, out_specs=[VMEM] * 2,...  3.59 us
    pallas_call x2, Pallas kernels, pick(): pl.pallas_call(functools.partial(pick_kernel, spans), in_specs=[SMEM, VME...  2.44 us
    unnamed x10, local copies, waits for them, and re-layouts  2.06 us
  transfers between devices with their start and end apart: 26, of which 10 were waited for; matrix products, arithmetic and copies ran while one was open for 2% of the time, Pallas kernels for 28%

profile of v8, /device:TPU:0, one launch (start us, length us, event | category | flops | bytes accessed | tf_op | source)
XLA Modules:
  0.0 97.9 jit_solution(12610837825600988548)
XLA Ops:
  0.6 0.7 pad_add_fusion
  1.3 0.1 copy.13
  1.4 0.1 reshape.62.id_ref
  1.5 4.0 %collective-permute-start.2 = (s32[32]{0:T(128)S(1)}, s32[32]{0:T(128)S(1)}, u32[]{:S(2)}, u32[]{:S(2)}) collective-permute-start(s32[32]{0:T(128)S(1)} %reshape.62.id_ref), channel_id=1, source_target_pairs={{0,12},{4,8},{8,4},{12,0},{1,13},{5,9},{9,5},{13,1},{2,14},{6,10},... | collective-permute-start | bytes 392 | tf_op jit(solution)/shard_map/ppermute | solution.py:46
  5.5 0.5 collective-permute-start.1
  6.0 0.1 collective-permute-start
  6.1 0.1 stack_reshape.3
  6.2 2.0 %copy-done.4 = bf16[1,2048,896]{2,1,0:T(8,128)(2,1)S(1)} copy-done((bf16[1,2048,896]{2,1,0:T(8,128)(2,1)S(1)}, bf16[1,2048,896]{2,1,0:T(8,128)(2,1)}, u32[]{:S(2)}) %copy-start.4) | copy-done | bytes 3670040
  8.3 1.2 %normalize_rows.1 = bf16[2048,896]{1,0:T(8,128)(2,1)S(1)} custom-call(bf16[2048,896]{1,0:T(8,128)(2,1)S(1)} %bitcast.31), custom_call_target="tpu_custom_call" | custom-call | tf_op jit(solution)/shard_map/normalize_rows/pallas_call | solution.py:59
  9.5 0.0 collective-permute-done
  9.5 1.1 %pick_rows.2 = (bf16[3,64,896]{2,1,0:T(8,128)(2,1)S(1)}, bf16[3,64,896]{2,1,0:T(8,128)(2,1)S(1)}, bf16[3,64,896]{2,1,0:T(8,128)(2,1)S(1)}, bf16[3,64,896]{2,1,0:T(8,128)(2,1)S(1)}) custom-call(s32[4,32]{1,0:T(4,128)S(1)} %pad_add_fusion.1.id_ref, bf16[16,2,64,896]{3,2,1,0:T(8,128)(2,1)S(1)} %bitcast.23), custom_call_target="tpu_custom_call" | custom-call | tf_op jit(solution)/shard_map/pick_rows/pallas_call | solution.py:106
  10.6 1.9 %collective-permute-start.3 = (bf16[3,64,896]{2,1,0:T(8,128)(2,1)S(1)}, bf16[3,64,896]{2,1,0:T(8,128)(2,1)S(1)}, u32[]{:S(2)}, u32[]{:S(2)}) collective-permute-start(bf16[3,64,896]{2,1,0:T(8,128)(2,1)S(1)} %get-tuple-element.101), channel_id=1, source_target_pairs={{0,4},{4,0},{8,12},{12,8},{1,5},{5,1},{9,13},{13,9},{2,6},{6,2},{1... | collective-permute-start | bytes 1032200 | tf_op jit(solution)/shard_map/ppermute | solution.py:46
  12.5 1.6 %collective-permute-start.4 = (bf16[3,64,896]{2,1,0:T(8,128)(2,1)S(1)}, bf16[3,64,896]{2,1,0:T(8,128)(2,1)S(1)}, u32[]{:S(2)}, u32[]{:S(2)}) collective-permute-start(bf16[3,64,896]{2,1,0:T(8,128)(2,1)S(1)} %get-tuple-element.104), channel_id=1, source_target_pairs={{0,8},{4,12},{8,0},{12,4},{1,9},{5,13},{9,1},{13,5},{2,10},{6,14},... | collective-permute-start | bytes 1032200 | tf_op jit(solution)/shard_map/ppermute | solution.py:46
  14.1 0.1 collective-permute-start.5
  14.2 1.4 %pick_rows.3 = (bf16[3,64,896]{2,1,0:T(8,128)(2,1)S(1)}, bf16[3,64,896]{2,1,0:T(8,128)(2,1)S(1)}, bf16[3,64,896]{2,1,0:T(8,128)(2,1)S(1)}, bf16[3,64,896]{2,1,0:...) custom-call(s32[4,32]{1,0:T(4,128)S(1)} %pad_add_fusion.1.id_ref, ...), custom_call_target="tpu_custom_call" | custom-call | tf_op jit(solution)/shard_map/pick_rows/pallas_call | solution.py:106
  15.6 6.1 %collective-permute-done.3.refs_1_ = bf16[3,64,896]{2,1,0:T(8,128)(2,1)S(1)} collective-permute-done((bf16[3,64,896]{2,1,0:T(8,128)(2,1)S(1)}, bf16[3,64,896]{2,1,0:T(8,128)(2,1)S(1)}, u32[]{:S(2)}, u32[]{:S(2)}) %collective-permute-start.3) | collective-permute-done | bytes 344096 | tf_op jit(solution)/shard_map/ppermute | solution.py:46
  21.7 1.8 %collective-permute-start.6 = (bf16[3,64,896]{2,1,0:T(8,128)(2,1)S(1)}, bf16[3,64,896]{2,1,0:T(8,128)(2,1)S(1)}, u32[]{:S(2)}, u32[]{:S(2)}) collective-permute-start(bf16[3,64,896]{2,1,0:T(8,128)(2,1)S(1)} %get-tuple-element.112), channel_id=1, source_target_pairs={{0,4},{4,0},{8,12},{12,8},{1,5},{5,1},{9,13},{13,9},{2,6},{6,2},{1... | collective-permute-start | bytes 1032200 | tf_op jit(solution)/shard_map/ppermute | solution.py:46
  23.5 5.5 %collective-permute-done.4.refs_2_ = bf16[3,64,896]{2,1,0:T(8,128)(2,1)S(1)} collective-permute-done((bf16[3,64,896]{2,1,0:T(8,128)(2,1)S(1)}, bf16[3,64,896]{2,1,0:T(8,128)(2,1)S(1)}, u32[]{:S(2)}, u32[]{:S(2)}) %collective-permute-start.4) | collective-permute-done | bytes 344096 | tf_op jit(solution)/shard_map/ppermute | solution.py:46
  29.0 2.5 %collective-permute-start.7 = (bf16[3,64,896]{2,1,0:T(8,128)(2,1)S(1)}, bf16[3,64,896]{2,1,0:T(8,128)(2,1)S(1)}, u32[]{:S(2)}, u32[]{:S(2)}) collective-permute-start(bf16[3,64,896]{2,1,0:T(8,128)(2,1)S(1)} %get-tuple-element.115), channel_id=1, source_target_pairs={{0,8},{4,12},{8,0},{12,4},{1,9},{5,13},{9,1},{13,5},{2,10},{6,14},... | collective-permute-start | bytes 1032200 | tf_op jit(solution)/shard_map/ppermute | solution.py:46
  31.5 0.3 collective-permute-start.8
  31.8 0.7 unpack_rows.2.rows_ref.refs_0_
  32.6 1.6 %collective-permute-start.9 = (bf16[6,64,896]{2,1,0:T(8,128)(2,1)S(1)}, bf16[6,64,896]{2,1,0:T(8,128)(2,1)S(1)}, u32[]{:S(2)}, u32[]{:S(2)}) collective-permute-start(bf16[6,64,896]{2,1,0:T(8,128)(2,1)S(1)} %unpack_rows.2.rows_ref.refs_0_), channel_id=1, source_target_pairs={{0,1},{1,0},{2,3},{3,2},{4,5},{5,4},{6,7},{7,6},{8,9},{9,8},{10,11... | collective-permute-start | bytes 2064392 | tf_op jit(solution)/shard_map/ppermute | solution.py:46
  34.2 1.8 %project_rows.2 = (bf16[3,128,1024]{2,1,0:T(8,128)(2,1)S(1)}, bf16[3,128,1024]{2,1,0:T(8,128)(2,1)S(1)}) custom-call(bf16[6,64,896]{2,1,0:T(8,128)(2,1)S(1)} %unpack_rows.2.rows_ref.refs_0_, bf16[896,1024]{1,0:T(8,128)(2,1)S(1)} %copy-done, bf16[896,1024]{1,0:T(8,128)(2,1)S(1)} %copy-done.1), custom_call_target="tpu_custom_call" | custom-call | tf_op jit(solution)/shard_map/project_rows/pallas_call | solution.py:199
  36.0 0.5 collective-permute-done.6.refs_1_
  36.5 7.6 %collective-permute-done.7.refs_2_ = bf16[3,64,896]{2,1,0:T(8,128)(2,1)S(1)} collective-permute-done((bf16[3,64,896]{2,1,0:T(8,128)(2,1)S(1)}, bf16[3,64,896]{2,1,0:T(8,128)(2,1)S(1)}, u32[]{:S(2)}, u32[]{:S(2)}) %collective-permute-start.7) | collective-permute-done | bytes 344096 | tf_op jit(solution)/shard_map/ppermute | solution.py:46
  44.1 0.7 unpack_rows.3.rows_ref.refs_0_
  44.9 1.5 %collective-permute-start.10 = (bf16[6,64,896]{2,1,0:T(8,128)(2,1)S(1)}, bf16[6,64,896]{2,1,0:T(8,128)(2,1)S(1)}, u32[]{:S(2)}, u32[]{:S(2)}) collective-permute-start(bf16[6,64,896]{2,1,0:T(8,128)(2,1)S(1)} %unpack_rows.3.rows_ref.refs_0_), channel_id=1, source_target_pairs={{0,1},{1,0},{2,3},{3,2},{4,5},{5,4},{6,7},{7,6},{8,9},{9,8},{10,11... | collective-permute-start | bytes 2064392 | tf_op jit(solution)/shard_map/ppermute | solution.py:46
  46.4 0.8 collective-permute-start.13
  47.2 1.3 %collective-permute-start.12 = (bf16[2,2,64,896]{3,2,1,0:T(8,128)(2,1)S(1)}, bf16[2,2,64,896]{3,2,1,0:T(8,128)(2,1)S(1)}, u32[]{:S(2)}, u32[]{:S(2)}) collective-permute-start(bf16[2,2,64,896]{3,2,1,0:T(8,128)(2,1)S(1)} %get-tuple-element.140), channel_id=1, source_target_pairs={{0,8},{4,12},{8,0},{12,4},{1,9},{5,13},{9,1},{13,5},{2,10},{6,14},... | collective-permute-start | bytes 1376264 | tf_op jit(solution)/shard_map/ppermute | solution.py:46
  48.6 1.3 %collective-permute-start.11 = (bf16[2,2,64,896]{3,2,1,0:T(8,128)(2,1)S(1)}, bf16[2,2,64,896]{3,2,1,0:T(8,128)(2,1)S(1)}, u32[]{:S(2)}, u32[]{:S(2)}) collective-permute-start(bf16[2,2,64,896]{3,2,1,0:T(8,128)(2,1)S(1)} %get-tuple-element.139), channel_id=1, source_target_pairs={{0,4},{4,0},{8,12},{12,8},{1,5},{5,1},{9,13},{13,9},{2,6},{6,2},{1... | collective-permute-start | bytes 1376264 | tf_op jit(solution)/shard_map/ppermute | solution.py:46
  49.9 1.8 %project_rows.3 = (bf16[3,128,1024]{2,1,0:T(8,128)(2,1)S(1)}, bf16[3,128,1024]{2,1,0:T(8,128)(2,1)S(1)}) custom-call(bf16[6,64,896]{2,1,0:T(8,128)(2,1)S(1)} %unpack_rows.3.rows_ref.refs_0_, bf16[896,1024]{1,0:T(8,128)(2,1)S(1)} %copy-done, bf16[896,1024]{1,0:T(8,128)(2,1)S(1)} %copy-done.1), custom_call_target="tpu_custom_call" | custom-call | tf_op jit(solution)/shard_map/project_rows/pallas_call | solution.py:199
  51.7 6.1 %attend_blocks.3 = (bf16[3,64,1024]{2,1,0:T(8,128)(2,1)S(1)}, bf16[3,64,1024]{2,1,0:T(8,128)(2,1)S(1)}, bf16[896,768]{1,0:T(8,128)(2,1)S(1)}, bf16[3,256,768]{2,...) custom-call(s32[32]{0:T(128)S(1)} %reshape.62.id_ref, ...), custom_call_target="tpu_custom_call" | custom-call | tf_op jit(solution)/shard_map/attend_blocks/pallas_call | solution.py:256
  57.8 2.3 %weigh_grads.6 = (f32[896,768]{1,0:T(8,128)S(1)}, f32[896,768]{1,0:T(8,128)S(1)}) custom-call(bf16[896,768]{1,0:T(8,128)(2,1)S(1)} %get-tuple-element.175.refs_0_, bf16[3,256,768]{2,1,0:T(8,128)(2,1)S(1)} %get-tuple-element.130.refs_1_, bf16[3,256,768]{2,1,0:T(8,128)(2,1)S(1)} %get-tuple-element.131.refs_2_), custom_call_target="tpu_custom_call" | custom-call | tf_op jit(solution)/shard_map/weigh_grads/pallas_call | solution.py:299
  60.1 0.5 collective-permute-done.10.refs_1_
  60.6 6.0 %attend_blocks.4 = (bf16[3,64,1024]{2,1,0:T(8,128)(2,1)S(1)}, bf16[3,64,1024]{2,1,0:T(8,128)(2,1)S(1)}, bf16[896,768]{1,0:T(8,128)(2,1)S(1)}, bf16[3,256,768]{2,...) custom-call(s32[32]{0:T(128)S(1)} %reshape.62.id_ref, ...), custom_call_target="tpu_custom_call" | custom-call | tf_op jit(solution)/shard_map/attend_blocks/pallas_call | solution.py:256
  66.6 5.7 %attend_blocks.5 = (bf16[2,64,1024]{2,1,0:T(8,128)(2,1)S(1)}, bf16[2,64,1024]{2,1,0:T(8,128)(2,1)S(1)}, bf16[896,512]{1,0:T(8,128)(2,1)S(1)}, bf16[2,256,768]{2,...) custom-call(s32[32]{0:T(128)S(1)} %reshape.62.id_ref, ...), custom_call_target="tpu_custom_call" | custom-call | tf_op jit(solution)/shard_map/attend_blocks/pallas_call | solution.py:256
  72.3 1.1 %weigh_grads.8 = bf16[448,768]{1,0:T(8,128)(2,1)S(1)} custom-call(bf16[896,768]{1,0:T(8,128)(2,1)S(1)} %get-tuple-element.170.refs_0_, bf16[896,512]{1,0:T(8,128)(2,1)S(1)} %get-tuple-element.152.refs_1_, bf16[3,256,768]{2,1,0:T(8,128)(2,1)S(1)} %get-tuple-element.153.refs_2_, bf16[2,256,768]{2,1,0:T(8,128)(2,1)S(1)} %get-tuple-element.154.refs_3_, ...), custom_call_target="tpu_custom_call" | custom-call | tf_op jit(solution)/shard_map/weigh_grads/pallas_call | solution.py:299
  73.4 0.1 collective-permute-start.14
  73.5 1.1 %weigh_grads.9 = bf16[448,768]{1,0:T(8,128)(2,1)S(1)} custom-call(bf16[896,768]{1,0:T(8,128)(2,1)S(1)} %get-tuple-element.170.refs_0_, bf16[896,512]{1,0:T(8,128)(2,1)S(1)} %get-tuple-element.152.refs_1_, bf16[3,256,768]{2,1,0:T(8,128)(2,1)S(1)} %get-tuple-element.155.refs_4_.refs_2_, bf16[2,256,768]{2,1,0:T(8,128)(2,1)S(1)} %get-tuple-element.156.refs_5_.refs_3_, ...), custom_call_target="tpu_custom_call" | custom-call | tf_op jit(solution)/shard_map/weigh_grads/pallas_call | solution.py:299
  74.5 0.6 collective-permute-start.15
  75.1 2.0 %weigh_grads.7 = (bf16[448,768]{1,0:T(8,128)(2,1)S(1)}, bf16[448,768]{1,0:T(8,128)(2,1)S(1)}) custom-call(bf16[896,768]{1,0:T(8,128)(2,1)S(1)} %get-tuple-element.170.refs_0_, bf16[896,512]{1,0:T(8,128)(2,1)S(1)} %get-tuple-element.152.refs_1_, bf16[3,256,768]{2,1,0:T(8,128)(2,1)S(1)} %get-tuple-element.153.refs_2_, ...), custom_call_target="tpu_custom_call" | custom-call | tf_op jit(solution)/shard_map/weigh_grads/pallas_call | solution.py:299
  77.1 0.3 fold_grads.4
  77.4 0.7 collective-permute-start.16
  78.1 1.4 %collective-permute-start.17 = (bf16[2,112,768]{2,1,0:T(8,128)(2,1)S(1)}, bf16[2,112,768]{2,1,0:T(8,128)(2,1)S(1)}, u32[]{:S(2)}, u32[]{:S(2)}) collective-permute-start(bf16[2,112,768]{2,1,0:T(8,128)(2,1)S(1)} %get-tuple-element.167), channel_id=1, source_target_pairs={{0,8},{4,12},{8,0},{12,4},{1,9},{5,13},{9,1},{13,5},{2,10},{6,14},... | collective-permute-start | bytes 1032200 | tf_op jit(solution)/shard_map/ppermute | solution.py:46
  79.5 0.9 weigh_grads.10
  80.4 1.4 %weigh_grads.11 = (bf16[448,256]{1,0:T(8,128)(2,1)S(1)}, bf16[448,256]{1,0:T(8,128)(2,1)S(1)}, bf16[448,256]{1,0:T(8,128)(2,1)S(1)}, bf16[448,256]{1,0:T(8,128)(2,1)S(1)}) custom-call(bf16[896,768]{1,0:T(8,128)(2,1)S(1)} %get-tuple-element.170.refs_0_, bf16[896,512]{1,0:T(8,128)(2,1)S(1)} %get-tuple-element.152.refs_1_, ...), custom_call_target="tpu_custom_call" | custom-call | tf_op jit(solution)/shard_map/weigh_grads/pallas_call | solution.py:299
  81.8 0.1 collective-permute-start.18
  81.9 0.5 collective-permute-start.19
  82.4 1.0 collective-permute-done.18
  83.3 0.3 collective-permute-done.19
  83.7 0.1 fold_grads.6
  83.8 1.6 %collective-permute-start.20 = (bf16[2,112,256]{2,1,0:T(8,128)(2,1)S(1)}, bf16[2,112,256]{2,1,0:T(8,128)(2,1)S(1)}, u32[]{:S(2)}, u32[]{:S(2)}) collective-permute-start(bf16[2,112,256]{2,1,0:T(8,128)(2,1)S(1)} %get-tuple-element.186), channel_id=1, source_target_pairs={{0,4},{4,0},{8,12},{12,8},{1,5},{5,1},{9,13},{13,9},{2,6},{6,2},{1... | collective-permute-start | bytes 344072 | tf_op jit(solution)/shard_map/ppermute | solution.py:46
  85.4 0.5 collective-permute-start.21
  85.8 2.5 %collective-permute-done.16.refs_2_ = bf16[2,112,768]{2,1,0:T(8,128)(2,1)S(1)} collective-permute-done((bf16[2,112,768]{2,1,0:T(8,128)(2,1)S(1)}, bf16[2,112,768]{2,1,0:T(8,128)(2,1)S(1)}, u32[]{:S(2)}, u32[]{:S(2)}) %collective-permute-start.16) | collective-permute-done | bytes 344096 | tf_op jit(solution)/shard_map/ppermute | solution.py:46
  88.4 0.2 fold_grads.5
  88.6 2.0 %collective-permute-start.22 = (bf16[1,112,768]{2,1,0:T(8,128)(2,1)S(1)}, bf16[1,112,768]{2,1,0:T(8,128)(2,1)S(1)}, u32[]{:S(2)}, u32[]{:S(2)}) collective-permute-start(bf16[1,112,768]{2,1,0:T(8,128)(2,1)S(1)} %get-tuple-element.190), channel_id=1, source_target_pairs={{0,8},{4,12},{8,0},{12,4},{1,9},{5,13},{9,1},{13,5},{2,10},{6,14},... | collective-permute-start | bytes 516104 | tf_op jit(solution)/shard_map/ppermute | solution.py:46
  90.5 1.7 %collective-permute-start.23 = (bf16[1,112,768]{2,1,0:T(8,128)(2,1)S(1)}, bf16[1,112,768]{2,1,0:T(8,128)(2,1)S(1)}, u32[]{:S(2)}, u32[]{:S(2)}) collective-permute-start(bf16[1,112,768]{2,1,0:T(8,128)(2,1)S(1)} %get-tuple-element.191), channel_id=1, source_target_pairs={{0,4},{4,0},{8,12},{12,8},{1,5},{5,1},{9,13},{13,9},{2,6},{6,2},{1... | collective-permute-start | bytes 516104 | tf_op jit(solution)/shard_map/ppermute | solution.py:46
  92.2 0.1 fold_grads.7
  92.3 0.3 collective-permute-start.24
  92.7 1.4 %collective-permute-start.25 = (bf16[1,112,256]{2,1,0:T(8,128)(2,1)S(1)}, bf16[1,112,256]{2,1,0:T(8,128)(2,1)S(1)}, u32[]{:S(2)}, u32[]{:S(2)}) collective-permute-start(bf16[1,112,256]{2,1,0:T(8,128)(2,1)S(1)} %get-tuple-element.193), channel_id=1, source_target_pairs={{0,4},{4,0},{8,12},{12,8},{1,5},{5,1},{9,13},{13,9},{2,6},{6,2},{1... | collective-permute-start | bytes 172040 | tf_op jit(solution)/shard_map/ppermute | solution.py:46
  94.1 1.6 %pad_maximum_fusion = (bf16[8,64,1024]{2,1,0:T(8,128)(2,1)}, bf16[8,64,1024]{2,1,0:T(8,128)(2,1)}) fusion(bf16[2,64,1024]{2,1,0:T(8,128)(2,1)S(1)} %get-tuple-element.147, bf16[3,64,1024]{2,1,0:T(8,128)(2,1)S(1)} %get-tuple-element.142, bf16[3,64,1024]{2,1,0:T(8,128)(2,1)S(1)} %get-tuple-element.128, bf16[2,64,1024]{2,1,0:T(8,128)(2,1)S(1)} %get-tuple-element.150, ...), kind=kLoop, calls=%fused_computation | loop fusion | flops 2097152 | bytes 4194304 | tf_op jit(solution)/shard_map/concatenate | solution.py:476
  95.6 0.9 collective-permute-done.24.refs_6_
  96.6 0.3 collective-permute-done.25.refs_7_
  96.8 1.0 %join_grads.1 = (f32[112,1024]{1,0:T(8,128)}, f32[112,1024]{1,0:T(8,128)}) custom-call(bf16[1,112,768]{2,1,0:T(8,128)(2,1)S(1)} %get-tuple-element.168.refs_0_, bf16[1,112,768]{2,1,0:T(8,128)(2,1)S(1)} %get-tuple-element.169.refs_1_, bf16[1,112,256]{2,1,0:T(8,128)(2,1)S(1)} %get-tuple-element.188.refs_2_, ...), custom_call_target="tpu_custom_call" | custom-call | tf_op jit(solution)/shard_map/join_grads/pallas_call | solution.py:350
  (25 shorter events, 0.1 us)
Async XLA Ops:
  1.5 8.0 %collective-permute-start.2 = (s32[32]{0:T(128)S(1)}, s32[32]{0:T(128)S(1)}, u32[]{:S(2)}, u32[]{:S(2)}) collective-permute-start(s32[32]{0:T(128)S(1)} %reshape.62.id_ref), channel_id=1, source_target_pairs={{0,12},{4,8},{8,4},{12,0},{1,13},{5,9},{9,5},{13,1},{2,14},{6,10},... | collective-permute-start | bytes 392 | tf_op jit(solution)/shard_map/ppermute | solution.py:46
  5.5 4.0 %collective-permute-start.1 = (s32[32]{0:T(128)S(1)}, s32[32]{0:T(128)S(1)}, u32[]{:S(2)}, u32[]{:S(2)}) collective-permute-start(s32[32]{0:T(128)S(1)} %reshape.62.id_ref), channel_id=1, source_target_pairs={{0,8},{4,12},{8,0},{12,4},{1,9},{5,13},{9,1},{13,5},{2,10},{6,14},... | collective-permute-start | bytes 392 | tf_op jit(solution)/shard_map/ppermute | solution.py:46
  6.0 3.5 %collective-permute-start = (s32[32]{0:T(128)S(1)}, s32[32]{0:T(128)S(1)}, u32[]{:S(2)}, u32[]{:S(2)}) collective-permute-start(s32[32]{0:T(128)S(1)} %reshape.62.id_ref), channel_id=1, source_target_pairs={{0,4},{4,0},{8,12},{12,8},{1,5},{5,1},{9,13},{13,9},{2,6},{6,2},{1... | collective-permute-start | bytes 392 | tf_op jit(solution)/shard_map/ppermute | solution.py:46
  6.2 2.0 %copy-start.4 = (bf16[1,2048,896]{2,1,0:T(8,128)(2,1)S(1)}, bf16[1,2048,896]{2,1,0:T(8,128)(2,1)}, u32[]{:S(2)}) copy-start(bf16[1,2048,896]{2,1,0:T(8,128)(2,1)} %param.8) | copy-start | bytes 11010052
  10.6 11.1 %collective-permute-start.3 = (bf16[3,64,896]{2,1,0:T(8,128)(2,1)S(1)}, bf16[3,64,896]{2,1,0:T(8,128)(2,1)S(1)}, u32[]{:S(2)}, u32[]{:S(2)}) collective-permute-start(bf16[3,64,896]{2,1,0:T(8,128)(2,1)S(1)} %get-tuple-element.101), channel_id=1, source_target_pairs={{0,4},{4,0},{8,12},{12,8},{1,5},{5,1},{9,13},{13,9},{2,6},{6,2},{1... | collective-permute-start | bytes 1032200 | tf_op jit(solution)/shard_map/ppermute | solution.py:46
  12.5 16.5 %collective-permute-start.4 = (bf16[3,64,896]{2,1,0:T(8,128)(2,1)S(1)}, bf16[3,64,896]{2,1,0:T(8,128)(2,1)S(1)}, u32[]{:S(2)}, u32[]{:S(2)}) collective-permute-start(bf16[3,64,896]{2,1,0:T(8,128)(2,1)S(1)} %get-tuple-element.104), channel_id=1, source_target_pairs={{0,8},{4,12},{8,0},{12,4},{1,9},{5,13},{9,1},{13,5},{2,10},{6,14},... | collective-permute-start | bytes 1032200 | tf_op jit(solution)/shard_map/ppermute | solution.py:46
  14.1 17.4 %collective-permute-start.5 = (bf16[3,64,896]{2,1,0:T(8,128)(2,1)S(1)}, bf16[3,64,896]{2,1,0:T(8,128)(2,1)S(1)}, u32[]{:S(2)}, u32[]{:S(2)}) collective-permute-start(bf16[3,64,896]{2,1,0:T(8,128)(2,1)S(1)} %get-tuple-element.107), channel_id=1, source_target_pairs={{0,12},{4,8},{8,4},{12,0},{1,13},{5,9},{9,5},{13,1},{2,14},{6,10},... | collective-permute-start | bytes 1032200 | tf_op jit(solution)/shard_map/ppermute | solution.py:46
  14.2 20.0 %copy-start.1 = (bf16[896,1024]{1,0:T(8,128)(2,1)S(1)}, bf16[896,1024]{1,0:T(8,128)(2,1)}, u32[]{:S(2)}) copy-start(bf16[896,1024]{1,0:T(8,128)(2,1)} %refs_5_.5) | copy-start | bytes 5505028
  15.6 18.7 %copy-start = (bf16[896,1024]{1,0:T(8,128)(2,1)S(1)}, bf16[896,1024]{1,0:T(8,128)(2,1)}, u32[]{:S(2)}) copy-start(bf16[896,1024]{1,0:T(8,128)(2,1)} %refs_4_.5) | copy-start | bytes 5505028
  21.7 14.8 %collective-permute-start.6 = (bf16[3,64,896]{2,1,0:T(8,128)(2,1)S(1)}, bf16[3,64,896]{2,1,0:T(8,128)(2,1)S(1)}, u32[]{:S(2)}, u32[]{:S(2)}) collective-permute-start(bf16[3,64,896]{2,1,0:T(8,128)(2,1)S(1)} %get-tuple-element.112), channel_id=1, source_target_pairs={{0,4},{4,0},{8,12},{12,8},{1,5},{5,1},{9,13},{13,9},{2,6},{6,2},{1... | collective-permute-start | bytes 1032200 | tf_op jit(solution)/shard_map/ppermute | solution.py:46
  29.0 15.1 %collective-permute-start.7 = (bf16[3,64,896]{2,1,0:T(8,128)(2,1)S(1)}, bf16[3,64,896]{2,1,0:T(8,128)(2,1)S(1)}, u32[]{:S(2)}, u32[]{:S(2)}) collective-permute-start(bf16[3,64,896]{2,1,0:T(8,128)(2,1)S(1)} %get-tuple-element.115), channel_id=1, source_target_pairs={{0,8},{4,12},{8,0},{12,4},{1,9},{5,13},{9,1},{13,5},{2,10},{6,14},... | collective-permute-start | bytes 1032200 | tf_op jit(solution)/shard_map/ppermute | solution.py:46
  31.5 12.6 %collective-permute-start.8 = (bf16[3,64,896]{2,1,0:T(8,128)(2,1)S(1)}, bf16[3,64,896]{2,1,0:T(8,128)(2,1)S(1)}, u32[]{:S(2)}, u32[]{:S(2)}) collective-permute-start(bf16[3,64,896]{2,1,0:T(8,128)(2,1)S(1)} %get-tuple-element.118), channel_id=1, source_target_pairs={{0,12},{4,8},{8,4},{12,0},{1,13},{5,9},{9,5},{13,1},{2,14},{6,10},... | collective-permute-start | bytes 1032200 | tf_op jit(solution)/shard_map/ppermute | solution.py:46
  32.6 19.1 %collective-permute-start.9 = (bf16[6,64,896]{2,1,0:T(8,128)(2,1)S(1)}, bf16[6,64,896]{2,1,0:T(8,128)(2,1)S(1)}, u32[]{:S(2)}, u32[]{:S(2)}) collective-permute-start(bf16[6,64,896]{2,1,0:T(8,128)(2,1)S(1)} %unpack_rows.2.rows_ref.refs_0_), channel_id=1, source_target_pairs={{0,1},{1,0},{2,3},{3,2},{4,5},{5,4},{6,7},{7,6},{8,9},{9,8},{10,11... | collective-permute-start | bytes 2064392 | tf_op jit(solution)/shard_map/ppermute | solution.py:46
  44.8 6.9 %copy-start.2 = (bf16[1,512,1024]{2,1,0:T(8,128)(2,1)S(1)}, bf16[1,512,1024]{2,1,0:T(8,128)(2,1)}, u32[]{:S(2)}) copy-start(bf16[1,512,1024]{2,1,0:T(8,128)(2,1)} %param.7) | copy-start | bytes 3145732
  44.9 6.9 %copy-start.3 = (bf16[1,512,1024]{2,1,0:T(8,128)(2,1)S(1)}, bf16[1,512,1024]{2,1,0:T(8,128)(2,1)}, u32[]{:S(2)}) copy-start(bf16[1,512,1024]{2,1,0:T(8,128)(2,1)} %param.13) | copy-start | bytes 3145732
  44.9 15.7 %collective-permute-start.10 = (bf16[6,64,896]{2,1,0:T(8,128)(2,1)S(1)}, bf16[6,64,896]{2,1,0:T(8,128)(2,1)S(1)}, u32[]{:S(2)}, u32[]{:S(2)}) collective-permute-start(bf16[6,64,896]{2,1,0:T(8,128)(2,1)S(1)} %unpack_rows.3.rows_ref.refs_0_), channel_id=1, source_target_pairs={{0,1},{1,0},{2,3},{3,2},{4,5},{5,4},{6,7},{7,6},{8,9},{9,8},{10,11... | collective-permute-start | bytes 2064392 | tf_op jit(solution)/shard_map/ppermute | solution.py:46
  46.4 20.2 %collective-permute-start.13 = (bf16[2,2,64,896]{3,2,1,0:T(8,128)(2,1)S(1)}, bf16[2,2,64,896]{3,2,1,0:T(8,128)(2,1)S(1)}, u32[]{:S(2)}, u32[]{:S(2)}) collective-permute-start(bf16[2,2,64,896]{3,2,1,0:T(8,128)(2,1)S(1)} %get-tuple-element.141), channel_id=1, source_target_pairs={{0,12},{4,8},{8,4},{12,0},{1,13},{5,9},{9,5},{13,1},{2,14},{6,10},... | collective-permute-start | bytes 1376264 | tf_op jit(solution)/shard_map/ppermute | solution.py:46
  47.2 19.4 %collective-permute-start.12 = (bf16[2,2,64,896]{3,2,1,0:T(8,128)(2,1)S(1)}, bf16[2,2,64,896]{3,2,1,0:T(8,128)(2,1)S(1)}, u32[]{:S(2)}, u32[]{:S(2)}) collective-permute-start(bf16[2,2,64,896]{3,2,1,0:T(8,128)(2,1)S(1)} %get-tuple-element.140), channel_id=1, source_target_pairs={{0,8},{4,12},{8,0},{12,4},{1,9},{5,13},{9,1},{13,5},{2,10},{6,14},... | collective-permute-start | bytes 1376264 | tf_op jit(solution)/shard_map/ppermute | solution.py:46
  48.6 18.1 %collective-permute-start.11 = (bf16[2,2,64,896]{3,2,1,0:T(8,128)(2,1)S(1)}, bf16[2,2,64,896]{3,2,1,0:T(8,128)(2,1)S(1)}, u32[]{:S(2)}, u32[]{:S(2)}) collective-permute-start(bf16[2,2,64,896]{3,2,1,0:T(8,128)(2,1)S(1)} %get-tuple-element.139), channel_id=1, source_target_pairs={{0,4},{4,0},{8,12},{12,8},{1,5},{5,1},{9,13},{13,9},{2,6},{6,2},{1... | collective-permute-start | bytes 1376264 | tf_op jit(solution)/shard_map/ppermute | solution.py:46
  73.4 3.7 %collective-permute-start.14 = (bf16[448,768]{1,0:T(8,128)(2,1)S(1)}, bf16[448,768]{1,0:T(8,128)(2,1)S(1)}, u32[]{:S(2)}, u32[]{:S(2)}) collective-permute-start(bf16[448,768]{1,0:T(8,128)(2,1)S(1)} %weigh_grads.8), channel_id=1, source_target_pairs={{0,16},{16,0},{1,17},{17,1},{2,18},{18,2},{3,19},{19,3},{4,20},{20... | collective-permute-start | bytes 2064392 | tf_op jit(solution)/shard_map/ppermute | solution.py:46
  74.5 2.5 %collective-permute-start.15 = (bf16[448,768]{1,0:T(8,128)(2,1)S(1)}, bf16[448,768]{1,0:T(8,128)(2,1)S(1)}, u32[]{:S(2)}, u32[]{:S(2)}) collective-permute-start(bf16[448,768]{1,0:T(8,128)(2,1)S(1)} %weigh_grads.9), channel_id=1, source_target_pairs={{0,16},{16,0},{1,17},{17,1},{2,18},{18,2},{3,19},{19,3},{4,20},{20... | collective-permute-start | bytes 2064392 | tf_op jit(solution)/shard_map/ppermute | solution.py:46
  77.4 11.0 %collective-permute-start.16 = (bf16[2,112,768]{2,1,0:T(8,128)(2,1)S(1)}, bf16[2,112,768]{2,1,0:T(8,128)(2,1)S(1)}, u32[]{:S(2)}, u32[]{:S(2)}) collective-permute-start(bf16[2,112,768]{2,1,0:T(8,128)(2,1)S(1)} %get-tuple-element.166), channel_id=1, source_target_pairs={{0,4},{4,0},{8,12},{12,8},{1,5},{5,1},{9,13},{13,9},{2,6},{6,2},{1... | collective-permute-start | bytes 1032200 | tf_op jit(solution)/shard_map/ppermute | solution.py:46
  78.1 10.3 %collective-permute-start.17 = (bf16[2,112,768]{2,1,0:T(8,128)(2,1)S(1)}, bf16[2,112,768]{2,1,0:T(8,128)(2,1)S(1)}, u32[]{:S(2)}, u32[]{:S(2)}) collective-permute-start(bf16[2,112,768]{2,1,0:T(8,128)(2,1)S(1)} %get-tuple-element.167), channel_id=1, source_target_pairs={{0,8},{4,12},{8,0},{12,4},{1,9},{5,13},{9,1},{13,5},{2,10},{6,14},... | collective-permute-start | bytes 1032200 | tf_op jit(solution)/shard_map/ppermute | solution.py:46
  81.8 1.6 %collective-permute-start.18 = (bf16[448,256]{1,0:T(8,128)(2,1)S(1)}, bf16[448,256]{1,0:T(8,128)(2,1)S(1)}, u32[]{:S(2)}, u32[]{:S(2)}) collective-permute-start(bf16[448,256]{1,0:T(8,128)(2,1)S(1)} %get-tuple-element.182), channel_id=1, source_target_pairs={{0,16},{16,0},{1,17},{17,1},{2,18},{18,2},{3,19},{19,3},{4,20},{20... | collective-permute-start | bytes 688136 | tf_op jit(solution)/shard_map/ppermute | solution.py:46
  81.9 1.8 %collective-permute-start.19 = (bf16[448,256]{1,0:T(8,128)(2,1)S(1)}, bf16[448,256]{1,0:T(8,128)(2,1)S(1)}, u32[]{:S(2)}, u32[]{:S(2)}) collective-permute-start(bf16[448,256]{1,0:T(8,128)(2,1)S(1)} %get-tuple-element.183), channel_id=1, source_target_pairs={{0,16},{16,0},{1,17},{17,1},{2,18},{18,2},{3,19},{19,3},{4,20},{20... | collective-permute-start | bytes 688136 | tf_op jit(solution)/shard_map/ppermute | solution.py:46
  83.8 8.5 %collective-permute-start.20 = (bf16[2,112,256]{2,1,0:T(8,128)(2,1)S(1)}, bf16[2,112,256]{2,1,0:T(8,128)(2,1)S(1)}, u32[]{:S(2)}, u32[]{:S(2)}) collective-permute-start(bf16[2,112,256]{2,1,0:T(8,128)(2,1)S(1)} %get-tuple-element.186), channel_id=1, source_target_pairs={{0,4},{4,0},{8,12},{12,8},{1,5},{5,1},{9,13},{13,9},{2,6},{6,2},{1... | collective-permute-start | bytes 344072 | tf_op jit(solution)/shard_map/ppermute | solution.py:46
  85.4 6.9 %collective-permute-start.21 = (bf16[2,112,256]{2,1,0:T(8,128)(2,1)S(1)}, bf16[2,112,256]{2,1,0:T(8,128)(2,1)S(1)}, u32[]{:S(2)}, u32[]{:S(2)}) collective-permute-start(bf16[2,112,256]{2,1,0:T(8,128)(2,1)S(1)} %get-tuple-element.187), channel_id=1, source_target_pairs={{0,8},{4,12},{8,0},{12,4},{1,9},{5,13},{9,1},{13,5},{2,10},{6,14},... | collective-permute-start | bytes 344072 | tf_op jit(solution)/shard_map/ppermute | solution.py:46
  88.6 8.3 %collective-permute-start.22 = (bf16[1,112,768]{2,1,0:T(8,128)(2,1)S(1)}, bf16[1,112,768]{2,1,0:T(8,128)(2,1)S(1)}, u32[]{:S(2)}, u32[]{:S(2)}) collective-permute-start(bf16[1,112,768]{2,1,0:T(8,128)(2,1)S(1)} %get-tuple-element.190), channel_id=1, source_target_pairs={{0,8},{4,12},{8,0},{12,4},{1,9},{5,13},{9,1},{13,5},{2,10},{6,14},... | collective-permute-start | bytes 516104 | tf_op jit(solution)/shard_map/ppermute | solution.py:46
  90.5 6.3 %collective-permute-start.23 = (bf16[1,112,768]{2,1,0:T(8,128)(2,1)S(1)}, bf16[1,112,768]{2,1,0:T(8,128)(2,1)S(1)}, u32[]{:S(2)}, u32[]{:S(2)}) collective-permute-start(bf16[1,112,768]{2,1,0:T(8,128)(2,1)S(1)} %get-tuple-element.191), channel_id=1, source_target_pairs={{0,4},{4,0},{8,12},{12,8},{1,5},{5,1},{9,13},{13,9},{2,6},{6,2},{1... | collective-permute-start | bytes 516104 | tf_op jit(solution)/shard_map/ppermute | solution.py:46
  92.3 4.2 %collective-permute-start.24 = (bf16[1,112,256]{2,1,0:T(8,128)(2,1)S(1)}, bf16[1,112,256]{2,1,0:T(8,128)(2,1)S(1)}, u32[]{:S(2)}, u32[]{:S(2)}) collective-permute-start(bf16[1,112,256]{2,1,0:T(8,128)(2,1)S(1)} %get-tuple-element.192), channel_id=1, source_target_pairs={{0,8},{4,12},{8,0},{12,4},{1,9},{5,13},{9,1},{13,5},{2,10},{6,14},... | collective-permute-start | bytes 172040 | tf_op jit(solution)/shard_map/ppermute | solution.py:46
  92.7 4.2 %collective-permute-start.25 = (bf16[1,112,256]{2,1,0:T(8,128)(2,1)S(1)}, bf16[1,112,256]{2,1,0:T(8,128)(2,1)S(1)}, u32[]{:S(2)}, u32[]{:S(2)}) collective-permute-start(bf16[1,112,256]{2,1,0:T(8,128)(2,1)S(1)} %get-tuple-element.193), channel_id=1, source_target_pairs={{0,4},{4,0},{8,12},{12,8},{1,5},{5,1},{9,13},{13,9},{2,6},{6,2},{1... | collective-permute-start | bytes 172040 | tf_op jit(solution)/shard_map/ppermute | solution.py:46

commit v9 on v8

--- a/solution.py
+++ b/solution.py
@@ -16,7 +16,7 @@
 ATTEND_MIB = 26
 WEIGH_MIB = 26
 PIECES = 2
-SIDES = ((((False,), (0,)), ((False,), (1,)), ((True,), (0, 1))), (((False, True), (0, 1)),))
+SIDES = ((((False,), (0,)), ((False,), (1,)), ((True,), (0,)), ((True,), (1,))), (((False, True), (0, 1)),))
 PROJECT_FIRST = True
 FIRST_PIECE = 6 / 8
 CHUNKS = ((3, True), (3, True), (2, False))
@@ -373,8 +373,8 @@
         dims = tuple((bit, left.index(bit)) for bit, left in zip(self.bit, self.left))
         for bit, left in zip(self.bit, self.left):
             left.remove(bit)
-        parts = fold(self.held, self.arrived, dims)
-        self.send, self.held = list(parts[:2]), list(parts[2:])
+        parts = [fold([held], [arrived], (dim,)) for held, arrived, dim in zip(self.held, self.arrived, dims)]
+        self.send, self.held = ([part[i] for part in parts] for i in range(2))
         self.steps += 1
 
     def exchange(self):

time: 98 us -> 97.9 us (level)
    pallas_call x6 -> x7, Pallas kernels: 8.66 us -> 8.81 us  [weigh(): pl.pallas_call(functools.partial(weigh_kernel, len(turned), len(grads), b...]
  transfers between devices with their start and end apart: 26 -> 26, of which waited for: 10 -> 9; matrix products, arithmetic and copies ran while one was open for 2% -> 2% of each run, Pallas kernels for 28% -> 29%
where the time goes in v9:
time: 97.9 us; the launch traced here: 97.7 us
  Pallas kernels  36.9 us (38%)
  starting transfers between devices  29.6 us (30%)
  waiting for transfers between devices  25.7 us (26%)
  local copies, waits for them, and re-layouts  2.33 us (2%)
  other arithmetic  2.27 us (2%)
    ppermute x26, starting transfers between devices, swap(): return lax.ppermute(array, axis, [(i, i ^ bit) for i in range(size)])  29.6 us
    ppermute x26, waiting for transfers between devices, swap(): return lax.ppermute(array, axis, [(i, i ^ bit) for i in range(size)])  25.7 us
    pallas_call x3, Pallas kernels, attend(): pl.pallas_call(functools.partial(attend_kernel, *settings), in_specs=[SME...  17.7 us
    pallas_call x7, Pallas kernels, weigh(): pl.pallas_call(functools.partial(weigh_kernel, len(turned), len(grads), b...  8.81 us
    pallas_call x2, Pallas kernels, project(): pl.pallas_call(project_kernel, in_specs=[VMEM] * 3, out_specs=[VMEM] * 2,...  3.59 us
    pallas_call x2, Pallas kernels, pick(): pl.pallas_call(functools.partial(pick_kernel, spans), in_specs=[SMEM, VME...  2.37 us
    unnamed x10, local copies, waits for them, and re-layouts  2.06 us
  transfers between devices with their start and end apart: 26, of which 9 were waited for; matrix products, arithmetic and copies ran while one was open for 2% of the time, Pallas kernels for 29%

profile of v9, /device:TPU:0, one launch (start us, length us, event | category | flops | bytes accessed | tf_op | source)
XLA Modules:
  0.0 97.7 jit_solution(7837528347296623065)
XLA Ops:
  0.6 0.7 pad_add_fusion
  1.3 0.1 copy.13
  1.4 0.1 reshape.62.id_ref
  1.5 4.0 %collective-permute-start.2 = (s32[32]{0:T(128)S(1)}, s32[32]{0:T(128)S(1)}, u32[]{:S(2)}, u32[]{:S(2)}) collective-permute-start(s32[32]{0:T(128)S(1)} %reshape.62.id_ref), channel_id=1, source_target_pairs={{0,12},{4,8},{8,4},{12,0},{1,13},{5,9},{9,5},{13,1},{2,14},{6,10},... | collective-permute-start | bytes 392 | tf_op jit(solution)/shard_map/ppermute | solution.py:46
  5.5 0.5 collective-permute-start.1
  6.0 0.1 collective-permute-start
  6.1 0.1 stack_reshape.3
  6.2 2.0 %copy-done.4 = bf16[1,2048,896]{2,1,0:T(8,128)(2,1)S(1)} copy-done((bf16[1,2048,896]{2,1,0:T(8,128)(2,1)S(1)}, bf16[1,2048,896]{2,1,0:T(8,128)(2,1)}, u32[]{:S(2)}) %copy-start.4) | copy-done | bytes 3670040
  8.3 1.2 %normalize_rows.1 = bf16[2048,896]{1,0:T(8,128)(2,1)S(1)} custom-call(bf16[2048,896]{1,0:T(8,128)(2,1)S(1)} %bitcast.31), custom_call_target="tpu_custom_call" | custom-call | tf_op jit(solution)/shard_map/normalize_rows/pallas_call | solution.py:59
  9.5 1.0 %pick_rows.2 = (bf16[3,64,896]{2,1,0:T(8,128)(2,1)S(1)}, bf16[3,64,896]{2,1,0:T(8,128)(2,1)S(1)}, bf16[3,64,896]{2,1,0:T(8,128)(2,1)S(1)}, bf16[3,64,896]{2,1,0:T(8,128)(2,1)S(1)}) custom-call(s32[4,32]{1,0:T(4,128)S(1)} %pad_add_fusion.1.id_ref, bf16[16,2,64,896]{3,2,1,0:T(8,128)(2,1)S(1)} %bitcast.23), custom_call_target="tpu_custom_call" | custom-call | tf_op jit(solution)/shard_map/pick_rows/pallas_call | solution.py:106
  10.6 2.0 %collective-permute-start.3 = (bf16[3,64,896]{2,1,0:T(8,128)(2,1)S(1)}, bf16[3,64,896]{2,1,0:T(8,128)(2,1)S(1)}, u32[]{:S(2)}, u32[]{:S(2)}) collective-permute-start(bf16[3,64,896]{2,1,0:T(8,128)(2,1)S(1)} %get-tuple-element.99), channel_id=1, source_target_pairs={{0,4},{4,0},{8,12},{12,8},{1,5},{5,1},{9,13},{13,9},{2,6},{6,2},{1... | collective-permute-start | bytes 1032200 | tf_op jit(solution)/shard_map/ppermute | solution.py:46
  12.6 1.4 %collective-permute-start.4 = (bf16[3,64,896]{2,1,0:T(8,128)(2,1)S(1)}, bf16[3,64,896]{2,1,0:T(8,128)(2,1)S(1)}, u32[]{:S(2)}, u32[]{:S(2)}) collective-permute-start(bf16[3,64,896]{2,1,0:T(8,128)(2,1)S(1)} %get-tuple-element.102), channel_id=1, source_target_pairs={{0,8},{4,12},{8,0},{12,4},{1,9},{5,13},{9,1},{13,5},{2,10},{6,14},... | collective-permute-start | bytes 1032200 | tf_op jit(solution)/shard_map/ppermute | solution.py:46
  14.0 0.1 collective-permute-start.5
  14.1 1.3 %pick_rows.3 = (bf16[3,64,896]{2,1,0:T(8,128)(2,1)S(1)}, bf16[3,64,896]{2,1,0:T(8,128)(2,1)S(1)}, bf16[3,64,896]{2,1,0:T(8,128)(2,1)S(1)}, bf16[3,64,896]{2,1,0:...) custom-call(s32[4,32]{1,0:T(4,128)S(1)} %pad_add_fusion.1.id_ref, ...), custom_call_target="tpu_custom_call" | custom-call | tf_op jit(solution)/shard_map/pick_rows/pallas_call | solution.py:106
  15.5 6.1 %collective-permute-done.3.refs_1_ = bf16[3,64,896]{2,1,0:T(8,128)(2,1)S(1)} collective-permute-done((bf16[3,64,896]{2,1,0:T(8,128)(2,1)S(1)}, bf16[3,64,896]{2,1,0:T(8,128)(2,1)S(1)}, u32[]{:S(2)}, u32[]{:S(2)}) %collective-permute-start.3) | collective-permute-done | bytes 344096 | tf_op jit(solution)/shard_map/ppermute | solution.py:46
  21.6 2.0 %collective-permute-start.6 = (bf16[3,64,896]{2,1,0:T(8,128)(2,1)S(1)}, bf16[3,64,896]{2,1,0:T(8,128)(2,1)S(1)}, u32[]{:S(2)}, u32[]{:S(2)}) collective-permute-start(bf16[3,64,896]{2,1,0:T(8,128)(2,1)S(1)} %get-tuple-element.110), channel_id=1, source_target_pairs={{0,4},{4,0},{8,12},{12,8},{1,5},{5,1},{9,13},{13,9},{2,6},{6,2},{1... | collective-permute-start | bytes 1032200 | tf_op jit(solution)/shard_map/ppermute | solution.py:46
  23.6 5.3 %collective-permute-done.4.refs_2_ = bf16[3,64,896]{2,1,0:T(8,128)(2,1)S(1)} collective-permute-done((bf16[3,64,896]{2,1,0:T(8,128)(2,1)S(1)}, bf16[3,64,896]{2,1,0:T(8,128)(2,1)S(1)}, u32[]{:S(2)}, u32[]{:S(2)}) %collective-permute-start.4) | collective-permute-done | bytes 344096 | tf_op jit(solution)/shard_map/ppermute | solution.py:46
  28.9 2.5 %collective-permute-start.7 = (bf16[3,64,896]{2,1,0:T(8,128)(2,1)S(1)}, bf16[3,64,896]{2,1,0:T(8,128)(2,1)S(1)}, u32[]{:S(2)}, u32[]{:S(2)}) collective-permute-start(bf16[3,64,896]{2,1,0:T(8,128)(2,1)S(1)} %get-tuple-element.113), channel_id=1, source_target_pairs={{0,8},{4,12},{8,0},{12,4},{1,9},{5,13},{9,1},{13,5},{2,10},{6,14},... | collective-permute-start | bytes 1032200 | tf_op jit(solution)/shard_map/ppermute | solution.py:46
  31.4 0.6 collective-permute-start.8
  31.9 0.7 unpack_rows.2.rows_ref.refs_0_
  32.7 1.6 %collective-permute-start.9 = (bf16[6,64,896]{2,1,0:T(8,128)(2,1)S(1)}, bf16[6,64,896]{2,1,0:T(8,128)(2,1)S(1)}, u32[]{:S(2)}, u32[]{:S(2)}) collective-permute-start(bf16[6,64,896]{2,1,0:T(8,128)(2,1)S(1)} %unpack_rows.2.rows_ref.refs_0_), channel_id=1, source_target_pairs={{0,1},{1,0},{2,3},{3,2},{4,5},{5,4},{6,7},{7,6},{8,9},{9,8},{10,11... | collective-permute-start | bytes 2064392 | tf_op jit(solution)/shard_map/ppermute | solution.py:46
  34.3 1.8 %project_rows.2 = (bf16[3,128,1024]{2,1,0:T(8,128)(2,1)S(1)}, bf16[3,128,1024]{2,1,0:T(8,128)(2,1)S(1)}) custom-call(bf16[6,64,896]{2,1,0:T(8,128)(2,1)S(1)} %unpack_rows.2.rows_ref.refs_0_, bf16[896,1024]{1,0:T(8,128)(2,1)S(1)} %copy-done, bf16[896,1024]{1,0:T(8,128)(2,1)S(1)} %copy-done.1), custom_call_target="tpu_custom_call" | custom-call | tf_op jit(solution)/shard_map/project_rows/pallas_call | solution.py:199
  36.1 0.3 collective-permute-done.6.refs_1_
  36.4 7.5 %collective-permute-done.7.refs_2_ = bf16[3,64,896]{2,1,0:T(8,128)(2,1)S(1)} collective-permute-done((bf16[3,64,896]{2,1,0:T(8,128)(2,1)S(1)}, bf16[3,64,896]{2,1,0:T(8,128)(2,1)S(1)}, u32[]{:S(2)}, u32[]{:S(2)}) %collective-permute-start.7) | collective-permute-done | bytes 344096 | tf_op jit(solution)/shard_map/ppermute | solution.py:46
  44.0 0.7 unpack_rows.3.rows_ref.refs_0_
  44.7 1.5 %collective-permute-start.10 = (bf16[6,64,896]{2,1,0:T(8,128)(2,1)S(1)}, bf16[6,64,896]{2,1,0:T(8,128)(2,1)S(1)}, u32[]{:S(2)}, u32[]{:S(2)}) collective-permute-start(bf16[6,64,896]{2,1,0:T(8,128)(2,1)S(1)} %unpack_rows.3.rows_ref.refs_0_), channel_id=1, source_target_pairs={{0,1},{1,0},{2,3},{3,2},{4,5},{5,4},{6,7},{7,6},{8,9},{9,8},{10,11... | collective-permute-start | bytes 2064392 | tf_op jit(solution)/shard_map/ppermute | solution.py:46
  46.2 1.0 %collective-permute-start.13 = (bf16[2,2,64,896]{3,2,1,0:T(8,128)(2,1)S(1)}, bf16[2,2,64,896]{3,2,1,0:T(8,128)(2,1)S(1)}, u32[]{:S(2)}, u32[]{:S(2)}) collective-permute-start(bf16[2,2,64,896]{3,2,1,0:T(8,128)(2,1)S(1)} %get-tuple-element.139), channel_id=1, source_target_pairs={{0,12},{4,8},{8,4},{12,0},{1,13},{5,9},{9,5},{13,1},{2,14},{6,10},... | collective-permute-start | bytes 1376264 | tf_op jit(solution)/shard_map/ppermute | solution.py:46
  47.2 1.3 %collective-permute-start.12 = (bf16[2,2,64,896]{3,2,1,0:T(8,128)(2,1)S(1)}, bf16[2,2,64,896]{3,2,1,0:T(8,128)(2,1)S(1)}, u32[]{:S(2)}, u32[]{:S(2)}) collective-permute-start(bf16[2,2,64,896]{3,2,1,0:T(8,128)(2,1)S(1)} %get-tuple-element.138), channel_id=1, source_target_pairs={{0,8},{4,12},{8,0},{12,4},{1,9},{5,13},{9,1},{13,5},{2,10},{6,14},... | collective-permute-start | bytes 1376264 | tf_op jit(solution)/shard_map/ppermute | solution.py:46
  48.5 1.2 %collective-permute-start.11 = (bf16[2,2,64,896]{3,2,1,0:T(8,128)(2,1)S(1)}, bf16[2,2,64,896]{3,2,1,0:T(8,128)(2,1)S(1)}, u32[]{:S(2)}, u32[]{:S(2)}) collective-permute-start(bf16[2,2,64,896]{3,2,1,0:T(8,128)(2,1)S(1)} %get-tuple-element.137), channel_id=1, source_target_pairs={{0,4},{4,0},{8,12},{12,8},{1,5},{5,1},{9,13},{13,9},{2,6},{6,2},{1... | collective-permute-start | bytes 1376264 | tf_op jit(solution)/shard_map/ppermute | solution.py:46
  49.7 1.8 %project_rows.3 = (bf16[3,128,1024]{2,1,0:T(8,128)(2,1)S(1)}, bf16[3,128,1024]{2,1,0:T(8,128)(2,1)S(1)}) custom-call(bf16[6,64,896]{2,1,0:T(8,128)(2,1)S(1)} %unpack_rows.3.rows_ref.refs_0_, bf16[896,1024]{1,0:T(8,128)(2,1)S(1)} %copy-done, bf16[896,1024]{1,0:T(8,128)(2,1)S(1)} %copy-done.1), custom_call_target="tpu_custom_call" | custom-call | tf_op jit(solution)/shard_map/project_rows/pallas_call | solution.py:199
  51.6 6.1 %attend_blocks.3 = (bf16[3,64,1024]{2,1,0:T(8,128)(2,1)S(1)}, bf16[3,64,1024]{2,1,0:T(8,128)(2,1)S(1)}, bf16[896,768]{1,0:T(8,128)(2,1)S(1)}, bf16[3,256,768]{2,...) custom-call(s32[32]{0:T(128)S(1)} %reshape.62.id_ref, ...), custom_call_target="tpu_custom_call" | custom-call | tf_op jit(solution)/shard_map/attend_blocks/pallas_call | solution.py:256
  57.6 2.3 %weigh_grads.7 = (f32[896,768]{1,0:T(8,128)S(1)}, f32[896,768]{1,0:T(8,128)S(1)}) custom-call(bf16[896,768]{1,0:T(8,128)(2,1)S(1)} %get-tuple-element.171.refs_0_, bf16[3,256,768]{2,1,0:T(8,128)(2,1)S(1)} %get-tuple-element.128.refs_1_, bf16[3,256,768]{2,1,0:T(8,128)(2,1)S(1)} %get-tuple-element.129.refs_2_), custom_call_target="tpu_custom_call" | custom-call | tf_op jit(solution)/shard_map/weigh_grads/pallas_call | solution.py:299
  60.0 0.6 collective-permute-done.10.refs_1_
  60.6 6.0 %attend_blocks.4 = (bf16[3,64,1024]{2,1,0:T(8,128)(2,1)S(1)}, bf16[3,64,1024]{2,1,0:T(8,128)(2,1)S(1)}, bf16[896,768]{1,0:T(8,128)(2,1)S(1)}, bf16[3,256,768]{2,...) custom-call(s32[32]{0:T(128)S(1)} %reshape.62.id_ref, ...), custom_call_target="tpu_custom_call" | custom-call | tf_op jit(solution)/shard_map/attend_blocks/pallas_call | solution.py:256
  66.7 5.7 %attend_blocks.5 = (bf16[2,64,1024]{2,1,0:T(8,128)(2,1)S(1)}, bf16[2,64,1024]{2,1,0:T(8,128)(2,1)S(1)}, bf16[896,512]{1,0:T(8,128)(2,1)S(1)}, bf16[2,256,768]{2,...) custom-call(s32[32]{0:T(128)S(1)} %reshape.62.id_ref, ...), custom_call_target="tpu_custom_call" | custom-call | tf_op jit(solution)/shard_map/attend_blocks/pallas_call | solution.py:256
  72.3 1.1 %weigh_grads.11 = bf16[448,768]{1,0:T(8,128)(2,1)S(1)} custom-call(bf16[896,768]{1,0:T(8,128)(2,1)S(1)} %get-tuple-element.166.refs_0_, bf16[896,512]{1,0:T(8,128)(2,1)S(1)} %get-tuple-element.150.refs_1_, bf16[3,256,768]{2,1,0:T(8,128)(2,1)S(1)} %get-tuple-element.157.refs_2_, bf16[2,256,768]{2,1,0:T(8,128)(2,1)S(1)} %get-tuple-element.158.refs_3_, ...), custom_call_target="tpu_custom_call" | custom-call | tf_op jit(solution)/shard_map/weigh_grads/pallas_call | solution.py:299
  73.4 0.1 collective-permute-start.15
  73.5 1.1 %weigh_grads.9 = bf16[448,768]{1,0:T(8,128)(2,1)S(1)} custom-call(bf16[896,768]{1,0:T(8,128)(2,1)S(1)} %get-tuple-element.166.refs_0_, bf16[896,512]{1,0:T(8,128)(2,1)S(1)} %get-tuple-element.150.refs_1_, bf16[3,256,768]{2,1,0:T(8,128)(2,1)S(1)} %get-tuple-element.151.refs_2_, bf16[2,256,768]{2,1,0:T(8,128)(2,1)S(1)} %get-tuple-element.152.refs_3_, ...), custom_call_target="tpu_custom_call" | custom-call | tf_op jit(solution)/shard_map/weigh_grads/pallas_call | solution.py:299
  74.5 0.6 collective-permute-start.14
  75.1 1.1 %weigh_grads.8 = bf16[448,768]{1,0:T(8,128)(2,1)S(1)} custom-call(bf16[896,768]{1,0:T(8,128)(2,1)S(1)} %get-tuple-element.166.refs_0_, bf16[896,512]{1,0:T(8,128)(2,1)S(1)} %get-tuple-element.150.refs_1_, bf16[3,256,768]{2,1,0:T(8,128)(2,1)S(1)} %get-tuple-element.151.refs_2_, bf16[2,256,768]{2,1,0:T(8,128)(2,1)S(1)} %get-tuple-element.152.refs_3_, ...), custom_call_target="tpu_custom_call" | custom-call | tf_op jit(solution)/shard_map/weigh_grads/pallas_call | solution.py:299
  76.2 1.1 %weigh_grads.10 = bf16[448,768]{1,0:T(8,128)(2,1)S(1)} custom-call(bf16[896,768]{1,0:T(8,128)(2,1)S(1)} %get-tuple-element.166.refs_0_, bf16[896,512]{1,0:T(8,128)(2,1)S(1)} %get-tuple-element.150.refs_1_, bf16[3,256,768]{2,1,0:T(8,128)(2,1)S(1)} %get-tuple-element.157.refs_2_, bf16[2,256,768]{2,1,0:T(8,128)(2,1)S(1)} %get-tuple-element.158.refs_3_, ...), custom_call_target="tpu_custom_call" | custom-call | tf_op jit(solution)/shard_map/weigh_grads/pallas_call | solution.py:299
  77.3 0.2 fold_grads.9
  77.5 0.2 fold_grads.8
  77.7 0.7 collective-permute-start.16
  78.4 1.3 %collective-permute-start.17 = (bf16[2,112,768]{2,1,0:T(8,128)(2,1)S(1)}, bf16[2,112,768]{2,1,0:T(8,128)(2,1)S(1)}, u32[]{:S(2)}, u32[]{:S(2)}) collective-permute-start(bf16[2,112,768]{2,1,0:T(8,128)(2,1)S(1)} %get-tuple-element.164), channel_id=1, source_target_pairs={{0,8},{4,12},{8,0},{12,4},{1,9},{5,13},{9,1},{13,5},{2,10},{6,14},... | collective-permute-start | bytes 1032200 | tf_op jit(solution)/shard_map/ppermute | solution.py:46
  79.7 0.9 weigh_grads.12
  80.6 1.4 %weigh_grads.13 = (bf16[448,256]{1,0:T(8,128)(2,1)S(1)}, bf16[448,256]{1,0:T(8,128)(2,1)S(1)}, bf16[448,256]{1,0:T(8,128)(2,1)S(1)}, bf16[448,256]{1,0:T(8,128)(2,1)S(1)}) custom-call(bf16[896,768]{1,0:T(8,128)(2,1)S(1)} %get-tuple-element.166.refs_0_, bf16[896,512]{1,0:T(8,128)(2,1)S(1)} %get-tuple-element.150.refs_1_, ...), custom_call_target="tpu_custom_call" | custom-call | tf_op jit(solution)/shard_map/weigh_grads/pallas_call | solution.py:299
  81.9 0.1 collective-permute-start.18
  82.0 0.5 collective-permute-start.20
  82.5 1.0 %collective-permute-done.18 = bf16[448,256]{1,0:T(8,128)(2,1)S(1)} collective-permute-done((bf16[448,256]{1,0:T(8,128)(2,1)S(1)}, bf16[448,256]{1,0:T(8,128)(2,1)S(1)}, u32[]{:S(2)}, u32[]{:S(2)}) %collective-permute-start.18) | collective-permute-done | bytes 229408 | tf_op jit(solution)/shard_map/ppermute | solution.py:46
  83.5 0.1 fold_grads.12
  83.6 1.6 %collective-permute-start.19 = (bf16[2,112,256]{2,1,0:T(8,128)(2,1)S(1)}, bf16[2,112,256]{2,1,0:T(8,128)(2,1)S(1)}, u32[]{:S(2)}, u32[]{:S(2)}) collective-permute-start(bf16[2,112,256]{2,1,0:T(8,128)(2,1)S(1)} %get-tuple-element.179), channel_id=1, source_target_pairs={{0,4},{4,0},{8,12},{12,8},{1,5},{5,1},{9,13},{13,9},{2,6},{6,2},{1... | collective-permute-start | bytes 344072 | tf_op jit(solution)/shard_map/ppermute | solution.py:46
  85.2 0.7 collective-permute-start.21
  85.9 2.8 %collective-permute-done.16.refs_1_ = bf16[2,112,768]{2,1,0:T(8,128)(2,1)S(1)} collective-permute-done((bf16[2,112,768]{2,1,0:T(8,128)(2,1)S(1)}, bf16[2,112,768]{2,1,0:T(8,128)(2,1)S(1)}, u32[]{:S(2)}, u32[]{:S(2)}) %collective-permute-start.16) | collective-permute-done | bytes 344096 | tf_op jit(solution)/shard_map/ppermute | solution.py:46
  88.7 0.1 fold_grads.10
  88.7 1.5 %collective-permute-start.22 = (bf16[1,112,768]{2,1,0:T(8,128)(2,1)S(1)}, bf16[1,112,768]{2,1,0:T(8,128)(2,1)S(1)}, u32[]{:S(2)}, u32[]{:S(2)}) collective-permute-start(bf16[1,112,768]{2,1,0:T(8,128)(2,1)S(1)} %get-tuple-element.186), channel_id=1, source_target_pairs={{0,8},{4,12},{8,0},{12,4},{1,9},{5,13},{9,1},{13,5},{2,10},{6,14},... | collective-permute-start | bytes 516104 | tf_op jit(solution)/shard_map/ppermute | solution.py:46
  90.2 0.1 fold_grads.11
  90.3 0.6 collective-permute-start.23
  90.9 1.5 %collective-permute-start.24 = (bf16[1,112,256]{2,1,0:T(8,128)(2,1)S(1)}, bf16[1,112,256]{2,1,0:T(8,128)(2,1)S(1)}, u32[]{:S(2)}, u32[]{:S(2)}) collective-permute-start(bf16[1,112,256]{2,1,0:T(8,128)(2,1)S(1)} %get-tuple-element.188), channel_id=1, source_target_pairs={{0,8},{4,12},{8,0},{12,4},{1,9},{5,13},{9,1},{13,5},{2,10},{6,14},... | collective-permute-start | bytes 172040 | tf_op jit(solution)/shard_map/ppermute | solution.py:46
  92.4 0.8 collective-permute-start.25
  93.2 1.6 %pad_maximum_fusion = (bf16[8,64,1024]{2,1,0:T(8,128)(2,1)}, bf16[8,64,1024]{2,1,0:T(8,128)(2,1)}) fusion(bf16[2,64,1024]{2,1,0:T(8,128)(2,1)S(1)} %get-tuple-element.145, bf16[3,64,1024]{2,1,0:T(8,128)(2,1)S(1)} %get-tuple-element.140, bf16[3,64,1024]{2,1,0:T(8,128)(2,1)S(1)} %get-tuple-element.126, bf16[2,64,1024]{2,1,0:T(8,128)(2,1)S(1)} %get-tuple-element.148, ...), kind=kLoop, calls=%fused_computation | loop fusion | flops 2097152 | bytes 4194304 | tf_op jit(solution)/shard_map/concatenate | solution.py:476
  94.8 0.7 collective-permute-done.24.refs_6_
  95.4 1.2 %collective-permute-done.25.refs_7_ = bf16[1,112,256]{2,1,0:T(8,128)(2,1)S(1)} collective-permute-done((bf16[1,112,256]{2,1,0:T(8,128)(2,1)S(1)}, bf16[1,112,256]{2,1,0:T(8,128)(2,1)S(1)}, u32[]{:S(2)}, u32[]{:S(2)}) %collective-permute-start.25) | collective-permute-done | bytes 57376 | tf_op jit(solution)/shard_map/ppermute | solution.py:46
  96.7 1.0 %join_grads.1 = (f32[112,1024]{1,0:T(8,128)}, f32[112,1024]{1,0:T(8,128)}) custom-call(bf16[1,112,768]{2,1,0:T(8,128)(2,1)S(1)} %get-tuple-element.162.refs_0_, bf16[1,112,768]{2,1,0:T(8,128)(2,1)S(1)} %get-tuple-element.165.refs_1_, bf16[1,112,256]{2,1,0:T(8,128)(2,1)S(1)} %get-tuple-element.180.refs_2_, ...), custom_call_target="tpu_custom_call" | custom-call | tf_op jit(solution)/shard_map/join_grads/pallas_call | solution.py:350
  (30 shorter events, 0.2 us)
Async XLA Ops:
  1.5 8.0 %collective-permute-start.2 = (s32[32]{0:T(128)S(1)}, s32[32]{0:T(128)S(1)}, u32[]{:S(2)}, u32[]{:S(2)}) collective-permute-start(s32[32]{0:T(128)S(1)} %reshape.62.id_ref), channel_id=1, source_target_pairs={{0,12},{4,8},{8,4},{12,0},{1,13},{5,9},{9,5},{13,1},{2,14},{6,10},... | collective-permute-start | bytes 392 | tf_op jit(solution)/shard_map/ppermute | solution.py:46
  5.5 4.0 %collective-permute-start.1 = (s32[32]{0:T(128)S(1)}, s32[32]{0:T(128)S(1)}, u32[]{:S(2)}, u32[]{:S(2)}) collective-permute-start(s32[32]{0:T(128)S(1)} %reshape.62.id_ref), channel_id=1, source_target_pairs={{0,8},{4,12},{8,0},{12,4},{1,9},{5,13},{9,1},{13,5},{2,10},{6,14},... | collective-permute-start | bytes 392 | tf_op jit(solution)/shard_map/ppermute | solution.py:46
  6.0 3.5 %collective-permute-start = (s32[32]{0:T(128)S(1)}, s32[32]{0:T(128)S(1)}, u32[]{:S(2)}, u32[]{:S(2)}) collective-permute-start(s32[32]{0:T(128)S(1)} %reshape.62.id_ref), channel_id=1, source_target_pairs={{0,4},{4,0},{8,12},{12,8},{1,5},{5,1},{9,13},{13,9},{2,6},{6,2},{1... | collective-permute-start | bytes 392 | tf_op jit(solution)/shard_map/ppermute | solution.py:46
  6.2 2.0 %copy-start.4 = (bf16[1,2048,896]{2,1,0:T(8,128)(2,1)S(1)}, bf16[1,2048,896]{2,1,0:T(8,128)(2,1)}, u32[]{:S(2)}) copy-start(bf16[1,2048,896]{2,1,0:T(8,128)(2,1)} %param.8) | copy-start | bytes 11010052
  10.6 11.1 %collective-permute-start.3 = (bf16[3,64,896]{2,1,0:T(8,128)(2,1)S(1)}, bf16[3,64,896]{2,1,0:T(8,128)(2,1)S(1)}, u32[]{:S(2)}, u32[]{:S(2)}) collective-permute-start(bf16[3,64,896]{2,1,0:T(8,128)(2,1)S(1)} %get-tuple-element.99), channel_id=1, source_target_pairs={{0,4},{4,0},{8,12},{12,8},{1,5},{5,1},{9,13},{13,9},{2,6},{6,2},{1... | collective-permute-start | bytes 1032200 | tf_op jit(solution)/shard_map/ppermute | solution.py:46
  12.6 16.3 %collective-permute-start.4 = (bf16[3,64,896]{2,1,0:T(8,128)(2,1)S(1)}, bf16[3,64,896]{2,1,0:T(8,128)(2,1)S(1)}, u32[]{:S(2)}, u32[]{:S(2)}) collective-permute-start(bf16[3,64,896]{2,1,0:T(8,128)(2,1)S(1)} %get-tuple-element.102), channel_id=1, source_target_pairs={{0,8},{4,12},{8,0},{12,4},{1,9},{5,13},{9,1},{13,5},{2,10},{6,14},... | collective-permute-start | bytes 1032200 | tf_op jit(solution)/shard_map/ppermute | solution.py:46
  14.0 17.3 %collective-permute-start.5 = (bf16[3,64,896]{2,1,0:T(8,128)(2,1)S(1)}, bf16[3,64,896]{2,1,0:T(8,128)(2,1)S(1)}, u32[]{:S(2)}, u32[]{:S(2)}) collective-permute-start(bf16[3,64,896]{2,1,0:T(8,128)(2,1)S(1)} %get-tuple-element.105), channel_id=1, source_target_pairs={{0,12},{4,8},{8,4},{12,0},{1,13},{5,9},{9,5},{13,1},{2,14},{6,10},... | collective-permute-start | bytes 1032200 | tf_op jit(solution)/shard_map/ppermute | solution.py:46
  14.1 20.2 %copy-start.1 = (bf16[896,1024]{1,0:T(8,128)(2,1)S(1)}, bf16[896,1024]{1,0:T(8,128)(2,1)}, u32[]{:S(2)}) copy-start(bf16[896,1024]{1,0:T(8,128)(2,1)} %refs_5_.5) | copy-start | bytes 5505028
  15.5 18.8 %copy-start = (bf16[896,1024]{1,0:T(8,128)(2,1)S(1)}, bf16[896,1024]{1,0:T(8,128)(2,1)}, u32[]{:S(2)}) copy-start(bf16[896,1024]{1,0:T(8,128)(2,1)} %refs_4_.5) | copy-start | bytes 5505028
  21.6 14.8 %collective-permute-start.6 = (bf16[3,64,896]{2,1,0:T(8,128)(2,1)S(1)}, bf16[3,64,896]{2,1,0:T(8,128)(2,1)S(1)}, u32[]{:S(2)}, u32[]{:S(2)}) collective-permute-start(bf16[3,64,896]{2,1,0:T(8,128)(2,1)S(1)} %get-tuple-element.110), channel_id=1, source_target_pairs={{0,4},{4,0},{8,12},{12,8},{1,5},{5,1},{9,13},{13,9},{2,6},{6,2},{1... | collective-permute-start | bytes 1032200 | tf_op jit(solution)/shard_map/ppermute | solution.py:46
  28.9 15.1 %collective-permute-start.7 = (bf16[3,64,896]{2,1,0:T(8,128)(2,1)S(1)}, bf16[3,64,896]{2,1,0:T(8,128)(2,1)S(1)}, u32[]{:S(2)}, u32[]{:S(2)}) collective-permute-start(bf16[3,64,896]{2,1,0:T(8,128)(2,1)S(1)} %get-tuple-element.113), channel_id=1, source_target_pairs={{0,8},{4,12},{8,0},{12,4},{1,9},{5,13},{9,1},{13,5},{2,10},{6,14},... | collective-permute-start | bytes 1032200 | tf_op jit(solution)/shard_map/ppermute | solution.py:46
  31.4 12.6 %collective-permute-start.8 = (bf16[3,64,896]{2,1,0:T(8,128)(2,1)S(1)}, bf16[3,64,896]{2,1,0:T(8,128)(2,1)S(1)}, u32[]{:S(2)}, u32[]{:S(2)}) collective-permute-start(bf16[3,64,896]{2,1,0:T(8,128)(2,1)S(1)} %get-tuple-element.116), channel_id=1, source_target_pairs={{0,12},{4,8},{8,4},{12,0},{1,13},{5,9},{9,5},{13,1},{2,14},{6,10},... | collective-permute-start | bytes 1032200 | tf_op jit(solution)/shard_map/ppermute | solution.py:46
  32.7 18.9 %collective-permute-start.9 = (bf16[6,64,896]{2,1,0:T(8,128)(2,1)S(1)}, bf16[6,64,896]{2,1,0:T(8,128)(2,1)S(1)}, u32[]{:S(2)}, u32[]{:S(2)}) collective-permute-start(bf16[6,64,896]{2,1,0:T(8,128)(2,1)S(1)} %unpack_rows.2.rows_ref.refs_0_), channel_id=1, source_target_pairs={{0,1},{1,0},{2,3},{3,2},{4,5},{5,4},{6,7},{7,6},{8,9},{9,8},{10,11... | collective-permute-start | bytes 2064392 | tf_op jit(solution)/shard_map/ppermute | solution.py:46
  44.7 6.9 %copy-start.2 = (bf16[1,512,1024]{2,1,0:T(8,128)(2,1)S(1)}, bf16[1,512,1024]{2,1,0:T(8,128)(2,1)}, u32[]{:S(2)}) copy-start(bf16[1,512,1024]{2,1,0:T(8,128)(2,1)} %param.7) | copy-start | bytes 3145732
  44.7 6.9 %copy-start.3 = (bf16[1,512,1024]{2,1,0:T(8,128)(2,1)S(1)}, bf16[1,512,1024]{2,1,0:T(8,128)(2,1)}, u32[]{:S(2)}) copy-start(bf16[1,512,1024]{2,1,0:T(8,128)(2,1)} %param.13) | copy-start | bytes 3145732
  44.7 15.9 %collective-permute-start.10 = (bf16[6,64,896]{2,1,0:T(8,128)(2,1)S(1)}, bf16[6,64,896]{2,1,0:T(8,128)(2,1)S(1)}, u32[]{:S(2)}, u32[]{:S(2)}) collective-permute-start(bf16[6,64,896]{2,1,0:T(8,128)(2,1)S(1)} %unpack_rows.3.rows_ref.refs_0_), channel_id=1, source_target_pairs={{0,1},{1,0},{2,3},{3,2},{4,5},{5,4},{6,7},{7,6},{8,9},{9,8},{10,11... | collective-permute-start | bytes 2064392 | tf_op jit(solution)/shard_map/ppermute | solution.py:46
  46.2 20.4 %collective-permute-start.13 = (bf16[2,2,64,896]{3,2,1,0:T(8,128)(2,1)S(1)}, bf16[2,2,64,896]{3,2,1,0:T(8,128)(2,1)S(1)}, u32[]{:S(2)}, u32[]{:S(2)}) collective-permute-start(bf16[2,2,64,896]{3,2,1,0:T(8,128)(2,1)S(1)} %get-tuple-element.139), channel_id=1, source_target_pairs={{0,12},{4,8},{8,4},{12,0},{1,13},{5,9},{9,5},{13,1},{2,14},{6,10},... | collective-permute-start | bytes 1376264 | tf_op jit(solution)/shard_map/ppermute | solution.py:46
  47.2 19.4 %collective-permute-start.12 = (bf16[2,2,64,896]{3,2,1,0:T(8,128)(2,1)S(1)}, bf16[2,2,64,896]{3,2,1,0:T(8,128)(2,1)S(1)}, u32[]{:S(2)}, u32[]{:S(2)}) collective-permute-start(bf16[2,2,64,896]{3,2,1,0:T(8,128)(2,1)S(1)} %get-tuple-element.138), channel_id=1, source_target_pairs={{0,8},{4,12},{8,0},{12,4},{1,9},{5,13},{9,1},{13,5},{2,10},{6,14},... | collective-permute-start | bytes 1376264 | tf_op jit(solution)/shard_map/ppermute | solution.py:46
  48.5 18.2 %collective-permute-start.11 = (bf16[2,2,64,896]{3,2,1,0:T(8,128)(2,1)S(1)}, bf16[2,2,64,896]{3,2,1,0:T(8,128)(2,1)S(1)}, u32[]{:S(2)}, u32[]{:S(2)}) collective-permute-start(bf16[2,2,64,896]{3,2,1,0:T(8,128)(2,1)S(1)} %get-tuple-element.137), channel_id=1, source_target_pairs={{0,4},{4,0},{8,12},{12,8},{1,5},{5,1},{9,13},{13,9},{2,6},{6,2},{1... | collective-permute-start | bytes 1376264 | tf_op jit(solution)/shard_map/ppermute | solution.py:46
  73.4 3.9 %collective-permute-start.15 = (bf16[448,768]{1,0:T(8,128)(2,1)S(1)}, bf16[448,768]{1,0:T(8,128)(2,1)S(1)}, u32[]{:S(2)}, u32[]{:S(2)}) collective-permute-start(bf16[448,768]{1,0:T(8,128)(2,1)S(1)} %weigh_grads.11), channel_id=1, source_target_pairs={{0,16},{16,0},{1,17},{17,1},{2,18},{18,2},{3,19},{19,3},{4,20},{20... | collective-permute-start | bytes 2064392 | tf_op jit(solution)/shard_map/ppermute | solution.py:46
  74.5 2.9 %collective-permute-start.14 = (bf16[448,768]{1,0:T(8,128)(2,1)S(1)}, bf16[448,768]{1,0:T(8,128)(2,1)S(1)}, u32[]{:S(2)}, u32[]{:S(2)}) collective-permute-start(bf16[448,768]{1,0:T(8,128)(2,1)S(1)} %weigh_grads.9), channel_id=1, source_target_pairs={{0,16},{16,0},{1,17},{17,1},{2,18},{18,2},{3,19},{19,3},{4,20},{20... | collective-permute-start | bytes 2064392 | tf_op jit(solution)/shard_map/ppermute | solution.py:46
  77.7 11.0 %collective-permute-start.16 = (bf16[2,112,768]{2,1,0:T(8,128)(2,1)S(1)}, bf16[2,112,768]{2,1,0:T(8,128)(2,1)S(1)}, u32[]{:S(2)}, u32[]{:S(2)}) collective-permute-start(bf16[2,112,768]{2,1,0:T(8,128)(2,1)S(1)} %get-tuple-element.161), channel_id=1, source_target_pairs={{0,4},{4,0},{8,12},{12,8},{1,5},{5,1},{9,13},{13,9},{2,6},{6,2},{1... | collective-permute-start | bytes 1032200 | tf_op jit(solution)/shard_map/ppermute | solution.py:46
  78.4 11.9 %collective-permute-start.17 = (bf16[2,112,768]{2,1,0:T(8,128)(2,1)S(1)}, bf16[2,112,768]{2,1,0:T(8,128)(2,1)S(1)}, u32[]{:S(2)}, u32[]{:S(2)}) collective-permute-start(bf16[2,112,768]{2,1,0:T(8,128)(2,1)S(1)} %get-tuple-element.164), channel_id=1, source_target_pairs={{0,8},{4,12},{8,0},{12,4},{1,9},{5,13},{9,1},{13,5},{2,10},{6,14},... | collective-permute-start | bytes 1032200 | tf_op jit(solution)/shard_map/ppermute | solution.py:46
  81.9 1.6 %collective-permute-start.18 = (bf16[448,256]{1,0:T(8,128)(2,1)S(1)}, bf16[448,256]{1,0:T(8,128)(2,1)S(1)}, u32[]{:S(2)}, u32[]{:S(2)}) collective-permute-start(bf16[448,256]{1,0:T(8,128)(2,1)S(1)} %get-tuple-element.177), channel_id=1, source_target_pairs={{0,16},{16,0},{1,17},{17,1},{2,18},{18,2},{3,19},{19,3},{4,20},{20... | collective-permute-start | bytes 688136 | tf_op jit(solution)/shard_map/ppermute | solution.py:46
  82.0 3.1 %collective-permute-start.20 = (bf16[448,256]{1,0:T(8,128)(2,1)S(1)}, bf16[448,256]{1,0:T(8,128)(2,1)S(1)}, u32[]{:S(2)}, u32[]{:S(2)}) collective-permute-start(bf16[448,256]{1,0:T(8,128)(2,1)S(1)} %get-tuple-element.182), channel_id=1, source_target_pairs={{0,16},{16,0},{1,17},{17,1},{2,18},{18,2},{3,19},{19,3},{4,20},{20... | collective-permute-start | bytes 688136 | tf_op jit(solution)/shard_map/ppermute | solution.py:46
  83.6 7.4 %collective-permute-start.19 = (bf16[2,112,256]{2,1,0:T(8,128)(2,1)S(1)}, bf16[2,112,256]{2,1,0:T(8,128)(2,1)S(1)}, u32[]{:S(2)}, u32[]{:S(2)}) collective-permute-start(bf16[2,112,256]{2,1,0:T(8,128)(2,1)S(1)} %get-tuple-element.179), channel_id=1, source_target_pairs={{0,4},{4,0},{8,12},{12,8},{1,5},{5,1},{9,13},{13,9},{2,6},{6,2},{1... | collective-permute-start | bytes 344072 | tf_op jit(solution)/shard_map/ppermute | solution.py:46
  85.2 7.2 %collective-permute-start.21 = (bf16[2,112,256]{2,1,0:T(8,128)(2,1)S(1)}, bf16[2,112,256]{2,1,0:T(8,128)(2,1)S(1)}, u32[]{:S(2)}, u32[]{:S(2)}) collective-permute-start(bf16[2,112,256]{2,1,0:T(8,128)(2,1)S(1)} %get-tuple-element.184), channel_id=1, source_target_pairs={{0,8},{4,12},{8,0},{12,4},{1,9},{5,13},{9,1},{13,5},{2,10},{6,14},... | collective-permute-start | bytes 344072 | tf_op jit(solution)/shard_map/ppermute | solution.py:46
  88.7 7.9 %collective-permute-start.22 = (bf16[1,112,768]{2,1,0:T(8,128)(2,1)S(1)}, bf16[1,112,768]{2,1,0:T(8,128)(2,1)S(1)}, u32[]{:S(2)}, u32[]{:S(2)}) collective-permute-start(bf16[1,112,768]{2,1,0:T(8,128)(2,1)S(1)} %get-tuple-element.186), channel_id=1, source_target_pairs={{0,8},{4,12},{8,0},{12,4},{1,9},{5,13},{9,1},{13,5},{2,10},{6,14},... | collective-permute-start | bytes 516104 | tf_op jit(solution)/shard_map/ppermute | solution.py:46
  90.3 6.4 %collective-permute-start.23 = (bf16[1,112,768]{2,1,0:T(8,128)(2,1)S(1)}, bf16[1,112,768]{2,1,0:T(8,128)(2,1)S(1)}, u32[]{:S(2)}, u32[]{:S(2)}) collective-permute-start(bf16[1,112,768]{2,1,0:T(8,128)(2,1)S(1)} %get-tuple-element.187), channel_id=1, source_target_pairs={{0,4},{4,0},{8,12},{12,8},{1,5},{5,1},{9,13},{13,9},{2,6},{6,2},{1... | collective-permute-start | bytes 516104 | tf_op jit(solution)/shard_map/ppermute | solution.py:46
  90.9 4.5 %collective-permute-start.24 = (bf16[1,112,256]{2,1,0:T(8,128)(2,1)S(1)}, bf16[1,112,256]{2,1,0:T(8,128)(2,1)S(1)}, u32[]{:S(2)}, u32[]{:S(2)}) collective-permute-start(bf16[1,112,256]{2,1,0:T(8,128)(2,1)S(1)} %get-tuple-element.188), channel_id=1, source_target_pairs={{0,8},{4,12},{8,0},{12,4},{1,9},{5,13},{9,1},{13,5},{2,10},{6,14},... | collective-permute-start | bytes 172040 | tf_op jit(solution)/shard_map/ppermute | solution.py:46
  92.4 4.2 %collective-permute-start.25 = (bf16[1,112,256]{2,1,0:T(8,128)(2,1)S(1)}, bf16[1,112,256]{2,1,0:T(8,128)(2,1)S(1)}, u32[]{:S(2)}, u32[]{:S(2)}) collective-permute-start(bf16[1,112,256]{2,1,0:T(8,128)(2,1)S(1)} %get-tuple-element.189), channel_id=1, source_target_pairs={{0,4},{4,0},{8,12},{12,8},{1,5},{5,1},{9,13},{13,9},{2,6},{6,2},{1... | collective-permute-start | bytes 172040 | tf_op jit(solution)/shard_map/ppermute | solution.py:46
